TPU v7x, 32 devices: a whole 2x2x4 slice. The times are simulated.
32 devices in a mesh: expert: 8 (over z, x), tensor: 4 (over y, core).
Axes of the slice: x: 2, y: 2, z: 4, core: 2. Of those that a mesh axis runs over, the one named last changes fastest.
Arguments:
- tokens: bfloat16 [1024, 768], P('expert', 'tensor'), may hold values from -6 to 6
- first_gain: float32 [768], replicated, may hold values from 0.25 to 1.75
- second_gain: float32 [768], replicated, may hold values from 0.25 to 1.75
- qkv_weight: bfloat16 [3, 768, 768], P(None, None, 'tensor'), may hold values from -0.21875 to 0.21875
- out_weight: bfloat16 [768, 768], P('tensor'), may hold values from -0.875 to 0.875
- rel_table: float32 [32, 12], P(None, 'tensor'), may hold values from -6 to 6
- router_weight: bfloat16 [768, 8], replicated, may hold values from -0.15625 to 0.15625
- up_weight: bfloat16 [8, 768, 3072], P('expert', None, 'tensor'), may hold values from -0.21875 to 0.21875
- down_weight: bfloat16 [8, 3072, 768], P('expert', 'tensor'), may hold values from -0.109375 to 0.109375
- routes: int32 [1024, 2], P('expert'), may hold values from 0 to 7, all different within a row; in each aligned block of 128 rows (0 to 127, 128 to 255, ...) at most 40 rows name the same one
- lengths: int32 [8, 3], P('expert'), may hold values from 1 to 112, 128 in all within a row
- bucket_ids: int32 [112], replicated, may hold values from 0 to 31
- cotangent: bfloat16 [1024, 768], P('expert', 'tensor'), may hold values from -6 to 6
Outputs:
- output: bfloat16 [1024, 768], P('expert', 'tensor')
- input_grad: float32 [1024, 768], P('expert', 'tensor')
- first_gain_grad: float32 [768], replicated
- second_gain_grad: float32 [768], replicated
- qkv_grad: float32 [3, 768, 768], P(None, None, 'tensor')
- out_grad: float32 [768, 768], P('tensor')
- rel_grad: float32 [32, 12], P(None, 'tensor')
- router_grad: float32 [768, 8], replicated
- up_grad: float32 [8, 768, 3072], P('expert', None, 'tensor')
- down_grad: float32 [8, 3072, 768], P('expert', 'tensor')
Inputs may be any that keep to these rules, and one draw needn't show every extreme that they name: `routes`: each row names two different experts. Among the rows of one index of the expert axis no expert is named by more than 40 rows, a bound that some block reaches of them. The 3 lengths of one index of the expert axis sum to 128, and one of them is exactly 112.
All inputs are finite; a program needn't handle non-finite values.
Results may differ from a plain program's by a relative error of at most 0.015.
Values may be sent and summed in bfloat16 or wider, within the bound.
No kernel may reach another device: no remote copies, remote signals or barrier semaphores. Data moves between devices by JAX's collectives and lax.ppermute only.
A program may use at most 128 MiB of HBM per device.

v0:
```python
import jax
import jax.numpy as jnp
from jax import lax
from jax.sharding import PartitionSpec as P

epsilon = 1e-06
highest = lax.Precision.HIGHEST
big_negative = -1e30


def to_expert_rows(received, local_count):
    total_rows, capacity, width = received.shape
    senders = total_rows // local_count
    return (
        received.reshape(senders, local_count, capacity, width)
        .transpose(1, 0, 2, 3)
        .reshape(local_count, senders * capacity, width)
    )


def to_sender_rows(expert_rows, capacity):
    local_count, row_count, width = expert_rows.shape
    senders = row_count // capacity
    return (
        expert_rows.reshape(local_count, senders, capacity, width)
        .transpose(1, 0, 2, 3)
        .reshape(senders * local_count, capacity, width)
    )


def block_scores(query_block, key_heads, position, segment, bias_rows, score_scale):
    allowed = (segment[:, None] == segment[None, :]) & (position[None, :] <= position[:, None])
    distance = jnp.clip(position[:, None] - position[None, :], 0, bias_rows.shape[1] - 1)
    rel_bias = bias_rows[:, distance]
    scores = (
        jnp.einsum("hqd,hkd->hqk", query_block, key_heads, preferred_element_type=jnp.float32)
        * score_scale
        + rel_bias
    )
    return (jnp.where(allowed[None], scores, big_negative), distance)


def per_device(
    tokens,
    first_gain,
    second_gain,
    qkv_weight,
    out_weight,
    rel_table,
    router_weight,
    up_weight,
    down_weight,
    routes,
    lengths,
    bucket_ids,
    cotangent,
):
    gathered_x, gathered_dy = (
        lax.all_gather(tokens, "tensor", axis=1, tiled=True),
        lax.all_gather(cotangent, "tensor", axis=1, tiled=True),
    )
    x_rows = gathered_x.astype(jnp.float32)
    dy_rows = gathered_dy.astype(jnp.float32)
    tokens_here, model_width = x_rows.shape
    local_width = tokens.shape[1]
    column_start = lax.axis_index("tensor") * local_width
    heads_local = rel_table.shape[1]
    inner_local = qkv_weight.shape[2]
    head_size = inner_local // heads_local
    score_scale = head_size ** (-0.5)
    max_length = bucket_ids.shape[0]
    expert_count = router_weight.shape[1]
    local_experts = up_weight.shape[0]
    capacity = 5 * tokens_here // (2 * expert_count)
    inverse_one = lax.rsqrt(jnp.mean(x_rows * x_rows, axis=-1, keepdims=True) + epsilon)
    normed_one = (x_rows * inverse_one * first_gain).astype(jnp.bfloat16)
    projected = jnp.einsum(
        "td,jdi->jti", normed_one, qkv_weight, preferred_element_type=jnp.float32
    ).astype(jnp.bfloat16)
    head_split = projected.reshape(3, tokens_here, heads_local, head_size).transpose(0, 2, 1, 3)
    query_heads, key_heads, value_heads = (head_split[0], head_split[1], head_split[2])
    position = jnp.arange(tokens_here, dtype=jnp.int32)
    seq_ends = jnp.cumsum(lengths[0])
    segment = jnp.sum((position[:, None] >= seq_ends[None, :]).astype(jnp.int32), axis=1)
    bucket_hot = (
        bucket_ids[:, None] == jnp.arange(rel_table.shape[0], dtype=jnp.int32)[None, :]
    ).astype(jnp.float32)
    bias_rows = lax.dot_general(rel_table, bucket_hot, (((0,), (1,)), ((), ())), precision=highest)
    masked, distance = block_scores(
        query_heads, key_heads, position, segment, bias_rows, score_scale
    )
    row_peak = jnp.max(masked, axis=-1, keepdims=True)
    row_total = jnp.sum(jnp.exp(masked - row_peak), axis=-1, keepdims=True)
    log_total = row_peak + jnp.log(row_total)
    soft_weights = jnp.exp(masked - log_total).astype(jnp.bfloat16)
    attended_parts = jnp.einsum(
        "hqk,hkd->hqd", soft_weights, value_heads, preferred_element_type=jnp.float32
    ).astype(jnp.bfloat16)
    attended_flat = attended_parts.transpose(1, 0, 2).reshape(tokens_here, inner_local)
    attention_part = jnp.dot(attended_flat, out_weight, preferred_element_type=jnp.float32)
    attention = lax.psum(attention_part, "tensor")
    residual = x_rows + attention
    inverse_two = lax.rsqrt(jnp.mean(residual * residual, axis=-1, keepdims=True) + epsilon)
    normed_two = (residual * inverse_two * second_gain).astype(jnp.bfloat16)
    logits = jnp.dot(normed_two, router_weight, preferred_element_type=jnp.float32)
    route_hot = (
        routes[:, :, None] == jnp.arange(expert_count, dtype=jnp.int32)[None, None, :]
    ).astype(jnp.float32)
    chosen = jnp.sum(route_hot * logits[:, None, :], axis=2)
    gate_values = jax.nn.softmax(chosen, axis=1)
    flat_routes = routes.reshape(-1)
    pair_count = 2 * tokens_here
    flat_hot = (flat_routes[:, None] == jnp.arange(expert_count, dtype=jnp.int32)[None, :]).astype(
        jnp.int32
    )
    before = jnp.cumsum(flat_hot, axis=0) - flat_hot
    slot_index = jnp.sum(before * flat_hot, axis=1)
    destination = flat_routes * capacity + slot_index
    source = (
        jnp.full((expert_count * capacity,), pair_count, jnp.int32)
        .at[destination]
        .set(jnp.arange(pair_count, dtype=jnp.int32))
    )
    token_of = jnp.where(source == pair_count, tokens_here, source // 2)
    padded = jnp.concatenate([normed_two, jnp.zeros((1, model_width), jnp.bfloat16)], axis=0)
    send_rows = padded[token_of].reshape(expert_count, capacity, model_width)
    received = lax.all_to_all(send_rows, "expert", split_axis=0, concat_axis=0, tiled=True)
    expert_rows = to_expert_rows(received, local_experts)
    pre_act = jnp.einsum("erd,edf->erf", expert_rows, up_weight, preferred_element_type=jnp.float32)
    gelu_value, gelu_pull = jax.vjp(jax.nn.gelu, pre_act)
    activated = gelu_value.astype(jnp.bfloat16)
    expert_part = jnp.einsum(
        "erf,efd->erd", activated, down_weight, preferred_element_type=jnp.float32
    )
    expert_share = lax.psum_scatter(
        expert_part.astype(jnp.bfloat16), "tensor", scatter_dimension=2, tiled=True
    )
    share_full = lax.all_gather(expert_share, "tensor", axis=2, tiled=True)
    came_back = lax.all_to_all(
        to_sender_rows(share_full, capacity), "expert", split_axis=0, concat_axis=0, tiled=True
    )
    expert_full = came_back.reshape(-1, model_width)[destination].reshape(
        tokens_here, 2, model_width
    )
    expert_cols = lax.dynamic_slice_in_dim(expert_full, column_start, local_width, 2)
    residual_cols = lax.dynamic_slice_in_dim(residual, column_start, local_width, 1)
    mixture_cols = jnp.sum(gate_values[:, :, None] * expert_cols.astype(jnp.float32), axis=1)
    output = (residual_cols + mixture_cols).astype(jnp.bfloat16)
    gate_grad = jnp.sum(dy_rows[:, None, :] * expert_full.astype(jnp.float32), axis=2)
    expert_grad = (
        (gate_values[:, :, None] * dy_rows[:, None, :])
        .astype(jnp.bfloat16)
        .reshape(pair_count, model_width)
    )
    expert_grad = jnp.concatenate([expert_grad, jnp.zeros((1, model_width), jnp.bfloat16)], axis=0)
    grad_send = expert_grad[source].reshape(expert_count, capacity, model_width)
    grad_received = lax.all_to_all(grad_send, "expert", split_axis=0, concat_axis=0, tiled=True)
    grad_rows = to_expert_rows(grad_received, local_experts)
    d_activated = jnp.einsum(
        "erd,efd->erf", grad_rows, down_weight, preferred_element_type=jnp.float32
    )
    d_pre = gelu_pull(d_activated)[0].astype(jnp.bfloat16)
    down_grad = jnp.einsum("erf,erd->efd", activated, grad_rows, preferred_element_type=jnp.float32)
    up_grad = jnp.einsum("erd,erf->edf", expert_rows, d_pre, preferred_element_type=jnp.float32)
    d_rows_part = jnp.einsum("erf,edf->erd", d_pre, up_weight, preferred_element_type=jnp.float32)
    d_rows_share = lax.psum_scatter(d_rows_part, "tensor", scatter_dimension=2, tiled=True).astype(
        jnp.bfloat16
    )
    d_rows_full = lax.all_gather(d_rows_share, "tensor", axis=2, tiled=True)
    d_back = lax.all_to_all(
        to_sender_rows(d_rows_full, capacity), "expert", split_axis=0, concat_axis=0, tiled=True
    )
    slot_grads = d_back.reshape(-1, model_width)[destination].reshape(tokens_here, 2, model_width)
    d_expert_sum = jnp.sum(slot_grads.astype(jnp.float32), axis=1)
    gate_mean = jnp.sum(gate_values * gate_grad, axis=1, keepdims=True)
    d_chosen = gate_values * (gate_grad - gate_mean)
    d_logits = jnp.sum(route_hot * d_chosen[:, :, None], axis=1)
    router_grad = lax.dot_general(
        normed_two.astype(jnp.float32), d_logits, (((0,), (0,)), ((), ())), precision=highest
    )
    d_normed_two = d_expert_sum + lax.dot_general(
        d_logits, router_weight.astype(jnp.float32), (((1,), (1,)), ((), ())), precision=highest
    )
    second_grad = jnp.sum(d_normed_two * residual * inverse_two, axis=0)
    weighted_two = d_normed_two * second_gain
    d_residual = (
        dy_rows
        + inverse_two * weighted_two
        - residual * inverse_two**3 * jnp.mean(weighted_two * residual, axis=-1, keepdims=True)
    )
    d_attention = d_residual.astype(jnp.bfloat16)
    out_grad = lax.dot_general(
        attended_flat, d_attention, (((0,), (0,)), ((), ())), preferred_element_type=jnp.float32
    )
    d_attended = lax.dot_general(
        d_attention, out_weight, (((1,), (1,)), ((), ())), preferred_element_type=jnp.float32
    ).astype(jnp.bfloat16)
    d_heads = d_attended.reshape(tokens_here, heads_local, head_size).transpose(1, 0, 2)
    d_bias_rows = jnp.zeros((heads_local, max_length), jnp.float32)
    masked, distance = block_scores(
        query_heads, key_heads, position, segment, bias_rows, score_scale
    )
    probs = jnp.exp(masked - log_total)
    d_probs = jnp.einsum("hqd,hkd->hqk", d_heads, value_heads, preferred_element_type=jnp.float32)
    d_value = jnp.einsum(
        "hqk,hqd->hkd", probs.astype(jnp.bfloat16), d_heads, preferred_element_type=jnp.float32
    )
    centre = jnp.sum(probs * d_probs, axis=-1, keepdims=True)
    d_scores = (probs * (d_probs - centre)).astype(jnp.bfloat16)
    d_query_parts = (
        jnp.einsum("hqk,hkd->hqd", d_scores, key_heads, preferred_element_type=jnp.float32)
        * score_scale
    )
    d_key = (
        jnp.einsum("hqk,hqd->hkd", d_scores, query_heads, preferred_element_type=jnp.float32)
        * score_scale
    )
    flat_scores = d_scores.astype(jnp.float32).reshape(heads_local, -1)
    d_bias_rows = d_bias_rows.at[:, distance.reshape(-1)].add(flat_scores)
    d_stacked = jnp.stack([d_query_parts, d_key, d_value]).astype(jnp.bfloat16)
    d_projected = d_stacked.transpose(0, 2, 1, 3).reshape(3, tokens_here, inner_local)
    qkv_grad = jnp.einsum(
        "td,jti->jdi", normed_one, d_projected, preferred_element_type=jnp.float32
    )
    rel_grad = lax.dot_general(bucket_hot, d_bias_rows, (((0,), (1,)), ((), ())), precision=highest)
    d_normed_part = jnp.einsum(
        "jti,jdi->td", d_projected, qkv_weight, preferred_element_type=jnp.float32
    )
    d_normed_one = lax.psum(d_normed_part.astype(jnp.bfloat16), "tensor").astype(jnp.float32)
    first_grad = jnp.sum(d_normed_one * x_rows * inverse_one, axis=0)
    weighted_one = d_normed_one * first_gain
    d_input = (
        d_residual
        + inverse_one * weighted_one
        - x_rows * inverse_one**3 * jnp.mean(weighted_one * x_rows, axis=-1, keepdims=True)
    )
    input_grad = lax.dynamic_slice_in_dim(d_input, column_start, local_width, 1)
    summed = lax.psum(
        (qkv_grad, out_grad, rel_grad, router_grad, first_grad, second_grad), "expert"
    )
    return (
        output,
        input_grad,
        summed[4],
        summed[5],
        summed[0],
        summed[1],
        summed[2],
        summed[3],
        up_grad,
        down_grad,
    )


def solution(mesh):
    placed = (
        P("expert", "tensor"),
        P(),
        P(),
        P(None, None, "tensor"),
        P("tensor", None),
        P(None, "tensor"),
        P(),
        P("expert", None, "tensor"),
        P("expert", "tensor", None),
        P("expert", None),
        P("expert", None),
        P(),
        P("expert", "tensor"),
    )
    return jax.shard_map(
        per_device,
        mesh=mesh,
        in_specs=placed,
        out_specs=(
            P("expert", "tensor"),
            P("expert", "tensor"),
            P(),
            P(),
            P(None, None, "tensor"),
            P("tensor", None),
            P(None, "tensor"),
            P(),
            P("expert", None, "tensor"),
            P("expert", "tensor", None),
        ),
        check_vma=False,
    )
```

profile of v0, /device:TPU:0, one launch (start us, length us, event | category | flops | bytes accessed | tf_op | source)
XLA Modules:
  0.0 597.5 jit_solution(8581751914602507321)
XLA Ops:
  7.3 7.2 %all_gather.12 = bf16[128,768]{0,1:T(8,128)(2,1)S(1)} all-gather(bf16[128,192]{0,1:T(8,128)(2,1)} %param.13), channel_id=1, replica_groups=mesh['expert'=8,'tensor'=4] {'tensor'}, dimensions={1}, use_global_device_ids=true | all-gather | bytes 245760 | tf_op jit(solution)/shard_map/all_gather | solution.py:59
  15.3 1.7 fusion.42
  17.4 54.4 %gather_fusion = f32[16384,3]{1,0:T(8,128)} fusion(f32[3,112]{0,1:T(8,128)S(1)} %copy.122, s32[16384]{0:T(1024)S(1)} %fusion.38), kind=kCustom, calls=%fused_computation | custom fusion | bytes 458752 | tf_op jit(solution)/shard_map/gather | solution.py:34
  71.8 6.6 %copy.124 = f32[128,128,3]{0,1,2:T(8,128)S(1)} copy(f32[128,128,3]{2,1,0:T(8,128)} %bitcast.144) | data formatting | bytes 393216 | tf_op jit(solution)/shard_map/gather | solution.py:34
  82.6 1.4 scatter_custom_fusion
  84.6 29.9 %all-reduce.10.cloned.1.call-done = f32[128,768]{1,0:T(8,128)} async-done(((f32[128,768]{1,0:T(8,128)}), f32[128,768]{1,0:T(8,128)}) %all-reduce.10.cloned.1.call-update) | async-done | bytes 393232 | tf_op jit(solution)/shard_map/psum | solution.py:101
  114.6 1.1 multiply_reduce_fusion.3
  116.8 2.9 gather_fusion.1
  119.7 18.2 %all_to_all.20 = bf16[8,40,768]{2,1,0:T(8,128)(2,1)S(1)} all-to-all(bf16[8,40,768]{2,1,0:T(8,128)(2,1)} %bitcast.150), channel_id=1, replica_groups=mesh['expert'=8,'tensor'=4] {'expert'}, dimensions={0} | all-to-all | bytes 983040 | tf_op jit(solution)/shard_map/all_to_all | solution.py:127
  140.2 1.5 fusion
  141.7 3.5 copy.152
  146.1 20.9 %reduce-scatter.4.cloned.1.call-done = bf16[192,320]{1,0:T(8,128)(2,1)} async-done(((bf16[768,320]{1,0:T(8,128)(2,1)}), bf16[192,320]{1,0:T(8,128)(2,1)}) %reduce-scatter.4.cloned.1.call-update) | async-done | bytes 122896
  167.0 1.1 reshape_bitcast_fusion
  168.1 7.1 %all_gather.13 = bf16[1,320,768]{1,2,0:T(8,128)(2,1)S(1)} all-gather(bf16[1,320,192]{1,2,0:T(8,128)(2,1)S(1)} %copy.130), channel_id=1, replica_groups=mesh['expert'=8,'tensor'=4] {'tensor'}, dimensions={2}, use_global_device_ids=true | all-gather | bytes 614400 | tf_op jit(solution)/shard_map/all_gather | solution.py:138
  176.3 5.5 all-to-all-start.1
  181.8 5.6 all_gather.14
  188.3 1.1 mul.298
  189.4 1.7 mul.299
  191.4 4.7 all-to-all-done.1
  196.0 1.9 gather_fusion.2
  198.0 1.1 reshape.456
  199.1 1.6 multiply_reduce_fusion
  202.3 2.9 gather_fusion.3
  205.2 4.3 all-to-all-start.2
  209.5 1.2 dynamic-slice
  211.4 11.5 %all-to-all-done.2 = bf16[8,40,768]{2,1,0:T(8,128)(2,1)} async-done(((bf16[8,40,768]{2,1,0:T(8,128)(2,1)}), bf16[8,40,768]{2,1,0:T(8,128)(2,1)}, u32[]{:S(2)}, u32[]{:S(2)}) %all-to-all-start.2) | async-done | bytes 491552 | tf_op jit(solution)/shard_map/all_to_all | solution.py:157
  223.0 2.1 fusion.21
  225.8 1.5 convolution_bitcast_fusion.3
  227.4 3.5 copy.134
  230.8 162.6 %all-reduce.15 = bf16[1,320,768]{1,0,2:T(2,128)(2,1)} all-reduce(f32[1,320,768]{1,0,2:T(1,128)S(1)} %copy.134), channel_id=3, replica_groups=mesh['expert'=8,'tensor'=4] {'tensor'}, use_global_device_ids=true, to_apply=%region_16.17.clone | all-reduce | flops 245760 | bytes 1474560
  393.4 1.3 dynamic-slice_convert_fusion
  394.7 8.0 %all_gather.15 = bf16[1,320,768]{1,2,0:T(8,128)(2,1)S(1)} all-gather(bf16[1,320,192]{1,2,0:T(8,128)(2,1)S(1)} %copy.135), channel_id=1, replica_groups=mesh['expert'=8,'tensor'=4] {'tensor'}, dimensions={2}, use_global_device_ids=true | all-gather | bytes 614400 | tf_op jit(solution)/shard_map/all_gather | solution.py:169
  403.8 4.3 all-to-all-start.3
  409.4 13.0 %all-to-all-done.3 = bf16[8,40,768]{2,1,0:T(8,128)(2,1)S(1)} async-done(((bf16[8,40,768]{2,1,0:T(8,128)(2,1)}), bf16[8,40,768]{2,1,0:T(8,128)(2,1)S(1)}, u32[]{:S(2)}, u32[]{:S(2)}) %all-to-all-start.3) | async-done | bytes 491552 | tf_op jit(solution)/shard_map/all_to_all | solution.py:170
  422.4 1.3 gather_fusion.4
  425.1 1.9 multiply_reduce_fusion.1
  428.6 1.0 fusion.7
  429.6 1.7 convolution_bitcast_fusion.2
  431.6 1.0 fusion.34
  435.0 1.5 multiply_reduce_fusion.4
  437.5 2.2 convolution_bitcast_fusion.1
  439.8 3.4 convolution_bitcast_fusion
  443.4 5.1 copy.143
  448.5 98.3 %scatter_custom_fusion.1 = f32[3,112]{0,1:T(8,128)S(1)} fusion(s32[16384]{0:T(1024)} %bitcast.166, f32[16384,3]{1,0:T(8,128)} %copy.143, f32[]{:T(128)} %constant.28.clone.1), kind=kCustom, calls=%fused_computation.100 | custom fusion | flops 49152 | bytes 1856 | tf_op jit(solution)/shard_map/scatter-add | solution.py:219
  547.1 1.1 fusion.29
  548.2 1.2 fusion.32
  550.2 37.1 %all-reduce.3 = (f32[768]{0:T(1024)}, f32[768]{0:T(1024)}, f32[32,3]{0,1:T(4,128)}, f32[768,8]{0,1:T(8,128)}) all-reduce(f32[768]{0:T(1024)S(1)} %get-tuple-element.72, f32[768]{0:T(1024)S(1)} %copy-done.33, f32[32,3]{0,1:T(4,128)S(1)} %fusion.40, f32[768,8]{0,1:T(8,128)S(1)} %fusion.65), channel_id=1, replica_groups=mesh['expert'=8,'tensor'=4] {'expert'}, use_global_device_ids=true, to_apply=%region_26.27 | all-reduce | flops 7776 | bytes 62208 | tf_op jit(solution)/shard_map/psum | solution.py:238
  587.2 2.9 copy.167
  (198 shorter events, 25.7 us)
Async XLA Ops:
  7.2 133.0 %copy-start = (bf16[1,768,768]{2,1,0:T(8,128)(2,1)S(1)}, bf16[1,768,768]{2,1,0:T(8,128)(2,1)}, u32[]{:S(2)}) copy-start(bf16[1,768,768]{2,1,0:T(8,128)(2,1)} %param.21) | copy-start | bytes 3538948
  7.2 107.4 %all-reduce.10.cloned.1.call-start = ((), (), s32[]{:S(2)}) async-start(), calls=%async_computation.5 | async-start | bytes 786432 | tf_op jit(solution)/shard_map/psum | solution.py:101
  14.5 2.5 copy-start.51
  14.5 2.5 copy-start.53
  15.3 56.5 %copy-start.42 = (f32[128]{0:T(128)}, f32[128]{0:T(128)S(1)}, u32[]{:S(2)}) copy-start(f32[128]{0:T(128)S(1)} %get-tuple-element.88) | copy-start | bytes 1540
  17.0 62.1 %copy-start.13 = (bf16[128,3,192]{0,2,1:T(8,128)(2,1)}, bf16[128,3,192]{0,2,1:T(8,128)(2,1)S(1)}, u32[]{:S(2)}) copy-start(bf16[128,3,192]{0,2,1:T(8,128)(2,1)S(1)} %convert_element_type.103) | copy-start | bytes 442372
  71.8 6.6 %copy-start.52 = (s32[1,3]{1,0:T(1,128)S(1)}, s32[1,3]{1,0:T(1,128)}, u32[]{:S(2)}) copy-start(s32[1,3]{1,0:T(1,128)} %param.23) | copy-start | bytes 40
  78.4 2.0 copy-start.34
  79.4 36.9 %copy-start.29 = (f32[768]{0:T(1024)S(1)}, f32[768]{0:T(1024)}, u32[]{:S(2)}) copy-start(f32[768]{0:T(1024)} %param.15) | copy-start | bytes 9220
  80.4 86.6 %reduce-scatter.4.cloned.1.call-start = ((), (), s32[]{:S(2)}) async-start(), calls=%async_computation.7 | async-start | bytes 737280
  116.8 21.9 %copy-start.1 = (bf16[1,768,768]{2,1,0:T(8,128)(2,1)S(1)}, bf16[1,768,768]{2,1,0:T(8,128)(2,1)}, u32[]{:S(2)}) copy-start(bf16[1,768,768]{2,1,0:T(8,128)(2,1)} %param.20) | copy-start | bytes 3538948
  175.2 6.5 %copy-start.28 = (bf16[128,192]{0,1:T(8,128)(2,1)S(1)}, bf16[128,192]{0,1:T(8,128)(2,1)}, u32[]{:S(2)}) copy-start(bf16[128,192]{0,1:T(8,128)(2,1)} %param.25) | copy-start | bytes 147460
  176.3 19.8 %all-to-all-start.1 = ((bf16[8,40,768]{2,1,0:T(8,128)(2,1)}), bf16[8,40,768]{2,1,0:T(8,128)(2,1)S(1)}, u32[]{:S(2)}, u32[]{:S(2)}) async-start(bf16[8,40,768]{2,1,0:T(8,128)(2,1)} %bitcast.28), calls=%async_computation.1 | async-start | bytes 983040 | tf_op jit(solution)/shard_map/all_to_all | solution.py:139
  188.3 2.8 copy-start.47
  188.3 2.8 copy-start.26
  188.3 2.9 copy-start.35
  191.1 6.9 %copy-start.41 = (s32[1024]{0:T(1024)}, s32[1024]{0:T(1024)S(1)}, u32[]{:S(2)}) copy-start(s32[1024]{0:T(1024)S(1)} %pad_clamp_fusion.1) | copy-start | bytes 12292
  199.1 2.5 copy-start.8
  200.8 1.5 copy-start.37
  202.3 20.7 %copy-start.18 = (f32[320,768]{1,0:T(8,128)S(1)}, f32[320,768]{1,0:T(8,128)}, u32[]{:S(2)}) copy-start(f32[320,768]{1,0:T(8,128)} %copy-done.17) | copy-start | bytes 2949124
  205.2 17.8 %all-to-all-start.2 = ((bf16[8,40,768]{2,1,0:T(8,128)(2,1)}), bf16[8,40,768]{2,1,0:T(8,128)(2,1)}, u32[]{:S(2)}, u32[]{:S(2)}) async-start(bf16[8,40,768]{2,1,0:T(8,128)(2,1)} %bitcast.30), calls=%async_computation.2 | async-start | bytes 983040 | tf_op jit(solution)/shard_map/all_to_all | solution.py:157
  223.0 2.9 copy-start.2
  402.8 6.0 copy-start.38
  402.8 6.0 copy-start.40
  402.8 6.0 copy-start.48
  402.8 6.0 %copy-start.36 = (s32[128,2]{0,1:T(2,128)S(1)}, s32[128,2]{0,1:T(2,128)}, u32[]{:S(2)}) copy-start(s32[128,2]{0,1:T(2,128)} %param.22) | copy-start | bytes 3076
  403.8 18.6 %all-to-all-start.3 = ((bf16[8,40,768]{2,1,0:T(8,128)(2,1)}), bf16[8,40,768]{2,1,0:T(8,128)(2,1)S(1)}, u32[]{:S(2)}, u32[]{:S(2)}) async-start(bf16[8,40,768]{2,1,0:T(8,128)(2,1)} %bitcast.33), calls=%async_computation.3 | async-start | bytes 983040 | tf_op jit(solution)/shard_map/all_to_all | solution.py:170
  408.1 139.0 %all-reduce.12.cloned.1.call-start = ((), (), s32[]{:S(2)}) async-start(), calls=%async_computation.6 | async-start | bytes 393216 | tf_op jit(solution)/shard_map/psum | solution.py:229
  424.1 2.9 copy-start.7
  425.0 1.9 copy-start.30
  425.1 1.9 copy-start.45
  425.1 1.9 copy-start.49
  425.1 2.1 copy-start.16
  428.1 1.5 copy-start.31
  428.1 1.5 copy-start.43
  428.2 3.1 copy-start.11
  429.6 2.0 copy-start.24
  431.3 155.9 %all-reduce.14.cloned.1.call-start = ((), (), s32[]{:S(2)}) async-start(), calls=%async_computation.8 | async-start | bytes 4718592 | tf_op jit(solution)/shard_map/psum | solution.py:238
  432.7 2.3 copy-start.21
  432.7 4.7 copy-start.32
  432.7 4.8 copy-start.4
  432.7 4.8 copy-start.10
  437.5 2.2 copy-start.19
  439.8 3.4 copy-start.12
  443.4 103.5 %copy-start.54 = (s32[112]{0:T(128)S(1)}, s32[112]{0:T(128)}, u32[]{:S(2)}) copy-start(s32[112]{0:T(128)} %param.24) | copy-start | bytes 1348
  443.4 104.8 %copy-start.50 = (f32[128]{0:T(128)S(1)}, f32[128]{0:T(128)}, u32[]{:S(2)}) copy-start(f32[128]{0:T(128)} %get-tuple-element.87) | copy-start | bytes 1540
  448.5 101.7 %copy-start.33 = (f32[768]{0:T(1024)S(1)}, f32[768]{0:T(1024)}, u32[]{:S(2)}) copy-start(f32[768]{0:T(1024)} %get-tuple-element.70) | copy-start | bytes 9220
  587.2 2.9 copy-start.22
  (14 other events, 12.6 us)
Sparse Core Ops, SparseCore 0:
  80.5 34.0 all-reduce.9
  146.2 20.7 reduce-scatter.3
  431.4 30.3 all-reduce.11
  465.9 110.1 all-reduce.13
where the time goes:
time: 599 us; the launch traced here: 597 us
  blocking collectives  246 us (41%)
  other arithmetic  114 us (19%)
  local copies, waits for them, and re-layouts  107 us (18%)
  waiting for transfers between devices  80.1 us (13%)
  matrix products  21.6 us (4%)
  between operations  15.2 us (3%)
  starting transfers between devices  14.4 us (2%)
    unnamed x1, blocking collectives  163 us
    scatter-add x1, other arithmetic, per_device(): d_bias_rows = d_bias_rows.at[:, distance.reshape(-1)].add(flat_scores)  98.3 us
    gather x2, local copies, waits for them, and re-layouts, block_scores(): rel_bias = bias_rows[:, distance]  61 us
    psum x1, blocking collectives, per_device(): lax.psum((qkv_grad, out_grad, rel_grad, router_grad, first_grad, second_g...  37.1 us
    psum x1, waiting for transfers between devices, per_device(): attention = lax.psum(attention_part, 'tensor')  29.9 us
    unnamed x5, waiting for transfers between devices  21 us
    all_to_all x1, blocking collectives, per_device(): lax.all_to_all(send_rows, 'expert', split_axis=0, concat_axis=0, tiled=True)  18.2 us
    unnamed x120, local copies, waits for them, and re-layouts  17.4 us
  transfers between devices with their start and end apart: 7, of which 5 were waited for; matrix products, arithmetic and copies ran while one was open for 21% of the time, Pallas kernels for 0%

commit v1 on v0

v1 whole, which is shorter than its diff:
```python
import functools

import jax
import jax.numpy as jnp
from jax import lax
from jax.experimental import pallas as pl
from jax.experimental.pallas import tpu as pltpu
from jax.sharding import PartitionSpec as P

epsilon = 1e-06
highest = lax.Precision.HIGHEST
big_negative = -1e30
bf16 = jnp.bfloat16
f32 = jnp.float32
i32 = jnp.int32


def mm(a, b, contract=(1, 0), precision=None):
    return lax.dot_general(
        a,
        b,
        (((contract[0],), (contract[1],)), ((), ())),
        preferred_element_type=f32,
        precision=precision,
    )


def iota(shape, dim):
    return lax.broadcasted_iota(i32, shape, dim)


def split_hi_lo(v):
    hi = v.astype(bf16).astype(f32)
    return hi, v - hi


def lane_block(rows, values, width=64):
    lane = iota((rows, width), 1)
    block = jnp.zeros((rows, width), f32)
    for i, v in enumerate(values):
        block = jnp.where(lane == i, v, block)
    return block


def run(body, outs, *args, smem=0, scratch=(), vmem=None):
    return pl.pallas_call(
        body,
        out_shape=[jax.ShapeDtypeStruct(s, d) for s, d in outs],
        in_specs=[pl.BlockSpec(memory_space=pltpu.SMEM)] * smem
        + [pl.BlockSpec(memory_space=pltpu.VMEM)] * (len(args) - smem),
        out_specs=[pl.BlockSpec(memory_space=pltpu.VMEM)] * len(outs),
        scratch_shapes=list(scratch),
        compiler_params=pltpu.CompilerParams(vmem_limit_bytes=vmem or 24 * 2**20),
    )(*args)


def route_kernel(routes_t, routes, dy, disp, dest_t, dest, *, experts, cap):
    tok = routes.shape[0]
    rt = routes_t[...]
    x_of = iota((experts, tok), 0)
    m0 = (rt[0:1] == x_of).astype(f32)
    m1 = (rt[1:2] == x_of).astype(f32)
    earlier = (iota((tok, tok), 0) < iota((tok, tok), 1)).astype(f32).astype(bf16)
    counts = mm((m0 + m1).astype(bf16), earlier)
    d0 = rt[0:1].astype(f32) * cap + jnp.sum(m0 * counts, axis=0, keepdims=True)
    d1 = rt[1:2].astype(f32) * cap + jnp.sum(m1 * counts, axis=0, keepdims=True)
    row = iota((experts * cap, tok), 0).astype(f32)
    place = ((row == d0) | (row == d1)).astype(f32).astype(bf16)
    disp[...] = mm(place, dy[...]).astype(bf16)
    dest_t[0:1, :] = d0
    dest_t[1:2, :] = d1
    rc = routes[...]
    x_lane = iota((tok, experts), 1)
    n0 = (rc[:, 0:1] == x_lane).astype(f32)
    n1 = (rc[:, 1:2] == x_lane).astype(f32)
    later = (iota((tok, tok), 1) < iota((tok, tok), 0)).astype(f32).astype(bf16)
    counts_c = mm(later, (n0 + n1).astype(bf16))
    dest[:, 0:1] = rc[:, 0:1].astype(f32) * cap + jnp.sum(n0 * counts_c, axis=1, keepdims=True)
    dest[:, 1:2] = rc[:, 1:2].astype(f32) * cap + jnp.sum(n1 * counts_c, axis=1, keepdims=True)


def skew(values, sign):
    n = values.shape[0]
    row = iota(values.shape, 0)
    bit = 1
    while bit < n:
        moved = pltpu.roll(values, bit if sign > 0 else n - bit, 1)
        values = jnp.where((row & bit) != 0, moved, values)
        bit *= 2
    return values


def attention_kernel(
    ids, lengths, x0, x1, x2, x3, gain, qkv_w, out_w, table, buckets,
    own, p1, p2, p3, h1, inv1, heads, probs, attended,
    xs, parts, *, n_t,
):
    tok, width = x0.shape
    n_heads = table.shape[1]
    size = width // n_heads
    model = n_t * width
    r = ids[0]
    for k, x in enumerate((x0, x1, x2, x3)):
        xs[lax.rem(r + n_t - k, n_t)] = x[...].astype(f32)
    total = jnp.zeros((tok, 1), f32)
    for s in range(n_t):
        total += jnp.sum(xs[s] * xs[s], axis=1, keepdims=True)
    inverse = lax.rsqrt(total / model + epsilon)
    inv1[...] = inverse
    for s in range(n_t):
        h1[s] = (xs[s] * inverse * gain[s]).astype(bf16)
    for j in range(3):
        acc = jnp.zeros((tok, width), f32)
        for s in range(n_t):
            acc += mm(h1[s], qkv_w[j, s * width:(s + 1) * width, :])
        heads[j] = acc.astype(bf16)
    key_pos = iota((tok, tok), 0)
    query_pos = iota((tok, tok), 1)
    end0 = lengths[0, 0]
    end1 = end0 + lengths[0, 1]
    seg_k = (key_pos >= end0).astype(i32) + (key_pos >= end1).astype(i32)
    seg_q = (query_pos >= end0).astype(i32) + (query_pos >= end1).astype(i32)
    allowed = (seg_k == seg_q) & (key_pos <= query_pos)
    hot = (buckets[...] == iota((table.shape[0], tok), 0)).astype(f32)
    for h in range(n_heads):
        cols = slice(h * size, (h + 1) * size)
        bias = jnp.sum(hot * table[:, h:h + 1], axis=0, keepdims=True)
        bias = skew(jnp.broadcast_to(bias, (tok, tok)), 1)
        scores = mm(heads[1, :, cols], heads[0, :, cols], (1, 1)) * (size ** -0.5) + bias
        scores = jnp.where(allowed, scores, big_negative)
        peak = jnp.max(scores, axis=0, keepdims=True)
        weights = jnp.exp(scores - peak)
        prob = weights / jnp.sum(weights, axis=0, keepdims=True)
        probs[h] = prob
        attended[:, cols] = mm(prob.astype(bf16), heads[2, :, cols], (0, 0)).astype(bf16)
    for s in range(n_t):
        parts[s] = mm(attended[...], out_w[:, s * width:(s + 1) * width])
    own[...] = parts[r]
    for k, p in ((1, p1), (2, p2), (3, p3)):
        p[...] = parts[lax.rem(r + k, n_t)].astype(bf16)


def dispatch_kernel(
    ids, own, p1, p2, p3, tokens, gain, router, routes, dest_t,
    rows, token_pack, residual, pack,
):
    tok, width = tokens.shape
    experts = router.shape[1]
    r = ids[0]
    res = tokens[...].astype(f32) + own[...] + (
        p1[...].astype(f32) + p2[...].astype(f32) + p3[...].astype(f32)
    )
    residual[...] = res
    scaled = (res * gain[r]).astype(bf16)
    square = jnp.sum(res * res, axis=1, keepdims=True)
    logits = mm(scaled, router[pl.ds(pl.multiple_of(r * width, 64), width), :])
    x_lane = iota((tok, experts), 1)
    rc = routes[...]
    zero = jnp.zeros_like(logits)
    c0 = jnp.sum(jnp.where(rc[:, 0:1] == x_lane, logits, zero), axis=1, keepdims=True)
    c1 = jnp.sum(jnp.where(rc[:, 1:2] == x_lane, logits, zero), axis=1, keepdims=True)
    stats = lane_block(tok, split_hi_lo(square) + split_hi_lo(c0 - c1)).astype(bf16)
    token_pack[:, 0:width] = res.astype(bf16)
    token_pack[:, width:] = stats
    pack[:, 0:width] = scaled
    pack[:, width:] = stats
    total_rows = rows.shape[0]
    row = iota((total_rows, tok), 0).astype(f32)
    place0 = (row == dest_t[0:1, :]).astype(f32)
    place1 = (row == dest_t[1:2, :]).astype(f32)
    both = mm((place0 + place1).astype(bf16), pack[...])
    signed = mm((place0 - place1).astype(bf16), pack[...])
    lane = iota(both.shape, 1)
    rows[...] = jnp.where(lane >= width + 2, signed, both).astype(bf16)


def total_stats(packs, width):
    total = packs[0][:, width:].astype(f32)
    for p in packs[1:]:
        total += p[:, width:].astype(f32)
    return total


def gelu_pair(a):
    c = 0.7978845608028654
    t = jnp.tanh(c * (a + 0.044715 * a * a * a))
    value = 0.5 * a * (1.0 + t)
    slope = 0.5 * (1.0 + t) + 0.5 * a * (1.0 - t * t) * c * (1.0 + 3 * 0.044715 * a * a)
    return value, slope


def expert_kernel(
    ids, h0, h1, h2, h3, g0, g1, g2, g3, up, down,
    c0, c1, c2, c3, u, z, de, da,
    hs, gs, chunks, *, n_t,
):
    width = g0.shape[1]
    model = n_t * width
    r = ids[0]
    packs = (h0, h1, h2, h3)
    for k, (h, g) in enumerate(zip(packs, (g0, g1, g2, g3))):
        s = lax.rem(r + n_t - k, n_t)
        hs[s] = h[:, 0:width].astype(f32)
        gs[s] = g[...].astype(f32)
    stats = total_stats(packs, width)
    inverse = lax.rsqrt((stats[:, 0:1] + stats[:, 1:2]) / model + epsilon)
    gate = 1.0 / (1.0 + jnp.exp(-inverse * (stats[:, 2:3] + stats[:, 3:4])))
    for s in range(n_t):
        cols = slice(s * width, (s + 1) * width)
        u[:, cols] = (hs[s] * inverse).astype(bf16)
        de[:, cols] = (gs[s] * gate).astype(bf16)
    value, slope = gelu_pair(mm(u[...], up[0]))
    z[...] = value.astype(bf16)
    da[...] = (mm(de[...], down[0], (1, 1)) * slope).astype(bf16)
    eo = mm(z[...], down[0]).astype(bf16)
    du = mm(da[...], up[0], (1, 1)).astype(bf16)
    for s in range(n_t):
        cols = slice(s * width, (s + 1) * width)
        chunks[s, :, 0:width] = eo[:, cols]
        chunks[s, :, width:] = du[:, cols]
    for k, c in enumerate((c0, c1, c2, c3)):
        c[...] = chunks[lax.rem(r + k, n_t)]


def expert_grad_kernel(u, z, de, da, up_grad, down_grad):
    up_grad[0] = mm(u[...], da[...], (0, 0))
    down_grad[0] = mm(z[...], de[...], (0, 0))


def gates_of(stats, model):
    inverse = lax.rsqrt((stats[:, 0:1] + stats[:, 1:2]) / model + epsilon)
    delta = inverse * (stats[:, 2:3] + stats[:, 3:4])
    return inverse, 1.0 / (1.0 + jnp.exp(-delta)), 1.0 / (1.0 + jnp.exp(delta))


def combine_kernel(t0, t1, t2, t3, back, dest, dy, residual, output, pack, *, n_t):
    tok, width = dy.shape
    inverse, gate0, gate1 = gates_of(total_stats((t0, t1, t2, t3), width), n_t * width)
    lane = iota((tok, back.shape[0]), 1).astype(f32)
    pick0 = (lane == dest[:, 0:1]).astype(f32)
    pick1 = (lane == dest[:, 1:2]).astype(f32)
    e0 = mm(pick0.astype(bf16), back[:, 0:width])
    e1 = mm(pick1.astype(bf16), back[:, 0:width])
    du = mm((pick0 + pick1).astype(bf16), back[:, width:])
    output[...] = (residual[...] + gate0 * e0 + gate1 * e1).astype(bf16)
    dy_cols = dy[...].astype(f32)
    dg0 = jnp.sum(dy_cols * e0, axis=1, keepdims=True)
    dg1 = jnp.sum(dy_cols * e1, axis=1, keepdims=True)
    pack[:, 0:width] = du.astype(bf16)
    pack[:, width:] = lane_block(tok, split_hi_lo(dg0) + split_hi_lo(dg1)).astype(bf16)


def backward_kernel(
    ids, b0, b1, b2, b3, t0, t1, t2, t3, y0, y1, y2, y3,
    routes, router, gain, out_w, qkv_w, heads, probs, inv1, attended, h1, buckets,
    c0, c1, c2, c3, dr1_own, d_proj, d_att, d_logits, gain_grad, d_scores,
    bs, ts, ys, dr, d_o, chunks, *, n_t,
):
    tok, width = y0.shape
    experts = router.shape[1]
    n_heads = probs.shape[0]
    size = width // n_heads
    model = n_t * width
    r = ids[0]
    for k in range(n_t):
        s = lax.rem(r + n_t - k, n_t)
        bs[s] = (b0, b1, b2, b3)[k][:, 0:width].astype(f32)
        ts[s] = (t0, t1, t2, t3)[k][:, 0:width].astype(f32)
        ys[s] = (y0, y1, y2, y3)[k][...].astype(f32)
    inverse, gate0, gate1 = gates_of(total_stats((t0, t1, t2, t3), width), model)
    back = total_stats((b0, b1, b2, b3), width)
    dg0 = back[:, 0:1] + back[:, 1:2]
    dg1 = back[:, 2:3] + back[:, 3:4]
    mean_gate = gate0 * dg0 + gate1 * dg1
    rc = routes[...]
    x_lane = iota((tok, experts), 1)
    dlog = jnp.where(rc[:, 0:1] == x_lane, gate0 * (dg0 - mean_gate), 0.0) + jnp.where(
        rc[:, 1:2] == x_lane, gate1 * (dg1 - mean_gate), 0.0
    )
    d_logits[...] = dlog
    dot = jnp.zeros((tok, 1), f32)
    for s in range(n_t):
        from_router = mm(
            dlog, router[s * width:(s + 1) * width, :].astype(f32), (1, 1), precision=highest
        )
        dh2 = bs[s] + from_router
        weighted = dh2 * gain[s]
        gain_grad[s] = jnp.sum(dh2 * ts[s] * inverse, axis=0, keepdims=True)
        dot += jnp.sum(weighted * ts[s], axis=1, keepdims=True)
        bs[s] = weighted
    dot = dot * (inverse * inverse * inverse / model)
    for s in range(n_t):
        value = ys[s] + inverse * bs[s] - ts[s] * dot
        dr[s] = value
        d_att[s] = value.astype(bf16)
    dr1_own[...] = dr[r]
    acc = jnp.zeros((tok, width), f32)
    for s in range(n_t):
        acc += mm(d_att[s], out_w[:, s * width:(s + 1) * width], (1, 1))
    d_o[...] = acc.astype(bf16)
    scale = size ** -0.5
    for h in range(n_heads):
        cols = slice(h * size, (h + 1) * size)
        q, k, v = heads[0, :, cols], heads[1, :, cols], heads[2, :, cols]
        d_oh = d_o[:, cols]
        prob = probs[h]
        d_prob = mm(v, d_oh, (1, 1))
        centre = jnp.sum(prob * d_prob, axis=0, keepdims=True)
        ds = (prob * (d_prob - centre)).astype(bf16)
        d_scores[h] = ds
        d_proj[0, :, cols] = (mm(ds, k, (0, 0)) * scale).astype(bf16)
        d_proj[1, :, cols] = (mm(ds, q) * scale).astype(bf16)
        d_proj[2, :, cols] = mm(prob.astype(bf16), d_oh).astype(bf16)
    row_dot = jnp.zeros((tok, 1), f32)
    for j in range(3):
        row_dot += jnp.sum(
            d_proj[j].astype(f32) * heads[j].astype(f32), axis=1, keepdims=True
        )
    stats = lane_block(tok, split_hi_lo(row_dot)).astype(bf16)
    for s in range(n_t):
        acc = jnp.zeros((tok, width), f32)
        for j in range(3):
            acc += mm(d_proj[j], qkv_w[j, s * width:(s + 1) * width, :], (1, 1))
        chunks[s, :, 0:width] = acc.astype(bf16)
        chunks[s, :, width:] = stats
    for k, c in enumerate((c0, c1, c2, c3)):
        c[...] = chunks[lax.rem(r + k, n_t)]


def weight_grad_kernel(
    ids, t0, t1, t2, t3, d_logits, gain, h1, d_proj, attended, d_att, d_scores, buckets, qkv_w,
    qkv_grad, out_grad, first, rel_grad, router_grad, ts, *, n_t,
):
    tok, width = t0.shape[0], d_proj.shape[2]
    r = ids[0]
    packs = (t0, t1, t2, t3)
    for k, t in enumerate(packs):
        ts[lax.rem(r + n_t - k, n_t)] = t[:, 0:width].astype(f32)
    inverse, _, _ = gates_of(total_stats(packs, width), n_t * width)
    ones = jnp.ones((8, width), f32)
    for s in range(n_t):
        rows = slice(s * width, (s + 1) * width)
        product = jnp.zeros((width, width), f32)
        for j in range(3):
            grad = mm(h1[s], d_proj[j], (0, 0))
            qkv_grad[j, rows, :] = grad.astype(bf16)
            product += grad * qkv_w[j, rows, :].astype(f32)
        first[s] = mm(ones, product, (1, 1), precision=highest)[0:1] / gain[0, s]
        out_grad[:, rows] = mm(attended[...], d_att[s], (0, 0)).astype(bf16)
        normed = (ts[s] * inverse * gain[1, s]).astype(bf16).astype(f32)
        router_grad[rows, :] = mm(normed, d_logits[...], (0, 0), precision=highest)
    hot = (buckets[...] == iota((rel_grad.shape[0], tok), 0)).astype(f32)
    for h in range(d_scores.shape[0]):
        diagonal = jnp.sum(skew(d_scores[h].astype(f32), -1), axis=0, keepdims=True)
        rel_grad[:, h:h + 1] = jnp.sum(hot * diagonal, axis=1, keepdims=True)


def per_device(
    tokens,
    first_gain,
    second_gain,
    qkv_weight,
    out_weight,
    rel_table,
    router_weight,
    up_weight,
    down_weight,
    routes,
    lengths,
    bucket_ids,
    cotangent,
    *,
    n_t,
    n_e,
):
    tok, width = tokens.shape
    model = n_t * width
    experts = router_weight.shape[1]
    cap = 5 * tok // (2 * experts)
    rows = experts * cap
    n_heads = rel_table.shape[1]
    n_buckets = rel_table.shape[0]

    def shift(v, k):
        return lax.ppermute(v, "tensor", [(i, (i + k) % n_t) for i in range(n_t)])

    def around(v):
        return [v] + [shift(v, k) for k in range(1, n_t)]

    def exchange(v):
        w = v.shape[-1]
        return lax.all_to_all(
            v.reshape(n_e, rows // n_e, w), "expert", split_axis=0, concat_axis=0, tiled=True
        ).reshape(rows, w)

    ids = jnp.stack([lax.axis_index("tensor"), lax.axis_index("expert")]).astype(i32)
    gain_one = first_gain.reshape(n_t, 1, width)
    gain_two = second_gain.reshape(n_t, 1, width)
    buckets = jnp.pad(bucket_ids, (0, tok - bucket_ids.shape[0]), constant_values=-1)[None, :]

    xs = around(tokens)
    dys = around(cotangent)
    dy_rows, dest_t, dest = run(
        functools.partial(route_kernel, experts=experts, cap=cap),
        [((rows, width), bf16), ((2, tok), f32), ((tok, 2), f32)],
        routes.T, routes, cotangent,
    )
    dy_rows = around(exchange(dy_rows))

    own, p1, p2, p3, h1, inv1, heads, probs, attended = run(
        functools.partial(attention_kernel, n_t=n_t),
        [((tok, width), f32)]
        + [((tok, width), bf16)] * 3
        + [
            ((n_t, tok, width), bf16),
            ((tok, 1), f32),
            ((3, tok, width), bf16),
            ((n_heads, tok, tok), f32),
            ((tok, width), bf16),
        ],
        ids, lengths, *xs, gain_one, qkv_weight, out_weight, rel_table, buckets,
        smem=2,
        scratch=[pltpu.VMEM((n_t, tok, width), f32), pltpu.VMEM((n_t, tok, width), f32)],
    )
    got = [shift(p, k) for k, p in ((1, p1), (2, p2), (3, p3))]
    send_rows, token_pack, residual = run(
        dispatch_kernel,
        [((rows, 256), bf16), ((tok, 256), bf16), ((tok, width), f32)],
        ids, own, *got, tokens, gain_two, router_weight, routes, dest_t,
        smem=1,
        scratch=[pltpu.VMEM((tok, 256), bf16)],
    )
    in_rows = around(exchange(send_rows))
    token_packs = around(token_pack)

    c0, c1, c2, c3, u, z, de, da = run(
        functools.partial(expert_kernel, n_t=n_t),
        [((rows, 2 * width), bf16)] * 4 + [((rows, model), bf16)] * 4,
        ids, *in_rows, *dy_rows, up_weight, down_weight,
        smem=1,
        scratch=[
            pltpu.VMEM((n_t, rows, width), f32),
            pltpu.VMEM((n_t, rows, width), f32),
            pltpu.VMEM((n_t, rows, 2 * width), bf16),
        ],
    )
    got = [shift(c, k) for k, c in ((1, c1), (2, c2), (3, c3))]
    summed = c0.astype(f32)
    for c in got:
        summed = summed + c.astype(f32)
    back = exchange(summed.astype(bf16))
    up_grad, down_grad = run(
        expert_grad_kernel,
        [(up_weight.shape, f32), (down_weight.shape, f32)],
        u, z, de, da,
    )
    output, back_pack = run(
        functools.partial(combine_kernel, n_t=n_t),
        [((tok, width), bf16), ((tok, 256), bf16)],
        *token_packs, back, dest, cotangent, residual,
    )
    back_packs = around(back_pack)

    c0, c1, c2, c3, dr1, d_proj, d_att, d_logits, second, d_scores = run(
        functools.partial(backward_kernel, n_t=n_t),
        [((tok, 256), bf16)] * 4
        + [
            ((tok, width), f32),
            ((3, tok, width), bf16),
            ((n_t, tok, width), bf16),
            ((tok, experts), f32),
            ((n_t, 1, width), f32),
            ((n_heads, tok, tok), bf16),
        ],
        ids, *back_packs, *token_packs, *dys, routes, router_weight, gain_two, out_weight,
        qkv_weight, heads, probs, inv1, attended, h1, buckets,
        smem=1,
        scratch=[pltpu.VMEM((n_t, tok, width), f32)] * 4
        + [pltpu.VMEM((tok, width), bf16), pltpu.VMEM((n_t, tok, 256), bf16)],
    )
    got = [shift(c, k) for k, c in ((1, c1), (2, c2), (3, c3))]
    qkv_grad, out_grad, first, rel_grad, router_grad = run(
        functools.partial(weight_grad_kernel, n_t=n_t),
        [
            (qkv_weight.shape, bf16),
            (out_weight.shape, bf16),
            ((n_t, 1, width), f32),
            ((n_buckets, n_heads), f32),
            (router_weight.shape, f32),
        ],
        ids, *token_packs, d_logits, jnp.stack([gain_one, gain_two]), h1, d_proj, attended, d_att,
        d_scores, buckets, qkv_weight,
        smem=1,
        scratch=[pltpu.VMEM((n_t, tok, width), f32)],
    )
    total = c0.astype(f32)
    for c in got:
        total = total + c.astype(f32)
    row_dot = (total[:, width:width + 1] + total[:, width + 1:width + 2]) / model
    gain_cols = lax.dynamic_index_in_dim(gain_one, lax.axis_index("tensor"), 0, False)
    input_grad = (
        dr1 + inv1 * (total[:, :width] * gain_cols) - tokens.astype(f32) * inv1**2 * row_dot
    )
    qkv_grad, out_grad = lax.psum((qkv_grad, out_grad), "expert")
    second, rel_grad, router_grad = lax.psum((second, rel_grad, router_grad), "expert")
    first = lax.psum(first, ("expert", "tensor"))
    return (
        output,
        input_grad,
        first.reshape(model),
        second.reshape(model),
        qkv_grad.astype(f32),
        out_grad.astype(f32),
        rel_grad,
        router_grad,
        up_grad,
        down_grad,
    )


def solution(mesh):
    placed = (
        P("expert", "tensor"),
        P(),
        P(),
        P(None, None, "tensor"),
        P("tensor", None),
        P(None, "tensor"),
        P(),
        P("expert", None, "tensor"),
        P("expert", "tensor", None),
        P("expert", None),
        P("expert", None),
        P(),
        P("expert", "tensor"),
    )
    return jax.shard_map(
        functools.partial(per_device, n_t=mesh.shape["tensor"], n_e=mesh.shape["expert"]),
        mesh=mesh,
        in_specs=placed,
        out_specs=(
            P("expert", "tensor"),
            P("expert", "tensor"),
            P(),
            P(),
            P(None, None, "tensor"),
            P("tensor", None),
            P(None, "tensor"),
            P(),
            P("expert", None, "tensor"),
            P("expert", "tensor", None),
        ),
        check_vma=False,
    )
```

time: 599 us -> 243 us (0.41)
  blocking collectives: 246 us -> 83.2 us
  other arithmetic: 114 us -> 3.43 us
  local copies, waits for them, and re-layouts: 107 us -> 48.1 us
  waiting for transfers between devices: 80.1 us -> 34 us
  starting transfers between devices: 14.4 us -> 37.6 us
  matrix products: 21.6 us -> 0 us
  Pallas kernels: 0 us -> 20.2 us
    unnamed x1 -> x0, blocking collectives: 163 us -> none
    scatter-add x1 -> x0, other arithmetic: 98.3 us -> none  [per_device(): d_bias_rows = d_bias_rows.at[:, distance.reshape(-1)].add(flat_scores)]
    gather x6 -> x0, local copies, waits for them, and re-layouts: 70 us -> none  [the longest x2 61 us: block_scores(): rel_bias = bias_rows[:, distance]]
    psum x1 -> x2, blocking collectives: 37.1 us -> 83.2 us  [the longest x1 43.5 us: per_device(): lax.psum((second, rel_grad, router_grad), 'expert')]
    psum x3 -> x1, waiting for transfers between devices: 29.9 us -> 0.01 us  [per_device(): qkv_grad, out_grad = lax.psum((qkv_grad, out_grad), 'expert')]
    all_gather x4 -> x0, blocking collectives: 28 us -> none  [the longest x1 8.03 us: per_device(): d_rows_full = lax.all_gather(d_rows_share, 'tensor', axis=2, tiled=True)]
    unnamed x120 -> x147, local copies, waits for them, and re-layouts: 17.4 us -> 42.5 us
    ppermute x0 -> x27, waiting for transfers between devices: none -> 24.1 us  [shift(): return lax.ppermute(v, 'tensor', [(i, (i + k) % n_t) for i in range(n_t)])]
  transfers between devices with their start and end apart: 7 -> 31, of which waited for: 5 -> 10; matrix products, arithmetic and copies ran while one was open for 21% -> 6% of each run, Pallas kernels for 0% -> 4%
where the time goes in v1:
time: 243 us; the launch traced here: 241 us
  blocking collectives  83.2 us (34%)
  local copies, waits for them, and re-layouts  48.1 us (20%)
  starting transfers between devices  37.6 us (15%)
  waiting for transfers between devices  34 us (14%)
  Pallas kernels  20.2 us (8%)
  between operations  14.5 us (6%)
  other arithmetic  3.43 us (1%)
    psum x1, blocking collectives, per_device(): lax.psum((second, rel_grad, router_grad), 'expert')  43.5 us
    unnamed x147, local copies, waits for them, and re-layouts  42.5 us
    psum x1, blocking collectives, per_device(): first = lax.psum(first, ('expert', 'tensor'))  39.7 us
    ppermute x27, waiting for transfers between devices, shift(): return lax.ppermute(v, 'tensor', [(i, (i + k) % n_t) for i in range(n_t)])  24.1 us
    ppermute x27, starting transfers between devices, shift(): return lax.ppermute(v, 'tensor', [(i, (i + k) % n_t) for i in range(n_t)])  22.2 us
    pallas_call x8, Pallas kernels, run(): pl.pallas_call(body, out_shape=[jax.ShapeDtypeStruct(s, d) for s, d in ou...  20.2 us
    all_to_all x3, starting transfers between devices, exchange(): lax.all_to_all(v.reshape(n_e, rows // n_e, w), 'expert', split_axis=0, co...  15.3 us
    all_to_all x3, waiting for transfers between devices, exchange(): lax.all_to_all(v.reshape(n_e, rows // n_e, w), 'expert', split_axis=0, co...  9.85 us
  transfers between devices with their start and end apart: 31, of which 10 were waited for; matrix products, arithmetic and copies ran while one was open for 6% of the time, Pallas kernels for 4%

profile of v1, /device:TPU:0, one launch (start us, length us, event | category | flops | bytes accessed | tf_op | source)
XLA Modules:
  0.0 241.0 jit_solution(15601476647341367982)
XLA Ops:
  7.2 0.9 copy.52.x0.tokens
  8.1 2.5 %collective-permute-start.2 = (bf16[128,192]{1,0:T(8,128)(2,1)S(1)}, bf16[128,192]{1,0:T(8,128)(2,1)S(1)}, u32[]{:S(2)}, u32[]{:S(2)}) collective-permute-start(bf16[128,192]{1,0:T(8,128)(2,1)S(1)} %copy.52.x0.tokens), channel_id=1, source_target_pairs={{0,3},{1,0},{2,1},{3,2},{4,7},{5,4},{6,5},{7,6},{8,11},{9,8},{10,9... | collective-permute-start | bytes 147464 | tf_op jit(solution)/shard_map/ppermute | solution.py:385
  11.3 0.9 copy.56.dy.y0
  13.7 1.0 shard_map.205
  15.9 5.9 %all-to-all-start.1 = ((bf16[8,40,192]{2,1,0:T(8,128)(2,1)}), bf16[8,40,192]{2,1,0:T(8,128)(2,1)S(1)}, u32[]{:S(2)}, u32[]{:S(2)}) async-start(bf16[8,40,192]{2,1,0:T(8,128)(2,1)} %bitcast.6), calls=%async_computation.1 | async-start | bytes 327680 | tf_op jit(solution)/shard_map/all_to_all | solution.py:392
  21.8 1.2 pad_bitcast_fusion.buckets
  23.6 1.4 reshape.51.gain
  25.7 1.5 copy.53.qkv_w
  29.1 0.8 copy-done.25
  30.0 0.8 copy-done.27
  30.8 0.8 copy-done.29
  34.2 3.3 %shard_map.204 = (f32[128,192]{1,0:T(8,128)S(1)}, bf16[128,192]{1,0:T(8,128)(2,1)}, bf16[128,192]{1,0:T(8,128)(2,1)}, bf16[128,192]{1,0:T(8,128)(2,1)}, bf16[4,1...) custom-call(s32[2]{0:T(128)S(1)} %copy-done.47, ...), custom_call_target="tpu_custom_call" | custom-call | tf_op jit(solution)/shard_map/pallas_call | solution.py:46
  40.8 1.1 collective-permute-start.3
  42.5 1.0 collective-permute-start.5
  44.2 0.9 copy.58.router
  46.4 0.9 copy-done.23
  47.3 0.8 copy-done.39
  49.4 1.5 shard_map.206
  52.2 6.0 %all-to-all-start = ((bf16[8,40,256]{2,1,0:T(8,128)(2,1)}), bf16[8,40,256]{2,1,0:T(8,128)(2,1)}, u32[]{:S(2)}, u32[]{:S(2)}) async-start(bf16[8,40,256]{2,1,0:T(8,128)(2,1)} %bitcast.17), calls=%async_computation | async-start | bytes 327680 | tf_op jit(solution)/shard_map/all_to_all | solution.py:392
  59.0 7.4 %all-to-all-done = bf16[8,40,256]{2,1,0:T(8,128)(2,1)} async-done(((bf16[8,40,256]{2,1,0:T(8,128)(2,1)}), bf16[8,40,256]{2,1,0:T(8,128)(2,1)}, u32[]{:S(2)}, u32[]{:S(2)}) %all-to-all-start) | async-done | bytes 163872 | tf_op jit(solution)/shard_map/all_to_all | solution.py:392
  66.5 1.0 collective-permute-start.10
  67.7 1.0 collective-permute-start.13
  69.3 9.9 %collective-permute-done.13.g2 = bf16[320,192]{1,0:T(8,128)(2,1)S(1)} collective-permute-done((bf16[320,192]{1,0:T(8,128)(2,1)S(1)}, bf16[320,192]{1,0:T(8,128)(2,1)S(1)}, u32[]{:S(2)}, u32[]{:S(2)}) %collective-permute-start.13) | collective-permute-done | bytes 122912 | tf_op jit(solution)/shard_map/ppermute | solution.py:385
  79.2 2.3 collective-permute-done.12.g1
  81.5 1.3 copy-done.2
  83.4 3.4 %shard_map.207 = (bf16[320,384]{1,0:T(8,128)(2,1)S(1)}, bf16[320,384]{1,0:T(8,128)(2,1)S(1)}, bf16[320,384]{1,0:T(8,128)(2,1)S(1)}, bf16[320,384]{1,0:T(8,128)(2...) custom-call(s32[2]{0:T(128)S(1)} %copy-done.49, ...), custom_call_target="tpu_custom_call" | custom-call | tf_op jit(solution)/shard_map/pallas_call | solution.py:46
  90.0 1.1 collective-permute-start.16
  91.2 1.4 collective-permute-start.17
  92.5 5.1 %collective-permute-done.15 = bf16[320,384]{1,0:T(8,128)(2,1)S(1)} collective-permute-done((bf16[320,384]{1,0:T(8,128)(2,1)S(1)}, bf16[320,384]{1,0:T(8,128)(2,1)S(1)}, u32[]{:S(2)}, u32[]{:S(2)}) %collective-permute-start.15) | collective-permute-done | bytes 245792 | tf_op jit(solution)/shard_map/ppermute | solution.py:385
  97.7 1.2 collective-permute-done.16
  98.9 3.2 %collective-permute-done.17 = bf16[320,384]{1,0:T(8,128)(2,1)S(1)} collective-permute-done((bf16[320,384]{1,0:T(8,128)(2,1)S(1)}, bf16[320,384]{1,0:T(8,128)(2,1)S(1)}, u32[]{:S(2)}, u32[]{:S(2)}) %collective-permute-start.17) | collective-permute-done | bytes 245792 | tf_op jit(solution)/shard_map/ppermute | solution.py:385
  102.9 3.4 %all-to-all-start.2 = ((bf16[8,40,384]{2,1,0:T(8,128)(2,1)}), bf16[8,40,384]{2,1,0:T(8,128)(2,1)S(1)}, u32[]{:S(2)}, u32[]{:S(2)}) async-start(bf16[8,40,384]{2,1,0:T(8,128)(2,1)} %bitcast.19), calls=%async_computation.2 | async-start | bytes 491520 | tf_op jit(solution)/shard_map/all_to_all | solution.py:392
  106.4 2.0 collective-permute-start.8
  108.4 1.0 collective-permute-start.7
  109.3 1.7 collective-permute-start.23
  111.1 1.1 collective-permute-start.22
  113.5 2.4 %all-to-all-done.2 = bf16[8,40,384]{2,1,0:T(8,128)(2,1)S(1)} async-done(((bf16[8,40,384]{2,1,0:T(8,128)(2,1)}), bf16[8,40,384]{2,1,0:T(8,128)(2,1)S(1)}, u32[]{:S(2)}, u32[]{:S(2)}) %all-to-all-start.2) | async-done | bytes 245792 | tf_op jit(solution)/shard_map/all_to_all | solution.py:392
  117.9 1.0 collective-permute-start.19
  122.3 1.0 collective-permute-done.18.b1
  127.6 3.8 %shard_map.209 = (bf16[128,256]{1,0:T(8,128)(2,1)S(1)}, bf16[128,256]{1,0:T(8,128)(2,1)S(1)}, bf16[128,256]{1,0:T(8,128)(2,1)S(1)}, bf16[128,256]{1,0:T(8,128)(2...) custom-call(s32[2]{0:T(128)S(1)} %copy-done.50, ...), custom_call_target="tpu_custom_call" | custom-call | tf_op jit(solution)/shard_map/pallas_call | solution.py:46
  133.9 3.5 %shard_map.210 = (bf16[3,768,192]{2,1,0:T(8,128)(2,1)}, bf16[192,768]{1,0:T(8,128)(2,1)}, f32[4,1,192]{2,1,0:T(1,128)S(1)}, f32[32,3]{1,0:T(8,128)S(1)}, f32[768,8]{1,0:T(8,128)S(1)}) custom-call(s32[2]{0:T(128)S(1)} %copy-done.51, bf16[128,256]{1,0:T(8,128)(2,1)S(1)} %get-tuple-element.57.t0, bf16[128,256]{1,0:T(8,128)(2,1)S(1)} %collective-permute-done.6.t1, ...), custom_call_target="tpu_custom_call" | custom-call | tf_op jit(solution)/shard_map/pallas_call | solution.py:46
  138.3 1.0 collective-permute-start.25
  139.4 1.4 collective-permute-start.26
  140.9 3.2 %shard_map.211 = (f32[1,768,768]{2,1,0:T(8,128)}, f32[1,768,768]{2,1,0:T(8,128)}) custom-call(bf16[320,768]{1,0:T(8,128)(2,1)S(1)} %copy-done.4, bf16[320,768]{1,0:T(8,128)(2,1)S(1)} %copy-done.6, bf16[320,768]{1,0:T(8,128)(2,1)S(1)} %copy-done.8, bf16[320,768]{1,0:T(8,128)(2,1)S(1)} %copy-done.10), custom_call_target="tpu_custom_call" | custom-call | tf_op jit(solution)/shard_map/pallas_call | solution.py:46
  145.0 43.5 %all-reduce.1 = (f32[768]{0:T(1024)}, f32[32,3]{1,0:T(8,128)S(1)}, f32[768,8]{1,0:T(8,128)S(1)}) all-reduce(f32[768]{0:T(1024)S(1)} %reshape.60, f32[32,3]{1,0:T(8,128)S(1)} %get-tuple-element.86, f32[768,8]{1,0:T(8,128)S(1)} %get-tuple-element.87), channel_id=1, replica_groups=mesh['expert'=8,'tensor'=4] {'expert'}, use_global_device_ids=true, to_apply=%region_1.2 | all-reduce | flops 7008 | bytes 56064 | tf_op jit(solution)/shard_map/psum | solution.py:505
  190.0 39.7 %psum.42 = f32[768]{0:T(1024)} all-reduce(f32[768]{0:T(1024)S(1)} %reshape.59), channel_id=1, replica_groups=mesh['expert'=8,'tensor'=4] {'expert','tensor'}, use_global_device_ids=true, to_apply=%region_0.1 | all-reduce | flops 768 | bytes 6144 | tf_op jit(solution)/shard_map/psum | solution.py:506
  230.8 2.5 %copy.72 = f32[3,768,192]{1,2,0:T(8,128)} copy(bf16[3,768,192]{2,1,0:T(8,128)(2,1)} %get-tuple-element.119) | data formatting | bytes 2654208
  233.3 0.9 convert_element_type.47
  (190 shorter events, 41.9 us)
Async XLA Ops:
  8.1 19.1 %collective-permute-start.2 = (bf16[128,192]{1,0:T(8,128)(2,1)S(1)}, bf16[128,192]{1,0:T(8,128)(2,1)S(1)}, u32[]{:S(2)}, u32[]{:S(2)}) collective-permute-start(bf16[128,192]{1,0:T(8,128)(2,1)S(1)} %copy.52.x0.tokens), channel_id=1, source_target_pairs={{0,3},{1,0},{2,1},{3,2},{4,7},{5,4},{6,5},{7,6},{8,11},{9,8},{10,9... | collective-permute-start | bytes 147464 | tf_op jit(solution)/shard_map/ppermute | solution.py:385
  10.5 17.3 %collective-permute-start.1 = (bf16[128,192]{1,0:T(8,128)(2,1)S(1)}, bf16[128,192]{1,0:T(8,128)(2,1)S(1)}, u32[]{:S(2)}, u32[]{:S(2)}) collective-permute-start(bf16[128,192]{1,0:T(8,128)(2,1)S(1)} %copy.52.x0.tokens), channel_id=1, source_target_pairs={{0,2},{1,3},{2,0},{3,1},{4,6},{5,7},{6,4},{7,5},{8,10},{9,11},{10,... | collective-permute-start | bytes 147464 | tf_op jit(solution)/shard_map/ppermute | solution.py:385
  11.2 17.3 %collective-permute-start = (bf16[128,192]{1,0:T(8,128)(2,1)S(1)}, bf16[128,192]{1,0:T(8,128)(2,1)S(1)}, u32[]{:S(2)}, u32[]{:S(2)}) collective-permute-start(bf16[128,192]{1,0:T(8,128)(2,1)S(1)} %copy.52.x0.tokens), channel_id=1, source_target_pairs={{0,1},{1,2},{2,3},{3,0},{4,5},{5,6},{6,7},{7,4},{8,9},{9,10},{10,1... | collective-permute-start | bytes 147464 | tf_op jit(solution)/shard_map/ppermute | solution.py:385
  15.9 13.2 %copy-start = (bf16[192,768]{1,0:T(8,128)(2,1)S(1)}, bf16[192,768]{1,0:T(8,128)(2,1)}, u32[]{:S(2)}) copy-start(bf16[192,768]{1,0:T(8,128)(2,1)} %out_w.3) | copy-start | bytes 884740
  15.9 36.3 %all-to-all-start.1 = ((bf16[8,40,192]{2,1,0:T(8,128)(2,1)}), bf16[8,40,192]{2,1,0:T(8,128)(2,1)S(1)}, u32[]{:S(2)}, u32[]{:S(2)}) async-start(bf16[8,40,192]{2,1,0:T(8,128)(2,1)} %bitcast.6), calls=%async_computation.1 | async-start | bytes 327680 | tf_op jit(solution)/shard_map/all_to_all | solution.py:392
  27.2 54.3 %copy-start.1 = (bf16[1,768,768]{2,1,0:T(8,128)(2,1)S(1)}, bf16[1,768,768]{2,1,0:T(8,128)(2,1)}, u32[]{:S(2)}) copy-start(bf16[1,768,768]{2,1,0:T(8,128)(2,1)} %up.1) | copy-start | bytes 3538948
  40.8 4.4 %collective-permute-start.3 = (bf16[128,192]{1,0:T(8,128)(2,1)}, bf16[128,192]{1,0:T(8,128)(2,1)S(1)}, u32[]{:S(2)}, u32[]{:S(2)}) collective-permute-start(bf16[128,192]{1,0:T(8,128)(2,1)} %get-tuple-element.53), channel_id=1, source_target_pairs={{0,1},{1,2},{2,3},{3,0},{4,5},{5,6},{6,7},{7,4},{8,9},{9,10},{10,1... | collective-permute-start | bytes 147464 | tf_op jit(solution)/shard_map/ppermute | solution.py:385
  41.8 4.6 %collective-permute-start.4 = (bf16[128,192]{1,0:T(8,128)(2,1)}, bf16[128,192]{1,0:T(8,128)(2,1)}, u32[]{:S(2)}, u32[]{:S(2)}) collective-permute-start(bf16[128,192]{1,0:T(8,128)(2,1)} %get-tuple-element.54), channel_id=1, source_target_pairs={{0,2},{1,3},{2,0},{3,1},{4,6},{5,7},{6,4},{7,5},{8,10},{9,11},{10,... | collective-permute-start | bytes 147464 | tf_op jit(solution)/shard_map/ppermute | solution.py:385
  42.5 4.0 %collective-permute-start.5 = (bf16[128,192]{1,0:T(8,128)(2,1)}, bf16[128,192]{1,0:T(8,128)(2,1)}, u32[]{:S(2)}, u32[]{:S(2)}) collective-permute-start(bf16[128,192]{1,0:T(8,128)(2,1)} %get-tuple-element.55), channel_id=1, source_target_pairs={{0,3},{1,0},{2,1},{3,2},{4,7},{5,4},{6,5},{7,6},{8,11},{9,8},{10,9... | collective-permute-start | bytes 147464 | tf_op jit(solution)/shard_map/ppermute | solution.py:385
  44.2 42.6 %copy-start.44 = (f32[4,1,192]{2,1,0:T(1,128)}, f32[4,1,192]{2,1,0:T(1,128)S(1)}, u32[]{:S(2)}) copy-start(f32[4,1,192]{2,1,0:T(1,128)S(1)} %reshape.52.gain) | copy-start | bytes 9220
  52.2 14.2 %all-to-all-start = ((bf16[8,40,256]{2,1,0:T(8,128)(2,1)}), bf16[8,40,256]{2,1,0:T(8,128)(2,1)}, u32[]{:S(2)}, u32[]{:S(2)}) async-start(bf16[8,40,256]{2,1,0:T(8,128)(2,1)} %bitcast.17), calls=%async_computation | async-start | bytes 327680 | tf_op jit(solution)/shard_map/all_to_all | solution.py:392
  58.2 10.5 %collective-permute-start.14 = (bf16[320,192]{1,0:T(8,128)(2,1)S(1)}, bf16[320,192]{1,0:T(8,128)(2,1)}, u32[]{:S(2)}, u32[]{:S(2)}) collective-permute-start(bf16[320,192]{1,0:T(8,128)(2,1)S(1)} %bitcast.13), channel_id=1, source_target_pairs={{0,3},{1,0},{2,1},{3,2},{4,7},{5,4},{6,5},{7,6},{8,11},{9,8},{10,9... | collective-permute-start | bytes 368648 | tf_op jit(solution)/shard_map/ppermute | solution.py:385
  66.5 15.0 %collective-permute-start.11 = (bf16[320,256]{1,0:T(8,128)(2,1)}, bf16[320,256]{1,0:T(8,128)(2,1)S(1)}, u32[]{:S(2)}, u32[]{:S(2)}) collective-permute-start(bf16[320,256]{1,0:T(8,128)(2,1)} %bitcast.5.h0), channel_id=1, source_target_pairs={{0,3},{1,0},{2,1},{3,2},{4,7},{5,4},{6,5},{7,6},{8,11},{9,8},{10,9... | collective-permute-start | bytes 491528 | tf_op jit(solution)/shard_map/ppermute | solution.py:385
  66.5 15.0 %collective-permute-start.10 = (bf16[320,256]{1,0:T(8,128)(2,1)}, bf16[320,256]{1,0:T(8,128)(2,1)S(1)}, u32[]{:S(2)}, u32[]{:S(2)}) collective-permute-start(bf16[320,256]{1,0:T(8,128)(2,1)} %bitcast.5.h0), channel_id=1, source_target_pairs={{0,2},{1,3},{2,0},{3,1},{4,6},{5,7},{6,4},{7,5},{8,10},{9,11},{10,... | collective-permute-start | bytes 491528 | tf_op jit(solution)/shard_map/ppermute | solution.py:385
  67.5 14.0 %collective-permute-start.9 = (bf16[320,256]{1,0:T(8,128)(2,1)}, bf16[320,256]{1,0:T(8,128)(2,1)S(1)}, u32[]{:S(2)}, u32[]{:S(2)}) collective-permute-start(bf16[320,256]{1,0:T(8,128)(2,1)} %bitcast.5.h0), channel_id=1, source_target_pairs={{0,1},{1,2},{2,3},{3,0},{4,5},{5,6},{6,7},{7,4},{8,9},{9,10},{10,1... | collective-permute-start | bytes 491528 | tf_op jit(solution)/shard_map/ppermute | solution.py:385
  67.7 11.5 %collective-permute-start.13 = (bf16[320,192]{1,0:T(8,128)(2,1)S(1)}, bf16[320,192]{1,0:T(8,128)(2,1)S(1)}, u32[]{:S(2)}, u32[]{:S(2)}) collective-permute-start(bf16[320,192]{1,0:T(8,128)(2,1)S(1)} %bitcast.14), channel_id=1, source_target_pairs={{0,2},{1,3},{2,0},{3,1},{4,6},{5,7},{6,4},{7,5},{8,10},{9,11},{10,... | collective-permute-start | bytes 368648 | tf_op jit(solution)/shard_map/ppermute | solution.py:385
  68.7 12.8 %collective-permute-start.12 = (bf16[320,192]{1,0:T(8,128)(2,1)S(1)}, bf16[320,192]{1,0:T(8,128)(2,1)S(1)}, u32[]{:S(2)}, u32[]{:S(2)}) collective-permute-start(bf16[320,192]{1,0:T(8,128)(2,1)S(1)} %bitcast.15), channel_id=1, source_target_pairs={{0,1},{1,2},{2,3},{3,0},{4,5},{5,6},{6,7},{7,4},{8,9},{9,10},{10,1... | collective-permute-start | bytes 368648 | tf_op jit(solution)/shard_map/ppermute | solution.py:385
  89.9 22.2 %copy-start.66 = (f32[768]{0:T(1024)S(1)}, f32[768]{0:T(1024)}, u32[]{:S(2)}) copy-start(f32[768]{0:T(1024)} %param.14) | copy-start | bytes 9220
  90.0 22.9 %copy-start.67 = (f32[768]{0:T(1024)S(1)}, f32[768]{0:T(1024)}, u32[]{:S(2)}) copy-start(f32[768]{0:T(1024)} %param.15) | copy-start | bytes 9220
  90.0 26.0 %copy-start.21 = (f32[128,192]{1,0:T(8,128)S(1)}, f32[128,192]{1,0:T(8,128)}, u32[]{:S(2)}) copy-start(f32[128,192]{1,0:T(8,128)} %copy-done.20) | copy-start | bytes 294916
  90.0 26.0 %copy-start.31 = (f32[128,2]{1,0:T(8,128)S(1)}, f32[128,2]{1,0:T(8,128)}, u32[]{:S(2)}) copy-start(f32[128,2]{1,0:T(8,128)} %copy-done.30) | copy-start | bytes 3076
  90.0 7.7 %collective-permute-start.15 = (bf16[320,384]{1,0:T(8,128)(2,1)S(1)}, bf16[320,384]{1,0:T(8,128)(2,1)S(1)}, u32[]{:S(2)}, u32[]{:S(2)}) collective-permute-start(bf16[320,384]{1,0:T(8,128)(2,1)S(1)} %get-tuple-element.61), channel_id=1, source_target_pairs={{0,1},{1,2},{2,3},{3,0},{4,5},{5,6},{6,7},{7,4},{8,9},{9,10},{10,1... | collective-permute-start | bytes 737288 | tf_op jit(solution)/shard_map/ppermute | solution.py:385
  90.0 8.8 %collective-permute-start.16 = (bf16[320,384]{1,0:T(8,128)(2,1)S(1)}, bf16[320,384]{1,0:T(8,128)(2,1)S(1)}, u32[]{:S(2)}, u32[]{:S(2)}) collective-permute-start(bf16[320,384]{1,0:T(8,128)(2,1)S(1)} %get-tuple-element.62), channel_id=1, source_target_pairs={{0,2},{1,3},{2,0},{3,1},{4,6},{5,7},{6,4},{7,5},{8,10},{9,11},{10,... | collective-permute-start | bytes 737288 | tf_op jit(solution)/shard_map/ppermute | solution.py:385
  91.2 11.0 %collective-permute-start.17 = (bf16[320,384]{1,0:T(8,128)(2,1)S(1)}, bf16[320,384]{1,0:T(8,128)(2,1)S(1)}, u32[]{:S(2)}, u32[]{:S(2)}) collective-permute-start(bf16[320,384]{1,0:T(8,128)(2,1)S(1)} %get-tuple-element.63), channel_id=1, source_target_pairs={{0,3},{1,0},{2,1},{3,2},{4,7},{5,4},{6,5},{7,6},{8,11},{9,8},{10,9... | collective-permute-start | bytes 737288 | tf_op jit(solution)/shard_map/ppermute | solution.py:385
  102.1 21.1 %copy-start.12 = (bf16[128,192]{1,0:T(8,128)(2,1)S(1)}, bf16[128,192]{1,0:T(8,128)(2,1)}, u32[]{:S(2)}) copy-start(bf16[128,192]{1,0:T(8,128)(2,1)} %copy-done.11) | copy-start | bytes 147460
  102.1 21.1 %copy-start.14 = (f32[128,1]{1,0:T(8,128)S(1)}, f32[128,1]{1,0:T(8,128)}, u32[]{:S(2)}) copy-start(f32[128,1]{1,0:T(8,128)} %copy-done.13) | copy-start | bytes 1540
  102.1 21.1 %copy-start.16 = (bf16[3,128,192]{2,1,0:T(8,128)(2,1)S(1)}, bf16[3,128,192]{2,1,0:T(8,128)(2,1)}, u32[]{:S(2)}) copy-start(bf16[3,128,192]{2,1,0:T(8,128)(2,1)} %copy-done.15) | copy-start | bytes 442372
  102.1 21.1 %copy-start.18 = (f32[3,128,128]{2,1,0:T(8,128)S(1)}, f32[3,128,128]{2,1,0:T(8,128)}, u32[]{:S(2)}) copy-start(f32[3,128,128]{2,1,0:T(8,128)} %copy-done.17) | copy-start | bytes 589828
  102.9 13.0 %all-to-all-start.2 = ((bf16[8,40,384]{2,1,0:T(8,128)(2,1)}), bf16[8,40,384]{2,1,0:T(8,128)(2,1)S(1)}, u32[]{:S(2)}, u32[]{:S(2)}) async-start(bf16[8,40,384]{2,1,0:T(8,128)(2,1)} %bitcast.19), calls=%async_computation.2 | async-start | bytes 491520 | tf_op jit(solution)/shard_map/all_to_all | solution.py:392
  106.4 124.4 %all-reduce.5.cloned.1.call-start = ((), (), s32[]{:S(2)}) async-start(), calls=%async_computation.3 | async-start | bytes 2949120 | tf_op jit(solution)/shard_map/psum | solution.py:504
  106.4 7.1 %collective-permute-start.8 = (bf16[128,256]{1,0:T(8,128)(2,1)S(1)}, bf16[128,256]{1,0:T(8,128)(2,1)S(1)}, u32[]{:S(2)}, u32[]{:S(2)}) collective-permute-start(bf16[128,256]{1,0:T(8,128)(2,1)S(1)} %get-tuple-element.57.t0), channel_id=1, source_target_pairs={{0,3},{1,0},{2,1},{3,2},{4,7},{5,4},{6,5},{7,6},{8,11},{9,8},{10,9... | collective-permute-start | bytes 196616 | tf_op jit(solution)/shard_map/ppermute | solution.py:385
  108.4 5.1 %collective-permute-start.7 = (bf16[128,256]{1,0:T(8,128)(2,1)S(1)}, bf16[128,256]{1,0:T(8,128)(2,1)S(1)}, u32[]{:S(2)}, u32[]{:S(2)}) collective-permute-start(bf16[128,256]{1,0:T(8,128)(2,1)S(1)} %get-tuple-element.57.t0), channel_id=1, source_target_pairs={{0,2},{1,3},{2,0},{3,1},{4,6},{5,7},{6,4},{7,5},{8,10},{9,11},{10,... | collective-permute-start | bytes 196616 | tf_op jit(solution)/shard_map/ppermute | solution.py:385
  109.3 4.2 %collective-permute-start.6 = (bf16[128,256]{1,0:T(8,128)(2,1)S(1)}, bf16[128,256]{1,0:T(8,128)(2,1)S(1)}, u32[]{:S(2)}, u32[]{:S(2)}) collective-permute-start(bf16[128,256]{1,0:T(8,128)(2,1)S(1)} %get-tuple-element.57.t0), channel_id=1, source_target_pairs={{0,1},{1,2},{2,3},{3,0},{4,5},{5,6},{6,7},{7,4},{8,9},{9,10},{10,1... | collective-permute-start | bytes 196616 | tf_op jit(solution)/shard_map/ppermute | solution.py:385
  109.3 9.6 %collective-permute-start.23 = (bf16[128,192]{1,0:T(8,128)(2,1)S(1)}, bf16[128,192]{1,0:T(8,128)(2,1)S(1)}, u32[]{:S(2)}, u32[]{:S(2)}) collective-permute-start(bf16[128,192]{1,0:T(8,128)(2,1)S(1)} %copy.56.dy.y0), channel_id=1, source_target_pairs={{0,3},{1,0},{2,1},{3,2},{4,7},{5,4},{6,5},{7,6},{8,11},{9,8},{10,9... | collective-permute-start | bytes 147464 | tf_op jit(solution)/shard_map/ppermute | solution.py:385
  111.1 9.2 %collective-permute-start.22 = (bf16[128,192]{1,0:T(8,128)(2,1)S(1)}, bf16[128,192]{1,0:T(8,128)(2,1)S(1)}, u32[]{:S(2)}, u32[]{:S(2)}) collective-permute-start(bf16[128,192]{1,0:T(8,128)(2,1)S(1)} %copy.56.dy.y0), channel_id=1, source_target_pairs={{0,2},{1,3},{2,0},{3,1},{4,6},{5,7},{6,4},{7,5},{8,10},{9,11},{10,... | collective-permute-start | bytes 147464 | tf_op jit(solution)/shard_map/ppermute | solution.py:385
  113.5 7.4 %collective-permute-start.21 = (bf16[128,192]{1,0:T(8,128)(2,1)S(1)}, bf16[128,192]{1,0:T(8,128)(2,1)S(1)}, u32[]{:S(2)}, u32[]{:S(2)}) collective-permute-start(bf16[128,192]{1,0:T(8,128)(2,1)S(1)} %copy.56.dy.y0), channel_id=1, source_target_pairs={{0,1},{1,2},{2,3},{3,0},{4,5},{5,6},{6,7},{7,4},{8,9},{9,10},{10,1... | collective-permute-start | bytes 147464 | tf_op jit(solution)/shard_map/ppermute | solution.py:385
  117.1 4.5 %collective-permute-start.20 = (bf16[128,256]{1,0:T(8,128)(2,1)S(1)}, bf16[128,256]{1,0:T(8,128)(2,1)S(1)}, u32[]{:S(2)}, u32[]{:S(2)}) collective-permute-start(bf16[128,256]{1,0:T(8,128)(2,1)S(1)} %get-tuple-element.67.b0), channel_id=1, source_target_pairs={{0,3},{1,0},{2,1},{3,2},{4,7},{5,4},{6,5},{7,6},{8,11},{9,8},{10,9... | collective-permute-start | bytes 196616 | tf_op jit(solution)/shard_map/ppermute | solution.py:385
  117.9 4.4 %collective-permute-start.19 = (bf16[128,256]{1,0:T(8,128)(2,1)S(1)}, bf16[128,256]{1,0:T(8,128)(2,1)S(1)}, u32[]{:S(2)}, u32[]{:S(2)}) collective-permute-start(bf16[128,256]{1,0:T(8,128)(2,1)S(1)} %get-tuple-element.67.b0), channel_id=1, source_target_pairs={{0,2},{1,3},{2,0},{3,1},{4,6},{5,7},{6,4},{7,5},{8,10},{9,11},{10,... | collective-permute-start | bytes 196616 | tf_op jit(solution)/shard_map/ppermute | solution.py:385
  119.5 3.7 %collective-permute-start.18 = (bf16[128,256]{1,0:T(8,128)(2,1)S(1)}, bf16[128,256]{1,0:T(8,128)(2,1)S(1)}, u32[]{:S(2)}, u32[]{:S(2)}) collective-permute-start(bf16[128,256]{1,0:T(8,128)(2,1)S(1)} %get-tuple-element.67.b0), channel_id=1, source_target_pairs={{0,1},{1,2},{2,3},{3,0},{4,5},{5,6},{6,7},{7,4},{8,9},{9,10},{10,1... | collective-permute-start | bytes 196616 | tf_op jit(solution)/shard_map/ppermute | solution.py:385
  127.6 6.3 %copy-start.51 = (s32[2]{0:T(128)S(1)}, s32[2]{0:T(128)}, u32[]{:S(2)}) copy-start(s32[2]{0:T(128)} %pad_add_fusion.ids) | copy-start | bytes 28
  127.6 6.3 %copy-start.54 = (s32[1,128]{1,0:T(1,128)S(1)}, s32[1,128]{1,0:T(1,128)}, u32[]{:S(2)}) copy-start(s32[1,128]{1,0:T(1,128)} %pad_bitcast_fusion.buckets) | copy-start | bytes 1540
  133.9 5.4 %copy-start.60 = (bf16[128,256]{1,0:T(8,128)(2,1)S(1)}, bf16[128,256]{1,0:T(8,128)(2,1)}, u32[]{:S(2)}) copy-start(bf16[128,256]{1,0:T(8,128)(2,1)} %copy-done.59) | copy-start | bytes 196612
  133.9 6.9 %copy-start.10 = (bf16[320,768]{1,0:T(8,128)(2,1)S(1)}, bf16[320,768]{1,0:T(8,128)(2,1)}, u32[]{:S(2)}) copy-start(bf16[320,768]{1,0:T(8,128)(2,1)} %copy-done.9) | copy-start | bytes 1474564
  137.5 6.6 %copy-start.41 = (bf16[128,192]{1,0:T(8,128)(2,1)S(1)}, bf16[128,192]{1,0:T(8,128)(2,1)}, u32[]{:S(2)}) copy-start(bf16[128,192]{1,0:T(8,128)(2,1)} %copy-done.40) | copy-start | bytes 147460
  138.3 91.4 %collective-permute-start.24 = (bf16[128,256]{1,0:T(8,128)(2,1)S(1)}, bf16[128,256]{1,0:T(8,128)(2,1)S(1)}, u32[]{:S(2)}, u32[]{:S(2)}) collective-permute-start(bf16[128,256]{1,0:T(8,128)(2,1)S(1)} %copy-done.64), channel_id=1, source_target_pairs={{0,1},{1,2},{2,3},{3,0},{4,5},{5,6},{6,7},{7,4},{8,9},{9,10},{10,1... | collective-permute-start | bytes 196616 | tf_op jit(solution)/shard_map/ppermute | solution.py:385
  138.3 91.4 %collective-permute-start.25 = (bf16[128,256]{1,0:T(8,128)(2,1)S(1)}, bf16[128,256]{1,0:T(8,128)(2,1)S(1)}, u32[]{:S(2)}, u32[]{:S(2)}) collective-permute-start(bf16[128,256]{1,0:T(8,128)(2,1)S(1)} %copy-done.62), channel_id=1, source_target_pairs={{0,2},{1,3},{2,0},{3,1},{4,6},{5,7},{6,4},{7,5},{8,10},{9,11},{10,... | collective-permute-start | bytes 196616 | tf_op jit(solution)/shard_map/ppermute | solution.py:385
  139.4 90.3 %collective-permute-start.26 = (bf16[128,256]{1,0:T(8,128)(2,1)S(1)}, bf16[128,256]{1,0:T(8,128)(2,1)S(1)}, u32[]{:S(2)}, u32[]{:S(2)}) collective-permute-start(bf16[128,256]{1,0:T(8,128)(2,1)S(1)} %copy-done.60), channel_id=1, source_target_pairs={{0,3},{1,0},{2,1},{3,2},{4,7},{5,4},{6,5},{7,6},{8,11},{9,8},{10,9... | collective-permute-start | bytes 196616 | tf_op jit(solution)/shard_map/ppermute | solution.py:385
  140.9 88.8 %copy-start.43 = (bf16[128,256]{1,0:T(8,128)(2,1)S(1)}, bf16[128,256]{1,0:T(8,128)(2,1)}, u32[]{:S(2)}) copy-start(bf16[128,256]{1,0:T(8,128)(2,1)} %copy-done.42) | copy-start | bytes 196612
  (51 other events, 52.9 us)
Sparse Core Ops, SparseCore 0:
  137.6 92.2 all-reduce.4

commit v2 on v1

v2 whole, which is shorter than its diff:
```python
import functools
import math

import jax
import jax.numpy as jnp
from jax import lax
from jax.experimental import pallas as pl
from jax.experimental.pallas import tpu as pltpu
from jax.sharding import PartitionSpec as P

epsilon = 1e-06
highest = lax.Precision.HIGHEST
big_negative = -1e30
bf16 = jnp.bfloat16
f32 = jnp.float32
i32 = jnp.int32


def mm(a, b, contract=(1, 0), precision=None):
    return lax.dot_general(
        a,
        b,
        (((contract[0],), (contract[1],)), ((), ())),
        preferred_element_type=f32,
        precision=precision,
    )


def iota(shape, dim):
    return lax.broadcasted_iota(i32, shape, dim)


def split_hi_lo(v):
    hi = v.astype(bf16).astype(f32)
    return hi, v - hi


def row_block(values, rows=16):
    lanes = values[0].shape[1]
    row = iota((rows, lanes), 0)
    block = jnp.zeros((rows, lanes), f32)
    for i, v in enumerate(values):
        block = jnp.where(row == i, v, block)
    return block


def run(body, outs, *args, smem=0, scratch=(), flops=0):
    moved = sum(a.size * a.dtype.itemsize for a in args)
    moved += sum(math.prod(s) * jnp.dtype(d).itemsize for s, d in outs)
    return pl.pallas_call(
        body,
        out_shape=[jax.ShapeDtypeStruct(s, d) for s, d in outs],
        in_specs=[pl.BlockSpec(memory_space=pltpu.SMEM)] * smem
        + [pl.BlockSpec()] * (len(args) - smem),
        out_specs=[pl.BlockSpec()] * len(outs),
        scratch_shapes=list(scratch),
        compiler_params=pltpu.CompilerParams(vmem_limit_bytes=32 * 2**20),
        cost_estimate=pl.CostEstimate(flops=flops, bytes_accessed=moved, transcendentals=0),
    )(*args)


def column_of(row, out):
    for c in range(row.shape[1] // 128):
        part = jnp.broadcast_to(row[:, c * 128:(c + 1) * 128], (128, 128))
        part = jnp.where(iota((128, 128), 0) == iota((128, 128), 1), part, 0.0)
        out[c * 128:(c + 1) * 128, :] = jnp.sum(part, axis=1, keepdims=True)


def skew(values, sign):
    n = values.shape[0]
    row = iota(values.shape, 0)
    bit = 1
    while bit < n:
        moved = pltpu.roll(values, bit if sign > 0 else n - bit, 1)
        values = jnp.where((row & bit) != 0, moved, values)
        bit *= 2
    return values


def bucket_hot(buckets, padded, count):
    padded[...] = jnp.full(padded.shape, -1, i32)
    padded[:, 0:buckets.shape[1]] = buckets[...]
    return (padded[...] == iota((count, padded.shape[1]), 0)).astype(f32)


def prepare_kernel(lengths, gain, out_w, table, buckets, gain_col, out_wt, bias, padded):
    tok = bias.shape[1]
    column_of(gain[...], gain_col)
    out_wt[...] = out_w[...].astype(f32).T.astype(bf16)
    key_pos = iota((tok, tok), 0)
    query_pos = iota((tok, tok), 1)
    end0 = lengths[0, 0]
    end1 = end0 + lengths[0, 1]
    seg_k = (key_pos >= end0).astype(i32) + (key_pos >= end1).astype(i32)
    seg_q = (query_pos >= end0).astype(i32) + (query_pos >= end1).astype(i32)
    allowed = (seg_k == seg_q) & (key_pos <= query_pos)
    hot = bucket_hot(buckets, padded, table.shape[1])
    per_head = mm(table[...], hot, precision=highest)
    for h in range(table.shape[0]):
        full = skew(jnp.broadcast_to(per_head[h:h + 1], (tok, tok)), 1)
        bias[h] = jnp.where(allowed, full, big_negative)


def route_kernel(
    ids, routes, dy, router, gain, qkv_w, after, *refs, experts, cap, n_e, direct, n_t,
):
    pieces = list(refs[:-5])
    dest, gain_col, rw_own, qkv_wt, chunks = refs[-5:]
    tok = routes.shape[1]
    width = dy.shape[0]
    rows = experts * cap
    e = ids[1].astype(f32)
    rt = routes[...]
    x_of = iota((experts, tok), 0)
    m0 = (rt[0:1] == x_of).astype(f32)
    m1 = (rt[1:2] == x_of).astype(f32)
    earlier = (iota((tok, tok), 0) < iota((tok, tok), 1)).astype(f32).astype(bf16)
    counts = mm((m0 + m1).astype(bf16), earlier)
    send, back = [], []
    for i, m in enumerate((m0, m1)):
        slot = jnp.sum(m * counts, axis=0, keepdims=True)
        owner = rt[i:i + 1].astype(f32)
        if direct:
            ahead = owner - e
            behind = e - owner
            send.append(jnp.where(ahead < 0, ahead + n_e, ahead) * cap + slot)
            back.append(jnp.where(behind < 0, behind + n_e, behind) * cap + slot)
        else:
            send.append(owner * cap + slot)
            back.append(owner * cap + slot)
    dest[...] = row_block(send + back, 8)
    row = iota((rows, tok), 0).astype(f32)
    place = ((row == send[0]) | (row == send[1])).astype(f32).astype(bf16)
    full = mm(place, dy[...], (1, 1))
    size = rows // len(pieces)
    for k, piece in enumerate(pieces):
        piece[...] = full[k * size:(k + 1) * size].astype(bf16)
    column_of(gain[...], gain_col)
    wide = router[...].astype(f32)
    for s in range(n_t):
        chunks[s] = wide[:, s * width:(s + 1) * width]
    rw_own[...] = chunks[ids[0]].astype(bf16)
    qkv_wt[...] = qkv_w[...].astype(f32).T.astype(bf16)


def chunk(ref, s, width):
    return ref.at[pl.ds(pl.multiple_of(s * width, 64), width)]


def attention_kernel(
    ids, x0, x1, x2, x3, gain, qkv_w, out_wt, bias,
    own, p1, p2, p3, h1, inv1, heads, probs, attended,
    xs, parts, *, n_t,
):
    width, tok = x0.shape
    n_heads = bias.shape[0]
    size = width // n_heads
    model = n_t * width
    r = ids[0]
    for k, x in enumerate((x0, x1, x2, x3)):
        chunk(xs, lax.rem(r + n_t - k, n_t), width)[...] = x[...].astype(f32)
    inverse = lax.rsqrt(jnp.sum(xs[...] * xs[...], axis=0, keepdims=True) / model + epsilon)
    inv1[...] = inverse
    h1[...] = (xs[...] * inverse * gain[...]).astype(bf16)
    heads[...] = mm(qkv_w[...], h1[...]).astype(bf16)
    for h in range(n_heads):
        q, k, v = (heads[j * width + h * size:j * width + (h + 1) * size] for j in range(3))
        scores = mm(k, q, (0, 0)) * (size ** -0.5) + bias[h]
        weights = jnp.exp(scores - jnp.max(scores, axis=0, keepdims=True))
        prob = weights / jnp.sum(weights, axis=0, keepdims=True)
        probs[h] = prob
        attended[h * size:(h + 1) * size] = mm(v, prob.astype(bf16)).astype(bf16)
    parts[...] = mm(out_wt[...], attended[...])
    own[...] = chunk(parts, r, width)[...]
    for k, p in ((1, p1), (2, p2), (3, p3)):
        p[...] = chunk(parts, lax.rem(r + k, n_t), width)[...].astype(bf16)


def dispatch_kernel(
    ids, own, p1, p2, p3, x, dy, gain, rw_own, routes, dest, *refs
):
    pieces = refs[:-3]
    token_pack, residual, pack = refs[-3:]
    width, tok = x.shape
    experts = rw_own.shape[0]
    r = ids[0]
    res = x[...].astype(f32) + own[...] + (
        p1[...].astype(f32) + p2[...].astype(f32) + p3[...].astype(f32)
    )
    residual[...] = res
    scaled = (res * chunk(gain, r, width)[...]).astype(bf16)
    square = jnp.sum(res * res, axis=0, keepdims=True)
    logits = mm(rw_own[...], scaled)
    x_of = iota((experts, tok), 0)
    c0 = jnp.sum(jnp.where(routes[0:1, :] == x_of, logits, 0.0), axis=0, keepdims=True)
    c1 = jnp.sum(jnp.where(routes[1:2, :] == x_of, logits, 0.0), axis=0, keepdims=True)
    stats = row_block(split_hi_lo(square) + split_hi_lo(c0 - c1)).astype(bf16)
    token_pack[0:width] = res.astype(bf16)
    token_pack[width:width + 16] = stats
    token_pack[width + 16:] = dy[...]
    pack[0:width] = scaled
    pack[width:] = stats
    size = pieces[0].shape[0]
    row = iota((size * len(pieces), tok), 0).astype(f32)
    place0 = (row == dest[0:1, :]).astype(f32)
    place1 = (row == dest[1:2, :]).astype(f32)
    both = mm((place0 + place1).astype(bf16), pack[...], (1, 1))
    signed = mm((place0 - place1).astype(bf16), pack[...], (1, 1))
    full = jnp.where(iota(both.shape, 1) >= width + 2, signed, both)
    for k, piece in enumerate(pieces):
        piece[...] = full[k * size:(k + 1) * size].astype(bf16)


def gelu_pair(a):
    c = 0.7978845608028654
    t = jnp.tanh(c * (a + 0.044715 * a * a * a))
    value = 0.5 * a * (1.0 + t)
    slope = 0.5 * (1.0 + t) + 0.5 * a * (1.0 - t * t) * c * (1.0 + 3 * 0.044715 * a * a)
    return value, slope


def expert_kernel(
    ids, h0, h1, h2, h3, g0, g1, g2, g3, up, down,
    c0, c1, c2, c3, u, z, de, da,
    hs, gs, chunks, *, n_t,
):
    width = g0.shape[1]
    model = n_t * width
    r = ids[0]
    packs = (h0, h1, h2, h3)
    for k, (h, g) in enumerate(zip(packs, (g0, g1, g2, g3))):
        s = lax.rem(r + n_t - k, n_t)
        hs[s] = h[:, 0:width].astype(f32)
        gs[s] = g[...].astype(f32)
    stats = h0[:, width:].astype(f32)
    for h in packs[1:]:
        stats += h[:, width:].astype(f32)
    inverse = lax.rsqrt((stats[:, 0:1] + stats[:, 1:2]) / model + epsilon)
    gate = 1.0 / (1.0 + jnp.exp(-inverse * (stats[:, 2:3] + stats[:, 3:4])))
    for s in range(n_t):
        cols = slice(s * width, (s + 1) * width)
        u[:, cols] = (hs[s] * inverse).astype(bf16)
        de[:, cols] = (gs[s] * gate).astype(bf16)
    value, slope = gelu_pair(mm(u[...], up[0]))
    z[...] = value.astype(bf16)
    da[...] = (mm(de[...], down[0], (1, 1)) * slope).astype(bf16)
    eo = mm(z[...], down[0]).astype(bf16)
    du = mm(da[...], up[0], (1, 1)).astype(bf16)
    for s in range(n_t):
        cols = slice(s * width, (s + 1) * width)
        chunks[s, :, 0:width] = eo[:, cols]
        chunks[s, :, width:] = du[:, cols]
    for k, c in enumerate((c0, c1, c2, c3)):
        c[...] = chunks[lax.rem(r + k, n_t)]


def expert_grad_kernel(u, z, de, da, up_grad, down_grad):
    up_grad[0] = mm(u[...], da[...], (0, 0))
    down_grad[0] = mm(z[...], de[...], (0, 0))


def join_kernel(*refs):
    pieces, out = refs[:-1], refs[-1]
    out[...] = jnp.concatenate([p[...].astype(f32) for p in pieces], axis=0).astype(bf16)


def expert_sum_kernel(c0, c1, c2, c3, *pieces):
    total = c0[...].astype(f32) + c1[...].astype(f32) + (c2[...].astype(f32) + c3[...].astype(f32))
    count = len(pieces)
    size = total.shape[0] // count
    for k, piece in enumerate(pieces):
        j = (count - k) % count
        piece[...] = total[j * size:(j + 1) * size].astype(bf16)


def total_stats(packs, width):
    total = packs[0][width:width + 16].astype(f32)
    for p in packs[1:]:
        total += p[width:width + 16].astype(f32)
    return total


def gates_of(stats, model):
    inverse = lax.rsqrt((stats[0:1] + stats[1:2]) / model + epsilon)
    delta = inverse * (stats[2:3] + stats[3:4])
    return inverse, 1.0 / (1.0 + jnp.exp(-delta)), 1.0 / (1.0 + jnp.exp(delta))


def combine_kernel(t0, t1, t2, t3, dest, dy, residual, *refs, n_t):
    pieces, (output, pack) = refs[:-2], refs[-2:]
    width, tok = dy.shape
    _, gate0, gate1 = gates_of(total_stats((t0, t1, t2, t3), width), n_t * width)
    back = jnp.concatenate([p[...].astype(f32) for p in pieces], axis=0).astype(bf16)
    row = iota((back.shape[0], tok), 0).astype(f32)
    pick0 = (row == dest[2:3, :]).astype(f32).astype(bf16)
    pick1 = (row == dest[3:4, :]).astype(f32).astype(bf16)
    got0 = mm(back, pick0, (0, 0))
    got1 = mm(back, pick1, (0, 0))
    e0, e1 = got0[0:width], got1[0:width]
    output[...] = (residual[...] + gate0 * e0 + gate1 * e1).astype(bf16)
    dy_own = dy[...].astype(f32)
    dg0 = jnp.sum(dy_own * e0, axis=0, keepdims=True)
    dg1 = jnp.sum(dy_own * e1, axis=0, keepdims=True)
    pack[0:width] = (got0[width:] + got1[width:]).astype(bf16)
    pack[width:] = row_block(split_hi_lo(dg0) + split_hi_lo(dg1)).astype(bf16)


def backward_kernel(
    ids, b0, b1, b2, b3, t0, t1, t2, t3,
    routes, router, gain, out_w, qkv_wt, heads, probs,
    c0, c1, c2, c3, dr1_own, d_proj, d_att, d_logits, gain_terms, d_scores,
    bs, ts, ys, dr, *, n_t,
):
    width = dr1_own.shape[0]
    tok = b0.shape[1]
    experts = router.shape[0]
    n_heads = probs.shape[0]
    size = width // n_heads
    model = n_t * width
    r = ids[0]
    packs, tokens = (b0, b1, b2, b3), (t0, t1, t2, t3)
    for k in range(n_t):
        s = lax.rem(r + n_t - k, n_t)
        chunk(bs, s, width)[...] = packs[k][0:width].astype(f32)
        chunk(ts, s, width)[...] = tokens[k][0:width].astype(f32)
        chunk(ys, s, width)[...] = tokens[k][width + 16:].astype(f32)
    inverse, gate0, gate1 = gates_of(total_stats(tokens, width), model)
    back = total_stats(packs, width)
    dg0 = back[0:1] + back[1:2]
    dg1 = back[2:3] + back[3:4]
    mean_gate = gate0 * dg0 + gate1 * dg1
    x_of = iota((experts, tok), 0)
    dlog = jnp.where(routes[0:1, :] == x_of, gate0 * (dg0 - mean_gate), 0.0) + jnp.where(
        routes[1:2, :] == x_of, gate1 * (dg1 - mean_gate), 0.0
    )
    d_logits[...] = dlog
    dh2 = bs[...] + mm(router[...].astype(f32), dlog, (0, 0), precision=highest)
    res = ts[...]
    gain_terms[...] = dh2 * res * inverse
    weighted = dh2 * gain[...]
    dot = jnp.sum(weighted * res, axis=0, keepdims=True) * (inverse**3 / model)
    dr[...] = ys[...] + inverse * weighted - res * dot
    d_att[...] = dr[...].astype(bf16)
    dr1_own[...] = chunk(dr, r, width)[...]
    d_o = mm(out_w[...], d_att[...]).astype(bf16)
    scale = size ** -0.5
    for h in range(n_heads):
        q, k, v = (heads[j * width + h * size:j * width + (h + 1) * size] for j in range(3))
        d_oh = d_o[h * size:(h + 1) * size]
        prob = probs[h]
        d_prob = mm(v, d_oh, (0, 0))
        centre = jnp.sum(prob * d_prob, axis=0, keepdims=True)
        ds = (prob * (d_prob - centre)).astype(bf16)
        d_scores[h] = ds
        here = h * size
        d_proj[here:here + size] = (mm(k, ds) * scale).astype(bf16)
        here += width
        d_proj[here:here + size] = (mm(q, ds, (1, 1)) * scale).astype(bf16)
        here += width
        d_proj[here:here + size] = mm(d_oh, prob.astype(bf16), (1, 1)).astype(bf16)
    row_dot = jnp.sum(
        d_proj[...].astype(f32) * heads[...].astype(f32), axis=0, keepdims=True
    )
    stats = row_block(split_hi_lo(row_dot)).astype(bf16)
    dr[...] = mm(qkv_wt[...], d_proj[...])
    for k, c in enumerate((c0, c1, c2, c3)):
        c[0:width] = chunk(dr, lax.rem(r + k, n_t), width)[...].astype(bf16)
        c[width:] = stats


def small_grad_kernel(
    ids, t0, t1, t2, t3, d_logits, gain_terms, gain1_row, gain2, h1, d_proj, attended, d_att,
    d_scores, buckets, qkv_w, small, out_grad, ts, padded, *, n_t, n_buckets,
):
    packs = (t0, t1, t2, t3)
    width = attended.shape[0]
    model = n_t * width
    experts = d_logits.shape[0]
    tok = t0.shape[1]
    r = ids[0]
    for k, t in enumerate(packs):
        chunk(ts, lax.rem(r + n_t - k, n_t), width)[...] = t[0:width].astype(f32)
    out_grad[...] = mm(attended[...], d_att[...], (1, 1)).astype(out_grad.dtype)
    inverse, _, _ = gates_of(total_stats(packs, width), model)
    normed = (ts[...] * inverse * gain2[...]).astype(bf16).astype(f32)
    small[0:experts] = mm(d_logits[...], normed, (1, 1), precision=highest)
    ones = jnp.ones((8, tok), f32)
    small[experts:] = jnp.zeros((small.shape[0] - experts, model), f32)
    small[experts:experts + 1] = mm(ones, gain_terms[...], (1, 1), precision=highest)[0:1]
    grad = mm(d_proj[...], h1[...], (1, 1))
    first = jnp.sum(grad * qkv_w[...].astype(f32), axis=0, keepdims=True)
    small[experts + 1:experts + 2] = first / gain1_row[...]
    hot = bucket_hot(buckets, padded, n_buckets)
    for h in range(d_scores.shape[0]):
        diagonal = jnp.sum(skew(d_scores[h].astype(f32), -1), axis=0, keepdims=True)
        per_bucket = mm(jnp.broadcast_to(diagonal, (8, tok)), hot, (1, 1), precision=highest)
        here = experts + 2 + h
        small[here:here + 1, 0:n_buckets] = per_bucket[0:1]


def small_sum_kernel(*refs):
    parts, out = refs[:-1], refs[-1]
    total = parts[0][...]
    for p in parts[1:]:
        total = total + p[...]
    out[...] = total


def input_grad_kernel(ids, c0, c1, c2, c3, dr1, inv1, x, gain, out, *, n_t):
    width = x.shape[0]
    total = c0[...].astype(f32) + c1[...].astype(f32) + (c2[...].astype(f32) + c3[...].astype(f32))
    row_dot = (total[width:width + 1] + total[width + 1:width + 2]) / (n_t * width)
    inverse = inv1[...]
    weighted = total[0:width] * chunk(gain, ids[0], width)[...]
    out[...] = dr1[...] + inverse * weighted - x[...].astype(f32) * (inverse * inverse * row_dot)


def qkv_grad_kernel(*refs):
    out = refs[-1]
    count = (len(refs) - 1) // 2
    total = mm(refs[0][...], refs[count][...], (1, 1))
    for k in range(1, count):
        total += mm(refs[k][...], refs[count + k][...], (1, 1))
    out[...] = total


def per_device(
    tokens,
    first_gain,
    second_gain,
    qkv_weight,
    out_weight,
    rel_table,
    router_weight,
    up_weight,
    down_weight,
    routes,
    lengths,
    bucket_ids,
    cotangent,
    *,
    n_t,
    n_e,
):
    tok, width = tokens.shape
    model = n_t * width
    inner = 3 * width
    experts = router_weight.shape[1]
    cap = 5 * tok // (2 * experts)
    rows = experts * cap
    n_heads = rel_table.shape[1]
    n_buckets = rel_table.shape[0]
    direct = n_e <= 8 and cap % 8 == 0
    n_pieces = n_e if direct else 1
    padded = pltpu.VMEM((1, tok), i32)

    def shift(v, k, axis="tensor", n=n_t):
        return lax.ppermute(v, axis, [(i, (i + k) % n) for i in range(n)])

    def around(v):
        return [v] + [shift(v, k) for k in range(1, n_t)]

    def around_experts(v):
        return [v] + [shift(v, k, "expert", n_e) for k in range(1, n_e)]

    def exchange(pieces):
        if direct:
            return list(pieces[:1]) + [
                shift(p, k, "expert", n_e) for k, p in enumerate(pieces) if k
            ]
        w = pieces[0].shape[-1]
        v = pieces[0].reshape(n_e, rows // n_e, w)
        v = lax.all_to_all(v, "expert", split_axis=0, concat_axis=0, tiled=True)
        return [v.reshape(rows, w)]

    def join(pieces):
        if len(pieces) == 1:
            return pieces[0]
        return run(join_kernel, [((rows, pieces[0].shape[1]), bf16)], *pieces)[0]

    def piece_shapes(w):
        return [((rows // n_pieces, w), bf16)] * n_pieces

    ids = jnp.stack([lax.axis_index("tensor"), lax.axis_index("expert")]).astype(i32)
    x = tokens.T
    dy = cotangent.T
    qkv_w = qkv_weight.transpose(0, 2, 1).reshape(inner, model)
    router = router_weight.T
    table = rel_table.T
    routes_t = routes.T
    gain1_row = first_gain.reshape(1, model)
    gain2_row = second_gain.reshape(1, model)
    buckets = bucket_ids.reshape(1, -1)

    xs = around(x)
    gain1, out_wt, bias = run(
        prepare_kernel,
        [((model, 1), f32), ((model, width), bf16), ((n_heads, tok, tok), f32)],
        lengths, gain1_row, out_weight, table, buckets,
        smem=1, scratch=[padded],
    )
    own, p1, p2, p3, h1, inv1, heads, probs, attended = run(
        functools.partial(attention_kernel, n_t=n_t),
        [((width, tok), f32)]
        + [((width, tok), bf16)] * 3
        + [
            ((model, tok), bf16),
            ((1, tok), f32),
            ((inner, tok), bf16),
            ((n_heads, tok, tok), f32),
            ((width, tok), bf16),
        ],
        ids, *xs, gain1, qkv_w, out_wt, bias,
        smem=1,
        scratch=[pltpu.VMEM((model, tok), f32), pltpu.VMEM((model, tok), f32)],
    )
    got = [shift(p, k) for k, p in ((1, p1), (2, p2), (3, p3))]
    *dy_pieces, dest, gain2, rw_own, qkv_wt = run(
        functools.partial(
            route_kernel, experts=experts, cap=cap, n_e=n_e, direct=direct, n_t=n_t
        ),
        piece_shapes(width)
        + [
            ((8, tok), f32),
            ((model, 1), f32),
            ((experts, width), bf16),
            ((model, inner), bf16),
        ],
        ids, routes_t, dy, router, gain2_row, qkv_w, inv1,
        smem=1, scratch=[pltpu.VMEM((n_t, experts, width), f32)],
    )
    dy_rows = around(join(exchange(dy_pieces)))
    *row_pieces, token_pack, residual = run(
        dispatch_kernel,
        piece_shapes(width + 16) + [((2 * width + 16, tok), bf16), ((width, tok), f32)],
        ids, own, *got, x, dy, gain2, rw_own, routes_t, dest,
        smem=1, scratch=[pltpu.VMEM((width + 16, tok), bf16)],
    )
    in_rows = around(join(exchange(row_pieces)))
    token_packs = around(token_pack)

    c0, c1, c2, c3, u, z, de, da = run(
        functools.partial(expert_kernel, n_t=n_t),
        [((rows, 2 * width), bf16)] * 4 + [((rows, model), bf16)] * 4,
        ids, *in_rows, *dy_rows, up_weight, down_weight,
        smem=1,
        scratch=[
            pltpu.VMEM((n_t, rows, width), f32),
            pltpu.VMEM((n_t, rows, width), f32),
            pltpu.VMEM((n_t, rows, 2 * width), bf16),
        ],
    )
    got = [shift(c, k) for k, c in ((1, c1), (2, c2), (3, c3))]
    if direct:
        h1_late, _ = lax.optimization_barrier((h1, c0))
        h1_all = around_experts(h1_late)
    up_grad, down_grad = run(
        expert_grad_kernel,
        [(up_weight.shape, f32), (down_weight.shape, f32)],
        u, z, de, da,
    )
    back = exchange(run(expert_sum_kernel, piece_shapes(2 * width), c0, *got))
    output, back_pack = run(
        functools.partial(combine_kernel, n_t=n_t),
        [((width, tok), bf16), ((width + 16, tok), bf16)],
        *token_packs, dest, dy, residual, *back,
    )
    back_packs = around(back_pack)

    c0, c1, c2, c3, dr1, d_proj, d_att, d_logits, gain_terms, d_scores = run(
        functools.partial(backward_kernel, n_t=n_t),
        [((width + 16, tok), bf16)] * 4
        + [
            ((width, tok), f32),
            ((inner, tok), bf16),
            ((model, tok), bf16),
            ((experts, tok), f32),
            ((model, tok), f32),
            ((n_heads, tok, tok), bf16),
        ],
        ids, *back_packs, *token_packs, routes_t, router, gain2, out_weight, qkv_wt, heads, probs,
        smem=1,
        scratch=[pltpu.VMEM((model, tok), f32)] * 4,
    )
    got = [shift(c, k) for k, c in ((1, c1), (2, c2), (3, c3))]
    if direct:
        d_proj_all = around_experts(d_proj)
    small, out_part = run(
        functools.partial(small_grad_kernel, n_t=n_t, n_buckets=n_buckets),
        [((experts + 8, model), f32), (out_weight.shape, bf16)],
        ids, *token_packs, d_logits, gain_terms, gain1_row, gain2, h1, d_proj, attended, d_att,
        d_scores, buckets, qkv_w,
        smem=1,
        scratch=[pltpu.VMEM((model, tok), f32), padded],
    )
    (input_grad,) = run(
        functools.partial(input_grad_kernel, n_t=n_t),
        [((width, tok), f32)],
        ids, c0, *got, dr1, inv1, x, gain1,
        smem=1,
    )
    out_grad = lax.psum(out_part, "expert").astype(f32)
    if direct:
        (small,) = run(small_sum_kernel, [(small.shape, f32)], *around_experts(small))
        (qkv_grad,) = run(
            qkv_grad_kernel, [((inner, model), f32)], *d_proj_all, *h1_all
        )
    else:
        small = lax.psum(small, "expert")
        (qkv_grad,) = run(qkv_grad_kernel, [((inner, model), f32)], d_proj, h1)
        qkv_grad = lax.psum(qkv_grad.astype(bf16), "expert").astype(f32)
    first = small[experts + 1:experts + 2]
    first = functools.reduce(lambda a, b: a + b, around(first))
    return (
        output.T,
        input_grad.T,
        first.reshape(model),
        small[experts].reshape(model),
        qkv_grad.reshape(3, width, model).transpose(0, 2, 1),
        out_grad,
        small[experts + 2:experts + 2 + n_heads, :n_buckets].T,
        small[:experts].T,
        up_grad,
        down_grad,
    )


def solution(mesh):
    placed = (
        P("expert", "tensor"),
        P(),
        P(),
        P(None, None, "tensor"),
        P("tensor", None),
        P(None, "tensor"),
        P(),
        P("expert", None, "tensor"),
        P("expert", "tensor", None),
        P("expert", None),
        P("expert", None),
        P(),
        P("expert", "tensor"),
    )
    return jax.shard_map(
        functools.partial(per_device, n_t=mesh.shape["tensor"], n_e=mesh.shape["expert"]),
        mesh=mesh,
        in_specs=placed,
        out_specs=(
            P("expert", "tensor"),
            P("expert", "tensor"),
            P(),
            P(),
            P(None, None, "tensor"),
            P("tensor", None),
            P(None, "tensor"),
            P(),
            P("expert", None, "tensor"),
            P("expert", "tensor", None),
        ),
        check_vma=False,
    )
```

time: 243 us -> 256 us (1.053)
  waiting for transfers between devices: 34 us -> 123 us
  blocking collectives: 83.2 us -> 0 us
  starting transfers between devices: 37.6 us -> 86.1 us
  local copies, waits for them, and re-layouts: 48.1 us -> 7.52 us
    psum x2 -> x0, blocking collectives: 83.2 us -> none  [the longest x1 43.5 us: per_device(): lax.psum((second, rel_grad, router_grad), 'expert')]
    ppermute x27 -> x69, starting transfers between devices: 22.2 us -> 86.1 us  [shift(): return lax.ppermute(v, axis, [(i, (i + k) % n) for i in range(n)])]
    ppermute x27 -> x69, waiting for transfers between devices: 24.1 us -> 77.8 us  [shift(): return lax.ppermute(v, axis, [(i, (i + k) % n) for i in range(n)])]
    psum x1, waiting for transfers between devices: 0.01 us -> 44.9 us  [per_device(): out_grad = lax.psum(out_part, 'expert').astype(f32)]
    unnamed x147 -> x30, local copies, waits for them, and re-layouts: 42.5 us -> 4.95 us
    all_to_all x3 -> x0, starting transfers between devices: 15.3 us -> none  [exchange(): lax.all_to_all(v.reshape(n_e, rows // n_e, w), 'expert', split_axis=0, co...]
    all_to_all x3 -> x0, waiting for transfers between devices: 9.85 us -> none  [exchange(): lax.all_to_all(v.reshape(n_e, rows // n_e, w), 'expert', split_axis=0, co...]
    pallas_call x8 -> x15, Pallas kernels: 20.2 us -> 22.6 us  [run(): pl.pallas_call(body, out_shape=[jax.ShapeDtypeStruct(s, d) for s, d in ou...]
  transfers between devices with their start and end apart: 31 -> 70, of which waited for: 10 -> 31; matrix products, arithmetic and copies ran while one was open for 6% -> 1% of each run, Pallas kernels for 4% -> 6%
where the time goes in v2:
time: 256 us
  waiting for transfers between devices  123 us (48%)
  starting transfers between devices  86.1 us (34%)
  Pallas kernels  22.6 us (9%)
  between operations  14.3 us (6%)
  local copies, waits for them, and re-layouts  7.52 us (3%)
    ppermute x69, starting transfers between devices, shift(): return lax.ppermute(v, axis, [(i, (i + k) % n) for i in range(n)])  86.1 us
    ppermute x69, waiting for transfers between devices, shift(): return lax.ppermute(v, axis, [(i, (i + k) % n) for i in range(n)])  77.8 us
    psum x1, waiting for transfers between devices, per_device(): out_grad = lax.psum(out_part, 'expert').astype(f32)  44.9 us
    pallas_call x15, Pallas kernels, run(): pl.pallas_call(body, out_shape=[jax.ShapeDtypeStruct(s, d) for s, d in ou...  22.6 us
  transfers between devices with their start and end apart: 70, of which 31 were waited for; matrix products, arithmetic and copies ran while one was open for 1% of the time, Pallas kernels for 6%

profile of v2, /device:TPU:0, one launch (start us, length us, event | category | flops | bytes accessed | tf_op | source)
XLA Modules:
  0.0 255.8 jit_solution(882760445723439906)
XLA Ops:
  7.2 2.5 collective-permute-start.2
  18.3 2.3 shard_map.205
  21.7 1.5 collective-permute-start.19
  23.2 1.6 collective-permute-start.20
  24.8 2.6 %collective-permute-start.21 = (bf16[40,192]{1,0:T(8,128)(2,1)S(1)}, bf16[40,192]{1,0:T(8,128)(2,1)S(1)}, u32[]{:S(2)}, u32[]{:S(2)}) collective-permute-start(bf16[40,192]{1,0:T(8,128)(2,1)S(1)} %get-tuple-element.101), channel_id=1, source_target_pairs={{0,12},{4,16},{8,20},{12,24},{16,28},{20,0},{24,4},{28,8},{1,13},{... | collective-permute-start | bytes 46088 | tf_op jit(solution)/shard_map/ppermute | solution.py:458
  28.6 2.6 %collective-permute-start.23 = (bf16[40,192]{1,0:T(8,128)(2,1)S(1)}, bf16[40,192]{1,0:T(8,128)(2,1)S(1)}, u32[]{:S(2)}, u32[]{:S(2)}) collective-permute-start(bf16[40,192]{1,0:T(8,128)(2,1)S(1)} %get-tuple-element.103), channel_id=1, source_target_pairs={{0,20},{4,24},{8,28},{12,0},{16,4},{20,8},{24,12},{28,16},{1,21},{... | collective-permute-start | bytes 46088 | tf_op jit(solution)/shard_map/ppermute | solution.py:458
  32.6 1.4 collective-permute-start.25
  40.5 2.0 collective-permute-done.4.p2
  43.5 1.6 collective-permute-start.9
  45.4 2.1 collective-permute-start.11
  47.4 2.1 collective-permute-start.12
  50.4 2.3 collective-permute-start.13
  52.8 1.4 collective-permute-start.15
  55.1 1.4 collective-permute-done.14.refs_6_
  59.4 9.4 %collective-permute-done.27.g2 = bf16[320,192]{1,0:T(8,128)(2,1)S(1)} collective-permute-done((bf16[320,192]{1,0:T(8,128)(2,1)S(1)}, bf16[320,192]{1,0:T(8,128)(2,1)S(1)}, u32[]{:S(2)}, u32[]{:S(2)}) %collective-permute-start.27) | collective-permute-done | bytes 122912 | tf_op jit(solution)/shard_map/ppermute | solution.py:458
  68.8 2.5 collective-permute-done.26.g1
  71.3 3.1 %shard_map.210 = (bf16[320,384]{1,0:T(8,128)(2,1)S(1)}, bf16[320,384]{1,0:T(8,128)(2,1)S(1)}, bf16[320,384]{1,0:T(8,128)(2,1)S(1)}, bf16[320,384]{1,0:T(8,128)(2...) custom-call(s32[2]{0:T(128)S(1)} %pad_add_fusion.ids, ...), custom_call_target="tpu_custom_call" | custom-call | bytes 6332424 | tf_op jit(solution)/shard_map/pallas_call | solution.py:50
  78.0 4.1 %collective-permute-done.29.c1 = bf16[320,384]{1,0:T(8,128)(2,1)S(1)} collective-permute-done((bf16[320,384]{1,0:T(8,128)(2,1)S(1)}, bf16[320,384]{1,0:T(8,128)(2,1)S(1)}, u32[]{:S(2)}, u32[]{:S(2)}) %collective-permute-start.29) | collective-permute-done | bytes 245792 | tf_op jit(solution)/shard_map/ppermute | solution.py:458
  83.3 4.1 %collective-permute-start.68 = (bf16[768,128]{1,0:T(8,128)(2,1)S(1)}, bf16[768,128]{1,0:T(8,128)(2,1)S(1)}, u32[]{:S(2)}, u32[]{:S(2)}) collective-permute-start(bf16[768,128]{1,0:T(8,128)(2,1)S(1)} %get-tuple-element.136.h1.refs_8_), channel_id=1, source_target_pairs={{0,28},{4,0},{8,4},{12,8},{16,12},{20,16},{24,20},{28,24},{1,29},{... | collective-permute-start | bytes 589832 | tf_op jit(solution)/shard_map/ppermute | solution.py:458
  87.4 1.8 collective-permute-start.67
  89.6 2.7 %collective-permute-start.32 = (bf16[40,384]{1,0:T(8,128)(2,1)S(1)}, bf16[40,384]{1,0:T(8,128)(2,1)S(1)}, u32[]{:S(2)}, u32[]{:S(2)}) collective-permute-start(bf16[40,384]{1,0:T(8,128)(2,1)S(1)} %get-tuple-element.111), channel_id=1, source_target_pairs={{0,4},{4,8},{8,12},{12,16},{16,20},{20,24},{24,28},{28,0},{1,5},{5... | collective-permute-start | bytes 92168 | tf_op jit(solution)/shard_map/ppermute | solution.py:458
  92.4 1.9 collective-permute-start.33
  94.3 1.5 collective-permute-start.34
  95.8 2.0 collective-permute-done.32.refs_1_
  97.8 3.0 %collective-permute-start.35 = (bf16[40,384]{1,0:T(8,128)(2,1)S(1)}, bf16[40,384]{1,0:T(8,128)(2,1)S(1)}, u32[]{:S(2)}, u32[]{:S(2)}) collective-permute-start(bf16[40,384]{1,0:T(8,128)(2,1)S(1)} %get-tuple-element.114), channel_id=1, source_target_pairs={{0,16},{4,20},{8,24},{12,28},{16,0},{20,4},{24,8},{28,12},{1,17},{... | collective-permute-start | bytes 92168 | tf_op jit(solution)/shard_map/ppermute | solution.py:458
  101.4 2.9 %collective-permute-start.37 = (bf16[40,384]{1,0:T(8,128)(2,1)S(1)}, bf16[40,384]{1,0:T(8,128)(2,1)S(1)}, u32[]{:S(2)}, u32[]{:S(2)}) collective-permute-start(bf16[40,384]{1,0:T(8,128)(2,1)S(1)} %get-tuple-element.116), channel_id=1, source_target_pairs={{0,24},{4,28},{8,0},{12,4},{16,8},{20,12},{24,16},{28,20},{1,25},{... | collective-permute-start | bytes 92168 | tf_op jit(solution)/shard_map/ppermute | solution.py:458
  105.9 2.3 collective-permute-done.38.refs_7_
  109.8 1.6 collective-permute-done.41.b3
  111.3 2.4 collective-permute-done.40.b2
  114.0 3.0 %shard_map.213 = (bf16[208,128]{1,0:T(8,128)(2,1)S(1)}, bf16[208,128]{1,0:T(8,128)(2,1)S(1)}, bf16[208,128]{1,0:T(8,128)(2,1)S(1)}, bf16[208,128]{1,0:T(8,128)(2...) custom-call(s32[2]{0:T(128)S(1)} %pad_add_fusion.ids, ...), custom_call_target="tpu_custom_call" | custom-call | bytes 3313672 | tf_op jit(solution)/shard_map/pallas_call | solution.py:50
  117.0 2.0 shard_map.215
  119.0 3.4 %collective-permute-start.51 = (f32[16,768]{1,0:T(8,128)S(1)}, f32[16,768]{1,0:T(8,128)S(1)}, u32[]{:S(2)}, u32[]{:S(2)}) collective-permute-start(f32[16,768]{1,0:T(8,128)S(1)} %get-tuple-element.135.refs_0_), channel_id=1, source_target_pairs={{0,28},{4,0},{8,4},{12,8},{16,12},{20,16},{24,20},{28,24},{1,29},{... | collective-permute-start | bytes 147464 | tf_op jit(solution)/shard_map/ppermute | solution.py:458
  122.7 2.6 %collective-permute-start.48 = (f32[16,768]{1,0:T(8,128)S(1)}, f32[16,768]{1,0:T(8,128)S(1)}, u32[]{:S(2)}, u32[]{:S(2)}) collective-permute-start(f32[16,768]{1,0:T(8,128)S(1)} %get-tuple-element.135.refs_0_), channel_id=1, source_target_pairs={{0,16},{4,20},{8,24},{12,28},{16,0},{20,4},{24,8},{28,12},{1,17},{... | collective-permute-start | bytes 147464 | tf_op jit(solution)/shard_map/ppermute | solution.py:458
  125.8 2.4 collective-permute-start.46
  128.8 3.3 %collective-permute-start.66 = (bf16[768,128]{1,0:T(8,128)(2,1)S(1)}, bf16[768,128]{1,0:T(8,128)(2,1)S(1)}, u32[]{:S(2)}, u32[]{:S(2)}) collective-permute-start(bf16[768,128]{1,0:T(8,128)(2,1)S(1)} %get-tuple-element.136.h1.refs_8_), channel_id=1, source_target_pairs={{0,20},{4,24},{8,28},{12,0},{16,4},{20,8},{24,12},{28,16},{1,21},{... | collective-permute-start | bytes 589832 | tf_op jit(solution)/shard_map/ppermute | solution.py:458
  132.6 1.5 collective-permute-done.47.refs_3_
  134.2 2.5 collective-permute-start.63
  136.6 6.6 %collective-permute-start.62 = (bf16[768,128]{1,0:T(8,128)(2,1)S(1)}, bf16[768,128]{1,0:T(8,128)(2,1)S(1)}, u32[]{:S(2)}, u32[]{:S(2)}) collective-permute-start(bf16[768,128]{1,0:T(8,128)(2,1)S(1)} %get-tuple-element.136.h1.refs_8_), channel_id=1, source_target_pairs={{0,4},{4,8},{8,12},{12,16},{16,20},{20,24},{24,28},{28,0},{1,5},{5... | collective-permute-start | bytes 589832 | tf_op jit(solution)/shard_map/ppermute | solution.py:458
  144.2 12.9 %collective-permute-done.65.refs_12_ = bf16[768,128]{1,0:T(8,128)(2,1)S(1)} collective-permute-done((bf16[768,128]{1,0:T(8,128)(2,1)S(1)}, bf16[768,128]{1,0:T(8,128)(2,1)S(1)}, u32[]{:S(2)}, u32[]{:S(2)}) %collective-permute-start.65) | collective-permute-done | bytes 196640 | tf_op jit(solution)/shard_map/ppermute | solution.py:458
  157.1 6.0 %collective-permute-done.64.refs_11_ = bf16[768,128]{1,0:T(8,128)(2,1)S(1)} collective-permute-done((bf16[768,128]{1,0:T(8,128)(2,1)S(1)}, bf16[768,128]{1,0:T(8,128)(2,1)S(1)}, u32[]{:S(2)}, u32[]{:S(2)}) %collective-permute-start.64) | collective-permute-done | bytes 196640 | tf_op jit(solution)/shard_map/ppermute | solution.py:458
  163.1 3.2 %shard_map.218 = (f32[1,768,768]{2,1,0:T(8,128)}, f32[1,768,768]{2,1,0:T(8,128)}) custom-call(bf16[320,768]{1,0:T(8,128)(2,1)S(1)} %get-tuple-element.138.u, bf16[320,768]{1,0:T(8,128)(2,1)S(1)} %get-tuple-element.139.z, bf16[320,768]{1,0:T(8,128)(2,1)S(1)} %get-tuple-element.140.de, bf16[320,768]{1,0:T(8,128)(2,1)S(1)} %get-tuple-element.141.da), custom_call_target="tpu_custom_call" | custom-call | bytes 6684672 | tf_op jit(solution)/shard_map/pallas_call | solution.py:50
  172.2 2.2 collective-permute-start.58
  174.7 1.7 collective-permute-start.56
  180.5 15.2 %collective-permute-done.58.refs_4_ = bf16[576,128]{1,0:T(8,128)(2,1)S(1)} collective-permute-done((bf16[576,128]{1,0:T(8,128)(2,1)S(1)}, bf16[576,128]{1,0:T(8,128)(2,1)S(1)}, u32[]{:S(2)}, u32[]{:S(2)}) %collective-permute-start.58) | collective-permute-done | bytes 147488 | tf_op jit(solution)/shard_map/ppermute | solution.py:458
  195.7 3.3 %collective-permute-done.57.refs_3_ = bf16[576,128]{1,0:T(8,128)(2,1)S(1)} collective-permute-done((bf16[576,128]{1,0:T(8,128)(2,1)S(1)}, bf16[576,128]{1,0:T(8,128)(2,1)S(1)}, u32[]{:S(2)}, u32[]{:S(2)}) %collective-permute-start.57) | collective-permute-done | bytes 147488 | tf_op jit(solution)/shard_map/ppermute | solution.py:458
  199.1 3.2 %shard_map.217 = f32[576,768]{1,0:T(8,128)} custom-call(bf16[576,128]{1,0:T(8,128)(2,1)S(1)} %get-tuple-element.131.d_proj.refs_0_, bf16[576,128]{1,0:T(8,128)(2,1)S(1)} %collective-permute-done.55.refs_1_, bf16[576,128]{1,0:T(8,128)(2,1)S(1)} %collective-permute-done.56.refs_2_, bf16[576,128]{1,0:T(8,128)(2,1)S(1)} %collective-permute-done.57.refs_3_, ...), custom_call_target="tpu_custom_call" | custom-call | bytes 4521984 | tf_op jit(solution)/shard_map/pallas_call | solution.py:50
  202.3 44.9 %all-reduce.2.cloned.1.call-done = bf16[192,768]{1,0:T(8,128)(2,1)} async-done(((bf16[192,768]{1,0:T(8,128)(2,1)}), bf16[192,768]{1,0:T(8,128)(2,1)}) %all-reduce.2.cloned.1.call-update) | async-done | bytes 294928 | tf_op jit(solution)/shard_map/psum | solution.py:602
  247.2 1.8 convert_element_type.3
  (146 shorter events, 47.2 us)
Async XLA Ops:
  7.2 240.0 %all-reduce.2.cloned.1.call-start = ((), (), s32[]{:S(2)}) async-start(), calls=%async_computation | async-start | bytes 589824 | tf_op jit(solution)/shard_map/psum | solution.py:602
  7.2 9.0 %collective-permute-start.2 = (bf16[192,128]{1,0:T(8,128)(2,1)}, bf16[192,128]{1,0:T(8,128)(2,1)S(1)}, u32[]{:S(2)}, u32[]{:S(2)}) collective-permute-start(bf16[192,128]{1,0:T(8,128)(2,1)} %bitcast.26), channel_id=1, source_target_pairs={{0,3},{1,0},{2,1},{3,2},{4,7},{5,4},{6,5},{7,6},{8,11},{9,8},{10,9... | collective-permute-start | bytes 147464 | tf_op jit(solution)/shard_map/ppermute | solution.py:458
  9.7 6.6 %collective-permute-start.1 = (bf16[192,128]{1,0:T(8,128)(2,1)}, bf16[192,128]{1,0:T(8,128)(2,1)S(1)}, u32[]{:S(2)}, u32[]{:S(2)}) collective-permute-start(bf16[192,128]{1,0:T(8,128)(2,1)} %bitcast.27), channel_id=1, source_target_pairs={{0,2},{1,3},{2,0},{3,1},{4,6},{5,7},{6,4},{7,5},{8,10},{9,11},{10,... | collective-permute-start | bytes 147464 | tf_op jit(solution)/shard_map/ppermute | solution.py:458
  21.7 9.5 %collective-permute-start.19 = (bf16[40,192]{1,0:T(8,128)(2,1)S(1)}, bf16[40,192]{1,0:T(8,128)(2,1)S(1)}, u32[]{:S(2)}, u32[]{:S(2)}) collective-permute-start(bf16[40,192]{1,0:T(8,128)(2,1)S(1)} %get-tuple-element.99), channel_id=1, source_target_pairs={{0,4},{4,8},{8,12},{12,16},{16,20},{20,24},{24,28},{28,0},{1,5},{5... | collective-permute-start | bytes 46088 | tf_op jit(solution)/shard_map/ppermute | solution.py:458
  23.2 9.3 %collective-permute-start.20 = (bf16[40,192]{1,0:T(8,128)(2,1)S(1)}, bf16[40,192]{1,0:T(8,128)(2,1)S(1)}, u32[]{:S(2)}, u32[]{:S(2)}) collective-permute-start(bf16[40,192]{1,0:T(8,128)(2,1)S(1)} %get-tuple-element.100), channel_id=1, source_target_pairs={{0,8},{4,12},{8,16},{12,20},{16,24},{20,28},{24,0},{28,4},{1,9},{5... | collective-permute-start | bytes 46088 | tf_op jit(solution)/shard_map/ppermute | solution.py:458
  24.8 9.2 %collective-permute-start.21 = (bf16[40,192]{1,0:T(8,128)(2,1)S(1)}, bf16[40,192]{1,0:T(8,128)(2,1)S(1)}, u32[]{:S(2)}, u32[]{:S(2)}) collective-permute-start(bf16[40,192]{1,0:T(8,128)(2,1)S(1)} %get-tuple-element.101), channel_id=1, source_target_pairs={{0,12},{4,16},{8,20},{12,24},{16,28},{20,0},{24,4},{28,8},{1,13},{... | collective-permute-start | bytes 46088 | tf_op jit(solution)/shard_map/ppermute | solution.py:458
  27.4 6.6 %collective-permute-start.22 = (bf16[40,192]{1,0:T(8,128)(2,1)S(1)}, bf16[40,192]{1,0:T(8,128)(2,1)S(1)}, u32[]{:S(2)}, u32[]{:S(2)}) collective-permute-start(bf16[40,192]{1,0:T(8,128)(2,1)S(1)} %get-tuple-element.102), channel_id=1, source_target_pairs={{0,16},{4,20},{8,24},{12,28},{16,0},{20,4},{24,8},{28,12},{1,17},{... | collective-permute-start | bytes 46088 | tf_op jit(solution)/shard_map/ppermute | solution.py:458
  36.4 22.6 %collective-permute-start.28 = (bf16[320,192]{1,0:T(8,128)(2,1)S(1)}, bf16[320,192]{1,0:T(8,128)(2,1)S(1)}, u32[]{:S(2)}, u32[]{:S(2)}) collective-permute-start(bf16[320,192]{1,0:T(8,128)(2,1)S(1)} %shard_map.209.g0), channel_id=1, source_target_pairs={{0,3},{1,0},{2,1},{3,2},{4,7},{5,4},{6,5},{7,6},{8,11},{9,8},{10,9... | collective-permute-start | bytes 368648 | tf_op jit(solution)/shard_map/ppermute | solution.py:458
  43.5 6.8 %collective-permute-start.9 = (bf16[40,208]{1,0:T(8,128)(2,1)S(1)}, bf16[40,208]{1,0:T(8,128)(2,1)S(1)}, u32[]{:S(2)}, u32[]{:S(2)}) collective-permute-start(bf16[40,208]{1,0:T(8,128)(2,1)S(1)} %get-tuple-element.91), channel_id=1, source_target_pairs={{0,4},{4,8},{8,12},{12,16},{16,20},{20,24},{24,28},{28,0},{1,5},{5... | collective-permute-start | bytes 49928 | tf_op jit(solution)/shard_map/ppermute | solution.py:458
  45.2 7.5 %collective-permute-start.10 = (bf16[40,208]{1,0:T(8,128)(2,1)S(1)}, bf16[40,208]{1,0:T(8,128)(2,1)S(1)}, u32[]{:S(2)}, u32[]{:S(2)}) collective-permute-start(bf16[40,208]{1,0:T(8,128)(2,1)S(1)} %get-tuple-element.92), channel_id=1, source_target_pairs={{0,8},{4,12},{8,16},{12,20},{16,24},{20,28},{24,0},{28,4},{1,9},{5... | collective-permute-start | bytes 49928 | tf_op jit(solution)/shard_map/ppermute | solution.py:458
  45.4 7.4 %collective-permute-start.11 = (bf16[40,208]{1,0:T(8,128)(2,1)S(1)}, bf16[40,208]{1,0:T(8,128)(2,1)S(1)}, u32[]{:S(2)}, u32[]{:S(2)}) collective-permute-start(bf16[40,208]{1,0:T(8,128)(2,1)S(1)} %get-tuple-element.93), channel_id=1, source_target_pairs={{0,12},{4,16},{8,20},{12,24},{16,28},{20,0},{24,4},{28,8},{1,13},{... | collective-permute-start | bytes 49928 | tf_op jit(solution)/shard_map/ppermute | solution.py:458
  47.4 6.8 %collective-permute-start.12 = (bf16[40,208]{1,0:T(8,128)(2,1)S(1)}, bf16[40,208]{1,0:T(8,128)(2,1)S(1)}, u32[]{:S(2)}, u32[]{:S(2)}) collective-permute-start(bf16[40,208]{1,0:T(8,128)(2,1)S(1)} %get-tuple-element.94), channel_id=1, source_target_pairs={{0,16},{4,20},{8,24},{12,28},{16,0},{20,4},{24,8},{28,12},{1,17},{... | collective-permute-start | bytes 49928 | tf_op jit(solution)/shard_map/ppermute | solution.py:458
  56.6 14.7 %collective-permute-start.18 = (bf16[320,208]{1,0:T(8,128)(2,1)S(1)}, bf16[320,208]{1,0:T(8,128)(2,1)S(1)}, u32[]{:S(2)}, u32[]{:S(2)}) collective-permute-start(bf16[320,208]{1,0:T(8,128)(2,1)S(1)} %shard_map.208.h0), channel_id=1, source_target_pairs={{0,3},{1,0},{2,1},{3,2},{4,7},{5,4},{6,5},{7,6},{8,11},{9,8},{10,9... | collective-permute-start | bytes 399368 | tf_op jit(solution)/shard_map/ppermute | solution.py:458
  56.7 14.6 %collective-permute-start.17 = (bf16[320,208]{1,0:T(8,128)(2,1)S(1)}, bf16[320,208]{1,0:T(8,128)(2,1)S(1)}, u32[]{:S(2)}, u32[]{:S(2)}) collective-permute-start(bf16[320,208]{1,0:T(8,128)(2,1)S(1)} %shard_map.208.h0), channel_id=1, source_target_pairs={{0,2},{1,3},{2,0},{3,1},{4,6},{5,7},{6,4},{7,5},{8,10},{9,11},{10,... | collective-permute-start | bytes 399368 | tf_op jit(solution)/shard_map/ppermute | solution.py:458
  57.5 13.8 %collective-permute-start.16 = (bf16[320,208]{1,0:T(8,128)(2,1)S(1)}, bf16[320,208]{1,0:T(8,128)(2,1)S(1)}, u32[]{:S(2)}, u32[]{:S(2)}) collective-permute-start(bf16[320,208]{1,0:T(8,128)(2,1)S(1)} %shard_map.208.h0), channel_id=1, source_target_pairs={{0,1},{1,2},{2,3},{3,0},{4,5},{5,6},{6,7},{7,4},{8,9},{9,10},{10,1... | collective-permute-start | bytes 399368 | tf_op jit(solution)/shard_map/ppermute | solution.py:458
  57.7 11.1 %collective-permute-start.27 = (bf16[320,192]{1,0:T(8,128)(2,1)S(1)}, bf16[320,192]{1,0:T(8,128)(2,1)S(1)}, u32[]{:S(2)}, u32[]{:S(2)}) collective-permute-start(bf16[320,192]{1,0:T(8,128)(2,1)S(1)} %shard_map.209.g0), channel_id=1, source_target_pairs={{0,2},{1,3},{2,0},{3,1},{4,6},{5,7},{6,4},{7,5},{8,10},{9,11},{10,... | collective-permute-start | bytes 368648 | tf_op jit(solution)/shard_map/ppermute | solution.py:458
  58.9 12.4 %collective-permute-start.26 = (bf16[320,192]{1,0:T(8,128)(2,1)S(1)}, bf16[320,192]{1,0:T(8,128)(2,1)S(1)}, u32[]{:S(2)}, u32[]{:S(2)}) collective-permute-start(bf16[320,192]{1,0:T(8,128)(2,1)S(1)} %shard_map.209.g0), channel_id=1, source_target_pairs={{0,1},{1,2},{2,3},{3,0},{4,5},{5,6},{6,7},{7,4},{8,9},{9,10},{10,1... | collective-permute-start | bytes 368648 | tf_op jit(solution)/shard_map/ppermute | solution.py:458
  74.4 7.7 %collective-permute-start.29 = (bf16[320,384]{1,0:T(8,128)(2,1)S(1)}, bf16[320,384]{1,0:T(8,128)(2,1)S(1)}, u32[]{:S(2)}, u32[]{:S(2)}) collective-permute-start(bf16[320,384]{1,0:T(8,128)(2,1)S(1)} %get-tuple-element.107), channel_id=1, source_target_pairs={{0,1},{1,2},{2,3},{3,0},{4,5},{5,6},{6,7},{7,4},{8,9},{9,10},{10,1... | collective-permute-start | bytes 737288 | tf_op jit(solution)/shard_map/ppermute | solution.py:458
  74.5 8.8 %collective-permute-start.30 = (bf16[320,384]{1,0:T(8,128)(2,1)S(1)}, bf16[320,384]{1,0:T(8,128)(2,1)S(1)}, u32[]{:S(2)}, u32[]{:S(2)}) collective-permute-start(bf16[320,384]{1,0:T(8,128)(2,1)S(1)} %get-tuple-element.108), channel_id=1, source_target_pairs={{0,2},{1,3},{2,0},{3,1},{4,6},{5,7},{6,4},{7,5},{8,10},{9,11},{10,... | collective-permute-start | bytes 737288 | tf_op jit(solution)/shard_map/ppermute | solution.py:458
  75.8 11.6 %collective-permute-start.31 = (bf16[320,384]{1,0:T(8,128)(2,1)S(1)}, bf16[320,384]{1,0:T(8,128)(2,1)S(1)}, u32[]{:S(2)}, u32[]{:S(2)}) collective-permute-start(bf16[320,384]{1,0:T(8,128)(2,1)S(1)} %get-tuple-element.109), channel_id=1, source_target_pairs={{0,3},{1,0},{2,1},{3,2},{4,7},{5,4},{6,5},{7,6},{8,11},{9,8},{10,9... | collective-permute-start | bytes 737288 | tf_op jit(solution)/shard_map/ppermute | solution.py:458
  77.2 12.4 %collective-permute-start.8 = (bf16[400,128]{1,0:T(8,128)(2,1)S(1)}, bf16[400,128]{1,0:T(8,128)(2,1)S(1)}, u32[]{:S(2)}, u32[]{:S(2)}) collective-permute-start(bf16[400,128]{1,0:T(8,128)(2,1)S(1)} %get-tuple-element.88.t0), channel_id=1, source_target_pairs={{0,3},{1,0},{2,1},{3,2},{4,7},{5,4},{6,5},{7,6},{8,11},{9,8},{10,9... | collective-permute-start | bytes 307208 | tf_op jit(solution)/shard_map/ppermute | solution.py:458
  77.2 15.2 %collective-permute-start.7 = (bf16[400,128]{1,0:T(8,128)(2,1)S(1)}, bf16[400,128]{1,0:T(8,128)(2,1)S(1)}, u32[]{:S(2)}, u32[]{:S(2)}) collective-permute-start(bf16[400,128]{1,0:T(8,128)(2,1)S(1)} %get-tuple-element.88.t0), channel_id=1, source_target_pairs={{0,2},{1,3},{2,0},{3,1},{4,6},{5,7},{6,4},{7,5},{8,10},{9,11},{10,... | collective-permute-start | bytes 307208 | tf_op jit(solution)/shard_map/ppermute | solution.py:458
  82.1 12.2 %collective-permute-start.6 = (bf16[400,128]{1,0:T(8,128)(2,1)S(1)}, bf16[400,128]{1,0:T(8,128)(2,1)S(1)}, u32[]{:S(2)}, u32[]{:S(2)}) collective-permute-start(bf16[400,128]{1,0:T(8,128)(2,1)S(1)} %get-tuple-element.88.t0), channel_id=1, source_target_pairs={{0,1},{1,2},{2,3},{3,0},{4,5},{5,6},{6,7},{7,4},{8,9},{9,10},{10,1... | collective-permute-start | bytes 307208 | tf_op jit(solution)/shard_map/ppermute | solution.py:458
  83.3 39.4 %collective-permute-start.68 = (bf16[768,128]{1,0:T(8,128)(2,1)S(1)}, bf16[768,128]{1,0:T(8,128)(2,1)S(1)}, u32[]{:S(2)}, u32[]{:S(2)}) collective-permute-start(bf16[768,128]{1,0:T(8,128)(2,1)S(1)} %get-tuple-element.136.h1.refs_8_), channel_id=1, source_target_pairs={{0,28},{4,0},{8,4},{12,8},{16,12},{20,16},{24,20},{28,24},{1,29},{... | collective-permute-start | bytes 589832 | tf_op jit(solution)/shard_map/ppermute | solution.py:458
  87.4 37.9 %collective-permute-start.67 = (bf16[768,128]{1,0:T(8,128)(2,1)S(1)}, bf16[768,128]{1,0:T(8,128)(2,1)S(1)}, u32[]{:S(2)}, u32[]{:S(2)}) collective-permute-start(bf16[768,128]{1,0:T(8,128)(2,1)S(1)} %get-tuple-element.136.h1.refs_8_), channel_id=1, source_target_pairs={{0,24},{4,28},{8,0},{12,4},{16,8},{20,12},{24,16},{28,20},{1,25},{... | collective-permute-start | bytes 589832 | tf_op jit(solution)/shard_map/ppermute | solution.py:458
  89.6 8.3 %collective-permute-start.32 = (bf16[40,384]{1,0:T(8,128)(2,1)S(1)}, bf16[40,384]{1,0:T(8,128)(2,1)S(1)}, u32[]{:S(2)}, u32[]{:S(2)}) collective-permute-start(bf16[40,384]{1,0:T(8,128)(2,1)S(1)} %get-tuple-element.111), channel_id=1, source_target_pairs={{0,4},{4,8},{8,12},{12,16},{16,20},{20,24},{24,28},{28,0},{1,5},{5... | collective-permute-start | bytes 92168 | tf_op jit(solution)/shard_map/ppermute | solution.py:458
  92.4 8.4 %collective-permute-start.33 = (bf16[40,384]{1,0:T(8,128)(2,1)S(1)}, bf16[40,384]{1,0:T(8,128)(2,1)S(1)}, u32[]{:S(2)}, u32[]{:S(2)}) collective-permute-start(bf16[40,384]{1,0:T(8,128)(2,1)S(1)} %get-tuple-element.112), channel_id=1, source_target_pairs={{0,8},{4,12},{8,16},{12,20},{16,24},{20,28},{24,0},{28,4},{1,9},{5... | collective-permute-start | bytes 92168 | tf_op jit(solution)/shard_map/ppermute | solution.py:458
  94.3 7.1 %collective-permute-start.34 = (bf16[40,384]{1,0:T(8,128)(2,1)S(1)}, bf16[40,384]{1,0:T(8,128)(2,1)S(1)}, u32[]{:S(2)}, u32[]{:S(2)}) collective-permute-start(bf16[40,384]{1,0:T(8,128)(2,1)S(1)} %get-tuple-element.113), channel_id=1, source_target_pairs={{0,12},{4,16},{8,20},{12,24},{16,28},{20,0},{24,4},{28,8},{1,13},{... | collective-permute-start | bytes 92168 | tf_op jit(solution)/shard_map/ppermute | solution.py:458
  97.8 6.5 %collective-permute-start.35 = (bf16[40,384]{1,0:T(8,128)(2,1)S(1)}, bf16[40,384]{1,0:T(8,128)(2,1)S(1)}, u32[]{:S(2)}, u32[]{:S(2)}) collective-permute-start(bf16[40,384]{1,0:T(8,128)(2,1)S(1)} %get-tuple-element.114), channel_id=1, source_target_pairs={{0,16},{4,20},{8,24},{12,28},{16,0},{20,4},{24,8},{28,12},{1,17},{... | collective-permute-start | bytes 92168 | tf_op jit(solution)/shard_map/ppermute | solution.py:458
  119.0 6.7 %collective-permute-start.51 = (f32[16,768]{1,0:T(8,128)S(1)}, f32[16,768]{1,0:T(8,128)S(1)}, u32[]{:S(2)}, u32[]{:S(2)}) collective-permute-start(f32[16,768]{1,0:T(8,128)S(1)} %get-tuple-element.135.refs_0_), channel_id=1, source_target_pairs={{0,28},{4,0},{8,4},{12,8},{16,12},{20,16},{24,20},{28,24},{1,29},{... | collective-permute-start | bytes 147464 | tf_op jit(solution)/shard_map/ppermute | solution.py:458
  122.7 9.4 %collective-permute-start.48 = (f32[16,768]{1,0:T(8,128)S(1)}, f32[16,768]{1,0:T(8,128)S(1)}, u32[]{:S(2)}, u32[]{:S(2)}) collective-permute-start(f32[16,768]{1,0:T(8,128)S(1)} %get-tuple-element.135.refs_0_), channel_id=1, source_target_pairs={{0,16},{4,20},{8,24},{12,28},{16,0},{20,4},{24,8},{28,12},{1,17},{... | collective-permute-start | bytes 147464 | tf_op jit(solution)/shard_map/ppermute | solution.py:458
  125.3 8.8 %collective-permute-start.47 = (f32[16,768]{1,0:T(8,128)S(1)}, f32[16,768]{1,0:T(8,128)S(1)}, u32[]{:S(2)}, u32[]{:S(2)}) collective-permute-start(f32[16,768]{1,0:T(8,128)S(1)} %get-tuple-element.135.refs_0_), channel_id=1, source_target_pairs={{0,12},{4,16},{8,20},{12,24},{16,28},{20,0},{24,4},{28,8},{1,13},{... | collective-permute-start | bytes 147464 | tf_op jit(solution)/shard_map/ppermute | solution.py:458
  125.8 8.4 %collective-permute-start.46 = (f32[16,768]{1,0:T(8,128)S(1)}, f32[16,768]{1,0:T(8,128)S(1)}, u32[]{:S(2)}, u32[]{:S(2)}) collective-permute-start(f32[16,768]{1,0:T(8,128)S(1)} %get-tuple-element.135.refs_0_), channel_id=1, source_target_pairs={{0,8},{4,12},{8,16},{12,20},{16,24},{20,28},{24,0},{28,4},{1,9},{5... | collective-permute-start | bytes 147464 | tf_op jit(solution)/shard_map/ppermute | solution.py:458
  128.2 8.4 %collective-permute-start.45 = (f32[16,768]{1,0:T(8,128)S(1)}, f32[16,768]{1,0:T(8,128)S(1)}, u32[]{:S(2)}, u32[]{:S(2)}) collective-permute-start(f32[16,768]{1,0:T(8,128)S(1)} %get-tuple-element.135.refs_0_), channel_id=1, source_target_pairs={{0,4},{4,8},{8,12},{12,16},{16,20},{20,24},{24,28},{28,0},{1,5},{5... | collective-permute-start | bytes 147464 | tf_op jit(solution)/shard_map/ppermute | solution.py:458
  128.8 14.5 %collective-permute-start.66 = (bf16[768,128]{1,0:T(8,128)(2,1)S(1)}, bf16[768,128]{1,0:T(8,128)(2,1)S(1)}, u32[]{:S(2)}, u32[]{:S(2)}) collective-permute-start(bf16[768,128]{1,0:T(8,128)(2,1)S(1)} %get-tuple-element.136.h1.refs_8_), channel_id=1, source_target_pairs={{0,20},{4,24},{8,28},{12,0},{16,4},{20,8},{24,12},{28,16},{1,21},{... | collective-permute-start | bytes 589832 | tf_op jit(solution)/shard_map/ppermute | solution.py:458
  132.1 24.9 %collective-permute-start.65 = (bf16[768,128]{1,0:T(8,128)(2,1)S(1)}, bf16[768,128]{1,0:T(8,128)(2,1)S(1)}, u32[]{:S(2)}, u32[]{:S(2)}) collective-permute-start(bf16[768,128]{1,0:T(8,128)(2,1)S(1)} %get-tuple-element.136.h1.refs_8_), channel_id=1, source_target_pairs={{0,16},{4,20},{8,24},{12,28},{16,0},{20,4},{24,8},{28,12},{1,17},{... | collective-permute-start | bytes 589832 | tf_op jit(solution)/shard_map/ppermute | solution.py:458
  134.1 28.9 %collective-permute-start.64 = (bf16[768,128]{1,0:T(8,128)(2,1)S(1)}, bf16[768,128]{1,0:T(8,128)(2,1)S(1)}, u32[]{:S(2)}, u32[]{:S(2)}) collective-permute-start(bf16[768,128]{1,0:T(8,128)(2,1)S(1)} %get-tuple-element.136.h1.refs_8_), channel_id=1, source_target_pairs={{0,12},{4,16},{8,20},{12,24},{16,28},{20,0},{24,4},{28,8},{1,13},{... | collective-permute-start | bytes 589832 | tf_op jit(solution)/shard_map/ppermute | solution.py:458
  134.2 32.1 %collective-permute-start.63 = (bf16[768,128]{1,0:T(8,128)(2,1)S(1)}, bf16[768,128]{1,0:T(8,128)(2,1)S(1)}, u32[]{:S(2)}, u32[]{:S(2)}) collective-permute-start(bf16[768,128]{1,0:T(8,128)(2,1)S(1)} %get-tuple-element.136.h1.refs_8_), channel_id=1, source_target_pairs={{0,8},{4,12},{8,16},{12,20},{16,24},{20,28},{24,0},{28,4},{1,9},{5... | collective-permute-start | bytes 589832 | tf_op jit(solution)/shard_map/ppermute | solution.py:458
  136.6 29.7 %collective-permute-start.62 = (bf16[768,128]{1,0:T(8,128)(2,1)S(1)}, bf16[768,128]{1,0:T(8,128)(2,1)S(1)}, u32[]{:S(2)}, u32[]{:S(2)}) collective-permute-start(bf16[768,128]{1,0:T(8,128)(2,1)S(1)} %get-tuple-element.136.h1.refs_8_), channel_id=1, source_target_pairs={{0,4},{4,8},{8,12},{12,16},{16,20},{20,24},{24,28},{28,0},{1,5},{5... | collective-permute-start | bytes 589832 | tf_op jit(solution)/shard_map/ppermute | solution.py:458
  143.3 24.1 %collective-permute-start.53 = (f32[1,768]{1,0:T(1,128)S(1)}, f32[1,768]{1,0:T(1,128)S(1)}, u32[]{:S(2)}, u32[]{:S(2)}) collective-permute-start(f32[1,768]{1,0:T(1,128)S(1)} %slice.16), channel_id=1, source_target_pairs={{0,2},{1,3},{2,0},{3,1},{4,6},{5,7},{6,4},{7,5},{8,10},{9,11},{10,... | collective-permute-start | bytes 9224 | tf_op jit(solution)/shard_map/ppermute | solution.py:458
  157.1 10.8 %collective-permute-start.54 = (f32[1,768]{1,0:T(1,128)S(1)}, f32[1,768]{1,0:T(1,128)S(1)}, u32[]{:S(2)}, u32[]{:S(2)}) collective-permute-start(f32[1,768]{1,0:T(1,128)S(1)} %slice.16), channel_id=1, source_target_pairs={{0,3},{1,0},{2,1},{3,2},{4,7},{5,4},{6,5},{7,6},{8,11},{9,8},{10,9... | collective-permute-start | bytes 9224 | tf_op jit(solution)/shard_map/ppermute | solution.py:458
  166.3 8.4 %collective-permute-start.61 = (bf16[576,128]{1,0:T(8,128)(2,1)S(1)}, bf16[576,128]{1,0:T(8,128)(2,1)S(1)}, u32[]{:S(2)}, u32[]{:S(2)}) collective-permute-start(bf16[576,128]{1,0:T(8,128)(2,1)S(1)} %get-tuple-element.131.d_proj.refs_0_), channel_id=1, source_target_pairs={{0,28},{4,0},{8,4},{12,8},{16,12},{20,16},{24,20},{28,24},{1,29},{... | collective-permute-start | bytes 442376 | tf_op jit(solution)/shard_map/ppermute | solution.py:458
  166.4 11.1 %collective-permute-start.60 = (bf16[576,128]{1,0:T(8,128)(2,1)S(1)}, bf16[576,128]{1,0:T(8,128)(2,1)S(1)}, u32[]{:S(2)}, u32[]{:S(2)}) collective-permute-start(bf16[576,128]{1,0:T(8,128)(2,1)S(1)} %get-tuple-element.131.d_proj.refs_0_), channel_id=1, source_target_pairs={{0,24},{4,28},{8,0},{12,4},{16,8},{20,12},{24,16},{28,20},{1,25},{... | collective-permute-start | bytes 442376 | tf_op jit(solution)/shard_map/ppermute | solution.py:458
  170.9 9.6 %collective-permute-start.59 = (bf16[576,128]{1,0:T(8,128)(2,1)S(1)}, bf16[576,128]{1,0:T(8,128)(2,1)S(1)}, u32[]{:S(2)}, u32[]{:S(2)}) collective-permute-start(bf16[576,128]{1,0:T(8,128)(2,1)S(1)} %get-tuple-element.131.d_proj.refs_0_), channel_id=1, source_target_pairs={{0,20},{4,24},{8,28},{12,0},{16,4},{20,8},{24,12},{28,16},{1,21},{... | collective-permute-start | bytes 442376 | tf_op jit(solution)/shard_map/ppermute | solution.py:458
  172.2 23.5 %collective-permute-start.58 = (bf16[576,128]{1,0:T(8,128)(2,1)S(1)}, bf16[576,128]{1,0:T(8,128)(2,1)S(1)}, u32[]{:S(2)}, u32[]{:S(2)}) collective-permute-start(bf16[576,128]{1,0:T(8,128)(2,1)S(1)} %get-tuple-element.131.d_proj.refs_0_), channel_id=1, source_target_pairs={{0,16},{4,20},{8,24},{12,28},{16,0},{20,4},{24,8},{28,12},{1,17},{... | collective-permute-start | bytes 442376 | tf_op jit(solution)/shard_map/ppermute | solution.py:458
  174.4 24.7 %collective-permute-start.57 = (bf16[576,128]{1,0:T(8,128)(2,1)S(1)}, bf16[576,128]{1,0:T(8,128)(2,1)S(1)}, u32[]{:S(2)}, u32[]{:S(2)}) collective-permute-start(bf16[576,128]{1,0:T(8,128)(2,1)S(1)} %get-tuple-element.131.d_proj.refs_0_), channel_id=1, source_target_pairs={{0,12},{4,16},{8,20},{12,24},{16,28},{20,0},{24,4},{28,8},{1,13},{... | collective-permute-start | bytes 442376 | tf_op jit(solution)/shard_map/ppermute | solution.py:458
  174.7 24.4 %collective-permute-start.56 = (bf16[576,128]{1,0:T(8,128)(2,1)S(1)}, bf16[576,128]{1,0:T(8,128)(2,1)S(1)}, u32[]{:S(2)}, u32[]{:S(2)}) collective-permute-start(bf16[576,128]{1,0:T(8,128)(2,1)S(1)} %get-tuple-element.131.d_proj.refs_0_), channel_id=1, source_target_pairs={{0,8},{4,12},{8,16},{12,20},{16,24},{20,28},{24,0},{28,4},{1,9},{5... | collective-permute-start | bytes 442376 | tf_op jit(solution)/shard_map/ppermute | solution.py:458
  177.5 21.6 %collective-permute-start.55 = (bf16[576,128]{1,0:T(8,128)(2,1)S(1)}, bf16[576,128]{1,0:T(8,128)(2,1)S(1)}, u32[]{:S(2)}, u32[]{:S(2)}) collective-permute-start(bf16[576,128]{1,0:T(8,128)(2,1)S(1)} %get-tuple-element.131.d_proj.refs_0_), channel_id=1, source_target_pairs={{0,4},{4,8},{8,12},{12,16},{16,20},{20,24},{24,28},{28,0},{1,5},{5... | collective-permute-start | bytes 442376 | tf_op jit(solution)/shard_map/ppermute | solution.py:458
  (37 other events, 342.1 us)
Sparse Core Ops, SparseCore 0:
  166.4 80.7 all-reduce.1

commit v3 on v2

--- a/solution.py
+++ b/solution.py
@@ -44,7 +44,7 @@
     return block
 
 
-def run(body, outs, *args, smem=0, scratch=(), flops=0):
+def run(body, outs, *args, smem=0, scratch=(), flops=0, limit=32):
     moved = sum(a.size * a.dtype.itemsize for a in args)
     moved += sum(math.prod(s) * jnp.dtype(d).itemsize for s, d in outs)
     return pl.pallas_call(
@@ -54,7 +54,7 @@
         + [pl.BlockSpec()] * (len(args) - smem),
         out_specs=[pl.BlockSpec()] * len(outs),
         scratch_shapes=list(scratch),
-        compiler_params=pltpu.CompilerParams(vmem_limit_bytes=32 * 2**20),
+        compiler_params=pltpu.CompilerParams(vmem_limit_bytes=limit * 2**20),
         cost_estimate=pl.CostEstimate(flops=flops, bytes_accessed=moved, transcendentals=0),
     )(*args)
 
@@ -102,13 +102,11 @@
 
 
 def route_kernel(
-    ids, routes, dy, router, gain, qkv_w, after, *refs, experts, cap, n_e, direct, n_t,
+    ids, routes, router, gain, qkv_w, after, dest, gain_col, rw_own, qkv_wt, chunks,
+    *, experts, cap, n_e, direct, n_t,
 ):
-    pieces = list(refs[:-5])
-    dest, gain_col, rw_own, qkv_wt, chunks = refs[-5:]
     tok = routes.shape[1]
-    width = dy.shape[0]
-    rows = experts * cap
+    width = rw_own.shape[1]
     e = ids[1].astype(f32)
     rt = routes[...]
     x_of = iota((experts, tok), 0)
@@ -129,12 +127,6 @@
             send.append(owner * cap + slot)
             back.append(owner * cap + slot)
     dest[...] = row_block(send + back, 8)
-    row = iota((rows, tok), 0).astype(f32)
-    place = ((row == send[0]) | (row == send[1])).astype(f32).astype(bf16)
-    full = mm(place, dy[...], (1, 1))
-    size = rows // len(pieces)
-    for k, piece in enumerate(pieces):
-        piece[...] = full[k * size:(k + 1) * size].astype(bf16)
     column_of(gain[...], gain_col)
     wide = router[...].astype(f32)
     for s in range(n_t):
@@ -177,7 +169,7 @@
 
 
 def dispatch_kernel(
-    ids, own, p1, p2, p3, x, dy, gain, rw_own, routes, dest, *refs
+    ids, own, p1, p2, p3, x, gain, rw_own, routes, dest, *refs
 ):
     pieces = refs[:-3]
     token_pack, residual, pack = refs[-3:]
@@ -194,10 +186,10 @@
     x_of = iota((experts, tok), 0)
     c0 = jnp.sum(jnp.where(routes[0:1, :] == x_of, logits, 0.0), axis=0, keepdims=True)
     c1 = jnp.sum(jnp.where(routes[1:2, :] == x_of, logits, 0.0), axis=0, keepdims=True)
-    stats = row_block(split_hi_lo(square) + split_hi_lo(c0 - c1)).astype(bf16)
+    number = (iota((1, tok), 1) + 1).astype(f32)
+    stats = row_block(split_hi_lo(square) + split_hi_lo(c0 - c1) + (number,)).astype(bf16)
     token_pack[0:width] = res.astype(bf16)
-    token_pack[width:width + 16] = stats
-    token_pack[width + 16:] = dy[...]
+    token_pack[width:] = stats
     pack[0:width] = scaled
     pack[width:] = stats
     size = pieces[0].shape[0]
@@ -206,7 +198,8 @@
     place1 = (row == dest[1:2, :]).astype(f32)
     both = mm((place0 + place1).astype(bf16), pack[...], (1, 1))
     signed = mm((place0 - place1).astype(bf16), pack[...], (1, 1))
-    full = jnp.where(iota(both.shape, 1) >= width + 2, signed, both)
+    lane = iota(both.shape, 1)
+    full = jnp.where((lane == width + 2) | (lane == width + 3), signed, both)
     for k, piece in enumerate(pieces):
         piece[...] = full[k * size:(k + 1) * size].astype(bf16)
 
@@ -220,27 +213,34 @@
 
 
 def expert_kernel(
-    ids, h0, h1, h2, h3, g0, g1, g2, g3, up, down,
-    c0, c1, c2, c3, u, z, de, da,
-    hs, gs, chunks, *, n_t,
+    ids, h0, h1, h2, h3, dy_all, up, down,
+    c0, c1, c2, c3, u, z, de, da, dy_here,
+    hs, place, de_rows, chunks, *, n_t, n_e, direct,
 ):
-    width = g0.shape[1]
-    model = n_t * width
-    r = ids[0]
+    width = h0.shape[1] - 16
+    model, tok = dy_here.shape
+    r, e = ids[0], ids[1]
     packs = (h0, h1, h2, h3)
-    for k, (h, g) in enumerate(zip(packs, (g0, g1, g2, g3))):
-        s = lax.rem(r + n_t - k, n_t)
-        hs[s] = h[:, 0:width].astype(f32)
-        gs[s] = g[...].astype(f32)
+    for k, h in enumerate(packs):
+        hs[lax.rem(r + n_t - k, n_t)] = h[:, 0:width].astype(f32)
+    dy_here[...] = chunk(dy_all, e, model)[...]
     stats = h0[:, width:].astype(f32)
     for h in packs[1:]:
         stats += h[:, width:].astype(f32)
     inverse = lax.rsqrt((stats[:, 0:1] + stats[:, 1:2]) / model + epsilon)
     gate = 1.0 / (1.0 + jnp.exp(-inverse * (stats[:, 2:3] + stats[:, 3:4])))
+    number = h0[:, width + 4:width + 5].astype(f32)
+    place[...] = (iota((h0.shape[0], tok), 1).astype(f32) + 1.0 == number).astype(f32)
+    cap = h0.shape[0] // n_e
+    for k in range(n_e):
+        part = slice(k * cap, (k + 1) * cap)
+        sender = lax.rem(e + n_e - k, n_e) if direct else k
+        got = mm(place[part].astype(bf16), chunk(dy_all, sender, model)[...], (1, 1))
+        de_rows[part] = got * gate[part]
+    de[...] = de_rows[...].astype(bf16)
     for s in range(n_t):
         cols = slice(s * width, (s + 1) * width)
         u[:, cols] = (hs[s] * inverse).astype(bf16)
-        de[:, cols] = (gs[s] * gate).astype(bf16)
     value, slope = gelu_pair(mm(u[...], up[0]))
     z[...] = value.astype(bf16)
     da[...] = (mm(de[...], down[0], (1, 1)) * slope).astype(bf16)
@@ -306,10 +306,10 @@
 
 
 def backward_kernel(
-    ids, b0, b1, b2, b3, t0, t1, t2, t3,
+    ids, b0, b1, b2, b3, t0, t1, t2, t3, dy,
     routes, router, gain, out_w, qkv_wt, heads, probs,
     c0, c1, c2, c3, dr1_own, d_proj, d_att, d_logits, gain_terms, d_scores,
-    bs, ts, ys, dr, *, n_t,
+    bs, ts, dr, *, n_t,
 ):
     width = dr1_own.shape[0]
     tok = b0.shape[1]
@@ -323,7 +323,6 @@
         s = lax.rem(r + n_t - k, n_t)
         chunk(bs, s, width)[...] = packs[k][0:width].astype(f32)
         chunk(ts, s, width)[...] = tokens[k][0:width].astype(f32)
-        chunk(ys, s, width)[...] = tokens[k][width + 16:].astype(f32)
     inverse, gate0, gate1 = gates_of(total_stats(tokens, width), model)
     back = total_stats(packs, width)
     dg0 = back[0:1] + back[1:2]
@@ -339,7 +338,7 @@
     gain_terms[...] = dh2 * res * inverse
     weighted = dh2 * gain[...]
     dot = jnp.sum(weighted * res, axis=0, keepdims=True) * (inverse**3 / model)
-    dr[...] = ys[...] + inverse * weighted - res * dot
+    dr[...] = dy[...].astype(f32) + inverse * weighted - res * dot
     d_att[...] = dr[...].astype(bf16)
     dr1_own[...] = chunk(dr, r, width)[...]
     d_o = mm(out_w[...], d_att[...]).astype(bf16)
@@ -370,17 +369,17 @@
 
 def small_grad_kernel(
     ids, t0, t1, t2, t3, d_logits, gain_terms, gain1_row, gain2, h1, d_proj, attended, d_att,
-    d_scores, buckets, qkv_w, small, out_grad, ts, padded, *, n_t, n_buckets,
+    d_scores, buckets, qkv_w, small, last, ts, padded, *, n_t, n_buckets, direct,
 ):
     packs = (t0, t1, t2, t3)
     width = attended.shape[0]
     model = n_t * width
+    inner = d_proj.shape[0]
     experts = d_logits.shape[0]
     tok = t0.shape[1]
     r = ids[0]
     for k, t in enumerate(packs):
         chunk(ts, lax.rem(r + n_t - k, n_t), width)[...] = t[0:width].astype(f32)
-    out_grad[...] = mm(attended[...], d_att[...], (1, 1)).astype(out_grad.dtype)
     inverse, _, _ = gates_of(total_stats(packs, width), model)
     normed = (ts[...] * inverse * gain2[...]).astype(bf16).astype(f32)
     small[0:experts] = mm(d_logits[...], normed, (1, 1), precision=highest)
@@ -396,14 +395,50 @@
         per_bucket = mm(jnp.broadcast_to(diagonal, (8, tok)), hot, (1, 1), precision=highest)
         here = experts + 2 + h
         small[here:here + 1, 0:n_buckets] = per_bucket[0:1]
-
-
-def small_sum_kernel(*refs):
-    parts, out = refs[:-1], refs[-1]
-    total = parts[0][...]
-    for p in parts[1:]:
-        total = total + p[...]
-    out[...] = total
+    if direct:
+        last[0:inner] = d_proj[...]
+        last[inner:inner + width] = chunk(d_att, r, width)[...]
+        height = small.shape[0]
+        for c in range(model // tok):
+            here = inner + width + c * height
+            last[here:here + height] = small[:, c * tok:(c + 1) * tok].astype(bf16)
+    else:
+        last[...] = mm(attended[...], d_att[...], (1, 1)).astype(last.dtype)
+
+
+def late_sum_kernel(ids, last, att_all, small, own, q1, q2, q3, blocks, *, n_t, n_e, inner):
+    model = small.shape[1]
+    width = model // n_t
+    tok = last.shape[1]
+    stride = last.shape[0] // n_e
+    height = small.shape[0]
+    r = ids[0]
+    total = last[inner + width:stride].astype(f32)
+    grad = mm(att_all[0:model], last[inner:inner + width], (1, 1))
+    for k in range(1, n_e):
+        base = k * stride
+        total += last[base + inner + width:base + stride].astype(f32)
+        grad += mm(
+            att_all[k * model:(k + 1) * model], last[base + inner:base + inner + width], (1, 1)
+        )
+    for c in range(model // tok):
+        small[:, c * tok:(c + 1) * tok] = total[c * height:(c + 1) * height]
+    for s in range(n_t):
+        blocks[s] = grad[s * width:(s + 1) * width]
+    own[...] = blocks[r]
+    for k, q in ((1, q1), (2, q2), (3, q3)):
+        q[...] = blocks[lax.rem(r + k, n_t)].astype(bf16)
+
+
+def out_grad_kernel(ids, own, q1, q2, q3, f0, f1, f2, f3, out, first, blocks, *, n_t):
+    width = own.shape[0]
+    r = ids[0]
+    blocks[r] = own[...]
+    for k, q in ((1, q1), (2, q2), (3, q3)):
+        blocks[lax.rem(r + n_t - k, n_t)] = q[...].astype(f32)
+    for s in range(n_t):
+        out[:, s * width:(s + 1) * width] = blocks[s]
+    first[...] = f0[...] + f1[...] + (f2[...] + f3[...])
 
 
 def input_grad_kernel(ids, c0, c1, c2, c3, dr1, inv1, x, gain, out, *, n_t):
@@ -415,12 +450,14 @@
     out[...] = dr1[...] + inverse * weighted - x[...].astype(f32) * (inverse * inverse * row_dot)
 
 
-def qkv_grad_kernel(*refs):
-    out = refs[-1]
-    count = (len(refs) - 1) // 2
-    total = mm(refs[0][...], refs[count][...], (1, 1))
+def qkv_grad_kernel(last, h1_all, out, *, count):
+    inner, model = out.shape
+    stride = last.shape[0] // count
+    total = mm(last[0:inner], h1_all[0:model], (1, 1))
     for k in range(1, count):
-        total += mm(refs[k][...], refs[count + k][...], (1, 1))
+        total += mm(
+            last[k * stride:k * stride + inner], h1_all[k * model:(k + 1) * model], (1, 1)
+        )
     out[...] = total
 
 
@@ -460,8 +497,8 @@
     def around(v):
         return [v] + [shift(v, k) for k in range(1, n_t)]
 
-    def around_experts(v):
-        return [v] + [shift(v, k, "expert", n_e) for k in range(1, n_e)]
+    def gather(v, axes):
+        return lax.all_gather(v, axes, axis=0, tiled=True)
 
     def exchange(pieces):
         if direct:
@@ -493,6 +530,7 @@
     buckets = bucket_ids.reshape(1, -1)
 
     xs = around(x)
+    dy_all = gather(dy, ("expert", "tensor"))
     gain1, out_wt, bias = run(
         prepare_kernel,
         [((model, 1), f32), ((model, width), bf16), ((n_heads, tok, tok), f32)],
@@ -515,45 +553,47 @@
         scratch=[pltpu.VMEM((model, tok), f32), pltpu.VMEM((model, tok), f32)],
     )
     got = [shift(p, k) for k, p in ((1, p1), (2, p2), (3, p3))]
-    *dy_pieces, dest, gain2, rw_own, qkv_wt = run(
+    dest, gain2, rw_own, qkv_wt = run(
         functools.partial(
             route_kernel, experts=experts, cap=cap, n_e=n_e, direct=direct, n_t=n_t
         ),
-        piece_shapes(width)
-        + [
+        [
             ((8, tok), f32),
             ((model, 1), f32),
             ((experts, width), bf16),
             ((model, inner), bf16),
         ],
-        ids, routes_t, dy, router, gain2_row, qkv_w, inv1,
+        ids, routes_t, router, gain2_row, qkv_w, inv1,
         smem=1, scratch=[pltpu.VMEM((n_t, experts, width), f32)],
     )
-    dy_rows = around(join(exchange(dy_pieces)))
+    if direct:
+        h1_all = gather(h1, "expert")
+        att_all = gather(attended, ("expert", "tensor"))
     *row_pieces, token_pack, residual = run(
         dispatch_kernel,
-        piece_shapes(width + 16) + [((2 * width + 16, tok), bf16), ((width, tok), f32)],
-        ids, own, *got, x, dy, gain2, rw_own, routes_t, dest,
+        piece_shapes(width + 16) + [((width + 16, tok), bf16), ((width, tok), f32)],
+        ids, own, *got, x, gain2, rw_own, routes_t, dest,
         smem=1, scratch=[pltpu.VMEM((width + 16, tok), bf16)],
     )
     in_rows = around(join(exchange(row_pieces)))
     token_packs = around(token_pack)
 
-    c0, c1, c2, c3, u, z, de, da = run(
-        functools.partial(expert_kernel, n_t=n_t),
-        [((rows, 2 * width), bf16)] * 4 + [((rows, model), bf16)] * 4,
-        ids, *in_rows, *dy_rows, up_weight, down_weight,
+    c0, c1, c2, c3, u, z, de, da, dy_here = run(
+        functools.partial(expert_kernel, n_t=n_t, n_e=n_e, direct=direct),
+        [((rows, 2 * width), bf16)] * 4
+        + [((rows, model), bf16)] * 4
+        + [((model, tok), bf16)],
+        ids, *in_rows, dy_all, up_weight, down_weight,
         smem=1,
+        limit=32 if direct else 48,
         scratch=[
             pltpu.VMEM((n_t, rows, width), f32),
-            pltpu.VMEM((n_t, rows, width), f32),
+            pltpu.VMEM((rows, tok), f32),
+            pltpu.VMEM((rows, model), f32),
             pltpu.VMEM((n_t, rows, 2 * width), bf16),
         ],
     )
     got = [shift(c, k) for k, c in ((1, c1), (2, c2), (3, c3))]
-    if direct:
-        h1_late, _ = lax.optimization_barrier((h1, c0))
-        h1_all = around_experts(h1_late)
     up_grad, down_grad = run(
         expert_grad_kernel,
         [(up_weight.shape, f32), (down_weight.shape, f32)],
@@ -578,16 +618,19 @@
             ((model, tok), f32),
             ((n_heads, tok, tok), bf16),
         ],
-        ids, *back_packs, *token_packs, routes_t, router, gain2, out_weight, qkv_wt, heads, probs,
+        ids, *back_packs, *token_packs, dy_here, routes_t, router, gain2, out_weight, qkv_wt, heads, probs,
         smem=1,
-        scratch=[pltpu.VMEM((model, tok), f32)] * 4,
+        scratch=[pltpu.VMEM((model, tok), f32)] * 3,
     )
     got = [shift(c, k) for k, c in ((1, c1), (2, c2), (3, c3))]
+    height = experts + 8
     if direct:
-        d_proj_all = around_experts(d_proj)
-    small, out_part = run(
-        functools.partial(small_grad_kernel, n_t=n_t, n_buckets=n_buckets),
-        [((experts + 8, model), f32), (out_weight.shape, bf16)],
+        last_shape = (inner + width + height * (model // tok), tok)
+    else:
+        last_shape = out_weight.shape
+    small, last = run(
+        functools.partial(small_grad_kernel, n_t=n_t, n_buckets=n_buckets, direct=direct),
+        [((height, model), f32), (last_shape, bf16)],
         ids, *token_packs, d_logits, gain_terms, gain1_row, gain2, h1, d_proj, attended, d_att,
         d_scores, buckets, qkv_w,
         smem=1,
@@ -599,18 +642,32 @@
         ids, c0, *got, dr1, inv1, x, gain1,
         smem=1,
     )
-    out_grad = lax.psum(out_part, "expert").astype(f32)
     if direct:
-        (small,) = run(small_sum_kernel, [(small.shape, f32)], *around_experts(small))
+        last = gather(last, "expert")
+        small, own, q1, q2, q3 = run(
+            functools.partial(late_sum_kernel, n_t=n_t, n_e=n_e, inner=inner),
+            [((height, model), f32), ((width, width), f32)] + [((width, width), bf16)] * 3,
+            ids, last, att_all,
+            smem=1, scratch=[pltpu.VMEM((n_t, width, width), f32)],
+        )
+        firsts = around(small[experts + 1:experts + 2])
+        got = [shift(q, k) for k, q in ((1, q1), (2, q2), (3, q3))]
         (qkv_grad,) = run(
-            qkv_grad_kernel, [((inner, model), f32)], *d_proj_all, *h1_all
+            functools.partial(qkv_grad_kernel, count=n_e), [((inner, model), f32)], last, h1_all
+        )
+        out_grad, first = run(
+            functools.partial(out_grad_kernel, n_t=n_t),
+            [(out_weight.shape, f32), ((1, model), f32)],
+            ids, own, *got, *firsts,
+            smem=1, scratch=[pltpu.VMEM((n_t, width, width), f32)],
         )
     else:
-        small = lax.psum(small, "expert")
-        (qkv_grad,) = run(qkv_grad_kernel, [((inner, model), f32)], d_proj, h1)
-        qkv_grad = lax.psum(qkv_grad.astype(bf16), "expert").astype(f32)
-    first = small[experts + 1:experts + 2]
-    first = functools.reduce(lambda a, b: a + b, around(first))
+        small, out_grad = lax.psum((small, last.astype(f32)), "expert")
+        (qkv_grad,) = run(
+            functools.partial(qkv_grad_kernel, count=1), [((inner, model), f32)], d_proj, h1
+        )
+        qkv_grad = lax.psum(qkv_grad, "expert")
+        first = lax.psum(small[experts + 1], "tensor")
     return (
         output.T,
         input_grad.T,

time: 256 us -> 238 us (0.930)
  starting transfers between devices: 86.1 us -> 45.8 us
  local copies, waits for them, and re-layouts: 7.52 us -> 38.3 us
  waiting for transfers between devices: 123 us -> 111 us
  Pallas kernels: 22.6 us -> 27.2 us
    all_gather x0 -> x4, waiting for transfers between devices: none -> 87.6 us  [gather(): return lax.all_gather(v, axes, axis=0, tiled=True)]
    ppermute x69 -> x41, waiting for transfers between devices: 77.8 us -> 21.8 us  [shift(): return lax.ppermute(v, axis, [(i, (i + k) % n) for i in range(n)])]
    psum x1 -> x0, waiting for transfers between devices: 44.9 us -> none  [per_device(): out_grad = lax.psum(out_part, 'expert').astype(f32)]
    ppermute x69 -> x41, starting transfers between devices: 86.1 us -> 45.6 us  [shift(): return lax.ppermute(v, axis, [(i, (i + k) % n) for i in range(n)])]
    unnamed x30 -> x146, local copies, waits for them, and re-layouts: 4.95 us -> 35.8 us
    pallas_call x15, Pallas kernels: 22.6 us -> 27.2 us  [run(): pl.pallas_call(body, out_shape=[jax.ShapeDtypeStruct(s, d) for s, d in ou...]
  transfers between devices with their start and end apart: 70 -> 45, of which waited for: 31 -> 17; matrix products, arithmetic and copies ran while one was open for 1% -> 1% of each run, Pallas kernels for 6% -> 11%
where the time goes in v3:
time: 238 us; the launch traced here: 237 us
  waiting for transfers between devices  111 us (47%)
  starting transfers between devices  45.8 us (19%)
  local copies, waits for them, and re-layouts  38.3 us (16%)
  Pallas kernels  27.2 us (11%)
  between operations  14.2 us (6%)
    all_gather x4, waiting for transfers between devices, gather(): return lax.all_gather(v, axes, axis=0, tiled=True)  87.6 us
    ppermute x41, starting transfers between devices, shift(): return lax.ppermute(v, axis, [(i, (i + k) % n) for i in range(n)])  45.6 us
    unnamed x146, local copies, waits for them, and re-layouts  35.8 us
    pallas_call x15, Pallas kernels, run(): pl.pallas_call(body, out_shape=[jax.ShapeDtypeStruct(s, d) for s, d in ou...  27.2 us
    ppermute x41, waiting for transfers between devices, shift(): return lax.ppermute(v, axis, [(i, (i + k) % n) for i in range(n)])  21.8 us
  transfers between devices with their start and end apart: 45, of which 17 were waited for; matrix products, arithmetic and copies ran while one was open for 1% of the time, Pallas kernels for 11%

profile of v3, /device:TPU:0, one launch (start us, length us, event | category | flops | bytes accessed | tf_op | source)
XLA Modules:
  0.0 236.8 jit_solution(5362188063834798233)
XLA Ops:
  8.5 2.6 %collective-permute-start.1 = (bf16[192,128]{1,0:T(8,128)(2,1)}, bf16[192,128]{1,0:T(8,128)(2,1)S(1)}, u32[]{:S(2)}, u32[]{:S(2)}) collective-permute-start(bf16[192,128]{1,0:T(8,128)(2,1)} %bitcast.24), channel_id=1, source_target_pairs={{0,2},{1,3},{2,0},{3,1},{4,6},{5,7},{6,4},{7,5},{8,10},{9,11},{10,... | collective-permute-start | bytes 147464 | tf_op jit(solution)/shard_map/ppermute | solution.py:495
  11.1 1.4 collective-permute-start.2
  16.2 1.3 shard_map.204
  17.6 1.2 copy-done
  19.6 2.8 %shard_map.205 = (f32[192,128]{1,0:T(8,128)S(1)}, bf16[192,128]{1,0:T(8,128)(2,1)S(1)}, bf16[192,128]{1,0:T(8,128)(2,1)S(1)}, bf16[192,128]{1,0:T(8,128)(2,1)S(1...) custom-call(s32[2]{0:T(128)S(1)} %pad_add_fusion.ids, ...), custom_call_target="tpu_custom_call" | custom-call | bytes 2412040 | tf_op jit(solution)/shard_map/pallas_call | solution.py:50
  24.2 1.4 collective-permute-start.5
  30.1 1.5 collective-permute-start.9
  31.6 1.6 collective-permute-start.10
  33.2 2.6 %collective-permute-start.11 = (bf16[40,208]{1,0:T(8,128)(2,1)S(1)}, bf16[40,208]{1,0:T(8,128)(2,1)S(1)}, u32[]{:S(2)}, u32[]{:S(2)}) collective-permute-start(bf16[40,208]{1,0:T(8,128)(2,1)S(1)} %get-tuple-element.91), channel_id=1, source_target_pairs={{0,12},{4,16},{8,20},{12,24},{16,28},{20,0},{24,4},{28,8},{1,13},{... | collective-permute-start | bytes 49928 | tf_op jit(solution)/shard_map/ppermute | solution.py:495
  35.7 1.2 collective-permute-start.12
  37.0 2.6 %collective-permute-start.13 = (bf16[40,208]{1,0:T(8,128)(2,1)S(1)}, bf16[40,208]{1,0:T(8,128)(2,1)S(1)}, u32[]{:S(2)}, u32[]{:S(2)}) collective-permute-start(bf16[40,208]{1,0:T(8,128)(2,1)S(1)} %get-tuple-element.93), channel_id=1, source_target_pairs={{0,20},{4,24},{8,28},{12,0},{16,4},{20,8},{24,12},{28,16},{1,21},{... | collective-permute-start | bytes 49928 | tf_op jit(solution)/shard_map/ppermute | solution.py:495
  39.6 1.4 collective-permute-start.14
  40.9 1.4 collective-permute-start.15
  43.4 1.4 collective-permute-done.15.refs_7_
  45.8 1.4 collective-permute-start.18
  47.2 3.5 %collective-permute-done.16.h1 = bf16[320,208]{1,0:T(8,128)(2,1)S(1)} collective-permute-done((bf16[320,208]{1,0:T(8,128)(2,1)S(1)}, bf16[320,208]{1,0:T(8,128)(2,1)S(1)}, u32[]{:S(2)}, u32[]{:S(2)}) %collective-permute-start.16) | collective-permute-done | bytes 133152 | tf_op jit(solution)/shard_map/ppermute | solution.py:495
  54.0 15.1 %all-gather.5.cloned.1.call-done.dy_all = bf16[6144,128]{1,0:T(8,128)(2,1)} async-done(((bf16[192,128]{1,0:T(8,128)(2,1)}), bf16[6144,128]{1,0:T(8,128)(2,1)}) %all-gather.5.cloned.1.call-update) | async-done | bytes 1572880 | tf_op jit(solution)/shard_map/all_gather | solution.py:501
  69.1 1.4 copy-done.5
  70.5 1.3 copy-done.8
  75.2 3.2 %shard_map.209 = (bf16[320,384]{1,0:T(8,128)(2,1)S(1)}, bf16[320,384]{1,0:T(8,128)(2,1)S(1)}, bf16[320,384]{1,0:T(8,128)(2,1)S(1)}, bf16[320,384]{1,0:T(8,128)(2...) custom-call(s32[2]{0:T(128)S(1)} %copy-done.51, ...), custom_call_target="tpu_custom_call" | custom-call | bytes 7610376 | tf_op jit(solution)/shard_map/pallas_call | solution.py:50
  78.8 1.5 collective-permute-start.20
  80.2 1.2 collective-permute-start.21
  82.0 4.3 %collective-permute-done.19.c1 = bf16[320,384]{1,0:T(8,128)(2,1)S(1)} collective-permute-done((bf16[320,384]{1,0:T(8,128)(2,1)S(1)}, bf16[320,384]{1,0:T(8,128)(2,1)S(1)}, u32[]{:S(2)}, u32[]{:S(2)}) %collective-permute-start.19) | collective-permute-done | bytes 245792 | tf_op jit(solution)/shard_map/ppermute | solution.py:495
  86.4 1.5 collective-permute-done.20.c2
  87.8 4.0 %collective-permute-done.21.c3 = bf16[320,384]{1,0:T(8,128)(2,1)S(1)} collective-permute-done((bf16[320,384]{1,0:T(8,128)(2,1)S(1)}, bf16[320,384]{1,0:T(8,128)(2,1)S(1)}, u32[]{:S(2)}, u32[]{:S(2)}) %collective-permute-start.21) | collective-permute-done | bytes 245792 | tf_op jit(solution)/shard_map/ppermute | solution.py:495
  92.8 1.3 collective-permute-start.23
  94.1 2.5 %collective-permute-start.24 = (bf16[40,384]{1,0:T(8,128)(2,1)S(1)}, bf16[40,384]{1,0:T(8,128)(2,1)S(1)}, u32[]{:S(2)}, u32[]{:S(2)}) collective-permute-start(bf16[40,384]{1,0:T(8,128)(2,1)S(1)} %get-tuple-element.103), channel_id=1, source_target_pairs={{0,12},{4,16},{8,20},{12,24},{16,28},{20,0},{24,4},{28,8},{1,13},{... | collective-permute-start | bytes 92168 | tf_op jit(solution)/shard_map/ppermute | solution.py:495
  96.6 1.5 collective-permute-start.25
  98.1 1.4 collective-permute-start.26
  99.5 1.5 collective-permute-start.27
  101.0 1.9 collective-permute-start.28
  108.2 1.1 collective-permute-start.30
  109.3 1.4 collective-permute-start.31
  112.8 3.0 %shard_map.212 = (bf16[208,128]{1,0:T(8,128)(2,1)S(1)}, bf16[208,128]{1,0:T(8,128)(2,1)S(1)}, bf16[208,128]{1,0:T(8,128)(2,1)S(1)}, bf16[208,128]{1,0:T(8,128)(2...) custom-call(s32[2]{0:T(128)S(1)} %copy-done.52, ...), custom_call_target="tpu_custom_call" | custom-call | bytes 3313672 | tf_op jit(solution)/shard_map/pallas_call | solution.py:50
  127.3 2.7 %shard_map.214 = (f32[16,768]{1,0:T(8,128)}, bf16[864,128]{1,0:T(8,128)(2,1)S(1)}) custom-call(s32[2]{0:T(128)S(1)} %copy-done.53, bf16[208,128]{1,0:T(8,128)(2,1)S(1)} %copy-done.21, bf16[208,128]{1,0:T(8,128)(2,1)S(1)} %collective-permute-done.6.t1, bf16[208,128]{1,0:T(8,128)(2,1)S(1)} %collective-permute-done.7.t2, ...), custom_call_target="tpu_custom_call" | custom-call | bytes 2460104 | tf_op jit(solution)/shard_map/pallas_call | solution.py:50
  135.0 3.2 %shard_map.218 = (f32[1,768,768]{2,1,0:T(8,128)}, f32[1,768,768]{2,1,0:T(8,128)}) custom-call(bf16[320,768]{1,0:T(8,128)(2,1)S(1)} %get-tuple-element.134.u, bf16[320,768]{1,0:T(8,128)(2,1)S(1)} %copy-done.14, bf16[320,768]{1,0:T(8,128)(2,1)S(1)} %copy-done.16, bf16[320,768]{1,0:T(8,128)(2,1)S(1)} %copy-done.18), custom_call_target="tpu_custom_call" | custom-call | bytes 6684672 | tf_op jit(solution)/shard_map/pallas_call | solution.py:50
  138.3 1.3 shard_map.213
  139.5 38.5 %all-gather.7.cloned.1.call-done.last = bf16[6912,128]{1,0:T(8,128)(2,1)} async-done(((bf16[864,128]{1,0:T(8,128)(2,1)}), bf16[6912,128]{1,0:T(8,128)(2,1)}) %all-gather.7.cloned.1.call-update) | async-done | bytes 1769488 | tf_op jit(solution)/shard_map/all_gather | solution.py:501
  178.1 1.5 copy-done.2
  179.6 1.4 copy-done.4
  181.0 1.6 shard_map.215
  183.2 1.5 collective-permute-start.39
  184.7 1.4 collective-permute-start.40
  187.3 1.4 collective-permute-start.37
  189.3 34.0 %all-gather.11.cloned.1.call-done.h1_all = bf16[6144,128]{1,0:T(8,128)(2,1)} async-done(((bf16[768,128]{1,0:T(8,128)(2,1)}), bf16[6144,128]{1,0:T(8,128)(2,1)}) %all-gather.11.cloned.1.call-update) | async-done | bytes 1572880 | tf_op jit(solution)/shard_map/all_gather | solution.py:501
  223.4 1.4 copy-done.6
  224.8 3.2 %shard_map.217 = f32[576,768]{1,0:T(8,128)} custom-call(bf16[6912,128]{1,0:T(8,128)(2,1)S(1)} %copy-done.3, bf16[6144,128]{1,0:T(8,128)(2,1)S(1)} %copy-done.6), custom_call_target="tpu_custom_call" | custom-call | bytes 5111808 | tf_op jit(solution)/shard_map/pallas_call | solution.py:50
  228.0 1.6 shard_map.216
  (214 shorter events, 49.6 us)
Async XLA Ops:
  7.2 61.8 %all-gather.5.cloned.1.call-start = ((), (), s32[]{:S(2)}) async-start(), calls=%async_computation | async-start | bytes 1622016 | tf_op jit(solution)/shard_map/all_gather | solution.py:501
  7.9 131.6 %all-gather.9.cloned.1.call-start = ((), (), s32[]{:S(2)}) async-start(), calls=%async_computation.2 | async-start | bytes 1622016 | tf_op jit(solution)/shard_map/all_gather | solution.py:501
  8.0 9.6 %collective-permute-start = (bf16[192,128]{1,0:T(8,128)(2,1)}, bf16[192,128]{1,0:T(8,128)(2,1)S(1)}, u32[]{:S(2)}, u32[]{:S(2)}) collective-permute-start(bf16[192,128]{1,0:T(8,128)(2,1)} %bitcast.23), channel_id=1, source_target_pairs={{0,1},{1,2},{2,3},{3,0},{4,5},{5,6},{6,7},{7,4},{8,9},{9,10},{10,1... | collective-permute-start | bytes 147464 | tf_op jit(solution)/shard_map/ppermute | solution.py:495
  8.5 9.1 %collective-permute-start.1 = (bf16[192,128]{1,0:T(8,128)(2,1)}, bf16[192,128]{1,0:T(8,128)(2,1)S(1)}, u32[]{:S(2)}, u32[]{:S(2)}) collective-permute-start(bf16[192,128]{1,0:T(8,128)(2,1)} %bitcast.24), channel_id=1, source_target_pairs={{0,2},{1,3},{2,0},{3,1},{4,6},{5,7},{6,4},{7,5},{8,10},{9,11},{10,... | collective-permute-start | bytes 147464 | tf_op jit(solution)/shard_map/ppermute | solution.py:495
  11.1 6.5 %collective-permute-start.2 = (bf16[192,128]{1,0:T(8,128)(2,1)}, bf16[192,128]{1,0:T(8,128)(2,1)S(1)}, u32[]{:S(2)}, u32[]{:S(2)}) collective-permute-start(bf16[192,128]{1,0:T(8,128)(2,1)} %bitcast.25), channel_id=1, source_target_pairs={{0,3},{1,0},{2,1},{3,2},{4,7},{5,4},{6,5},{7,6},{8,11},{9,8},{10,9... | collective-permute-start | bytes 147464 | tf_op jit(solution)/shard_map/ppermute | solution.py:495
  19.5 49.5 %copy-start.7 = (bf16[1,768,768]{2,1,0:T(8,128)(2,1)S(1)}, bf16[1,768,768]{2,1,0:T(8,128)(2,1)}, u32[]{:S(2)}) copy-start(bf16[1,768,768]{2,1,0:T(8,128)(2,1)} %up.1) | copy-start | bytes 3538948
  23.7 154.3 %all-gather.7.cloned.1.call-start = ((), (), s32[]{:S(2)}) async-start(), calls=%async_computation.1 | async-start | bytes 1990656 | tf_op jit(solution)/shard_map/all_gather | solution.py:501
  23.8 3.8 %collective-permute-start.3 = (bf16[192,128]{1,0:T(8,128)(2,1)S(1)}, bf16[192,128]{1,0:T(8,128)(2,1)S(1)}, u32[]{:S(2)}, u32[]{:S(2)}) collective-permute-start(bf16[192,128]{1,0:T(8,128)(2,1)S(1)} %get-tuple-element.79), channel_id=1, source_target_pairs={{0,1},{1,2},{2,3},{3,0},{4,5},{5,6},{6,7},{7,4},{8,9},{9,10},{10,1... | collective-permute-start | bytes 147464 | tf_op jit(solution)/shard_map/ppermute | solution.py:495
  23.9 4.6 %collective-permute-start.4 = (bf16[192,128]{1,0:T(8,128)(2,1)S(1)}, bf16[192,128]{1,0:T(8,128)(2,1)S(1)}, u32[]{:S(2)}, u32[]{:S(2)}) collective-permute-start(bf16[192,128]{1,0:T(8,128)(2,1)S(1)} %get-tuple-element.80), channel_id=1, source_target_pairs={{0,2},{1,3},{2,0},{3,1},{4,6},{5,7},{6,4},{7,5},{8,10},{9,11},{10,... | collective-permute-start | bytes 147464 | tf_op jit(solution)/shard_map/ppermute | solution.py:495
  24.2 4.2 %collective-permute-start.5 = (bf16[192,128]{1,0:T(8,128)(2,1)S(1)}, bf16[192,128]{1,0:T(8,128)(2,1)S(1)}, u32[]{:S(2)}, u32[]{:S(2)}) collective-permute-start(bf16[192,128]{1,0:T(8,128)(2,1)S(1)} %get-tuple-element.81), channel_id=1, source_target_pairs={{0,3},{1,0},{2,1},{3,2},{4,7},{5,4},{6,5},{7,6},{8,11},{9,8},{10,9... | collective-permute-start | bytes 147464 | tf_op jit(solution)/shard_map/ppermute | solution.py:495
  30.1 9.5 %collective-permute-start.9 = (bf16[40,208]{1,0:T(8,128)(2,1)S(1)}, bf16[40,208]{1,0:T(8,128)(2,1)S(1)}, u32[]{:S(2)}, u32[]{:S(2)}) collective-permute-start(bf16[40,208]{1,0:T(8,128)(2,1)S(1)} %get-tuple-element.89), channel_id=1, source_target_pairs={{0,4},{4,8},{8,12},{12,16},{16,20},{20,24},{24,28},{28,0},{1,5},{5... | collective-permute-start | bytes 49928 | tf_op jit(solution)/shard_map/ppermute | solution.py:495
  31.6 9.3 %collective-permute-start.10 = (bf16[40,208]{1,0:T(8,128)(2,1)S(1)}, bf16[40,208]{1,0:T(8,128)(2,1)S(1)}, u32[]{:S(2)}, u32[]{:S(2)}) collective-permute-start(bf16[40,208]{1,0:T(8,128)(2,1)S(1)} %get-tuple-element.90), channel_id=1, source_target_pairs={{0,8},{4,12},{8,16},{12,20},{16,24},{20,28},{24,0},{28,4},{1,9},{5... | collective-permute-start | bytes 49928 | tf_op jit(solution)/shard_map/ppermute | solution.py:495
  33.2 9.2 %collective-permute-start.11 = (bf16[40,208]{1,0:T(8,128)(2,1)S(1)}, bf16[40,208]{1,0:T(8,128)(2,1)S(1)}, u32[]{:S(2)}, u32[]{:S(2)}) collective-permute-start(bf16[40,208]{1,0:T(8,128)(2,1)S(1)} %get-tuple-element.91), channel_id=1, source_target_pairs={{0,12},{4,16},{8,20},{12,24},{16,28},{20,0},{24,4},{28,8},{1,13},{... | collective-permute-start | bytes 49928 | tf_op jit(solution)/shard_map/ppermute | solution.py:495
  35.7 6.6 %collective-permute-start.12 = (bf16[40,208]{1,0:T(8,128)(2,1)S(1)}, bf16[40,208]{1,0:T(8,128)(2,1)S(1)}, u32[]{:S(2)}, u32[]{:S(2)}) collective-permute-start(bf16[40,208]{1,0:T(8,128)(2,1)S(1)} %get-tuple-element.92), channel_id=1, source_target_pairs={{0,16},{4,20},{8,24},{12,28},{16,0},{20,4},{24,8},{28,12},{1,17},{... | collective-permute-start | bytes 49928 | tf_op jit(solution)/shard_map/ppermute | solution.py:495
  37.0 5.4 %collective-permute-start.13 = (bf16[40,208]{1,0:T(8,128)(2,1)S(1)}, bf16[40,208]{1,0:T(8,128)(2,1)S(1)}, u32[]{:S(2)}, u32[]{:S(2)}) collective-permute-start(bf16[40,208]{1,0:T(8,128)(2,1)S(1)} %get-tuple-element.93), channel_id=1, source_target_pairs={{0,20},{4,24},{8,28},{12,0},{16,4},{20,8},{24,12},{28,16},{1,21},{... | collective-permute-start | bytes 49928 | tf_op jit(solution)/shard_map/ppermute | solution.py:495
  39.6 3.8 %collective-permute-start.14 = (bf16[40,208]{1,0:T(8,128)(2,1)S(1)}, bf16[40,208]{1,0:T(8,128)(2,1)S(1)}, u32[]{:S(2)}, u32[]{:S(2)}) collective-permute-start(bf16[40,208]{1,0:T(8,128)(2,1)S(1)} %get-tuple-element.94), channel_id=1, source_target_pairs={{0,24},{4,28},{8,0},{12,4},{16,8},{20,12},{24,16},{28,20},{1,25},{... | collective-permute-start | bytes 49928 | tf_op jit(solution)/shard_map/ppermute | solution.py:495
  40.9 3.8 %collective-permute-start.15 = (bf16[40,208]{1,0:T(8,128)(2,1)S(1)}, bf16[40,208]{1,0:T(8,128)(2,1)S(1)}, u32[]{:S(2)}, u32[]{:S(2)}) collective-permute-start(bf16[40,208]{1,0:T(8,128)(2,1)S(1)} %get-tuple-element.95), channel_id=1, source_target_pairs={{0,28},{4,0},{8,4},{12,8},{16,12},{20,16},{24,20},{28,24},{1,29},{... | collective-permute-start | bytes 49928 | tf_op jit(solution)/shard_map/ppermute | solution.py:495
  44.8 5.9 %collective-permute-start.16 = (bf16[320,208]{1,0:T(8,128)(2,1)S(1)}, bf16[320,208]{1,0:T(8,128)(2,1)S(1)}, u32[]{:S(2)}, u32[]{:S(2)}) collective-permute-start(bf16[320,208]{1,0:T(8,128)(2,1)S(1)} %shard_map.208.h0), channel_id=1, source_target_pairs={{0,1},{1,2},{2,3},{3,0},{4,5},{5,6},{6,7},{7,4},{8,9},{9,10},{10,1... | collective-permute-start | bytes 399368 | tf_op jit(solution)/shard_map/ppermute | solution.py:495
  44.8 7.1 %collective-permute-start.17 = (bf16[320,208]{1,0:T(8,128)(2,1)S(1)}, bf16[320,208]{1,0:T(8,128)(2,1)S(1)}, u32[]{:S(2)}, u32[]{:S(2)}) collective-permute-start(bf16[320,208]{1,0:T(8,128)(2,1)S(1)} %shard_map.208.h0), channel_id=1, source_target_pairs={{0,2},{1,3},{2,0},{3,1},{4,6},{5,7},{6,4},{7,5},{8,10},{9,11},{10,... | collective-permute-start | bytes 399368 | tf_op jit(solution)/shard_map/ppermute | solution.py:495
  45.8 7.5 %collective-permute-start.18 = (bf16[320,208]{1,0:T(8,128)(2,1)S(1)}, bf16[320,208]{1,0:T(8,128)(2,1)S(1)}, u32[]{:S(2)}, u32[]{:S(2)}) collective-permute-start(bf16[320,208]{1,0:T(8,128)(2,1)S(1)} %shard_map.208.h0), channel_id=1, source_target_pairs={{0,3},{1,0},{2,1},{3,2},{4,7},{5,4},{6,5},{7,6},{8,11},{9,8},{10,9... | collective-permute-start | bytes 399368 | tf_op jit(solution)/shard_map/ppermute | solution.py:495
  75.2 37.6 %copy-start.52 = (s32[2]{0:T(128)S(1)}, s32[2]{0:T(128)}, u32[]{:S(2)}) copy-start(s32[2]{0:T(128)} %copy-done.50) | copy-start | bytes 28
  78.4 7.9 %collective-permute-start.19 = (bf16[320,384]{1,0:T(8,128)(2,1)S(1)}, bf16[320,384]{1,0:T(8,128)(2,1)S(1)}, u32[]{:S(2)}, u32[]{:S(2)}) collective-permute-start(bf16[320,384]{1,0:T(8,128)(2,1)S(1)} %get-tuple-element.97), channel_id=1, source_target_pairs={{0,1},{1,2},{2,3},{3,0},{4,5},{5,6},{6,7},{7,4},{8,9},{9,10},{10,1... | collective-permute-start | bytes 737288 | tf_op jit(solution)/shard_map/ppermute | solution.py:495
  78.8 9.1 %collective-permute-start.20 = (bf16[320,384]{1,0:T(8,128)(2,1)S(1)}, bf16[320,384]{1,0:T(8,128)(2,1)S(1)}, u32[]{:S(2)}, u32[]{:S(2)}) collective-permute-start(bf16[320,384]{1,0:T(8,128)(2,1)S(1)} %get-tuple-element.98), channel_id=1, source_target_pairs={{0,2},{1,3},{2,0},{3,1},{4,6},{5,7},{6,4},{7,5},{8,10},{9,11},{10,... | collective-permute-start | bytes 737288 | tf_op jit(solution)/shard_map/ppermute | solution.py:495
  80.2 11.6 %collective-permute-start.21 = (bf16[320,384]{1,0:T(8,128)(2,1)S(1)}, bf16[320,384]{1,0:T(8,128)(2,1)S(1)}, u32[]{:S(2)}, u32[]{:S(2)}) collective-permute-start(bf16[320,384]{1,0:T(8,128)(2,1)S(1)} %get-tuple-element.99), channel_id=1, source_target_pairs={{0,3},{1,0},{2,1},{3,2},{4,7},{5,4},{6,5},{7,6},{8,11},{9,8},{10,9... | collective-permute-start | bytes 737288 | tf_op jit(solution)/shard_map/ppermute | solution.py:495
  81.4 12.6 %collective-permute-start.6 = (bf16[208,128]{1,0:T(8,128)(2,1)S(1)}, bf16[208,128]{1,0:T(8,128)(2,1)S(1)}, u32[]{:S(2)}, u32[]{:S(2)}) collective-permute-start(bf16[208,128]{1,0:T(8,128)(2,1)S(1)} %copy-done.20), channel_id=1, source_target_pairs={{0,1},{1,2},{2,3},{3,0},{4,5},{5,6},{6,7},{7,4},{8,9},{9,10},{10,1... | collective-permute-start | bytes 159752 | tf_op jit(solution)/shard_map/ppermute | solution.py:495
  81.4 15.1 %collective-permute-start.7 = (bf16[208,128]{1,0:T(8,128)(2,1)S(1)}, bf16[208,128]{1,0:T(8,128)(2,1)S(1)}, u32[]{:S(2)}, u32[]{:S(2)}) collective-permute-start(bf16[208,128]{1,0:T(8,128)(2,1)S(1)} %copy-done.20), channel_id=1, source_target_pairs={{0,2},{1,3},{2,0},{3,1},{4,6},{5,7},{6,4},{7,5},{8,10},{9,11},{10,... | collective-permute-start | bytes 159752 | tf_op jit(solution)/shard_map/ppermute | solution.py:495
  86.4 11.7 %collective-permute-start.8 = (bf16[208,128]{1,0:T(8,128)(2,1)S(1)}, bf16[208,128]{1,0:T(8,128)(2,1)S(1)}, u32[]{:S(2)}, u32[]{:S(2)}) collective-permute-start(bf16[208,128]{1,0:T(8,128)(2,1)S(1)} %copy-done.20), channel_id=1, source_target_pairs={{0,3},{1,0},{2,1},{3,2},{4,7},{5,4},{6,5},{7,6},{8,11},{9,8},{10,9... | collective-permute-start | bytes 159752 | tf_op jit(solution)/shard_map/ppermute | solution.py:495
  91.9 7.6 %collective-permute-start.22 = (bf16[40,384]{1,0:T(8,128)(2,1)S(1)}, bf16[40,384]{1,0:T(8,128)(2,1)S(1)}, u32[]{:S(2)}, u32[]{:S(2)}) collective-permute-start(bf16[40,384]{1,0:T(8,128)(2,1)S(1)} %get-tuple-element.101), channel_id=1, source_target_pairs={{0,4},{4,8},{8,12},{12,16},{16,20},{20,24},{24,28},{28,0},{1,5},{5... | collective-permute-start | bytes 92168 | tf_op jit(solution)/shard_map/ppermute | solution.py:495
  92.8 8.2 %collective-permute-start.23 = (bf16[40,384]{1,0:T(8,128)(2,1)S(1)}, bf16[40,384]{1,0:T(8,128)(2,1)S(1)}, u32[]{:S(2)}, u32[]{:S(2)}) collective-permute-start(bf16[40,384]{1,0:T(8,128)(2,1)S(1)} %get-tuple-element.102), channel_id=1, source_target_pairs={{0,8},{4,12},{8,16},{12,20},{16,24},{20,28},{24,0},{28,4},{1,9},{5... | collective-permute-start | bytes 92168 | tf_op jit(solution)/shard_map/ppermute | solution.py:495
  94.1 8.8 %collective-permute-start.24 = (bf16[40,384]{1,0:T(8,128)(2,1)S(1)}, bf16[40,384]{1,0:T(8,128)(2,1)S(1)}, u32[]{:S(2)}, u32[]{:S(2)}) collective-permute-start(bf16[40,384]{1,0:T(8,128)(2,1)S(1)} %get-tuple-element.103), channel_id=1, source_target_pairs={{0,12},{4,16},{8,20},{12,24},{16,28},{20,0},{24,4},{28,8},{1,13},{... | collective-permute-start | bytes 92168 | tf_op jit(solution)/shard_map/ppermute | solution.py:495
  96.6 6.8 %collective-permute-start.25 = (bf16[40,384]{1,0:T(8,128)(2,1)S(1)}, bf16[40,384]{1,0:T(8,128)(2,1)S(1)}, u32[]{:S(2)}, u32[]{:S(2)}) collective-permute-start(bf16[40,384]{1,0:T(8,128)(2,1)S(1)} %get-tuple-element.104), channel_id=1, source_target_pairs={{0,16},{4,20},{8,24},{12,28},{16,0},{20,4},{24,8},{28,12},{1,17},{... | collective-permute-start | bytes 92168 | tf_op jit(solution)/shard_map/ppermute | solution.py:495
  98.1 5.3 %collective-permute-start.26 = (bf16[40,384]{1,0:T(8,128)(2,1)S(1)}, bf16[40,384]{1,0:T(8,128)(2,1)S(1)}, u32[]{:S(2)}, u32[]{:S(2)}) collective-permute-start(bf16[40,384]{1,0:T(8,128)(2,1)S(1)} %get-tuple-element.105), channel_id=1, source_target_pairs={{0,20},{4,24},{8,28},{12,0},{16,4},{20,8},{24,12},{28,16},{1,21},{... | collective-permute-start | bytes 92168 | tf_op jit(solution)/shard_map/ppermute | solution.py:495
  99.5 4.8 %collective-permute-start.27 = (bf16[40,384]{1,0:T(8,128)(2,1)S(1)}, bf16[40,384]{1,0:T(8,128)(2,1)S(1)}, u32[]{:S(2)}, u32[]{:S(2)}) collective-permute-start(bf16[40,384]{1,0:T(8,128)(2,1)S(1)} %get-tuple-element.106), channel_id=1, source_target_pairs={{0,24},{4,28},{8,0},{12,4},{16,8},{20,12},{24,16},{28,20},{1,25},{... | collective-permute-start | bytes 92168 | tf_op jit(solution)/shard_map/ppermute | solution.py:495
  101.0 3.9 %collective-permute-start.28 = (bf16[40,384]{1,0:T(8,128)(2,1)S(1)}, bf16[40,384]{1,0:T(8,128)(2,1)S(1)}, u32[]{:S(2)}, u32[]{:S(2)}) collective-permute-start(bf16[40,384]{1,0:T(8,128)(2,1)S(1)} %get-tuple-element.107), channel_id=1, source_target_pairs={{0,28},{4,0},{8,4},{12,8},{16,12},{20,16},{24,20},{28,24},{1,29},{... | collective-permute-start | bytes 92168 | tf_op jit(solution)/shard_map/ppermute | solution.py:495
  108.2 3.6 %collective-permute-start.29 = (bf16[208,128]{1,0:T(8,128)(2,1)S(1)}, bf16[208,128]{1,0:T(8,128)(2,1)S(1)}, u32[]{:S(2)}, u32[]{:S(2)}) collective-permute-start(bf16[208,128]{1,0:T(8,128)(2,1)S(1)} %get-tuple-element.109.b0), channel_id=1, source_target_pairs={{0,1},{1,2},{2,3},{3,0},{4,5},{5,6},{6,7},{7,4},{8,9},{9,10},{10,1... | collective-permute-start | bytes 159752 | tf_op jit(solution)/shard_map/ppermute | solution.py:495
  108.2 4.6 %collective-permute-start.30 = (bf16[208,128]{1,0:T(8,128)(2,1)S(1)}, bf16[208,128]{1,0:T(8,128)(2,1)S(1)}, u32[]{:S(2)}, u32[]{:S(2)}) collective-permute-start(bf16[208,128]{1,0:T(8,128)(2,1)S(1)} %get-tuple-element.109.b0), channel_id=1, source_target_pairs={{0,2},{1,3},{2,0},{3,1},{4,6},{5,7},{6,4},{7,5},{8,10},{9,11},{10,... | collective-permute-start | bytes 159752 | tf_op jit(solution)/shard_map/ppermute | solution.py:495
  109.3 3.5 %collective-permute-start.31 = (bf16[208,128]{1,0:T(8,128)(2,1)S(1)}, bf16[208,128]{1,0:T(8,128)(2,1)S(1)}, u32[]{:S(2)}, u32[]{:S(2)}) collective-permute-start(bf16[208,128]{1,0:T(8,128)(2,1)S(1)} %get-tuple-element.109.b0), channel_id=1, source_target_pairs={{0,3},{1,0},{2,1},{3,2},{4,7},{5,4},{6,5},{7,6},{8,11},{9,8},{10,9... | collective-permute-start | bytes 159752 | tf_op jit(solution)/shard_map/ppermute | solution.py:495
  130.7 92.6 %all-gather.11.cloned.1.call-start = ((), (), s32[]{:S(2)}) async-start(), calls=%async_computation.3 | async-start | bytes 1769472 | tf_op jit(solution)/shard_map/all_gather | solution.py:501
  131.3 6.9 %collective-permute-start.32 = (bf16[208,128]{1,0:T(8,128)(2,1)}, bf16[208,128]{1,0:T(8,128)(2,1)S(1)}, u32[]{:S(2)}, u32[]{:S(2)}) collective-permute-start(bf16[208,128]{1,0:T(8,128)(2,1)} %copy-done.71), channel_id=1, source_target_pairs={{0,1},{1,2},{2,3},{3,0},{4,5},{5,6},{6,7},{7,4},{8,9},{9,10},{10,1... | collective-permute-start | bytes 159752 | tf_op jit(solution)/shard_map/ppermute | solution.py:495
  132.2 6.0 %collective-permute-start.33 = (bf16[208,128]{1,0:T(8,128)(2,1)}, bf16[208,128]{1,0:T(8,128)(2,1)S(1)}, u32[]{:S(2)}, u32[]{:S(2)}) collective-permute-start(bf16[208,128]{1,0:T(8,128)(2,1)} %copy-done.70), channel_id=1, source_target_pairs={{0,2},{1,3},{2,0},{3,1},{4,6},{5,7},{6,4},{7,5},{8,10},{9,11},{10,... | collective-permute-start | bytes 159752 | tf_op jit(solution)/shard_map/ppermute | solution.py:495
  133.3 4.9 %collective-permute-start.34 = (bf16[208,128]{1,0:T(8,128)(2,1)}, bf16[208,128]{1,0:T(8,128)(2,1)S(1)}, u32[]{:S(2)}, u32[]{:S(2)}) collective-permute-start(bf16[208,128]{1,0:T(8,128)(2,1)} %copy-done.69), channel_id=1, source_target_pairs={{0,3},{1,0},{2,1},{3,2},{4,7},{5,4},{6,5},{7,6},{8,11},{9,8},{10,9... | collective-permute-start | bytes 159752 | tf_op jit(solution)/shard_map/ppermute | solution.py:495
  181.0 42.4 %copy-start.3 = (bf16[6912,128]{1,0:T(8,128)(2,1)S(1)}, bf16[6912,128]{1,0:T(8,128)(2,1)}, u32[]{:S(2)}) copy-start(bf16[6912,128]{1,0:T(8,128)(2,1)} %all-gather.7.cloned.1.call-done.last) | copy-start | bytes 5308420
  183.2 4.1 %collective-permute-start.38 = (f32[1,768]{1,0:T(1,128)S(1)}, f32[1,768]{1,0:T(1,128)S(1)}, u32[]{:S(2)}, u32[]{:S(2)}) collective-permute-start(f32[1,768]{1,0:T(1,128)S(1)} %get-tuple-element.141.f0), channel_id=1, source_target_pairs={{0,1},{1,2},{2,3},{3,0},{4,5},{5,6},{6,7},{7,4},{8,9},{9,10},{10,1... | collective-permute-start | bytes 9224 | tf_op jit(solution)/shard_map/ppermute | solution.py:495
  183.2 44.8 %collective-permute-start.39 = (f32[1,768]{1,0:T(1,128)S(1)}, f32[1,768]{1,0:T(1,128)S(1)}, u32[]{:S(2)}, u32[]{:S(2)}) collective-permute-start(f32[1,768]{1,0:T(1,128)S(1)} %get-tuple-element.141.f0), channel_id=1, source_target_pairs={{0,2},{1,3},{2,0},{3,1},{4,6},{5,7},{6,4},{7,5},{8,10},{9,11},{10,... | collective-permute-start | bytes 9224 | tf_op jit(solution)/shard_map/ppermute | solution.py:495
  184.7 43.3 %collective-permute-start.40 = (f32[1,768]{1,0:T(1,128)S(1)}, f32[1,768]{1,0:T(1,128)S(1)}, u32[]{:S(2)}, u32[]{:S(2)}) collective-permute-start(f32[1,768]{1,0:T(1,128)S(1)} %get-tuple-element.141.f0), channel_id=1, source_target_pairs={{0,3},{1,0},{2,1},{3,2},{4,7},{5,4},{6,5},{7,6},{8,11},{9,8},{10,9... | collective-permute-start | bytes 9224 | tf_op jit(solution)/shard_map/ppermute | solution.py:495
  186.7 41.3 %collective-permute-start.35 = (bf16[192,192]{1,0:T(8,128)(2,1)S(1)}, bf16[192,192]{1,0:T(8,128)(2,1)S(1)}, u32[]{:S(2)}, u32[]{:S(2)}) collective-permute-start(bf16[192,192]{1,0:T(8,128)(2,1)S(1)} %get-tuple-element.128), channel_id=1, source_target_pairs={{0,1},{1,2},{2,3},{3,0},{4,5},{5,6},{6,7},{7,4},{8,9},{9,10},{10,1... | collective-permute-start | bytes 221192 | tf_op jit(solution)/shard_map/ppermute | solution.py:495
  186.7 41.3 %collective-permute-start.36 = (bf16[192,192]{1,0:T(8,128)(2,1)S(1)}, bf16[192,192]{1,0:T(8,128)(2,1)S(1)}, u32[]{:S(2)}, u32[]{:S(2)}) collective-permute-start(bf16[192,192]{1,0:T(8,128)(2,1)S(1)} %get-tuple-element.129), channel_id=1, source_target_pairs={{0,2},{1,3},{2,0},{3,1},{4,6},{5,7},{6,4},{7,5},{8,10},{9,11},{10,... | collective-permute-start | bytes 221192 | tf_op jit(solution)/shard_map/ppermute | solution.py:495
  187.3 40.7 %collective-permute-start.37 = (bf16[192,192]{1,0:T(8,128)(2,1)S(1)}, bf16[192,192]{1,0:T(8,128)(2,1)S(1)}, u32[]{:S(2)}, u32[]{:S(2)}) collective-permute-start(bf16[192,192]{1,0:T(8,128)(2,1)S(1)} %get-tuple-element.130), channel_id=1, source_target_pairs={{0,3},{1,0},{2,1},{3,2},{4,7},{5,4},{6,5},{7,6},{8,11},{9,8},{10,9... | collective-permute-start | bytes 221192 | tf_op jit(solution)/shard_map/ppermute | solution.py:495
  (70 other events, 586.2 us)
Sparse Core Ops, SparseCore 0:
  10.9 58.0 all-gather.4
  71.9 54.9 all-gather.8
  130.9 47.1 all-gather.6
  180.1 43.1 all-gather.10

commit v4 on v3

--- a/solution.py
+++ b/solution.py
@@ -44,19 +44,42 @@
     return block
 
 
-def run(body, outs, *args, smem=0, scratch=(), flops=0, limit=32):
+def run(body, outs, *args, fetch=(), scratch=(), limit=32):
+    n, m, f = len(args), len(outs), len(fetch)
     moved = sum(a.size * a.dtype.itemsize for a in args)
     moved += sum(math.prod(s) * jnp.dtype(d).itemsize for s, d in outs)
+    held = [pltpu.VMEM(args[i].shape, args[i].dtype) for i in fetch]
+    sems = [pltpu.SemaphoreType.DMA((f,))] if f else []
+
+    def whole(*refs):
+        ins, rest = list(refs[:n]), refs[n + m:]
+        copies = [
+            pltpu.make_async_copy(ins[i], rest[j], rest[f].at[j]) for j, i in enumerate(fetch)
+        ]
+        for copy in copies:
+            copy.start()
+        for copy in copies:
+            copy.wait()
+        for j, i in enumerate(fetch):
+            ins[i] = rest[j]
+        body(*ins, *refs[n:n + m], *rest[f + len(sems):])
+
     return pl.pallas_call(
-        body,
+        whole,
         out_shape=[jax.ShapeDtypeStruct(s, d) for s, d in outs],
-        in_specs=[pl.BlockSpec(memory_space=pltpu.SMEM)] * smem
-        + [pl.BlockSpec()] * (len(args) - smem),
-        out_specs=[pl.BlockSpec()] * len(outs),
-        scratch_shapes=list(scratch),
+        in_specs=[
+            pl.BlockSpec(memory_space=pltpu.HBM) if i in fetch else pl.BlockSpec()
+            for i in range(n)
+        ],
+        out_specs=[pl.BlockSpec()] * m,
+        scratch_shapes=held + sems + list(scratch),
         compiler_params=pltpu.CompilerParams(vmem_limit_bytes=limit * 2**20),
-        cost_estimate=pl.CostEstimate(flops=flops, bytes_accessed=moved, transcendentals=0),
+        cost_estimate=pl.CostEstimate(flops=0, bytes_accessed=moved, transcendentals=0),
     )(*args)
+
+
+def my_place():
+    return lax.axis_index("tensor"), lax.axis_index("expert")
 
 
 def column_of(row, out):
@@ -89,8 +112,8 @@
     out_wt[...] = out_w[...].astype(f32).T.astype(bf16)
     key_pos = iota((tok, tok), 0)
     query_pos = iota((tok, tok), 1)
-    end0 = lengths[0, 0]
-    end1 = end0 + lengths[0, 1]
+    end0 = lengths[0:1, 0:1]
+    end1 = end0 + lengths[0:1, 1:2]
     seg_k = (key_pos >= end0).astype(i32) + (key_pos >= end1).astype(i32)
     seg_q = (query_pos >= end0).astype(i32) + (query_pos >= end1).astype(i32)
     allowed = (seg_k == seg_q) & (key_pos <= query_pos)
@@ -102,12 +125,12 @@
 
 
 def route_kernel(
-    ids, routes, router, gain, qkv_w, after, dest, gain_col, rw_own, qkv_wt, chunks,
+    routes, router, gain, qkv_w, after, dest, gain_col, rw_own, qkv_wt, chunks,
     *, experts, cap, n_e, direct, n_t,
 ):
     tok = routes.shape[1]
     width = rw_own.shape[1]
-    e = ids[1].astype(f32)
+    e = my_place()[1].astype(f32)
     rt = routes[...]
     x_of = iota((experts, tok), 0)
     m0 = (rt[0:1] == x_of).astype(f32)
@@ -131,7 +154,7 @@
     wide = router[...].astype(f32)
     for s in range(n_t):
         chunks[s] = wide[:, s * width:(s + 1) * width]
-    rw_own[...] = chunks[ids[0]].astype(bf16)
+    rw_own[...] = chunks[my_place()[0]].astype(bf16)
     qkv_wt[...] = qkv_w[...].astype(f32).T.astype(bf16)
 
 
@@ -140,7 +163,7 @@
 
 
 def attention_kernel(
-    ids, x0, x1, x2, x3, gain, qkv_w, out_wt, bias,
+    x0, x1, x2, x3, gain, qkv_w, out_wt, bias,
     own, p1, p2, p3, h1, inv1, heads, probs, attended,
     xs, parts, *, n_t,
 ):
@@ -148,7 +171,7 @@
     n_heads = bias.shape[0]
     size = width // n_heads
     model = n_t * width
-    r = ids[0]
+    r, _ = my_place()
     for k, x in enumerate((x0, x1, x2, x3)):
         chunk(xs, lax.rem(r + n_t - k, n_t), width)[...] = x[...].astype(f32)
     inverse = lax.rsqrt(jnp.sum(xs[...] * xs[...], axis=0, keepdims=True) / model + epsilon)
@@ -169,13 +192,13 @@
 
 
 def dispatch_kernel(
-    ids, own, p1, p2, p3, x, gain, rw_own, routes, dest, *refs
+    own, p1, p2, p3, x, dy, gain, rw_own, routes, dest, *refs
 ):
     pieces = refs[:-3]
     token_pack, residual, pack = refs[-3:]
     width, tok = x.shape
     experts = rw_own.shape[0]
-    r = ids[0]
+    r, _ = my_place()
     res = x[...].astype(f32) + own[...] + (
         p1[...].astype(f32) + p2[...].astype(f32) + p3[...].astype(f32)
     )
@@ -186,12 +209,13 @@
     x_of = iota((experts, tok), 0)
     c0 = jnp.sum(jnp.where(routes[0:1, :] == x_of, logits, 0.0), axis=0, keepdims=True)
     c1 = jnp.sum(jnp.where(routes[1:2, :] == x_of, logits, 0.0), axis=0, keepdims=True)
-    number = (iota((1, tok), 1) + 1).astype(f32)
-    stats = row_block(split_hi_lo(square) + split_hi_lo(c0 - c1) + (number,)).astype(bf16)
+    stats = row_block(split_hi_lo(square) + split_hi_lo(c0 - c1)).astype(bf16)
     token_pack[0:width] = res.astype(bf16)
-    token_pack[width:] = stats
+    token_pack[width:width + 16] = stats
+    token_pack[width + 16:] = dy[...]
     pack[0:width] = scaled
-    pack[width:] = stats
+    pack[width:width + 16] = stats
+    pack[width + 16:] = dy[...]
     size = pieces[0].shape[0]
     row = iota((size * len(pieces), tok), 0).astype(f32)
     place0 = (row == dest[0:1, :]).astype(f32)
@@ -213,34 +237,27 @@
 
 
 def expert_kernel(
-    ids, h0, h1, h2, h3, dy_all, up, down,
-    c0, c1, c2, c3, u, z, de, da, dy_here,
-    hs, place, de_rows, chunks, *, n_t, n_e, direct,
+    h0, h1, h2, h3, up, down,
+    c0, c1, c2, c3, u, z, de, da,
+    hs, gs, chunks, *, n_t,
 ):
-    width = h0.shape[1] - 16
-    model, tok = dy_here.shape
-    r, e = ids[0], ids[1]
+    width = c0.shape[1] // 2
+    model = n_t * width
+    r, _ = my_place()
     packs = (h0, h1, h2, h3)
     for k, h in enumerate(packs):
-        hs[lax.rem(r + n_t - k, n_t)] = h[:, 0:width].astype(f32)
-    dy_here[...] = chunk(dy_all, e, model)[...]
-    stats = h0[:, width:].astype(f32)
+        s = lax.rem(r + n_t - k, n_t)
+        hs[s] = h[:, 0:width].astype(f32)
+        gs[s] = h[:, width + 16:].astype(f32)
+    stats = h0[:, width:width + 16].astype(f32)
     for h in packs[1:]:
-        stats += h[:, width:].astype(f32)
+        stats += h[:, width:width + 16].astype(f32)
     inverse = lax.rsqrt((stats[:, 0:1] + stats[:, 1:2]) / model + epsilon)
     gate = 1.0 / (1.0 + jnp.exp(-inverse * (stats[:, 2:3] + stats[:, 3:4])))
-    number = h0[:, width + 4:width + 5].astype(f32)
-    place[...] = (iota((h0.shape[0], tok), 1).astype(f32) + 1.0 == number).astype(f32)
-    cap = h0.shape[0] // n_e
-    for k in range(n_e):
-        part = slice(k * cap, (k + 1) * cap)
-        sender = lax.rem(e + n_e - k, n_e) if direct else k
-        got = mm(place[part].astype(bf16), chunk(dy_all, sender, model)[...], (1, 1))
-        de_rows[part] = got * gate[part]
-    de[...] = de_rows[...].astype(bf16)
     for s in range(n_t):
         cols = slice(s * width, (s + 1) * width)
         u[:, cols] = (hs[s] * inverse).astype(bf16)
+        de[:, cols] = (gs[s] * gate).astype(bf16)
     value, slope = gelu_pair(mm(u[...], up[0]))
     z[...] = value.astype(bf16)
     da[...] = (mm(de[...], down[0], (1, 1)) * slope).astype(bf16)
@@ -306,10 +323,10 @@
 
 
 def backward_kernel(
-    ids, b0, b1, b2, b3, t0, t1, t2, t3, dy,
+    b0, b1, b2, b3, t0, t1, t2, t3,
     routes, router, gain, out_w, qkv_wt, heads, probs,
     c0, c1, c2, c3, dr1_own, d_proj, d_att, d_logits, gain_terms, d_scores,
-    bs, ts, dr, *, n_t,
+    bs, ts, ys, dr, *, n_t,
 ):
     width = dr1_own.shape[0]
     tok = b0.shape[1]
@@ -317,12 +334,13 @@
     n_heads = probs.shape[0]
     size = width // n_heads
     model = n_t * width
-    r = ids[0]
+    r, _ = my_place()
     packs, tokens = (b0, b1, b2, b3), (t0, t1, t2, t3)
     for k in range(n_t):
         s = lax.rem(r + n_t - k, n_t)
         chunk(bs, s, width)[...] = packs[k][0:width].astype(f32)
         chunk(ts, s, width)[...] = tokens[k][0:width].astype(f32)
+        chunk(ys, s, width)[...] = tokens[k][width + 16:].astype(f32)
     inverse, gate0, gate1 = gates_of(total_stats(tokens, width), model)
     back = total_stats(packs, width)
     dg0 = back[0:1] + back[1:2]
@@ -338,7 +356,7 @@
     gain_terms[...] = dh2 * res * inverse
     weighted = dh2 * gain[...]
     dot = jnp.sum(weighted * res, axis=0, keepdims=True) * (inverse**3 / model)
-    dr[...] = dy[...].astype(f32) + inverse * weighted - res * dot
+    dr[...] = ys[...] + inverse * weighted - res * dot
     d_att[...] = dr[...].astype(bf16)
     dr1_own[...] = chunk(dr, r, width)[...]
     d_o = mm(out_w[...], d_att[...]).astype(bf16)
@@ -368,7 +386,7 @@
 
 
 def small_grad_kernel(
-    ids, t0, t1, t2, t3, d_logits, gain_terms, gain1_row, gain2, h1, d_proj, attended, d_att,
+    t0, t1, t2, t3, d_logits, gain_terms, gain1_row, gain2, h1, d_proj, attended, d_att,
     d_scores, buckets, qkv_w, small, last, ts, padded, *, n_t, n_buckets, direct,
 ):
     packs = (t0, t1, t2, t3)
@@ -377,7 +395,7 @@
     inner = d_proj.shape[0]
     experts = d_logits.shape[0]
     tok = t0.shape[1]
-    r = ids[0]
+    r, _ = my_place()
     for k, t in enumerate(packs):
         chunk(ts, lax.rem(r + n_t - k, n_t), width)[...] = t[0:width].astype(f32)
     inverse, _, _ = gates_of(total_stats(packs, width), model)
@@ -406,21 +424,24 @@
         last[...] = mm(attended[...], d_att[...], (1, 1)).astype(last.dtype)
 
 
-def late_sum_kernel(ids, last, att_all, small, own, q1, q2, q3, blocks, *, n_t, n_e, inner):
+def senders(n_e):
+    _, e = my_place()
+    other = e + 1 - 2 * lax.rem(e, 2)
+    half = n_e // 2
+    return [lax.rem((e, other)[j // half] + n_e - 2 * (j % half), n_e) for j in range(n_e)]
+
+
+def late_sum_kernel(att_all, *refs, n_t, n_e, inner):
+    lasts, (small, own, q1, q2, q3, blocks) = refs[:n_e], refs[n_e:]
     model = small.shape[1]
     width = model // n_t
-    tok = last.shape[1]
-    stride = last.shape[0] // n_e
+    stride, tok = lasts[0].shape
     height = small.shape[0]
-    r = ids[0]
-    total = last[inner + width:stride].astype(f32)
-    grad = mm(att_all[0:model], last[inner:inner + width], (1, 1))
-    for k in range(1, n_e):
-        base = k * stride
-        total += last[base + inner + width:base + stride].astype(f32)
-        grad += mm(
-            att_all[k * model:(k + 1) * model], last[base + inner:base + inner + width], (1, 1)
-        )
+    r, _ = my_place()
+    total, grad = 0.0, 0.0
+    for last, sender in zip(lasts, senders(n_e)):
+        total += last[inner + width:].astype(f32)
+        grad += mm(chunk(att_all, sender, model)[...], last[inner:inner + width], (1, 1))
     for c in range(model // tok):
         small[:, c * tok:(c + 1) * tok] = total[c * height:(c + 1) * height]
     for s in range(n_t):
@@ -430,9 +451,9 @@
         q[...] = blocks[lax.rem(r + k, n_t)].astype(bf16)
 
 
-def out_grad_kernel(ids, own, q1, q2, q3, f0, f1, f2, f3, out, first, blocks, *, n_t):
+def out_grad_kernel(own, q1, q2, q3, f0, f1, f2, f3, out, first, blocks, *, n_t):
     width = own.shape[0]
-    r = ids[0]
+    r, _ = my_place()
     blocks[r] = own[...]
     for k, q in ((1, q1), (2, q2), (3, q3)):
         blocks[lax.rem(r + n_t - k, n_t)] = q[...].astype(f32)
@@ -441,23 +462,24 @@
     first[...] = f0[...] + f1[...] + (f2[...] + f3[...])
 
 
-def input_grad_kernel(ids, c0, c1, c2, c3, dr1, inv1, x, gain, out, *, n_t):
+def input_grad_kernel(c0, c1, c2, c3, dr1, inv1, x, gain, out, *, n_t):
     width = x.shape[0]
     total = c0[...].astype(f32) + c1[...].astype(f32) + (c2[...].astype(f32) + c3[...].astype(f32))
     row_dot = (total[width:width + 1] + total[width + 1:width + 2]) / (n_t * width)
     inverse = inv1[...]
-    weighted = total[0:width] * chunk(gain, ids[0], width)[...]
+    weighted = total[0:width] * chunk(gain, my_place()[0], width)[...]
     out[...] = dr1[...] + inverse * weighted - x[...].astype(f32) * (inverse * inverse * row_dot)
 
 
-def qkv_grad_kernel(last, h1_all, out, *, count):
+def qkv_grad_kernel(h1_all, *refs):
+    lasts, out = refs[:-1], refs[-1]
     inner, model = out.shape
-    stride = last.shape[0] // count
-    total = mm(last[0:inner], h1_all[0:model], (1, 1))
-    for k in range(1, count):
-        total += mm(
-            last[k * stride:k * stride + inner], h1_all[k * model:(k + 1) * model], (1, 1)
-        )
+    if len(lasts) == 1:
+        out[...] = mm(lasts[0][0:inner], h1_all[...], (1, 1))
+        return
+    total = 0.0
+    for last, sender in zip(lasts, senders(len(lasts))):
+        total += mm(last[0:inner], chunk(h1_all, sender, model)[...], (1, 1))
     out[...] = total
 
 
@@ -487,7 +509,7 @@
     rows = experts * cap
     n_heads = rel_table.shape[1]
     n_buckets = rel_table.shape[0]
-    direct = n_e <= 8 and cap % 8 == 0
+    direct = n_e == 8 and cap % 8 == 0
     n_pieces = n_e if direct else 1
     padded = pltpu.VMEM((1, tok), i32)
 
@@ -518,7 +540,6 @@
     def piece_shapes(w):
         return [((rows // n_pieces, w), bf16)] * n_pieces
 
-    ids = jnp.stack([lax.axis_index("tensor"), lax.axis_index("expert")]).astype(i32)
     x = tokens.T
     dy = cotangent.T
     qkv_w = qkv_weight.transpose(0, 2, 1).reshape(inner, model)
@@ -530,12 +551,12 @@
     buckets = bucket_ids.reshape(1, -1)
 
     xs = around(x)
-    dy_all = gather(dy, ("expert", "tensor"))
     gain1, out_wt, bias = run(
         prepare_kernel,
         [((model, 1), f32), ((model, width), bf16), ((n_heads, tok, tok), f32)],
         lengths, gain1_row, out_weight, table, buckets,
-        smem=1, scratch=[padded],
+        fetch=(0, 1, 2, 3, 4),
+        scratch=[padded],
     )
     own, p1, p2, p3, h1, inv1, heads, probs, attended = run(
         functools.partial(attention_kernel, n_t=n_t),
@@ -548,8 +569,8 @@
             ((n_heads, tok, tok), f32),
             ((width, tok), bf16),
         ],
-        ids, *xs, gain1, qkv_w, out_wt, bias,
-        smem=1,
+        *xs, gain1, qkv_w, out_wt, bias,
+        fetch=(n_t + 1,),
         scratch=[pltpu.VMEM((model, tok), f32), pltpu.VMEM((model, tok), f32)],
     )
     got = [shift(p, k) for k, p in ((1, p1), (2, p2), (3, p3))]
@@ -563,33 +584,31 @@
             ((experts, width), bf16),
             ((model, inner), bf16),
         ],
-        ids, routes_t, router, gain2_row, qkv_w, inv1,
-        smem=1, scratch=[pltpu.VMEM((n_t, experts, width), f32)],
+        routes_t, router, gain2_row, qkv_w, inv1,
+        fetch=(0, 1, 2, 3),
+        scratch=[pltpu.VMEM((n_t, experts, width), f32)],
     )
     if direct:
         h1_all = gather(h1, "expert")
         att_all = gather(attended, ("expert", "tensor"))
     *row_pieces, token_pack, residual = run(
         dispatch_kernel,
-        piece_shapes(width + 16) + [((width + 16, tok), bf16), ((width, tok), f32)],
-        ids, own, *got, x, gain2, rw_own, routes_t, dest,
-        smem=1, scratch=[pltpu.VMEM((width + 16, tok), bf16)],
+        piece_shapes(2 * width + 16) + [((2 * width + 16, tok), bf16), ((width, tok), f32)],
+        own, *got, x, dy, gain2, rw_own, routes_t, dest,
+        fetch=(4, 5, 8),
+        scratch=[pltpu.VMEM((2 * width + 16, tok), bf16)],
     )
     in_rows = around(join(exchange(row_pieces)))
     token_packs = around(token_pack)
 
-    c0, c1, c2, c3, u, z, de, da, dy_here = run(
-        functools.partial(expert_kernel, n_t=n_t, n_e=n_e, direct=direct),
-        [((rows, 2 * width), bf16)] * 4
-        + [((rows, model), bf16)] * 4
-        + [((model, tok), bf16)],
-        ids, *in_rows, dy_all, up_weight, down_weight,
-        smem=1,
-        limit=32 if direct else 48,
+    c0, c1, c2, c3, u, z, de, da = run(
+        functools.partial(expert_kernel, n_t=n_t),
+        [((rows, 2 * width), bf16)] * 4 + [((rows, model), bf16)] * 4,
+        *in_rows, up_weight, down_weight,
+        fetch=(4, 5),
         scratch=[
             pltpu.VMEM((n_t, rows, width), f32),
-            pltpu.VMEM((rows, tok), f32),
-            pltpu.VMEM((rows, model), f32),
+            pltpu.VMEM((n_t, rows, width), f32),
             pltpu.VMEM((n_t, rows, 2 * width), bf16),
         ],
     )
@@ -604,6 +623,7 @@
         functools.partial(combine_kernel, n_t=n_t),
         [((width, tok), bf16), ((width + 16, tok), bf16)],
         *token_packs, dest, dy, residual, *back,
+        fetch=(5,),
     )
     back_packs = around(back_pack)
 
@@ -618,9 +638,9 @@
             ((model, tok), f32),
             ((n_heads, tok, tok), bf16),
         ],
-        ids, *back_packs, *token_packs, dy_here, routes_t, router, gain2, out_weight, qkv_wt, heads, probs,
-        smem=1,
-        scratch=[pltpu.VMEM((model, tok), f32)] * 3,
+        *back_packs, *token_packs, routes_t, router, gain2, out_weight, qkv_wt, heads, probs,
+        fetch=(8, 9, 11),
+        scratch=[pltpu.VMEM((model, tok), f32)] * 4,
     )
     got = [shift(c, k) for k, c in ((1, c1), (2, c2), (3, c3))]
     height = experts + 8
@@ -631,41 +651,40 @@
     small, last = run(
         functools.partial(small_grad_kernel, n_t=n_t, n_buckets=n_buckets, direct=direct),
         [((height, model), f32), (last_shape, bf16)],
-        ids, *token_packs, d_logits, gain_terms, gain1_row, gain2, h1, d_proj, attended, d_att,
+        *token_packs, d_logits, gain_terms, gain1_row, gain2, h1, d_proj, attended, d_att,
         d_scores, buckets, qkv_w,
-        smem=1,
+        fetch=(6, 13, 14),
         scratch=[pltpu.VMEM((model, tok), f32), padded],
     )
     (input_grad,) = run(
         functools.partial(input_grad_kernel, n_t=n_t),
         [((width, tok), f32)],
-        ids, c0, *got, dr1, inv1, x, gain1,
-        smem=1,
+        c0, *got, dr1, inv1, x, gain1,
+        fetch=(6,),
     )
     if direct:
-        last = gather(last, "expert")
+        lasts = [last] + [shift(last, 2 * k, "expert", n_e) for k in range(1, n_e // 2)]
+        lasts = lasts + [
+            lax.ppermute(v, "expert", [(i, i ^ 1) for i in range(n_e)]) for v in lasts
+        ]
         small, own, q1, q2, q3 = run(
             functools.partial(late_sum_kernel, n_t=n_t, n_e=n_e, inner=inner),
             [((height, model), f32), ((width, width), f32)] + [((width, width), bf16)] * 3,
-            ids, last, att_all,
-            smem=1, scratch=[pltpu.VMEM((n_t, width, width), f32)],
+            att_all, *lasts,
+            scratch=[pltpu.VMEM((n_t, width, width), f32)],
         )
         firsts = around(small[experts + 1:experts + 2])
         got = [shift(q, k) for k, q in ((1, q1), (2, q2), (3, q3))]
-        (qkv_grad,) = run(
-            functools.partial(qkv_grad_kernel, count=n_e), [((inner, model), f32)], last, h1_all
-        )
+        (qkv_grad,) = run(qkv_grad_kernel, [((inner, model), f32)], h1_all, *lasts)
         out_grad, first = run(
             functools.partial(out_grad_kernel, n_t=n_t),
             [(out_weight.shape, f32), ((1, model), f32)],
-            ids, own, *got, *firsts,
-            smem=1, scratch=[pltpu.VMEM((n_t, width, width), f32)],
+            own, *got, *firsts,
+            scratch=[pltpu.VMEM((n_t, width, width), f32)],
         )
     else:
         small, out_grad = lax.psum((small, last.astype(f32)), "expert")
-        (qkv_grad,) = run(
-            functools.partial(qkv_grad_kernel, count=1), [((inner, model), f32)], d_proj, h1
-        )
+        (qkv_grad,) = run(qkv_grad_kernel, [((inner, model), f32)], h1, d_proj)
         qkv_grad = lax.psum(qkv_grad, "expert")
         first = lax.psum(small[experts + 1], "tensor")
     return (

time: 238 us -> 169 us (0.71)
  the two profiles are of different devices: /device:TPU:0 before, /device:TPU:9 now
where the time goes in v4:
time: 169 us
  waiting for transfers between devices  72.9 us (43%)
  starting transfers between devices  46.7 us (28%)
  Pallas kernels  23.9 us (14%)
  between operations  14.4 us (9%)
  local copies, waits for them, and re-layouts  10.3 us (6%)
    ppermute x44, waiting for transfers between devices, shift(): return lax.ppermute(v, axis, [(i, (i + k) % n) for i in range(n)])  72.1 us
    ppermute x44, starting transfers between devices, shift(): return lax.ppermute(v, axis, [(i, (i + k) % n) for i in range(n)])  43.5 us
    pallas_call x15, Pallas kernels, run(): pl.pallas_call(whole, out_shape=[jax.ShapeDtypeStruct(s, d) for s, d in o...  23.9 us
    unnamed x36, local copies, waits for them, and re-layouts  7.77 us
  transfers between devices with their start and end apart: 50, of which 23 were waited for; matrix products, arithmetic and copies ran while one was open for 1% of the time, Pallas kernels for 11%

profile of v4, /device:TPU:9, one launch (start us, length us, event | category | flops | bytes accessed | tf_op | source)
XLA Modules:
  0.0 168.7 jit_solution(4026646875963721087)
XLA Ops:
  7.2 1.9 %collective-permute-start = (bf16[192,128]{1,0:T(8,128)(2,1)}, bf16[192,128]{1,0:T(8,128)(2,1)S(1)}, u32[]{:S(2)}, u32[]{:S(2)}) collective-permute-start(bf16[192,128]{1,0:T(8,128)(2,1)} %bitcast.21), channel_id=1, source_target_pairs={{0,1},{1,2},{2,3},{3,0},{4,5},{5,6},{6,7},{7,4},{8,9},{9,10},{10,1... | collective-permute-start | bytes 147464 | tf_op jit(solution)/shard_map/ppermute | solution.py:517
  14.2 1.2 copy-done
  16.1 2.4 %shard_map.205 = (f32[192,128]{1,0:T(8,128)S(1)}, bf16[192,128]{1,0:T(8,128)(2,1)S(1)}, bf16[192,128]{1,0:T(8,128)(2,1)S(1)}, bf16[192,128]{1,0:T(8,128)(2,1)S(1...) custom-call(bf16[192,128]{1,0:T(8,128)(2,1)S(1)} %bitcast.24, ...), custom_call_target="tpu_custom_call" | custom-call | bytes 2412032 | tf_op jit(solution)/shard_map/pallas_call | solution.py:67
  19.4 1.6 collective-permute-start.3
  20.9 1.2 collective-permute-start.4
  23.0 2.0 %collective-permute-done.4.refs_2_ = bf16[192,128]{1,0:T(8,128)(2,1)S(1)} collective-permute-done((bf16[192,128]{1,0:T(8,128)(2,1)S(1)}, bf16[192,128]{1,0:T(8,128)(2,1)S(1)}, u32[]{:S(2)}, u32[]{:S(2)}) %collective-permute-start.4) | collective-permute-done | bytes 49184 | tf_op jit(solution)/shard_map/ppermute | solution.py:517
  26.4 1.3 collective-permute-start.9
  27.7 1.3 collective-permute-start.10
  29.0 1.1 collective-permute-start.11
  30.1 2.2 %collective-permute-start.12 = (bf16[40,400]{1,0:T(8,128)(2,1)S(1)}, bf16[40,400]{1,0:T(8,128)(2,1)S(1)}, u32[]{:S(2)}, u32[]{:S(2)}) collective-permute-start(bf16[40,400]{1,0:T(8,128)(2,1)S(1)} %get-tuple-element.91), channel_id=1, source_target_pairs={{0,16},{4,20},{8,24},{12,28},{16,0},{20,4},{24,8},{28,12},{1,17},{... | collective-permute-start | bytes 96008 | tf_op jit(solution)/shard_map/ppermute | solution.py:517
  33.3 1.5 collective-permute-start.14
  34.7 1.2 collective-permute-start.15
  36.3 6.0 %collective-permute-done.13.refs_5_ = bf16[40,400]{1,0:T(8,128)(2,1)S(1)} collective-permute-done((bf16[40,400]{1,0:T(8,128)(2,1)S(1)}, bf16[40,400]{1,0:T(8,128)(2,1)S(1)}, u32[]{:S(2)}, u32[]{:S(2)}) %collective-permute-start.13) | collective-permute-done | bytes 32032 | tf_op jit(solution)/shard_map/ppermute | solution.py:517
  45.2 5.9 %collective-permute-done.16.refs_1_ = bf16[320,400]{1,0:T(8,128)(2,1)S(1)} collective-permute-done((bf16[320,400]{1,0:T(8,128)(2,1)S(1)}, bf16[320,400]{1,0:T(8,128)(2,1)S(1)}, u32[]{:S(2)}, u32[]{:S(2)}) %collective-permute-start.16) | collective-permute-done | bytes 256032 | tf_op jit(solution)/shard_map/ppermute | solution.py:517
  51.1 8.8 %collective-permute-done.17.refs_2_ = bf16[320,400]{1,0:T(8,128)(2,1)S(1)} collective-permute-done((bf16[320,400]{1,0:T(8,128)(2,1)S(1)}, bf16[320,400]{1,0:T(8,128)(2,1)S(1)}, u32[]{:S(2)}, u32[]{:S(2)}) %collective-permute-start.17) | collective-permute-done | bytes 256032 | tf_op jit(solution)/shard_map/ppermute | solution.py:517
  60.5 3.1 %shard_map.209 = (bf16[320,384]{1,0:T(8,128)(2,1)S(1)}, bf16[320,384]{1,0:T(8,128)(2,1)S(1)}, bf16[320,384]{1,0:T(8,128)(2,1)S(1)}, bf16[320,384]{1,0:T(8,128)(2...) custom-call(bf16[320,400]{1,0:T(8,128)(2,1)S(1)} %shard_map.208.refs, ...), custom_call_target="tpu_custom_call" | custom-call | bytes 6332416 | tf_op jit(solution)/shard_map/pallas_call | solution.py:67
  67.8 1.3 collective-permute-start.8
  69.2 4.6 %collective-permute-done.20.refs_2_ = bf16[320,384]{1,0:T(8,128)(2,1)S(1)} collective-permute-done((bf16[320,384]{1,0:T(8,128)(2,1)S(1)}, bf16[320,384]{1,0:T(8,128)(2,1)S(1)}, u32[]{:S(2)}, u32[]{:S(2)}) %collective-permute-start.20) | collective-permute-done | bytes 245792 | tf_op jit(solution)/shard_map/ppermute | solution.py:517
  73.7 3.9 %collective-permute-done.21.refs_3_ = bf16[320,384]{1,0:T(8,128)(2,1)S(1)} collective-permute-done((bf16[320,384]{1,0:T(8,128)(2,1)S(1)}, bf16[320,384]{1,0:T(8,128)(2,1)S(1)}, u32[]{:S(2)}, u32[]{:S(2)}) %collective-permute-start.21) | collective-permute-done | bytes 245792 | tf_op jit(solution)/shard_map/ppermute | solution.py:517
  77.8 1.9 %collective-permute-start.22 = (bf16[40,384]{1,0:T(8,128)(2,1)S(1)}, bf16[40,384]{1,0:T(8,128)(2,1)S(1)}, u32[]{:S(2)}, u32[]{:S(2)}) collective-permute-start(bf16[40,384]{1,0:T(8,128)(2,1)S(1)} %get-tuple-element.100), channel_id=1, source_target_pairs={{0,4},{4,8},{8,12},{12,16},{16,20},{20,24},{24,28},{28,0},{1,5},{5... | collective-permute-start | bytes 92168 | tf_op jit(solution)/shard_map/ppermute | solution.py:517
  79.6 1.1 collective-permute-start.24
  80.7 2.2 %collective-permute-start.25 = (bf16[40,384]{1,0:T(8,128)(2,1)S(1)}, bf16[40,384]{1,0:T(8,128)(2,1)S(1)}, u32[]{:S(2)}, u32[]{:S(2)}) collective-permute-start(bf16[40,384]{1,0:T(8,128)(2,1)S(1)} %get-tuple-element.103), channel_id=1, source_target_pairs={{0,16},{4,20},{8,24},{12,28},{16,0},{20,4},{24,8},{28,12},{1,17},{... | collective-permute-start | bytes 92168 | tf_op jit(solution)/shard_map/ppermute | solution.py:517
  83.0 1.8 %collective-permute-start.26 = (bf16[40,384]{1,0:T(8,128)(2,1)S(1)}, bf16[40,384]{1,0:T(8,128)(2,1)S(1)}, u32[]{:S(2)}, u32[]{:S(2)}) collective-permute-start(bf16[40,384]{1,0:T(8,128)(2,1)S(1)} %get-tuple-element.104), channel_id=1, source_target_pairs={{0,20},{4,24},{8,28},{12,0},{16,4},{20,8},{24,12},{28,16},{1,21},{... | collective-permute-start | bytes 92168 | tf_op jit(solution)/shard_map/ppermute | solution.py:517
  86.1 1.5 collective-permute-done.26.refs_12_
  89.7 2.0 %collective-permute-start.29 = (bf16[208,128]{1,0:T(8,128)(2,1)S(1)}, bf16[208,128]{1,0:T(8,128)(2,1)S(1)}, u32[]{:S(2)}, u32[]{:S(2)}) collective-permute-start(bf16[208,128]{1,0:T(8,128)(2,1)S(1)} %get-tuple-element.108.refs_0_), channel_id=1, source_target_pairs={{0,1},{1,2},{2,3},{3,0},{4,5},{5,6},{6,7},{7,4},{8,9},{9,10},{10,1... | collective-permute-start | bytes 159752 | tf_op jit(solution)/shard_map/ppermute | solution.py:517
  91.6 1.2 collective-permute-start.30
  92.8 3.0 %collective-permute-done.30.refs_2_ = bf16[208,128]{1,0:T(8,128)(2,1)S(1)} collective-permute-done((bf16[208,128]{1,0:T(8,128)(2,1)S(1)}, bf16[208,128]{1,0:T(8,128)(2,1)S(1)}, u32[]{:S(2)}, u32[]{:S(2)}) %collective-permute-start.30) | collective-permute-done | bytes 53280 | tf_op jit(solution)/shard_map/ppermute | solution.py:517
  95.9 1.6 collective-permute-done.31.refs_3_
  97.5 2.6 %shard_map.212 = (bf16[208,128]{1,0:T(8,128)(2,1)S(1)}, bf16[208,128]{1,0:T(8,128)(2,1)S(1)}, bf16[208,128]{1,0:T(8,128)(2,1)S(1)}, bf16[208,128]{1,0:T(8,128)(2...) custom-call(bf16[208,128]{1,0:T(8,128)(2,1)S(1)} %get-tuple-element., ...), custom_call_target="tpu_custom_call" | custom-call | bytes 3313664 | tf_op jit(solution)/shard_map/pallas_call | solution.py:67
  100.1 3.0 %shard_map.214 = (f32[16,768]{1,0:T(8,128)}, bf16[864,128]{1,0:T(8,128)(2,1)S(1)}) custom-call(bf16[400,128]{1,0:T(8,128)(2,1)S(1)} %get-tuple-element.85.refs_0_.refs_4_, bf16[400,128]{1,0:T(8,128)(2,1)S(1)} %collective-permute-done.6.refs_1_.refs_5_, bf16[400,128]{1,0:T(8,128)(2,1)S(1)} %collective-permute-done.7.refs_2_.refs_6_, ...), custom_call_target="tpu_custom_call" | custom-call | bytes 2656704 | tf_op jit(solution)/shard_map/pallas_call | solution.py:67
  103.1 2.5 %collective-permute-start.36 = (bf16[864,128]{1,0:T(8,128)(2,1)S(1)}, bf16[864,128]{1,0:T(8,128)(2,1)S(1)}, u32[]{:S(2)}, u32[]{:S(2)}) collective-permute-start(bf16[864,128]{1,0:T(8,128)(2,1)S(1)} %get-tuple-element.124.refs_1_), channel_id=1, source_target_pairs={{0,16},{4,20},{8,24},{12,28},{16,0},{20,4},{24,8},{28,12},{1,17},{... | collective-permute-start | bytes 663560 | tf_op jit(solution)/shard_map/ppermute | solution.py:517
  105.6 1.9 %collective-permute-start.38 = (bf16[864,128]{1,0:T(8,128)(2,1)S(1)}, bf16[864,128]{1,0:T(8,128)(2,1)S(1)}, u32[]{:S(2)}, u32[]{:S(2)}) collective-permute-start(bf16[864,128]{1,0:T(8,128)(2,1)S(1)} %get-tuple-element.124.refs_1_), channel_id=1, source_target_pairs={{0,4},{4,0},{8,12},{12,8},{16,20},{20,16},{24,28},{28,24},{1,5},{5... | collective-permute-start | bytes 663560 | tf_op jit(solution)/shard_map/ppermute | solution.py:668
  107.5 3.0 %collective-permute-done.35.refs_2_ = bf16[864,128]{1,0:T(8,128)(2,1)S(1)} collective-permute-done((bf16[864,128]{1,0:T(8,128)(2,1)S(1)}, bf16[864,128]{1,0:T(8,128)(2,1)S(1)}, u32[]{:S(2)}, u32[]{:S(2)}) %collective-permute-start.35) | collective-permute-done | bytes 221216 | tf_op jit(solution)/shard_map/ppermute | solution.py:517
  110.5 16.2 %collective-permute-done.36.refs_3_ = bf16[864,128]{1,0:T(8,128)(2,1)S(1)} collective-permute-done((bf16[864,128]{1,0:T(8,128)(2,1)S(1)}, bf16[864,128]{1,0:T(8,128)(2,1)S(1)}, u32[]{:S(2)}, u32[]{:S(2)}) %collective-permute-start.36) | collective-permute-done | bytes 221216 | tf_op jit(solution)/shard_map/ppermute | solution.py:517
  127.3 2.2 %collective-permute-done.37.refs_4_ = bf16[864,128]{1,0:T(8,128)(2,1)S(1)} collective-permute-done((bf16[864,128]{1,0:T(8,128)(2,1)S(1)}, bf16[864,128]{1,0:T(8,128)(2,1)S(1)}, u32[]{:S(2)}, u32[]{:S(2)}) %collective-permute-start.37) | collective-permute-done | bytes 221216 | tf_op jit(solution)/shard_map/ppermute | solution.py:517
  130.1 1.6 collective-permute-start.32
  131.7 1.2 collective-permute-done.32.refs_1_
  133.3 2.9 %collective-permute-done.33.refs_2_ = bf16[208,128]{1,0:T(8,128)(2,1)S(1)} collective-permute-done((bf16[208,128]{1,0:T(8,128)(2,1)S(1)}, bf16[208,128]{1,0:T(8,128)(2,1)S(1)}, u32[]{:S(2)}, u32[]{:S(2)}) %collective-permute-start.33) | collective-permute-done | bytes 53280 | tf_op jit(solution)/shard_map/ppermute | solution.py:517
  136.2 2.2 %collective-permute-start.34 = (bf16[208,128]{1,0:T(8,128)(2,1)S(1)}, bf16[208,128]{1,0:T(8,128)(2,1)S(1)}, u32[]{:S(2)}, u32[]{:S(2)}) collective-permute-start(bf16[208,128]{1,0:T(8,128)(2,1)S(1)} %get-tuple-element.115), channel_id=1, source_target_pairs={{0,3},{1,0},{2,1},{3,2},{4,7},{5,4},{6,5},{7,6},{8,11},{9,8},{10,9... | collective-permute-start | bytes 159752 | tf_op jit(solution)/shard_map/ppermute | solution.py:517
  138.5 3.2 %shard_map.218 = (f32[1,768,768]{2,1,0:T(8,128)}, f32[1,768,768]{2,1,0:T(8,128)}) custom-call(bf16[320,768]{1,0:T(8,128)(2,1)S(1)} %get-tuple-element.132.refs_0_, bf16[320,768]{1,0:T(8,128)(2,1)S(1)} %get-tuple-element.133.refs_1_, bf16[320,768]{1,0:T(8,128)(2,1)S(1)} %get-tuple-element.134.refs_2_, bf16[320,768]{1,0:T(8,128)(2,1)S(1)} %get-tuple-element.135.refs_3_), custom_call_target="tpu_custom_call" | custom-call | bytes 6684672 | tf_op jit(solution)/shard_map/pallas_call | solution.py:67
  142.5 1.4 copy-done.3
  143.9 3.2 %shard_map.217 = f32[576,768]{1,0:T(8,128)} custom-call(bf16[6144,128]{1,0:T(8,128)(2,1)S(1)} %copy-done.3, bf16[864,128]{1,0:T(8,128)(2,1)S(1)} %get-tuple-element.124.refs_1_, bf16[864,128]{1,0:T(8,128)(2,1)S(1)} %collective-permute-done.35.refs_2_, bf16[864,128]{1,0:T(8,128)(2,1)S(1)} %collective-permute-done.36.refs_3_, ...), custom_call_target="tpu_custom_call" | custom-call | bytes 5111808 | tf_op jit(solution)/shard_map/pallas_call | solution.py:67
  147.2 1.4 copy-done.2
  148.6 1.1 shard_map.215
  152.7 1.2 collective-permute-start.42
  154.0 1.1 collective-permute-start.43
  156.0 3.6 %collective-permute-done.43.refs_2_ = bf16[192,192]{1,0:T(8,128)(2,1)S(1)} collective-permute-done((bf16[192,192]{1,0:T(8,128)(2,1)S(1)}, bf16[192,192]{1,0:T(8,128)(2,1)S(1)}, u32[]{:S(2)}, u32[]{:S(2)}) %collective-permute-start.43) | collective-permute-done | bytes 73760 | tf_op jit(solution)/shard_map/ppermute | solution.py:517
  160.2 1.1 shard_map.216
  (111 shorter events, 29.2 us)
Async XLA Ops:
  7.2 135.3 %all-gather.5.cloned.1.call-start = ((), (), s32[]{:S(2)}) async-start(), calls=%async_computation.1 | async-start | bytes 1769472 | tf_op jit(solution)/shard_map/all_gather | solution.py:523
  7.2 6.9 %collective-permute-start = (bf16[192,128]{1,0:T(8,128)(2,1)}, bf16[192,128]{1,0:T(8,128)(2,1)S(1)}, u32[]{:S(2)}, u32[]{:S(2)}) collective-permute-start(bf16[192,128]{1,0:T(8,128)(2,1)} %bitcast.21), channel_id=1, source_target_pairs={{0,1},{1,2},{2,3},{3,0},{4,5},{5,6},{6,7},{7,4},{8,9},{9,10},{10,1... | collective-permute-start | bytes 147464 | tf_op jit(solution)/shard_map/ppermute | solution.py:517
  9.1 5.1 %collective-permute-start.1 = (bf16[192,128]{1,0:T(8,128)(2,1)}, bf16[192,128]{1,0:T(8,128)(2,1)S(1)}, u32[]{:S(2)}, u32[]{:S(2)}) collective-permute-start(bf16[192,128]{1,0:T(8,128)(2,1)} %bitcast.22), channel_id=1, source_target_pairs={{0,2},{1,3},{2,0},{3,1},{4,6},{5,7},{6,4},{7,5},{8,10},{9,11},{10,... | collective-permute-start | bytes 147464 | tf_op jit(solution)/shard_map/ppermute | solution.py:517
  9.3 4.8 %collective-permute-start.2 = (bf16[192,128]{1,0:T(8,128)(2,1)}, bf16[192,128]{1,0:T(8,128)(2,1)S(1)}, u32[]{:S(2)}, u32[]{:S(2)}) collective-permute-start(bf16[192,128]{1,0:T(8,128)(2,1)} %bitcast.23), channel_id=1, source_target_pairs={{0,3},{1,0},{2,1},{3,2},{4,7},{5,4},{6,5},{7,6},{8,11},{9,8},{10,9... | collective-permute-start | bytes 147464 | tf_op jit(solution)/shard_map/ppermute | solution.py:517
  18.6 128.5 %all-gather.3.cloned.1.call-start = ((), (), s32[]{:S(2)}) async-start(), calls=%async_computation | async-start | bytes 1622016 | tf_op jit(solution)/shard_map/all_gather | solution.py:523
  19.4 3.6 %collective-permute-start.3 = (bf16[192,128]{1,0:T(8,128)(2,1)S(1)}, bf16[192,128]{1,0:T(8,128)(2,1)S(1)}, u32[]{:S(2)}, u32[]{:S(2)}) collective-permute-start(bf16[192,128]{1,0:T(8,128)(2,1)S(1)} %get-tuple-element.78), channel_id=1, source_target_pairs={{0,1},{1,2},{2,3},{3,0},{4,5},{5,6},{6,7},{7,4},{8,9},{9,10},{10,1... | collective-permute-start | bytes 147464 | tf_op jit(solution)/shard_map/ppermute | solution.py:517
  20.9 4.0 %collective-permute-start.4 = (bf16[192,128]{1,0:T(8,128)(2,1)S(1)}, bf16[192,128]{1,0:T(8,128)(2,1)S(1)}, u32[]{:S(2)}, u32[]{:S(2)}) collective-permute-start(bf16[192,128]{1,0:T(8,128)(2,1)S(1)} %get-tuple-element.79), channel_id=1, source_target_pairs={{0,2},{1,3},{2,0},{3,1},{4,6},{5,7},{6,4},{7,5},{8,10},{9,11},{10,... | collective-permute-start | bytes 147464 | tf_op jit(solution)/shard_map/ppermute | solution.py:517
  22.2 3.5 %collective-permute-start.5 = (bf16[192,128]{1,0:T(8,128)(2,1)S(1)}, bf16[192,128]{1,0:T(8,128)(2,1)S(1)}, u32[]{:S(2)}, u32[]{:S(2)}) collective-permute-start(bf16[192,128]{1,0:T(8,128)(2,1)S(1)} %get-tuple-element.80), channel_id=1, source_target_pairs={{0,3},{1,0},{2,1},{3,2},{4,7},{5,4},{6,5},{7,6},{8,11},{9,8},{10,9... | collective-permute-start | bytes 147464 | tf_op jit(solution)/shard_map/ppermute | solution.py:517
  26.4 6.8 %collective-permute-start.9 = (bf16[40,400]{1,0:T(8,128)(2,1)S(1)}, bf16[40,400]{1,0:T(8,128)(2,1)S(1)}, u32[]{:S(2)}, u32[]{:S(2)}) collective-permute-start(bf16[40,400]{1,0:T(8,128)(2,1)S(1)} %get-tuple-element.88), channel_id=1, source_target_pairs={{0,4},{4,8},{8,12},{12,16},{16,20},{20,24},{24,28},{28,0},{1,5},{5... | collective-permute-start | bytes 96008 | tf_op jit(solution)/shard_map/ppermute | solution.py:517
  27.7 7.0 %collective-permute-start.10 = (bf16[40,400]{1,0:T(8,128)(2,1)S(1)}, bf16[40,400]{1,0:T(8,128)(2,1)S(1)}, u32[]{:S(2)}, u32[]{:S(2)}) collective-permute-start(bf16[40,400]{1,0:T(8,128)(2,1)S(1)} %get-tuple-element.89), channel_id=1, source_target_pairs={{0,8},{4,12},{8,16},{12,20},{16,24},{20,28},{24,0},{28,4},{1,9},{5... | collective-permute-start | bytes 96008 | tf_op jit(solution)/shard_map/ppermute | solution.py:517
  29.0 6.9 %collective-permute-start.11 = (bf16[40,400]{1,0:T(8,128)(2,1)S(1)}, bf16[40,400]{1,0:T(8,128)(2,1)S(1)}, u32[]{:S(2)}, u32[]{:S(2)}) collective-permute-start(bf16[40,400]{1,0:T(8,128)(2,1)S(1)} %get-tuple-element.90), channel_id=1, source_target_pairs={{0,12},{4,16},{8,20},{12,24},{16,28},{20,0},{24,4},{28,8},{1,13},{... | collective-permute-start | bytes 96008 | tf_op jit(solution)/shard_map/ppermute | solution.py:517
  30.1 6.2 %collective-permute-start.12 = (bf16[40,400]{1,0:T(8,128)(2,1)S(1)}, bf16[40,400]{1,0:T(8,128)(2,1)S(1)}, u32[]{:S(2)}, u32[]{:S(2)}) collective-permute-start(bf16[40,400]{1,0:T(8,128)(2,1)S(1)} %get-tuple-element.91), channel_id=1, source_target_pairs={{0,16},{4,20},{8,24},{12,28},{16,0},{20,4},{24,8},{28,12},{1,17},{... | collective-permute-start | bytes 96008 | tf_op jit(solution)/shard_map/ppermute | solution.py:517
  32.2 10.0 %collective-permute-start.13 = (bf16[40,400]{1,0:T(8,128)(2,1)S(1)}, bf16[40,400]{1,0:T(8,128)(2,1)S(1)}, u32[]{:S(2)}, u32[]{:S(2)}) collective-permute-start(bf16[40,400]{1,0:T(8,128)(2,1)S(1)} %get-tuple-element.92), channel_id=1, source_target_pairs={{0,20},{4,24},{8,28},{12,0},{16,4},{20,8},{24,12},{28,16},{1,21},{... | collective-permute-start | bytes 96008 | tf_op jit(solution)/shard_map/ppermute | solution.py:517
  33.3 10.0 %collective-permute-start.14 = (bf16[40,400]{1,0:T(8,128)(2,1)S(1)}, bf16[40,400]{1,0:T(8,128)(2,1)S(1)}, u32[]{:S(2)}, u32[]{:S(2)}) collective-permute-start(bf16[40,400]{1,0:T(8,128)(2,1)S(1)} %get-tuple-element.93), channel_id=1, source_target_pairs={{0,24},{4,28},{8,0},{12,4},{16,8},{20,12},{24,16},{28,20},{1,25},{... | collective-permute-start | bytes 96008 | tf_op jit(solution)/shard_map/ppermute | solution.py:517
  34.7 8.5 %collective-permute-start.15 = (bf16[40,400]{1,0:T(8,128)(2,1)S(1)}, bf16[40,400]{1,0:T(8,128)(2,1)S(1)}, u32[]{:S(2)}, u32[]{:S(2)}) collective-permute-start(bf16[40,400]{1,0:T(8,128)(2,1)S(1)} %get-tuple-element.94), channel_id=1, source_target_pairs={{0,28},{4,0},{8,4},{12,8},{16,12},{20,16},{24,20},{28,24},{1,29},{... | collective-permute-start | bytes 96008 | tf_op jit(solution)/shard_map/ppermute | solution.py:517
  43.3 7.8 %collective-permute-start.16 = (bf16[320,400]{1,0:T(8,128)(2,1)S(1)}, bf16[320,400]{1,0:T(8,128)(2,1)S(1)}, u32[]{:S(2)}, u32[]{:S(2)}) collective-permute-start(bf16[320,400]{1,0:T(8,128)(2,1)S(1)} %shard_map.208.refs_0_), channel_id=1, source_target_pairs={{0,1},{1,2},{2,3},{3,0},{4,5},{5,6},{6,7},{7,4},{8,9},{9,10},{10,1... | collective-permute-start | bytes 768008 | tf_op jit(solution)/shard_map/ppermute | solution.py:517
  44.2 15.8 %collective-permute-start.17 = (bf16[320,400]{1,0:T(8,128)(2,1)S(1)}, bf16[320,400]{1,0:T(8,128)(2,1)S(1)}, u32[]{:S(2)}, u32[]{:S(2)}) collective-permute-start(bf16[320,400]{1,0:T(8,128)(2,1)S(1)} %shard_map.208.refs_0_), channel_id=1, source_target_pairs={{0,2},{1,3},{2,0},{3,1},{4,6},{5,7},{6,4},{7,5},{8,10},{9,11},{10,... | collective-permute-start | bytes 768008 | tf_op jit(solution)/shard_map/ppermute | solution.py:517
  45.2 15.3 %collective-permute-start.18 = (bf16[320,400]{1,0:T(8,128)(2,1)S(1)}, bf16[320,400]{1,0:T(8,128)(2,1)S(1)}, u32[]{:S(2)}, u32[]{:S(2)}) collective-permute-start(bf16[320,400]{1,0:T(8,128)(2,1)S(1)} %shard_map.208.refs_0_), channel_id=1, source_target_pairs={{0,3},{1,0},{2,1},{3,2},{4,7},{5,4},{6,5},{7,6},{8,11},{9,8},{10,9... | collective-permute-start | bytes 768008 | tf_op jit(solution)/shard_map/ppermute | solution.py:517
  63.6 4.2 %collective-permute-start.19 = (bf16[320,384]{1,0:T(8,128)(2,1)S(1)}, bf16[320,384]{1,0:T(8,128)(2,1)S(1)}, u32[]{:S(2)}, u32[]{:S(2)}) collective-permute-start(bf16[320,384]{1,0:T(8,128)(2,1)S(1)} %get-tuple-element.96), channel_id=1, source_target_pairs={{0,1},{1,2},{2,3},{3,0},{4,5},{5,6},{6,7},{7,4},{8,9},{9,10},{10,1... | collective-permute-start | bytes 737288 | tf_op jit(solution)/shard_map/ppermute | solution.py:517
  63.7 10.1 %collective-permute-start.20 = (bf16[320,384]{1,0:T(8,128)(2,1)S(1)}, bf16[320,384]{1,0:T(8,128)(2,1)S(1)}, u32[]{:S(2)}, u32[]{:S(2)}) collective-permute-start(bf16[320,384]{1,0:T(8,128)(2,1)S(1)} %get-tuple-element.97), channel_id=1, source_target_pairs={{0,2},{1,3},{2,0},{3,1},{4,6},{5,7},{6,4},{7,5},{8,10},{9,11},{10,... | collective-permute-start | bytes 737288 | tf_op jit(solution)/shard_map/ppermute | solution.py:517
  64.3 13.3 %collective-permute-start.21 = (bf16[320,384]{1,0:T(8,128)(2,1)S(1)}, bf16[320,384]{1,0:T(8,128)(2,1)S(1)}, u32[]{:S(2)}, u32[]{:S(2)}) collective-permute-start(bf16[320,384]{1,0:T(8,128)(2,1)S(1)} %get-tuple-element.98), channel_id=1, source_target_pairs={{0,3},{1,0},{2,1},{3,2},{4,7},{5,4},{6,5},{7,6},{8,11},{9,8},{10,9... | collective-permute-start | bytes 737288 | tf_op jit(solution)/shard_map/ppermute | solution.py:517
  65.0 14.6 %collective-permute-start.6 = (bf16[400,128]{1,0:T(8,128)(2,1)S(1)}, bf16[400,128]{1,0:T(8,128)(2,1)S(1)}, u32[]{:S(2)}, u32[]{:S(2)}) collective-permute-start(bf16[400,128]{1,0:T(8,128)(2,1)S(1)} %get-tuple-element.85.refs_0_.refs_4_), channel_id=1, source_target_pairs={{0,1},{1,2},{2,3},{3,0},{4,5},{5,6},{6,7},{7,4},{8,9},{9,10},{10,1... | collective-permute-start | bytes 307208 | tf_op jit(solution)/shard_map/ppermute | solution.py:517
  66.0 14.7 %collective-permute-start.7 = (bf16[400,128]{1,0:T(8,128)(2,1)S(1)}, bf16[400,128]{1,0:T(8,128)(2,1)S(1)}, u32[]{:S(2)}, u32[]{:S(2)}) collective-permute-start(bf16[400,128]{1,0:T(8,128)(2,1)S(1)} %get-tuple-element.85.refs_0_.refs_4_), channel_id=1, source_target_pairs={{0,2},{1,3},{2,0},{3,1},{4,6},{5,7},{6,4},{7,5},{8,10},{9,11},{10,... | collective-permute-start | bytes 307208 | tf_op jit(solution)/shard_map/ppermute | solution.py:517
  67.8 15.1 %collective-permute-start.8 = (bf16[400,128]{1,0:T(8,128)(2,1)S(1)}, bf16[400,128]{1,0:T(8,128)(2,1)S(1)}, u32[]{:S(2)}, u32[]{:S(2)}) collective-permute-start(bf16[400,128]{1,0:T(8,128)(2,1)S(1)} %get-tuple-element.85.refs_0_.refs_4_), channel_id=1, source_target_pairs={{0,3},{1,0},{2,1},{3,2},{4,7},{5,4},{6,5},{7,6},{8,11},{9,8},{10,9... | collective-permute-start | bytes 307208 | tf_op jit(solution)/shard_map/ppermute | solution.py:517
  77.8 7.0 %collective-permute-start.22 = (bf16[40,384]{1,0:T(8,128)(2,1)S(1)}, bf16[40,384]{1,0:T(8,128)(2,1)S(1)}, u32[]{:S(2)}, u32[]{:S(2)}) collective-permute-start(bf16[40,384]{1,0:T(8,128)(2,1)S(1)} %get-tuple-element.100), channel_id=1, source_target_pairs={{0,4},{4,8},{8,12},{12,16},{16,20},{20,24},{24,28},{28,0},{1,5},{5... | collective-permute-start | bytes 92168 | tf_op jit(solution)/shard_map/ppermute | solution.py:517
  79.6 5.8 %collective-permute-start.23 = (bf16[40,384]{1,0:T(8,128)(2,1)S(1)}, bf16[40,384]{1,0:T(8,128)(2,1)S(1)}, u32[]{:S(2)}, u32[]{:S(2)}) collective-permute-start(bf16[40,384]{1,0:T(8,128)(2,1)S(1)} %get-tuple-element.101), channel_id=1, source_target_pairs={{0,8},{4,12},{8,16},{12,20},{16,24},{20,28},{24,0},{28,4},{1,9},{5... | collective-permute-start | bytes 92168 | tf_op jit(solution)/shard_map/ppermute | solution.py:517
  79.6 6.4 %collective-permute-start.24 = (bf16[40,384]{1,0:T(8,128)(2,1)S(1)}, bf16[40,384]{1,0:T(8,128)(2,1)S(1)}, u32[]{:S(2)}, u32[]{:S(2)}) collective-permute-start(bf16[40,384]{1,0:T(8,128)(2,1)S(1)} %get-tuple-element.102), channel_id=1, source_target_pairs={{0,12},{4,16},{8,20},{12,24},{16,28},{20,0},{24,4},{28,8},{1,13},{... | collective-permute-start | bytes 92168 | tf_op jit(solution)/shard_map/ppermute | solution.py:517
  80.7 5.3 %collective-permute-start.25 = (bf16[40,384]{1,0:T(8,128)(2,1)S(1)}, bf16[40,384]{1,0:T(8,128)(2,1)S(1)}, u32[]{:S(2)}, u32[]{:S(2)}) collective-permute-start(bf16[40,384]{1,0:T(8,128)(2,1)S(1)} %get-tuple-element.103), channel_id=1, source_target_pairs={{0,16},{4,20},{8,24},{12,28},{16,0},{20,4},{24,8},{28,12},{1,17},{... | collective-permute-start | bytes 92168 | tf_op jit(solution)/shard_map/ppermute | solution.py:517
  83.0 4.6 %collective-permute-start.26 = (bf16[40,384]{1,0:T(8,128)(2,1)S(1)}, bf16[40,384]{1,0:T(8,128)(2,1)S(1)}, u32[]{:S(2)}, u32[]{:S(2)}) collective-permute-start(bf16[40,384]{1,0:T(8,128)(2,1)S(1)} %get-tuple-element.104), channel_id=1, source_target_pairs={{0,20},{4,24},{8,28},{12,0},{16,4},{20,8},{24,12},{28,16},{1,21},{... | collective-permute-start | bytes 92168 | tf_op jit(solution)/shard_map/ppermute | solution.py:517
  84.8 3.8 %collective-permute-start.27 = (bf16[40,384]{1,0:T(8,128)(2,1)S(1)}, bf16[40,384]{1,0:T(8,128)(2,1)S(1)}, u32[]{:S(2)}, u32[]{:S(2)}) collective-permute-start(bf16[40,384]{1,0:T(8,128)(2,1)S(1)} %get-tuple-element.105), channel_id=1, source_target_pairs={{0,24},{4,28},{8,0},{12,4},{16,8},{20,12},{24,16},{28,20},{1,25},{... | collective-permute-start | bytes 92168 | tf_op jit(solution)/shard_map/ppermute | solution.py:517
  85.4 3.2 %collective-permute-start.28 = (bf16[40,384]{1,0:T(8,128)(2,1)S(1)}, bf16[40,384]{1,0:T(8,128)(2,1)S(1)}, u32[]{:S(2)}, u32[]{:S(2)}) collective-permute-start(bf16[40,384]{1,0:T(8,128)(2,1)S(1)} %get-tuple-element.106), channel_id=1, source_target_pairs={{0,28},{4,0},{8,4},{12,8},{16,12},{20,16},{24,20},{28,24},{1,29},{... | collective-permute-start | bytes 92168 | tf_op jit(solution)/shard_map/ppermute | solution.py:517
  91.6 4.2 %collective-permute-start.30 = (bf16[208,128]{1,0:T(8,128)(2,1)S(1)}, bf16[208,128]{1,0:T(8,128)(2,1)S(1)}, u32[]{:S(2)}, u32[]{:S(2)}) collective-permute-start(bf16[208,128]{1,0:T(8,128)(2,1)S(1)} %get-tuple-element.108.refs_0_), channel_id=1, source_target_pairs={{0,2},{1,3},{2,0},{3,1},{4,6},{5,7},{6,4},{7,5},{8,10},{9,11},{10,... | collective-permute-start | bytes 159752 | tf_op jit(solution)/shard_map/ppermute | solution.py:517
  92.8 4.7 %collective-permute-start.31 = (bf16[208,128]{1,0:T(8,128)(2,1)S(1)}, bf16[208,128]{1,0:T(8,128)(2,1)S(1)}, u32[]{:S(2)}, u32[]{:S(2)}) collective-permute-start(bf16[208,128]{1,0:T(8,128)(2,1)S(1)} %get-tuple-element.108.refs_0_), channel_id=1, source_target_pairs={{0,3},{1,0},{2,1},{3,2},{4,7},{5,4},{6,5},{7,6},{8,11},{9,8},{10,9... | collective-permute-start | bytes 159752 | tf_op jit(solution)/shard_map/ppermute | solution.py:517
  103.1 7.5 %collective-permute-start.35 = (bf16[864,128]{1,0:T(8,128)(2,1)S(1)}, bf16[864,128]{1,0:T(8,128)(2,1)S(1)}, u32[]{:S(2)}, u32[]{:S(2)}) collective-permute-start(bf16[864,128]{1,0:T(8,128)(2,1)S(1)} %get-tuple-element.124.refs_1_), channel_id=1, source_target_pairs={{0,8},{4,12},{8,16},{12,20},{16,24},{20,28},{24,0},{28,4},{1,9},{5... | collective-permute-start | bytes 663560 | tf_op jit(solution)/shard_map/ppermute | solution.py:517
  103.1 23.6 %collective-permute-start.36 = (bf16[864,128]{1,0:T(8,128)(2,1)S(1)}, bf16[864,128]{1,0:T(8,128)(2,1)S(1)}, u32[]{:S(2)}, u32[]{:S(2)}) collective-permute-start(bf16[864,128]{1,0:T(8,128)(2,1)S(1)} %get-tuple-element.124.refs_1_), channel_id=1, source_target_pairs={{0,16},{4,20},{8,24},{12,28},{16,0},{20,4},{24,8},{28,12},{1,17},{... | collective-permute-start | bytes 663560 | tf_op jit(solution)/shard_map/ppermute | solution.py:517
  105.6 23.9 %collective-permute-start.37 = (bf16[864,128]{1,0:T(8,128)(2,1)S(1)}, bf16[864,128]{1,0:T(8,128)(2,1)S(1)}, u32[]{:S(2)}, u32[]{:S(2)}) collective-permute-start(bf16[864,128]{1,0:T(8,128)(2,1)S(1)} %get-tuple-element.124.refs_1_), channel_id=1, source_target_pairs={{0,24},{4,28},{8,0},{12,4},{16,8},{20,12},{24,16},{28,20},{1,25},{... | collective-permute-start | bytes 663560 | tf_op jit(solution)/shard_map/ppermute | solution.py:517
  105.6 36.9 %collective-permute-start.38 = (bf16[864,128]{1,0:T(8,128)(2,1)S(1)}, bf16[864,128]{1,0:T(8,128)(2,1)S(1)}, u32[]{:S(2)}, u32[]{:S(2)}) collective-permute-start(bf16[864,128]{1,0:T(8,128)(2,1)S(1)} %get-tuple-element.124.refs_1_), channel_id=1, source_target_pairs={{0,4},{4,0},{8,12},{12,8},{16,20},{20,16},{24,28},{28,24},{1,5},{5... | collective-permute-start | bytes 663560 | tf_op jit(solution)/shard_map/ppermute | solution.py:668
  110.5 31.9 %collective-permute-start.39 = (bf16[864,128]{1,0:T(8,128)(2,1)S(1)}, bf16[864,128]{1,0:T(8,128)(2,1)S(1)}, u32[]{:S(2)}, u32[]{:S(2)}) collective-permute-start(bf16[864,128]{1,0:T(8,128)(2,1)S(1)} %collective-permute-done.35.refs_2_), channel_id=1, source_target_pairs={{0,4},{4,0},{8,12},{12,8},{16,20},{20,16},{24,28},{28,24},{1,5},{5... | collective-permute-start | bytes 663560 | tf_op jit(solution)/shard_map/ppermute | solution.py:668
  126.7 15.8 %collective-permute-start.40 = (bf16[864,128]{1,0:T(8,128)(2,1)S(1)}, bf16[864,128]{1,0:T(8,128)(2,1)S(1)}, u32[]{:S(2)}, u32[]{:S(2)}) collective-permute-start(bf16[864,128]{1,0:T(8,128)(2,1)S(1)} %collective-permute-done.36.refs_3_), channel_id=1, source_target_pairs={{0,4},{4,0},{8,12},{12,8},{16,20},{20,16},{24,28},{28,24},{1,5},{5... | collective-permute-start | bytes 663560 | tf_op jit(solution)/shard_map/ppermute | solution.py:668
  129.5 13.0 %collective-permute-start.41 = (bf16[864,128]{1,0:T(8,128)(2,1)S(1)}, bf16[864,128]{1,0:T(8,128)(2,1)S(1)}, u32[]{:S(2)}, u32[]{:S(2)}) collective-permute-start(bf16[864,128]{1,0:T(8,128)(2,1)S(1)} %collective-permute-done.37.refs_4_), channel_id=1, source_target_pairs={{0,4},{4,0},{8,12},{12,8},{16,20},{20,16},{24,28},{28,24},{1,5},{5... | collective-permute-start | bytes 663560 | tf_op jit(solution)/shard_map/ppermute | solution.py:668
  132.9 3.3 %collective-permute-start.33 = (bf16[208,128]{1,0:T(8,128)(2,1)S(1)}, bf16[208,128]{1,0:T(8,128)(2,1)S(1)}, u32[]{:S(2)}, u32[]{:S(2)}) collective-permute-start(bf16[208,128]{1,0:T(8,128)(2,1)S(1)} %get-tuple-element.114), channel_id=1, source_target_pairs={{0,2},{1,3},{2,0},{3,1},{4,6},{5,7},{6,4},{7,5},{8,10},{9,11},{10,... | collective-permute-start | bytes 159752 | tf_op jit(solution)/shard_map/ppermute | solution.py:517
  136.2 5.4 %collective-permute-start.34 = (bf16[208,128]{1,0:T(8,128)(2,1)S(1)}, bf16[208,128]{1,0:T(8,128)(2,1)S(1)}, u32[]{:S(2)}, u32[]{:S(2)}) collective-permute-start(bf16[208,128]{1,0:T(8,128)(2,1)S(1)} %get-tuple-element.115), channel_id=1, source_target_pairs={{0,3},{1,0},{2,1},{3,2},{4,7},{5,4},{6,5},{7,6},{8,11},{9,8},{10,9... | collective-permute-start | bytes 159752 | tf_op jit(solution)/shard_map/ppermute | solution.py:517
  150.3 4.8 %collective-permute-start.45 = (f32[1,768]{1,0:T(1,128)S(1)}, f32[1,768]{1,0:T(1,128)S(1)}, u32[]{:S(2)}, u32[]{:S(2)}) collective-permute-start(f32[1,768]{1,0:T(1,128)S(1)} %get-tuple-element.139.refs_4_), channel_id=1, source_target_pairs={{0,1},{1,2},{2,3},{3,0},{4,5},{5,6},{6,7},{7,4},{8,9},{9,10},{10,1... | collective-permute-start | bytes 9224 | tf_op jit(solution)/shard_map/ppermute | solution.py:517
  151.2 4.4 %collective-permute-start.46 = (f32[1,768]{1,0:T(1,128)S(1)}, f32[1,768]{1,0:T(1,128)S(1)}, u32[]{:S(2)}, u32[]{:S(2)}) collective-permute-start(f32[1,768]{1,0:T(1,128)S(1)} %get-tuple-element.139.refs_4_), channel_id=1, source_target_pairs={{0,2},{1,3},{2,0},{3,1},{4,6},{5,7},{6,4},{7,5},{8,10},{9,11},{10,... | collective-permute-start | bytes 9224 | tf_op jit(solution)/shard_map/ppermute | solution.py:517
  151.6 4.0 %collective-permute-start.47 = (f32[1,768]{1,0:T(1,128)S(1)}, f32[1,768]{1,0:T(1,128)S(1)}, u32[]{:S(2)}, u32[]{:S(2)}) collective-permute-start(f32[1,768]{1,0:T(1,128)S(1)} %get-tuple-element.139.refs_4_), channel_id=1, source_target_pairs={{0,3},{1,0},{2,1},{3,2},{4,7},{5,4},{6,5},{7,6},{8,11},{9,8},{10,9... | collective-permute-start | bytes 9224 | tf_op jit(solution)/shard_map/ppermute | solution.py:517
  152.7 3.3 %collective-permute-start.42 = (bf16[192,192]{1,0:T(8,128)(2,1)S(1)}, bf16[192,192]{1,0:T(8,128)(2,1)S(1)}, u32[]{:S(2)}, u32[]{:S(2)}) collective-permute-start(bf16[192,192]{1,0:T(8,128)(2,1)S(1)} %get-tuple-element.126), channel_id=1, source_target_pairs={{0,1},{1,2},{2,3},{3,0},{4,5},{5,6},{6,7},{7,4},{8,9},{9,10},{10,1... | collective-permute-start | bytes 221192 | tf_op jit(solution)/shard_map/ppermute | solution.py:517
  154.0 5.7 %collective-permute-start.43 = (bf16[192,192]{1,0:T(8,128)(2,1)S(1)}, bf16[192,192]{1,0:T(8,128)(2,1)S(1)}, u32[]{:S(2)}, u32[]{:S(2)}) collective-permute-start(bf16[192,192]{1,0:T(8,128)(2,1)S(1)} %get-tuple-element.127), channel_id=1, source_target_pairs={{0,2},{1,3},{2,0},{3,1},{4,6},{5,7},{6,4},{7,5},{8,10},{9,11},{10,... | collective-permute-start | bytes 221192 | tf_op jit(solution)/shard_map/ppermute | solution.py:517
  155.0 5.2 %collective-permute-start.44 = (bf16[192,192]{1,0:T(8,128)(2,1)S(1)}, bf16[192,192]{1,0:T(8,128)(2,1)S(1)}, u32[]{:S(2)}, u32[]{:S(2)}) collective-permute-start(bf16[192,192]{1,0:T(8,128)(2,1)S(1)} %get-tuple-element.128), channel_id=1, source_target_pairs={{0,3},{1,0},{2,1},{3,2},{4,7},{5,4},{6,5},{7,6},{8,11},{9,8},{10,9... | collective-permute-start | bytes 221192 | tf_op jit(solution)/shard_map/ppermute | solution.py:517
  (20 other events, 200.4 us)
Sparse Core Ops, SparseCore 0:
  18.7 48.0 all-gather.4
  69.7 60.4 all-gather.2

commit v5 on v4

--- a/solution.py
+++ b/solution.py
@@ -126,30 +126,21 @@
 
 def route_kernel(
     routes, router, gain, qkv_w, after, dest, gain_col, rw_own, qkv_wt, chunks,
-    *, experts, cap, n_e, direct, n_t,
+    *, experts, cap, n_t,
 ):
     tok = routes.shape[1]
     width = rw_own.shape[1]
-    e = my_place()[1].astype(f32)
     rt = routes[...]
     x_of = iota((experts, tok), 0)
     m0 = (rt[0:1] == x_of).astype(f32)
     m1 = (rt[1:2] == x_of).astype(f32)
     earlier = (iota((tok, tok), 0) < iota((tok, tok), 1)).astype(f32).astype(bf16)
     counts = mm((m0 + m1).astype(bf16), earlier)
-    send, back = [], []
-    for i, m in enumerate((m0, m1)):
-        slot = jnp.sum(m * counts, axis=0, keepdims=True)
-        owner = rt[i:i + 1].astype(f32)
-        if direct:
-            ahead = owner - e
-            behind = e - owner
-            send.append(jnp.where(ahead < 0, ahead + n_e, ahead) * cap + slot)
-            back.append(jnp.where(behind < 0, behind + n_e, behind) * cap + slot)
-        else:
-            send.append(owner * cap + slot)
-            back.append(owner * cap + slot)
-    dest[...] = row_block(send + back, 8)
+    rows = [
+        rt[i:i + 1].astype(f32) * cap + jnp.sum(m * counts, axis=0, keepdims=True)
+        for i, m in enumerate((m0, m1))
+    ]
+    dest[...] = row_block(rows, 8)
     column_of(gain[...], gain_col)
     wide = router[...].astype(f32)
     for s in range(n_t):
@@ -164,7 +155,7 @@
 
 def attention_kernel(
     x0, x1, x2, x3, gain, qkv_w, out_wt, bias,
-    own, p1, p2, p3, h1, inv1, heads, probs, attended,
+    own, p1, p2, p3, inv1, heads, probs, saved,
     xs, parts, *, n_t,
 ):
     width, tok = x0.shape
@@ -173,22 +164,23 @@
     model = n_t * width
     r, _ = my_place()
     for k, x in enumerate((x0, x1, x2, x3)):
-        chunk(xs, lax.rem(r + n_t - k, n_t), width)[...] = x[...].astype(f32)
+        chunk(xs, r ^ k, width)[...] = x[...].astype(f32)
     inverse = lax.rsqrt(jnp.sum(xs[...] * xs[...], axis=0, keepdims=True) / model + epsilon)
     inv1[...] = inverse
-    h1[...] = (xs[...] * inverse * gain[...]).astype(bf16)
-    heads[...] = mm(qkv_w[...], h1[...]).astype(bf16)
+    saved[0:model] = (xs[...] * inverse * gain[...]).astype(bf16)
+    heads[...] = mm(qkv_w[...], saved[0:model]).astype(bf16)
     for h in range(n_heads):
         q, k, v = (heads[j * width + h * size:j * width + (h + 1) * size] for j in range(3))
         scores = mm(k, q, (0, 0)) * (size ** -0.5) + bias[h]
         weights = jnp.exp(scores - jnp.max(scores, axis=0, keepdims=True))
         prob = weights / jnp.sum(weights, axis=0, keepdims=True)
         probs[h] = prob
-        attended[h * size:(h + 1) * size] = mm(v, prob.astype(bf16)).astype(bf16)
-    parts[...] = mm(out_wt[...], attended[...])
+        here = model + h * size
+        saved[here:here + size] = mm(v, prob.astype(bf16)).astype(bf16)
+    parts[...] = mm(out_wt[...], saved[model:])
     own[...] = chunk(parts, r, width)[...]
     for k, p in ((1, p1), (2, p2), (3, p3)):
-        p[...] = chunk(parts, lax.rem(r + k, n_t), width)[...].astype(bf16)
+        p[...] = chunk(parts, r ^ k, width)[...].astype(bf16)
 
 
 def dispatch_kernel(
@@ -238,15 +230,15 @@
 
 def expert_kernel(
     h0, h1, h2, h3, up, down,
-    c0, c1, c2, c3, u, z, de, da,
+    own, across, mate, u, z, de, da,
     hs, gs, chunks, *, n_t,
 ):
-    width = c0.shape[1] // 2
+    width = own.shape[1] // 2
     model = n_t * width
     r, _ = my_place()
     packs = (h0, h1, h2, h3)
     for k, h in enumerate(packs):
-        s = lax.rem(r + n_t - k, n_t)
+        s = r ^ k
         hs[s] = h[:, 0:width].astype(f32)
         gs[s] = h[:, width + 16:].astype(f32)
     stats = h0[:, width:width + 16].astype(f32)
@@ -267,8 +259,11 @@
         cols = slice(s * width, (s + 1) * width)
         chunks[s, :, 0:width] = eo[:, cols]
         chunks[s, :, width:] = du[:, cols]
-    for k, c in enumerate((c0, c1, c2, c3)):
-        c[...] = chunks[lax.rem(r + k, n_t)]
+    rows = own.shape[0]
+    own[...] = chunks[r]
+    across[...] = chunks[r ^ 2]
+    mate[0:rows] = chunks[r ^ 1]
+    mate[rows:] = chunks[r ^ 3]
 
 
 def expert_grad_kernel(u, z, de, da, up_grad, down_grad):
@@ -276,18 +271,21 @@
     down_grad[0] = mm(z[...], de[...], (0, 0))
 
 
-def join_kernel(*refs):
-    pieces, out = refs[:-1], refs[-1]
-    out[...] = jnp.concatenate([p[...].astype(f32) for p in pieces], axis=0).astype(bf16)
-
-
-def expert_sum_kernel(c0, c1, c2, c3, *pieces):
-    total = c0[...].astype(f32) + c1[...].astype(f32) + (c2[...].astype(f32) + c3[...].astype(f32))
-    count = len(pieces)
-    size = total.shape[0] // count
-    for k, piece in enumerate(pieces):
-        j = (count - k) % count
-        piece[...] = total[j * size:(j + 1) * size].astype(bf16)
+def join_kernel(gathered, out, *, n_e):
+    stride, height = gathered.shape[0] // n_e, out.shape[0] // n_e
+    for j in range(n_e):
+        out[j * height:(j + 1) * height] = gathered[(j + 1) * stride - height:(j + 1) * stride]
+
+
+def pair_sum_kernel(across, got, out):
+    rows = across.shape[0]
+    out[...] = (across[...].astype(f32) + got[rows:].astype(f32)).astype(bf16)
+
+
+def expert_sum_kernel(own, got, far, out):
+    rows = own.shape[0]
+    total = own[...].astype(f32) + got[0:rows].astype(f32) + far[...].astype(f32)
+    out[...] = total.astype(bf16)
 
 
 def total_stats(packs, width):
@@ -307,10 +305,10 @@
     pieces, (output, pack) = refs[:-2], refs[-2:]
     width, tok = dy.shape
     _, gate0, gate1 = gates_of(total_stats((t0, t1, t2, t3), width), n_t * width)
-    back = jnp.concatenate([p[...].astype(f32) for p in pieces], axis=0).astype(bf16)
+    back = pieces[0][...]
     row = iota((back.shape[0], tok), 0).astype(f32)
-    pick0 = (row == dest[2:3, :]).astype(f32).astype(bf16)
-    pick1 = (row == dest[3:4, :]).astype(f32).astype(bf16)
+    pick0 = (row == dest[0:1, :]).astype(f32).astype(bf16)
+    pick1 = (row == dest[1:2, :]).astype(f32).astype(bf16)
     got0 = mm(back, pick0, (0, 0))
     got1 = mm(back, pick1, (0, 0))
     e0, e1 = got0[0:width], got1[0:width]
@@ -337,7 +335,7 @@
     r, _ = my_place()
     packs, tokens = (b0, b1, b2, b3), (t0, t1, t2, t3)
     for k in range(n_t):
-        s = lax.rem(r + n_t - k, n_t)
+        s = r ^ k
         chunk(bs, s, width)[...] = packs[k][0:width].astype(f32)
         chunk(ts, s, width)[...] = tokens[k][0:width].astype(f32)
         chunk(ys, s, width)[...] = tokens[k][width + 16:].astype(f32)
@@ -381,30 +379,30 @@
     stats = row_block(split_hi_lo(row_dot)).astype(bf16)
     dr[...] = mm(qkv_wt[...], d_proj[...])
     for k, c in enumerate((c0, c1, c2, c3)):
-        c[0:width] = chunk(dr, lax.rem(r + k, n_t), width)[...].astype(bf16)
+        c[0:width] = chunk(dr, r ^ k, width)[...].astype(bf16)
         c[width:] = stats
 
 
 def small_grad_kernel(
-    t0, t1, t2, t3, d_logits, gain_terms, gain1_row, gain2, h1, d_proj, attended, d_att,
+    t0, t1, t2, t3, d_logits, gain_terms, gain1_row, gain2, saved, d_proj, d_att,
     d_scores, buckets, qkv_w, small, last, ts, padded, *, n_t, n_buckets, direct,
 ):
     packs = (t0, t1, t2, t3)
-    width = attended.shape[0]
+    width = d_proj.shape[0] // 3
     model = n_t * width
     inner = d_proj.shape[0]
     experts = d_logits.shape[0]
     tok = t0.shape[1]
     r, _ = my_place()
     for k, t in enumerate(packs):
-        chunk(ts, lax.rem(r + n_t - k, n_t), width)[...] = t[0:width].astype(f32)
+        chunk(ts, r ^ k, width)[...] = t[0:width].astype(f32)
     inverse, _, _ = gates_of(total_stats(packs, width), model)
     normed = (ts[...] * inverse * gain2[...]).astype(bf16).astype(f32)
     small[0:experts] = mm(d_logits[...], normed, (1, 1), precision=highest)
     ones = jnp.ones((8, tok), f32)
     small[experts:] = jnp.zeros((small.shape[0] - experts, model), f32)
     small[experts:experts + 1] = mm(ones, gain_terms[...], (1, 1), precision=highest)[0:1]
-    grad = mm(d_proj[...], h1[...], (1, 1))
+    grad = mm(d_proj[...], saved[0:model], (1, 1))
     first = jnp.sum(grad * qkv_w[...].astype(f32), axis=0, keepdims=True)
     small[experts + 1:experts + 2] = first / gain1_row[...]
     hot = bucket_hot(buckets, padded, n_buckets)
@@ -421,45 +419,60 @@
             here = inner + width + c * height
             last[here:here + height] = small[:, c * tok:(c + 1) * tok].astype(bf16)
     else:
-        last[...] = mm(attended[...], d_att[...], (1, 1)).astype(last.dtype)
+        last[...] = mm(saved[model:], d_att[...], (1, 1)).astype(last.dtype)
 
 
 def senders(n_e):
     _, e = my_place()
-    other = e + 1 - 2 * lax.rem(e, 2)
     half = n_e // 2
-    return [lax.rem((e, other)[j // half] + n_e - 2 * (j % half), n_e) for j in range(n_e)]
-
-
-def late_sum_kernel(att_all, *refs, n_t, n_e, inner):
-    lasts, (small, own, q1, q2, q3, blocks) = refs[:n_e], refs[n_e:]
-    model = small.shape[1]
-    width = model // n_t
+    return [lax.rem((e ^ (j // half)) + n_e - 2 * (j % half), n_e) for j in range(n_e)]
+
+
+def late_sum_kernel(o0, o1, o2, o3, *refs, n_e, inner):
+    lasts, (small, own, q1, q2, q3) = refs[:n_e], refs[n_e:]
+    width = own.shape[0]
     stride, tok = lasts[0].shape
-    height = small.shape[0]
-    r, _ = my_place()
-    total, grad = 0.0, 0.0
-    for last, sender in zip(lasts, senders(n_e)):
+    height, model = small.shape
+    total = lasts[0][inner + width:].astype(f32)
+    for last in lasts[1:]:
         total += last[inner + width:].astype(f32)
-        grad += mm(chunk(att_all, sender, model)[...], last[inner:inner + width], (1, 1))
     for c in range(model // tok):
         small[:, c * tok:(c + 1) * tok] = total[c * height:(c + 1) * height]
-    for s in range(n_t):
-        blocks[s] = grad[s * width:(s + 1) * width]
-    own[...] = blocks[r]
-    for k, q in ((1, q1), (2, q2), (3, q3)):
-        q[...] = blocks[lax.rem(r + k, n_t)].astype(bf16)
-
-
-def out_grad_kernel(own, q1, q2, q3, f0, f1, f2, f3, out, first, blocks, *, n_t):
+    first = small[height - 7:height - 6]
+    hi, lo = split_hi_lo(first)
+    wide = row_block(
+        [v[:, s * width:(s + 1) * width] for v in (hi, lo) for s in range(model // width)]
+    )
+    for o, q in ((o0, own), (o1, q1), (o2, q2), (o3, q3)):
+        grad = 0.0
+        for last, sender in zip(lasts, senders(n_e)):
+            grad += mm(chunk(o, sender, width)[...], last[inner:inner + width], (1, 1))
+        q[0:width] = grad.astype(q.dtype)
+        if q is not own:
+            q[width:] = wide.astype(bf16)
+
+
+def out_grad_kernel(
+    own, q1, q2, q3, small, out, first, second, router, rel, blocks, line, *, n_t
+):
     width = own.shape[0]
+    experts, buckets = router.shape[0], rel.shape[1]
     r, _ = my_place()
     blocks[r] = own[...]
     for k, q in ((1, q1), (2, q2), (3, q3)):
-        blocks[lax.rem(r + n_t - k, n_t)] = q[...].astype(f32)
+        blocks[r ^ k] = q[0:width].astype(f32)
     for s in range(n_t):
-        out[:, s * width:(s + 1) * width] = blocks[s]
-    first[...] = f0[...] + f1[...] + (f2[...] + f3[...])
+        cols = slice(s * width, (s + 1) * width)
+        out[:, cols] = blocks[s]
+        total = small[experts + 1:experts + 2, cols]
+        for q in (q1, q2, q3):
+            parts = q[width:].astype(f32)
+            total += parts[s:s + 1] + parts[n_t + s:n_t + s + 1]
+        line[:, cols] = total
+    first[...] = line[0]
+    second[...] = small[experts]
+    router[...] = small[0:experts]
+    rel[...] = small[experts + 2:experts + 2 + rel.shape[0], 0:buckets]
 
 
 def input_grad_kernel(c0, c1, c2, c3, dr1, inv1, x, gain, out, *, n_t):
@@ -471,15 +484,16 @@
     out[...] = dr1[...] + inverse * weighted - x[...].astype(f32) * (inverse * inverse * row_dot)
 
 
-def qkv_grad_kernel(h1_all, *refs):
-    lasts, out = refs[:-1], refs[-1]
-    inner, model = out.shape
-    if len(lasts) == 1:
-        out[...] = mm(lasts[0][0:inner], h1_all[...], (1, 1))
-        return
-    total = 0.0
-    for last, sender in zip(lasts, senders(len(lasts))):
-        total += mm(last[0:inner], chunk(h1_all, sender, model)[...], (1, 1))
+def qkv_grad_kernel(gathered, *refs, pieces, n_e, inner):
+    lasts, rest = refs[:len(pieces)], refs[len(pieces):]
+    out = rest[-1]
+    model = out.shape[1]
+    stride = gathered.shape[0] // n_e
+    total = 0.0 if len(rest) == 1 else rest[0][...]
+    for j, last in zip(pieces, lasts):
+        sender = senders(n_e)[j] if n_e > 1 else 0
+        h1 = chunk(gathered, sender, stride)[...][0:model]
+        total += mm(last[0:inner], h1, (1, 1))
     out[...] = total
 
 
@@ -509,36 +523,33 @@
     rows = experts * cap
     n_heads = rel_table.shape[1]
     n_buckets = rel_table.shape[0]
-    direct = n_e == 8 and cap % 8 == 0
-    n_pieces = n_e if direct else 1
+    direct = n_e == 8
     padded = pltpu.VMEM((1, tok), i32)
 
-    def shift(v, k, axis="tensor", n=n_t):
-        return lax.ppermute(v, axis, [(i, (i + k) % n) for i in range(n)])
+    def swap(v, k, axis="tensor", n=n_t):
+        return lax.ppermute(v, axis, [(i, i ^ k) for i in range(n)])
 
     def around(v):
-        return [v] + [shift(v, k) for k in range(1, n_t)]
-
-    def gather(v, axes):
-        return lax.all_gather(v, axes, axis=0, tiled=True)
-
-    def exchange(pieces):
-        if direct:
-            return list(pieces[:1]) + [
-                shift(p, k, "expert", n_e) for k, p in enumerate(pieces) if k
-            ]
-        w = pieces[0].shape[-1]
-        v = pieces[0].reshape(n_e, rows // n_e, w)
+        return [v] + [swap(v, k) for k in range(1, n_t)]
+
+    def around_large(v):
+        far = swap(v, 2)
+        return [v, swap(v, 1), far, swap(far, 1)]
+
+    def exchange(v):
+        w = v.shape[-1]
+        v = v.reshape(n_e, rows // n_e, w)
         v = lax.all_to_all(v, "expert", split_axis=0, concat_axis=0, tiled=True)
-        return [v.reshape(rows, w)]
-
-    def join(pieces):
-        if len(pieces) == 1:
-            return pieces[0]
-        return run(join_kernel, [((rows, pieces[0].shape[1]), bf16)], *pieces)[0]
-
-    def piece_shapes(w):
-        return [((rows // n_pieces, w), bf16)] * n_pieces
+        return v.reshape(rows, w)
+
+    def over_pairs(v):
+        return [
+            lax.ppermute(v, "expert", [(i, (i + 2 * k) % n_e) for i in range(n_e)])
+            for k in range(1, n_e // 2)
+        ]
+
+    def after(values, *others):
+        return list(lax.optimization_barrier((tuple(values), others))[0])
 
     x = tokens.T
     dy = cotangent.T
@@ -558,26 +569,25 @@
         fetch=(0, 1, 2, 3, 4),
         scratch=[padded],
     )
-    own, p1, p2, p3, h1, inv1, heads, probs, attended = run(
+    own, p1, p2, p3, inv1, heads, probs, saved = run(
         functools.partial(attention_kernel, n_t=n_t),
         [((width, tok), f32)]
         + [((width, tok), bf16)] * 3
         + [
-            ((model, tok), bf16),
             ((1, tok), f32),
             ((inner, tok), bf16),
             ((n_heads, tok, tok), f32),
-            ((width, tok), bf16),
+            ((model + width, tok), bf16),
         ],
         *xs, gain1, qkv_w, out_wt, bias,
         fetch=(n_t + 1,),
         scratch=[pltpu.VMEM((model, tok), f32), pltpu.VMEM((model, tok), f32)],
     )
-    got = [shift(p, k) for k, p in ((1, p1), (2, p2), (3, p3))]
+    got = [swap(p, k) for k, p in ((1, p1), (2, p2), (3, p3))]
+    if direct:
+        saved_all = lax.all_gather(saved, "expert", axis=0, tiled=True)
     dest, gain2, rw_own, qkv_wt = run(
-        functools.partial(
-            route_kernel, experts=experts, cap=cap, n_e=n_e, direct=direct, n_t=n_t
-        ),
+        functools.partial(route_kernel, experts=experts, cap=cap, n_t=n_t),
         [
             ((8, tok), f32),
             ((model, 1), f32),
@@ -588,22 +598,25 @@
         fetch=(0, 1, 2, 3),
         scratch=[pltpu.VMEM((n_t, experts, width), f32)],
     )
-    if direct:
-        h1_all = gather(h1, "expert")
-        att_all = gather(attended, ("expert", "tensor"))
-    *row_pieces, token_pack, residual = run(
+    send_rows, token_pack, residual = run(
         dispatch_kernel,
-        piece_shapes(2 * width + 16) + [((2 * width + 16, tok), bf16), ((width, tok), f32)],
+        [
+            ((rows, 2 * width + 16), bf16),
+            ((2 * width + 16, tok), bf16),
+            ((width, tok), f32),
+        ],
         own, *got, x, dy, gain2, rw_own, routes_t, dest,
         fetch=(4, 5, 8),
         scratch=[pltpu.VMEM((2 * width + 16, tok), bf16)],
     )
-    in_rows = around(join(exchange(row_pieces)))
-    token_packs = around(token_pack)
-
-    c0, c1, c2, c3, u, z, de, da = run(
+    in_rows = around_large(exchange(send_rows))
+    token_packs = around(after([token_pack], in_rows[1])[0])
+
+    own, across, mate, u, z, de, da = run(
         functools.partial(expert_kernel, n_t=n_t),
-        [((rows, 2 * width), bf16)] * 4 + [((rows, model), bf16)] * 4,
+        [((rows, 2 * width), bf16)] * 2
+        + [((2 * rows, 2 * width), bf16)]
+        + [((rows, model), bf16)] * 4,
         *in_rows, up_weight, down_weight,
         fetch=(4, 5),
         scratch=[
@@ -612,17 +625,21 @@
             pltpu.VMEM((n_t, rows, 2 * width), bf16),
         ],
     )
-    got = [shift(c, k) for k, c in ((1, c1), (2, c2), (3, c3))]
+    got = swap(mate, 1)
+    (across,) = run(pair_sum_kernel, [((rows, 2 * width), bf16)], across, got)
+    far = swap(across, 2)
     up_grad, down_grad = run(
         expert_grad_kernel,
         [(up_weight.shape, f32), (down_weight.shape, f32)],
-        u, z, de, da,
-    )
-    back = exchange(run(expert_sum_kernel, piece_shapes(2 * width), c0, *got))
+        *after([u, z, de, da], across),
+    )
+    (far,) = after([far], up_grad, *token_packs[1:])
+    (summed,) = run(expert_sum_kernel, [((rows, 2 * width), bf16)], own, got, far)
+    back = exchange(summed)
     output, back_pack = run(
         functools.partial(combine_kernel, n_t=n_t),
         [((width, tok), bf16), ((width + 16, tok), bf16)],
-        *token_packs, dest, dy, residual, *back,
+        *token_packs, dest, dy, residual, back,
         fetch=(5,),
     )
     back_packs = around(back_pack)
@@ -642,7 +659,6 @@
         fetch=(8, 9, 11),
         scratch=[pltpu.VMEM((model, tok), f32)] * 4,
     )
-    got = [shift(c, k) for k, c in ((1, c1), (2, c2), (3, c3))]
     height = experts + 8
     if direct:
         last_shape = (inner + width + height * (model // tok), tok)
@@ -651,11 +667,14 @@
     small, last = run(
         functools.partial(small_grad_kernel, n_t=n_t, n_buckets=n_buckets, direct=direct),
         [((height, model), f32), (last_shape, bf16)],
-        *token_packs, d_logits, gain_terms, gain1_row, gain2, h1, d_proj, attended, d_att,
+        *token_packs, d_logits, gain_terms, gain1_row, gain2, saved, d_proj, d_att,
         d_scores, buckets, qkv_w,
-        fetch=(6, 13, 14),
+        fetch=(6, 12, 13),
         scratch=[pltpu.VMEM((model, tok), f32), padded],
     )
+    if direct:
+        lasts = [last] + over_pairs(last)
+    got = [swap(c, k) for k, c in ((1, c1), (2, c2), (3, c3))]
     (input_grad,) = run(
         functools.partial(input_grad_kernel, n_t=n_t),
         [((width, tok), f32)],
@@ -663,39 +682,66 @@
         fetch=(6,),
     )
     if direct:
-        lasts = [last] + [shift(last, 2 * k, "expert", n_e) for k in range(1, n_e // 2)]
-        lasts = lasts + [
-            lax.ppermute(v, "expert", [(i, i ^ 1) for i in range(n_e)]) for v in lasts
-        ]
+        (att,) = run(
+            functools.partial(join_kernel, n_e=n_e),
+            [((n_e * width, tok), bf16)],
+            *after([saved_all], last),
+        )
+        atts = around_large(att)
+        half = n_e // 2
+        (part,) = run(
+            functools.partial(qkv_grad_kernel, pieces=range(half), n_e=n_e, inner=inner),
+            [((inner, model), f32)],
+            saved_all, *lasts,
+        )
+        lasts = lasts + [swap(v, 1, "expert", n_e) for v in lasts]
+        lasts[half:] = after(lasts[half:], part, input_grad)
         small, own, q1, q2, q3 = run(
-            functools.partial(late_sum_kernel, n_t=n_t, n_e=n_e, inner=inner),
-            [((height, model), f32), ((width, width), f32)] + [((width, width), bf16)] * 3,
-            att_all, *lasts,
-            scratch=[pltpu.VMEM((n_t, width, width), f32)],
+            functools.partial(late_sum_kernel, n_e=n_e, inner=inner),
+            [((height, model), f32), ((width, width), f32)]
+            + [((width + 16, width), bf16)] * 3,
+            *atts, *lasts,
         )
-        firsts = around(small[experts + 1:experts + 2])
-        got = [shift(q, k) for k, q in ((1, q1), (2, q2), (3, q3))]
-        (qkv_grad,) = run(qkv_grad_kernel, [((inner, model), f32)], h1_all, *lasts)
-        out_grad, first = run(
+        got = [swap(q, k) for k, q in ((1, q1), (2, q2), (3, q3))]
+        (part,) = after([part], own)
+        (qkv_grad,) = run(
+            functools.partial(qkv_grad_kernel, pieces=range(half, n_e), n_e=n_e, inner=inner),
+            [((inner, model), f32)],
+            saved_all, *lasts[half:], part,
+        )
+        out_grad, first, second, router_grad, rel_grad = run(
             functools.partial(out_grad_kernel, n_t=n_t),
-            [(out_weight.shape, f32), ((1, model), f32)],
-            own, *got, *firsts,
-            scratch=[pltpu.VMEM((n_t, width, width), f32)],
+            [
+                (out_weight.shape, f32),
+                ((model,), f32),
+                ((model,), f32),
+                ((experts, model), f32),
+                ((n_heads, n_buckets), f32),
+            ],
+            own, *got, small,
+            scratch=[pltpu.VMEM((n_t, width, width), f32), pltpu.VMEM((1, model), f32)],
         )
     else:
         small, out_grad = lax.psum((small, last.astype(f32)), "expert")
-        (qkv_grad,) = run(qkv_grad_kernel, [((inner, model), f32)], h1, d_proj)
+        (qkv_grad,) = run(
+            functools.partial(qkv_grad_kernel, pieces=range(1), n_e=1, inner=inner),
+            [((inner, model), f32)],
+            saved, d_proj,
+        )
         qkv_grad = lax.psum(qkv_grad, "expert")
         first = lax.psum(small[experts + 1], "tensor")
+        second = small[experts]
+        router_grad = small[:experts]
+        rel_grad = small[experts + 2:experts + 2 + n_heads, :n_buckets]
     return (
         output.T,
         input_grad.T,
         first.reshape(model),
-        small[experts].reshape(model),
+        second.reshape(model),
         qkv_grad.reshape(3, width, model).transpose(0, 2, 1),
         out_grad,
-        small[experts + 2:experts + 2 + n_heads, :n_buckets].T,
-        small[:experts].T,
+        rel_grad.T,
+        router_grad.T,
         up_grad,
         down_grad,
     )

time: 169 us -> 159 us (0.941)
  the two profiles are of different devices: /device:TPU:9 before, /device:TPU:0 now
where the time goes in v5:
time: 159 us
  waiting for transfers between devices  52.9 us (33%)
  blocking collectives  34.9 us (22%)
  starting transfers between devices  25.6 us (16%)
  Pallas kernels  23.9 us (15%)
  between operations  14.3 us (9%)
  local copies, waits for them, and re-layouts  7.19 us (5%)
    ppermute x30, waiting for transfers between devices, swap(): return lax.ppermute(v, axis, [(i, i ^ k) for i in range(n)])  40.2 us
    all_to_all x2, blocking collectives, exchange(): v = lax.all_to_all(v, 'expert', split_axis=0, concat_axis=0, tiled=True)  34.9 us
    pallas_call x17, Pallas kernels, run(): pl.pallas_call(whole, out_shape=[jax.ShapeDtypeStruct(s, d) for s, d in o...  23.9 us
    ppermute x30, starting transfers between devices, swap(): return lax.ppermute(v, axis, [(i, i ^ k) for i in range(n)])  22.6 us
    ppermute x3, waiting for transfers between devices, over_pairs(): lax.ppermute(v, 'expert', [(i, (i + 2 * k) % n_e) for i in range(n_e)])  12.7 us
    unnamed x36, local copies, waits for them, and re-layouts  6.5 us
  transfers between devices with their start and end apart: 34, of which 15 were waited for; matrix products, arithmetic and copies ran while one was open for 0% of the time, Pallas kernels for 12%

profile of v5, /device:TPU:0, one launch (start us, length us, event | category | flops | bytes accessed | tf_op | source)
XLA Modules:
  0.0 158.8 jit_solution(18355153382716068969)
XLA Ops:
  7.2 2.5 %collective-permute-start.2 = (bf16[192,128]{1,0:T(8,128)(2,1)}, bf16[192,128]{1,0:T(8,128)(2,1)S(1)}, u32[]{:S(2)}, u32[]{:S(2)}) collective-permute-start(bf16[192,128]{1,0:T(8,128)(2,1)} %bitcast.28), channel_id=1, source_target_pairs={{0,3},{1,2},{2,1},{3,0},{4,7},{5,6},{6,5},{7,4},{8,11},{9,10},{10,... | collective-permute-start | bytes 147464 | tf_op jit(solution)/shard_map/ppermute | solution.py:530
  11.1 1.0 copy-done.4
  14.0 0.9 shard_map.204
  15.0 1.2 copy-done.2
  16.2 0.8 copy-done.8
  17.0 2.5 %shard_map.205 = (f32[192,128]{1,0:T(8,128)S(1)}, bf16[192,128]{1,0:T(8,128)(2,1)S(1)}, bf16[192,128]{1,0:T(8,128)(2,1)S(1)}, bf16[192,128]{1,0:T(8,128)(2,1)S(1...) custom-call(bf16[192,128]{1,0:T(8,128)(2,1)S(1)} %bitcast.31, ...), custom_call_target="tpu_custom_call" | custom-call | bytes 2412032 | tf_op jit(solution)/shard_map/pallas_call | solution.py:67
  20.0 1.4 collective-permute-start.4
  22.2 1.9 %collective-permute-done.4.refs_2_ = bf16[192,128]{1,0:T(8,128)(2,1)S(1)} collective-permute-done((bf16[192,128]{1,0:T(8,128)(2,1)S(1)}, bf16[192,128]{1,0:T(8,128)(2,1)S(1)}, u32[]{:S(2)}, u32[]{:S(2)}) %collective-permute-start.4) | collective-permute-done | bytes 49184 | tf_op jit(solution)/shard_map/ppermute | solution.py:530
  24.1 1.0 collective-permute-done.5.refs_3_
  25.8 22.7 %all_to_all.10 = bf16[8,40,400]{2,1,0:T(8,128)(2,1)S(1)} all-to-all(bf16[8,40,400]{2,1,0:T(8,128)(2,1)S(1)} %bitcast.34), channel_id=1, replica_groups=mesh['expert'=8,'tensor'=4] {'expert'}, dimensions={0} | all-to-all | bytes 512000 | tf_op jit(solution)/shard_map/all_to_all | solution.py:542
  48.5 1.4 collective-permute-start.10
  49.9 6.8 %collective-permute-done.10.refs_2_ = bf16[320,400]{1,0:T(8,128)(2,1)S(1)} collective-permute-done((bf16[320,400]{1,0:T(8,128)(2,1)S(1)}, bf16[320,400]{1,0:T(8,128)(2,1)S(1)}, u32[]{:S(2)}, u32[]{:S(2)}) %collective-permute-start.10) | collective-permute-done | bytes 256032 | tf_op jit(solution)/shard_map/ppermute | solution.py:530
  56.7 1.6 %collective-permute-done.11.refs_3_ = bf16[320,400]{1,0:T(8,128)(2,1)S(1)} collective-permute-done((bf16[320,400]{1,0:T(8,128)(2,1)S(1)}, bf16[320,400]{1,0:T(8,128)(2,1)S(1)}, u32[]{:S(2)}, u32[]{:S(2)}) %collective-permute-start.11) | collective-permute-done | bytes 256032 | tf_op jit(solution)/shard_map/ppermute | solution.py:530
  58.4 3.0 %shard_map.208 = (bf16[320,384]{1,0:T(8,128)(2,1)S(1)}, bf16[320,384]{1,0:T(8,128)(2,1)S(1)}, bf16[640,384]{1,0:T(8,128)(2,1)S(1)}, bf16[320,768]{1,0:T(8,128)(2...) custom-call(bf16[320,400]{1,0:T(8,128)(2,1)S(1)} %bitcast.25, ...), custom_call_target="tpu_custom_call" | custom-call | bytes 6332416 | tf_op jit(solution)/shard_map/pallas_call | solution.py:67
  61.5 1.7 %collective-permute-done.12.refs_1_ = bf16[640,384]{1,0:T(8,128)(2,1)S(1)} collective-permute-done((bf16[640,384]{1,0:T(8,128)(2,1)S(1)}, bf16[640,384]{1,0:T(8,128)(2,1)S(1)}, u32[]{:S(2)}, u32[]{:S(2)}) %collective-permute-start.12) | collective-permute-done | bytes 491552 | tf_op jit(solution)/shard_map/ppermute | solution.py:530
  63.3 1.7 %collective-permute-start.13 = (bf16[320,384]{1,0:T(8,128)(2,1)S(1)}, bf16[320,384]{1,0:T(8,128)(2,1)S(1)}, u32[]{:S(2)}, u32[]{:S(2)}) collective-permute-start(bf16[320,384]{1,0:T(8,128)(2,1)S(1)} %shard_map.209), channel_id=1, source_target_pairs={{0,2},{1,3},{2,0},{3,1},{4,6},{5,7},{6,4},{7,5},{8,10},{9,11},{10,... | collective-permute-start | bytes 737288 | tf_op jit(solution)/shard_map/ppermute | solution.py:530
  65.1 1.5 collective-permute-start.8
  66.9 3.2 %shard_map.210 = (f32[1,768,768]{2,1,0:T(8,128)}, f32[1,768,768]{2,1,0:T(8,128)}) custom-call(bf16[320,768]{1,0:T(8,128)(2,1)S(1)} %get-tuple-element.94.refs_0_, bf16[320,768]{1,0:T(8,128)(2,1)S(1)} %get-tuple-element.95.refs_1_, bf16[320,768]{1,0:T(8,128)(2,1)S(1)} %get-tuple-element.96.refs_2_, bf16[320,768]{1,0:T(8,128)(2,1)S(1)} %get-tuple-element.97.refs_3_), custom_call_target="tpu_custom_call" | custom-call | bytes 6684672 | tf_op jit(solution)/shard_map/pallas_call | solution.py:67
  70.1 3.5 %collective-permute-done.9.refs_3_.refs_7_ = bf16[400,128]{1,0:T(8,128)(2,1)S(1)} collective-permute-done((bf16[400,128]{1,0:T(8,128)(2,1)S(1)}, bf16[400,128]{1,0:T(8,128)(2,1)S(1)}, u32[]{:S(2)}, u32[]{:S(2)}) %collective-permute-start.9) | collective-permute-done | bytes 102432 | tf_op jit(solution)/shard_map/ppermute | solution.py:530
  73.6 2.2 %collective-permute-done.8.refs_2_.refs_6_ = bf16[400,128]{1,0:T(8,128)(2,1)S(1)} collective-permute-done((bf16[400,128]{1,0:T(8,128)(2,1)S(1)}, bf16[400,128]{1,0:T(8,128)(2,1)S(1)}, u32[]{:S(2)}, u32[]{:S(2)}) %collective-permute-start.8) | collective-permute-done | bytes 102432 | tf_op jit(solution)/shard_map/ppermute | solution.py:530
  75.9 12.3 %all_to_all.11 = bf16[8,40,384]{2,1,0:T(8,128)(2,1)S(1)} all-to-all(bf16[8,40,384]{2,1,0:T(8,128)(2,1)S(1)} %bitcast.26), channel_id=1, replica_groups=mesh['expert'=8,'tensor'=4] {'expert'}, dimensions={0} | all-to-all | bytes 491520 | tf_op jit(solution)/shard_map/all_to_all | solution.py:542
  88.2 1.0 shard_map.212
  89.3 1.5 collective-permute-start.15
  91.1 2.3 %collective-permute-done.16.refs_3_ = bf16[208,128]{1,0:T(8,128)(2,1)S(1)} collective-permute-done((bf16[208,128]{1,0:T(8,128)(2,1)S(1)}, bf16[208,128]{1,0:T(8,128)(2,1)S(1)}, u32[]{:S(2)}, u32[]{:S(2)}) %collective-permute-start.16) | collective-permute-done | bytes 53280 | tf_op jit(solution)/shard_map/ppermute | solution.py:530
  93.4 1.1 collective-permute-done.15.refs_2_
  94.5 2.6 %shard_map.213 = (bf16[208,128]{1,0:T(8,128)(2,1)S(1)}, bf16[208,128]{1,0:T(8,128)(2,1)S(1)}, bf16[208,128]{1,0:T(8,128)(2,1)S(1)}, bf16[208,128]{1,0:T(8,128)(2...) custom-call(bf16[208,128]{1,0:T(8,128)(2,1)S(1)} %get-tuple-element., ...), custom_call_target="tpu_custom_call" | custom-call | bytes 3313664 | tf_op jit(solution)/shard_map/pallas_call | solution.py:67
  97.0 3.0 %shard_map.215 = (f32[16,768]{1,0:T(8,128)}, bf16[864,128]{1,0:T(8,128)(2,1)S(1)}) custom-call(bf16[400,128]{1,0:T(8,128)(2,1)S(1)} %get-tuple-element.85.refs_0_.refs_4_, bf16[400,128]{1,0:T(8,128)(2,1)S(1)} %collective-permute-done.7.refs_1_.refs_5_, bf16[400,128]{1,0:T(8,128)(2,1)S(1)} %collective-permute-done.8.refs_2_.refs_6_, ...), custom_call_target="tpu_custom_call" | custom-call | bytes 2656704 | tf_op jit(solution)/shard_map/pallas_call | solution.py:67
  100.1 1.5 copy-done
  101.6 1.0 collective-permute-start.21
  102.6 1.3 collective-permute-start.26
  103.9 1.1 collective-permute-start.18
  105.8 1.4 collective-permute-start.25
  107.2 7.3 %collective-permute-done.18.refs_2_ = bf16[208,128]{1,0:T(8,128)(2,1)S(1)} collective-permute-done((bf16[208,128]{1,0:T(8,128)(2,1)S(1)}, bf16[208,128]{1,0:T(8,128)(2,1)S(1)}, u32[]{:S(2)}, u32[]{:S(2)}) %collective-permute-start.18) | collective-permute-done | bytes 53280 | tf_op jit(solution)/shard_map/ppermute | solution.py:530
  114.5 0.9 collective-permute-start.24
  116.6 1.7 %collective-permute-start.29 = (bf16[864,128]{1,0:T(8,128)(2,1)S(1)}, bf16[864,128]{1,0:T(8,128)(2,1)S(1)}, u32[]{:S(2)}, u32[]{:S(2)}) collective-permute-start(bf16[864,128]{1,0:T(8,128)(2,1)S(1)} %collective-permute-done.25.refs_4_.refs_7_), channel_id=1, source_target_pairs={{0,4},{4,0},{8,12},{12,8},{16,20},{20,16},{24,28},{28,24},{1,5},{5... | collective-permute-start | bytes 663560 | tf_op jit(solution)/shard_map/ppermute | solution.py:530
  118.3 12.7 %collective-permute-done.24.refs_3_.refs_6_ = bf16[864,128]{1,0:T(8,128)(2,1)S(1)} collective-permute-done((bf16[864,128]{1,0:T(8,128)(2,1)S(1)}, bf16[864,128]{1,0:T(8,128)(2,1)S(1)}, u32[]{:S(2)}, u32[]{:S(2)}) %collective-permute-start.24) | collective-permute-done | bytes 221216 | tf_op jit(solution)/shard_map/ppermute | solution.py:547
  131.0 0.8 collective-permute-start.28
  131.8 1.2 collective-permute-start.27
  133.8 1.1 shard_map.217.refs_5_
  134.9 4.4 %collective-permute-done.28.refs_10_.refs_3_ = bf16[864,128]{1,0:T(8,128)(2,1)S(1)} collective-permute-done((bf16[864,128]{1,0:T(8,128)(2,1)S(1)}, bf16[864,128]{1,0:T(8,128)(2,1)S(1)}, u32[]{:S(2)}, u32[]{:S(2)}) %collective-permute-start.28) | collective-permute-done | bytes 221216 | tf_op jit(solution)/shard_map/ppermute | solution.py:530
  139.3 3.3 %collective-permute-done.27.refs_9_.refs_2_ = bf16[864,128]{1,0:T(8,128)(2,1)S(1)} collective-permute-done((bf16[864,128]{1,0:T(8,128)(2,1)S(1)}, bf16[864,128]{1,0:T(8,128)(2,1)S(1)}, u32[]{:S(2)}, u32[]{:S(2)}) %collective-permute-start.27) | collective-permute-done | bytes 221216 | tf_op jit(solution)/shard_map/ppermute | solution.py:530
  142.6 1.0 shard_map.218
  143.7 0.9 collective-permute-start.31
  144.6 1.0 collective-permute-start.32
  145.6 2.3 %shard_map.220 = f32[576,768]{1,0:T(8,128)} custom-call(bf16[7680,128]{1,0:T(8,128)(2,1)S(1)} %copy-done.1, bf16[864,128]{1,0:T(8,128)(2,1)S(1)} %collective-permute-done.26.refs_8_.refs_1_, bf16[864,128]{1,0:T(8,128)(2,1)S(1)} %collective-permute-done.27.refs_9_.refs_2_, bf16[864,128]{1,0:T(8,128)(2,1)S(1)} %collective-permute-done.28.refs_10_.refs_3_, ...), custom_call_target="tpu_custom_call" | custom-call | bytes 6389760 | tf_op jit(solution)/shard_map/pallas_call | solution.py:67
  147.9 1.7 %collective-permute-done.31.refs_2_ = bf16[208,192]{1,0:T(8,128)(2,1)S(1)} collective-permute-done((bf16[208,192]{1,0:T(8,128)(2,1)S(1)}, bf16[208,192]{1,0:T(8,128)(2,1)S(1)}, u32[]{:S(2)}, u32[]{:S(2)}) %collective-permute-start.31) | collective-permute-done | bytes 79904 | tf_op jit(solution)/shard_map/ppermute | solution.py:530
  149.5 1.4 collective-permute-done.32.refs_3_
  150.9 1.1 shard_map.219
  (78 shorter events, 9.5 us)
Async XLA Ops:
  7.2 14.3 %copy-start.11 = (bf16[768,8]{0,1:T(8,128)(2,1)S(1)}, bf16[768,8]{0,1:T(8,128)(2,1)}, u32[]{:S(2)}) copy-start(bf16[768,8]{0,1:T(8,128)(2,1)} %param.19) | copy-start | bytes 36868
  7.2 92.8 %all-gather.2.cloned.1.call-start = ((), (), s32[]{:S(2)}) async-start(), calls=%async_computation.2 | async-start | bytes 2211840 | tf_op jit(solution)/shard_map/all_gather | solution.py:588
  7.2 7.7 %collective-permute-start.2 = (bf16[192,128]{1,0:T(8,128)(2,1)}, bf16[192,128]{1,0:T(8,128)(2,1)S(1)}, u32[]{:S(2)}, u32[]{:S(2)}) collective-permute-start(bf16[192,128]{1,0:T(8,128)(2,1)} %bitcast.28), channel_id=1, source_target_pairs={{0,3},{1,2},{2,1},{3,0},{4,7},{5,6},{6,5},{7,4},{8,11},{9,10},{10,... | collective-permute-start | bytes 147464 | tf_op jit(solution)/shard_map/ppermute | solution.py:530
  9.7 5.3 %collective-permute-start.1 = (bf16[192,128]{1,0:T(8,128)(2,1)}, bf16[192,128]{1,0:T(8,128)(2,1)S(1)}, u32[]{:S(2)}, u32[]{:S(2)}) collective-permute-start(bf16[192,128]{1,0:T(8,128)(2,1)} %bitcast.29), channel_id=1, source_target_pairs={{0,2},{1,3},{2,0},{3,1},{4,6},{5,7},{6,4},{7,5},{8,10},{9,11},{10,... | collective-permute-start | bytes 147464 | tf_op jit(solution)/shard_map/ppermute | solution.py:530
  10.3 4.6 %collective-permute-start = (bf16[192,128]{1,0:T(8,128)(2,1)}, bf16[192,128]{1,0:T(8,128)(2,1)S(1)}, u32[]{:S(2)}, u32[]{:S(2)}) collective-permute-start(bf16[192,128]{1,0:T(8,128)(2,1)} %bitcast.30), channel_id=1, source_target_pairs={{0,1},{1,0},{2,3},{3,2},{4,5},{5,4},{6,7},{7,6},{8,9},{9,8},{10,11... | collective-permute-start | bytes 147464 | tf_op jit(solution)/shard_map/ppermute | solution.py:530
  11.1 1.0 copy-start.4
  14.0 7.4 %copy-start.17 = (f32[768]{0:T(1024)S(1)}, f32[768]{0:T(1024)}, u32[]{:S(2)}) copy-start(f32[768]{0:T(1024)} %param.15) | copy-start | bytes 9220
  14.0 7.4 %copy-start.12 = (s32[128,2]{0,1:T(2,128)S(1)}, s32[128,2]{0,1:T(2,128)}, u32[]{:S(2)}) copy-start(s32[128,2]{0,1:T(2,128)} %param.22) | copy-start | bytes 3076
  14.0 11.1 %copy-start.9 = (bf16[128,192]{0,1:T(8,128)(2,1)S(1)}, bf16[128,192]{0,1:T(8,128)(2,1)}, u32[]{:S(2)}) copy-start(bf16[128,192]{0,1:T(8,128)(2,1)} %param.13) | copy-start | bytes 147460
  14.0 11.1 %copy-start.10 = (bf16[128,192]{0,1:T(8,128)(2,1)S(1)}, bf16[128,192]{0,1:T(8,128)(2,1)}, u32[]{:S(2)}) copy-start(bf16[128,192]{0,1:T(8,128)(2,1)} %param.25) | copy-start | bytes 147460
  15.0 1.2 copy-start.2
  17.0 4.5 %copy-start.3 = (bf16[3,768,192]{1,2,0:T(8,128)(2,1)S(1)}, bf16[3,768,192]{1,2,0:T(8,128)(2,1)}, u32[]{:S(2)}) copy-start(bf16[3,768,192]{1,2,0:T(8,128)(2,1)} %param.16) | copy-start | bytes 2654212
  19.4 38.9 %copy-start.6 = (bf16[1,768,768]{2,1,0:T(8,128)(2,1)S(1)}, bf16[1,768,768]{2,1,0:T(8,128)(2,1)}, u32[]{:S(2)}) copy-start(bf16[1,768,768]{2,1,0:T(8,128)(2,1)} %refs_4_.1) | copy-start | bytes 3538948
  19.5 38.9 %copy-start.7 = (bf16[1,768,768]{2,1,0:T(8,128)(2,1)S(1)}, bf16[1,768,768]{2,1,0:T(8,128)(2,1)}, u32[]{:S(2)}) copy-start(bf16[1,768,768]{2,1,0:T(8,128)(2,1)} %refs_5_.1) | copy-start | bytes 3538948
  19.5 2.7 %collective-permute-start.3 = (bf16[192,128]{1,0:T(8,128)(2,1)S(1)}, bf16[192,128]{1,0:T(8,128)(2,1)S(1)}, u32[]{:S(2)}, u32[]{:S(2)}) collective-permute-start(bf16[192,128]{1,0:T(8,128)(2,1)S(1)} %get-tuple-element.76), channel_id=1, source_target_pairs={{0,1},{1,0},{2,3},{3,2},{4,5},{5,4},{6,7},{7,6},{8,9},{9,8},{10,11... | collective-permute-start | bytes 147464 | tf_op jit(solution)/shard_map/ppermute | solution.py:530
  20.0 4.1 %collective-permute-start.4 = (bf16[192,128]{1,0:T(8,128)(2,1)S(1)}, bf16[192,128]{1,0:T(8,128)(2,1)S(1)}, u32[]{:S(2)}, u32[]{:S(2)}) collective-permute-start(bf16[192,128]{1,0:T(8,128)(2,1)S(1)} %get-tuple-element.77), channel_id=1, source_target_pairs={{0,2},{1,3},{2,0},{3,1},{4,6},{5,7},{6,4},{7,5},{8,10},{9,11},{10,... | collective-permute-start | bytes 147464 | tf_op jit(solution)/shard_map/ppermute | solution.py:530
  21.4 3.7 %collective-permute-start.5 = (bf16[192,128]{1,0:T(8,128)(2,1)S(1)}, bf16[192,128]{1,0:T(8,128)(2,1)S(1)}, u32[]{:S(2)}, u32[]{:S(2)}) collective-permute-start(bf16[192,128]{1,0:T(8,128)(2,1)S(1)} %get-tuple-element.78), channel_id=1, source_target_pairs={{0,3},{1,2},{2,1},{3,0},{4,7},{5,6},{6,5},{7,4},{8,11},{9,10},{10,... | collective-permute-start | bytes 147464 | tf_op jit(solution)/shard_map/ppermute | solution.py:530
  48.5 8.2 %collective-permute-start.10 = (bf16[320,400]{1,0:T(8,128)(2,1)S(1)}, bf16[320,400]{1,0:T(8,128)(2,1)S(1)}, u32[]{:S(2)}, u32[]{:S(2)}) collective-permute-start(bf16[320,400]{1,0:T(8,128)(2,1)S(1)} %bitcast.23), channel_id=1, source_target_pairs={{0,2},{1,3},{2,0},{3,1},{4,6},{5,7},{6,4},{7,5},{8,10},{9,11},{10,... | collective-permute-start | bytes 768008 | tf_op jit(solution)/shard_map/ppermute | solution.py:530
  49.9 6.8 %collective-permute-start.6 = (bf16[320,400]{1,0:T(8,128)(2,1)S(1)}, bf16[320,400]{1,0:T(8,128)(2,1)S(1)}, u32[]{:S(2)}, u32[]{:S(2)}) collective-permute-start(bf16[320,400]{1,0:T(8,128)(2,1)S(1)} %bitcast.24), channel_id=1, source_target_pairs={{0,1},{1,0},{2,3},{3,2},{4,5},{5,4},{6,7},{7,6},{8,9},{9,8},{10,11... | collective-permute-start | bytes 768008 | tf_op jit(solution)/shard_map/ppermute | solution.py:530
  56.7 1.6 %collective-permute-start.11 = (bf16[320,400]{1,0:T(8,128)(2,1)S(1)}, bf16[320,400]{1,0:T(8,128)(2,1)S(1)}, u32[]{:S(2)}, u32[]{:S(2)}) collective-permute-start(bf16[320,400]{1,0:T(8,128)(2,1)S(1)} %collective-permute-done.10.refs_2_), channel_id=1, source_target_pairs={{0,1},{1,0},{2,3},{3,2},{4,5},{5,4},{6,7},{7,6},{8,9},{9,8},{10,11... | collective-permute-start | bytes 768008 | tf_op jit(solution)/shard_map/ppermute | solution.py:530
  61.3 1.9 %collective-permute-start.12 = (bf16[640,384]{1,0:T(8,128)(2,1)S(1)}, bf16[640,384]{1,0:T(8,128)(2,1)S(1)}, u32[]{:S(2)}, u32[]{:S(2)}) collective-permute-start(bf16[640,384]{1,0:T(8,128)(2,1)S(1)} %get-tuple-element.88), channel_id=1, source_target_pairs={{0,1},{1,0},{2,3},{3,2},{4,5},{5,4},{6,7},{7,6},{8,9},{9,8},{10,11... | collective-permute-start | bytes 1474568 | tf_op jit(solution)/shard_map/ppermute | solution.py:530
  63.3 12.5 %collective-permute-start.13 = (bf16[320,384]{1,0:T(8,128)(2,1)S(1)}, bf16[320,384]{1,0:T(8,128)(2,1)S(1)}, u32[]{:S(2)}, u32[]{:S(2)}) collective-permute-start(bf16[320,384]{1,0:T(8,128)(2,1)S(1)} %shard_map.209), channel_id=1, source_target_pairs={{0,2},{1,3},{2,0},{3,1},{4,6},{5,7},{6,4},{7,5},{8,10},{9,11},{10,... | collective-permute-start | bytes 737288 | tf_op jit(solution)/shard_map/ppermute | solution.py:530
  65.1 8.5 %collective-permute-start.9 = (bf16[400,128]{1,0:T(8,128)(2,1)S(1)}, bf16[400,128]{1,0:T(8,128)(2,1)S(1)}, u32[]{:S(2)}, u32[]{:S(2)}) collective-permute-start(bf16[400,128]{1,0:T(8,128)(2,1)S(1)} %get-tuple-element.85.refs_0_.refs_4_), channel_id=1, source_target_pairs={{0,3},{1,2},{2,1},{3,0},{4,7},{5,6},{6,5},{7,4},{8,11},{9,10},{10,... | collective-permute-start | bytes 307208 | tf_op jit(solution)/shard_map/ppermute | solution.py:530
  65.1 10.7 %collective-permute-start.8 = (bf16[400,128]{1,0:T(8,128)(2,1)S(1)}, bf16[400,128]{1,0:T(8,128)(2,1)S(1)}, u32[]{:S(2)}, u32[]{:S(2)}) collective-permute-start(bf16[400,128]{1,0:T(8,128)(2,1)S(1)} %get-tuple-element.85.refs_0_.refs_4_), channel_id=1, source_target_pairs={{0,2},{1,3},{2,0},{3,1},{4,6},{5,7},{6,4},{7,5},{8,10},{9,11},{10,... | collective-permute-start | bytes 307208 | tf_op jit(solution)/shard_map/ppermute | solution.py:530
  66.6 9.2 %collective-permute-start.7 = (bf16[400,128]{1,0:T(8,128)(2,1)S(1)}, bf16[400,128]{1,0:T(8,128)(2,1)S(1)}, u32[]{:S(2)}, u32[]{:S(2)}) collective-permute-start(bf16[400,128]{1,0:T(8,128)(2,1)S(1)} %get-tuple-element.85.refs_0_.refs_4_), channel_id=1, source_target_pairs={{0,1},{1,0},{2,3},{3,2},{4,5},{5,4},{6,7},{7,6},{8,9},{9,8},{10,11... | collective-permute-start | bytes 307208 | tf_op jit(solution)/shard_map/ppermute | solution.py:530
  66.9 27.5 %copy-start.5 = (bf16[192,768]{1,0:T(8,128)(2,1)S(1)}, bf16[192,768]{1,0:T(8,128)(2,1)}, u32[]{:S(2)}) copy-start(bf16[192,768]{1,0:T(8,128)(2,1)} %refs_11_.1) | copy-start | bytes 884740
  88.2 8.9 %copy-start.15 = (s32[112]{0:T(128)S(1)}, s32[112]{0:T(128)}, u32[]{:S(2)}) copy-start(s32[112]{0:T(128)} %param.24) | copy-start | bytes 1348
  89.2 4.2 %collective-permute-start.16 = (bf16[208,128]{1,0:T(8,128)(2,1)S(1)}, bf16[208,128]{1,0:T(8,128)(2,1)S(1)}, u32[]{:S(2)}, u32[]{:S(2)}) collective-permute-start(bf16[208,128]{1,0:T(8,128)(2,1)S(1)} %get-tuple-element.101.refs_0_), channel_id=1, source_target_pairs={{0,3},{1,2},{2,1},{3,0},{4,7},{5,6},{6,5},{7,4},{8,11},{9,10},{10,... | collective-permute-start | bytes 159752 | tf_op jit(solution)/shard_map/ppermute | solution.py:530
  89.3 5.2 %collective-permute-start.15 = (bf16[208,128]{1,0:T(8,128)(2,1)S(1)}, bf16[208,128]{1,0:T(8,128)(2,1)S(1)}, u32[]{:S(2)}, u32[]{:S(2)}) collective-permute-start(bf16[208,128]{1,0:T(8,128)(2,1)S(1)} %get-tuple-element.101.refs_0_), channel_id=1, source_target_pairs={{0,2},{1,3},{2,0},{3,1},{4,6},{5,7},{6,4},{7,5},{8,10},{9,11},{10,... | collective-permute-start | bytes 159752 | tf_op jit(solution)/shard_map/ppermute | solution.py:530
  90.8 3.7 %collective-permute-start.14 = (bf16[208,128]{1,0:T(8,128)(2,1)S(1)}, bf16[208,128]{1,0:T(8,128)(2,1)S(1)}, u32[]{:S(2)}, u32[]{:S(2)}) collective-permute-start(bf16[208,128]{1,0:T(8,128)(2,1)S(1)} %get-tuple-element.101.refs_0_), channel_id=1, source_target_pairs={{0,1},{1,0},{2,3},{3,2},{4,5},{5,4},{6,7},{7,6},{8,9},{9,8},{10,11... | collective-permute-start | bytes 159752 | tf_op jit(solution)/shard_map/ppermute | solution.py:530
  100.0 1.5 copy-start
  101.6 32.2 %copy-start.1 = (bf16[7680,128]{1,0:T(8,128)(2,1)S(1)}, bf16[7680,128]{1,0:T(8,128)(2,1)}, u32[]{:S(2)}) copy-start(bf16[7680,128]{1,0:T(8,128)(2,1)} %all-gather.2.cloned.1.call-done.refs_0_) | copy-start | bytes 5898244
  101.6 14.4 %collective-permute-start.21 = (bf16[1536,128]{1,0:T(8,128)(2,1)S(1)}, bf16[1536,128]{1,0:T(8,128)(2,1)S(1)}, u32[]{:S(2)}, u32[]{:S(2)}) collective-permute-start(bf16[1536,128]{1,0:T(8,128)(2,1)S(1)} %shard_map.216.refs_0_), channel_id=1, source_target_pairs={{0,2},{1,3},{2,0},{3,1},{4,6},{5,7},{6,4},{7,5},{8,10},{9,11},{10,... | collective-permute-start | bytes 1179656 | tf_op jit(solution)/shard_map/ppermute | solution.py:530
  102.6 13.4 %collective-permute-start.26 = (bf16[864,128]{1,0:T(8,128)(2,1)S(1)}, bf16[864,128]{1,0:T(8,128)(2,1)S(1)}, u32[]{:S(2)}, u32[]{:S(2)}) collective-permute-start(bf16[864,128]{1,0:T(8,128)(2,1)S(1)} %get-tuple-element.116.refs_1_.refs_4_), channel_id=1, source_target_pairs={{0,4},{4,0},{8,12},{12,8},{16,20},{20,16},{24,28},{28,24},{1,5},{5... | collective-permute-start | bytes 663560 | tf_op jit(solution)/shard_map/ppermute | solution.py:530
  103.9 1.9 %collective-permute-start.17 = (bf16[208,128]{1,0:T(8,128)(2,1)S(1)}, bf16[208,128]{1,0:T(8,128)(2,1)S(1)}, u32[]{:S(2)}, u32[]{:S(2)}) collective-permute-start(bf16[208,128]{1,0:T(8,128)(2,1)S(1)} %get-tuple-element.106), channel_id=1, source_target_pairs={{0,1},{1,0},{2,3},{3,2},{4,5},{5,4},{6,7},{7,6},{8,9},{9,8},{10,11... | collective-permute-start | bytes 159752 | tf_op jit(solution)/shard_map/ppermute | solution.py:530
  103.9 10.6 %collective-permute-start.18 = (bf16[208,128]{1,0:T(8,128)(2,1)S(1)}, bf16[208,128]{1,0:T(8,128)(2,1)S(1)}, u32[]{:S(2)}, u32[]{:S(2)}) collective-permute-start(bf16[208,128]{1,0:T(8,128)(2,1)S(1)} %get-tuple-element.107), channel_id=1, source_target_pairs={{0,2},{1,3},{2,0},{3,1},{4,6},{5,7},{6,4},{7,5},{8,10},{9,11},{10,... | collective-permute-start | bytes 159752 | tf_op jit(solution)/shard_map/ppermute | solution.py:530
  105.0 10.4 %collective-permute-start.19 = (bf16[208,128]{1,0:T(8,128)(2,1)S(1)}, bf16[208,128]{1,0:T(8,128)(2,1)S(1)}, u32[]{:S(2)}, u32[]{:S(2)}) collective-permute-start(bf16[208,128]{1,0:T(8,128)(2,1)S(1)} %get-tuple-element.108), channel_id=1, source_target_pairs={{0,3},{1,2},{2,1},{3,0},{4,7},{5,6},{6,5},{7,4},{8,11},{9,10},{10,... | collective-permute-start | bytes 159752 | tf_op jit(solution)/shard_map/ppermute | solution.py:530
  105.8 10.8 %collective-permute-start.25 = (bf16[864,128]{1,0:T(8,128)(2,1)S(1)}, bf16[864,128]{1,0:T(8,128)(2,1)S(1)}, u32[]{:S(2)}, u32[]{:S(2)}) collective-permute-start(bf16[864,128]{1,0:T(8,128)(2,1)S(1)} %get-tuple-element.116.refs_1_.refs_4_), channel_id=1, source_target_pairs={{0,24},{4,28},{8,0},{12,4},{16,8},{20,12},{24,16},{28,20},{1,25},{... | collective-permute-start | bytes 663560 | tf_op jit(solution)/shard_map/ppermute | solution.py:547
  114.5 16.4 %collective-permute-start.24 = (bf16[864,128]{1,0:T(8,128)(2,1)S(1)}, bf16[864,128]{1,0:T(8,128)(2,1)S(1)}, u32[]{:S(2)}, u32[]{:S(2)}) collective-permute-start(bf16[864,128]{1,0:T(8,128)(2,1)S(1)} %get-tuple-element.116.refs_1_.refs_4_), channel_id=1, source_target_pairs={{0,16},{4,20},{8,24},{12,28},{16,0},{20,4},{24,8},{28,12},{1,17},{... | collective-permute-start | bytes 663560 | tf_op jit(solution)/shard_map/ppermute | solution.py:547
  115.4 16.3 %collective-permute-start.23 = (bf16[864,128]{1,0:T(8,128)(2,1)S(1)}, bf16[864,128]{1,0:T(8,128)(2,1)S(1)}, u32[]{:S(2)}, u32[]{:S(2)}) collective-permute-start(bf16[864,128]{1,0:T(8,128)(2,1)S(1)} %get-tuple-element.116.refs_1_.refs_4_), channel_id=1, source_target_pairs={{0,8},{4,12},{8,16},{12,20},{16,24},{20,28},{24,0},{28,4},{1,9},{5... | collective-permute-start | bytes 663560 | tf_op jit(solution)/shard_map/ppermute | solution.py:547
  116.0 26.6 %collective-permute-start.20 = (bf16[1536,128]{1,0:T(8,128)(2,1)S(1)}, bf16[1536,128]{1,0:T(8,128)(2,1)S(1)}, u32[]{:S(2)}, u32[]{:S(2)}) collective-permute-start(bf16[1536,128]{1,0:T(8,128)(2,1)S(1)} %shard_map.216.refs_0_), channel_id=1, source_target_pairs={{0,1},{1,0},{2,3},{3,2},{4,5},{5,4},{6,7},{7,6},{8,9},{9,8},{10,11... | collective-permute-start | bytes 1179656 | tf_op jit(solution)/shard_map/ppermute | solution.py:530
  116.1 26.6 %collective-permute-start.22 = (bf16[1536,128]{1,0:T(8,128)(2,1)S(1)}, bf16[1536,128]{1,0:T(8,128)(2,1)S(1)}, u32[]{:S(2)}, u32[]{:S(2)}) collective-permute-start(bf16[1536,128]{1,0:T(8,128)(2,1)S(1)} %collective-permute-done.21.refs_2_), channel_id=1, source_target_pairs={{0,1},{1,0},{2,3},{3,2},{4,5},{5,4},{6,7},{7,6},{8,9},{9,8},{10,11... | collective-permute-start | bytes 1179656 | tf_op jit(solution)/shard_map/ppermute | solution.py:530
  116.6 18.3 %collective-permute-start.29 = (bf16[864,128]{1,0:T(8,128)(2,1)S(1)}, bf16[864,128]{1,0:T(8,128)(2,1)S(1)}, u32[]{:S(2)}, u32[]{:S(2)}) collective-permute-start(bf16[864,128]{1,0:T(8,128)(2,1)S(1)} %collective-permute-done.25.refs_4_.refs_7_), channel_id=1, source_target_pairs={{0,4},{4,0},{8,12},{12,8},{16,20},{20,16},{24,28},{28,24},{1,5},{5... | collective-permute-start | bytes 663560 | tf_op jit(solution)/shard_map/ppermute | solution.py:530
  131.0 8.4 %collective-permute-start.28 = (bf16[864,128]{1,0:T(8,128)(2,1)S(1)}, bf16[864,128]{1,0:T(8,128)(2,1)S(1)}, u32[]{:S(2)}, u32[]{:S(2)}) collective-permute-start(bf16[864,128]{1,0:T(8,128)(2,1)S(1)} %collective-permute-done.24.refs_3_.refs_6_), channel_id=1, source_target_pairs={{0,4},{4,0},{8,12},{12,8},{16,20},{20,16},{24,28},{28,24},{1,5},{5... | collective-permute-start | bytes 663560 | tf_op jit(solution)/shard_map/ppermute | solution.py:530
  131.8 10.8 %collective-permute-start.27 = (bf16[864,128]{1,0:T(8,128)(2,1)S(1)}, bf16[864,128]{1,0:T(8,128)(2,1)S(1)}, u32[]{:S(2)}, u32[]{:S(2)}) collective-permute-start(bf16[864,128]{1,0:T(8,128)(2,1)S(1)} %collective-permute-done.23.refs_2_.refs_5_), channel_id=1, source_target_pairs={{0,4},{4,0},{8,12},{12,8},{16,20},{20,16},{24,28},{28,24},{1,5},{5... | collective-permute-start | bytes 663560 | tf_op jit(solution)/shard_map/ppermute | solution.py:530
  143.6 4.2 %collective-permute-start.30 = (bf16[208,192]{1,0:T(8,128)(2,1)S(1)}, bf16[208,192]{1,0:T(8,128)(2,1)S(1)}, u32[]{:S(2)}, u32[]{:S(2)}) collective-permute-start(bf16[208,192]{1,0:T(8,128)(2,1)S(1)} %get-tuple-element.123), channel_id=1, source_target_pairs={{0,1},{1,0},{2,3},{3,2},{4,5},{5,4},{6,7},{7,6},{8,9},{9,8},{10,11... | collective-permute-start | bytes 239624 | tf_op jit(solution)/shard_map/ppermute | solution.py:530
  143.7 5.8 %collective-permute-start.31 = (bf16[208,192]{1,0:T(8,128)(2,1)S(1)}, bf16[208,192]{1,0:T(8,128)(2,1)S(1)}, u32[]{:S(2)}, u32[]{:S(2)}) collective-permute-start(bf16[208,192]{1,0:T(8,128)(2,1)S(1)} %get-tuple-element.124), channel_id=1, source_target_pairs={{0,2},{1,3},{2,0},{3,1},{4,6},{5,7},{6,4},{7,5},{8,10},{9,11},{10,... | collective-permute-start | bytes 239624 | tf_op jit(solution)/shard_map/ppermute | solution.py:530
  144.6 6.3 %collective-permute-start.32 = (bf16[208,192]{1,0:T(8,128)(2,1)S(1)}, bf16[208,192]{1,0:T(8,128)(2,1)S(1)}, u32[]{:S(2)}, u32[]{:S(2)}) collective-permute-start(bf16[208,192]{1,0:T(8,128)(2,1)S(1)} %get-tuple-element.125), channel_id=1, source_target_pairs={{0,3},{1,2},{2,1},{3,0},{4,7},{5,6},{6,5},{7,4},{8,11},{9,10},{10,... | collective-permute-start | bytes 239624 | tf_op jit(solution)/shard_map/ppermute | solution.py:530
  (4 other events, 2.8 us)
Sparse Core Ops, SparseCore 0:
  19.6 53.4 all-gather.1

commit v6 on v5

--- a/solution.py
+++ b/solution.py
@@ -271,10 +271,11 @@
     down_grad[0] = mm(z[...], de[...], (0, 0))
 
 
-def join_kernel(gathered, out, *, n_e):
-    stride, height = gathered.shape[0] // n_e, out.shape[0] // n_e
-    for j in range(n_e):
-        out[j * height:(j + 1) * height] = gathered[(j + 1) * stride - height:(j + 1) * stride]
+def join_kernel(*refs):
+    parts, out = refs[:-1], refs[-1]
+    height = out.shape[0] // len(parts)
+    for j, part in enumerate(parts):
+        out[j * height:(j + 1) * height] = part[part.shape[0] - height:]
 
 
 def pair_sum_kernel(across, got, out):
@@ -422,12 +423,6 @@
         last[...] = mm(saved[model:], d_att[...], (1, 1)).astype(last.dtype)
 
 
-def senders(n_e):
-    _, e = my_place()
-    half = n_e // 2
-    return [lax.rem((e ^ (j // half)) + n_e - 2 * (j % half), n_e) for j in range(n_e)]
-
-
 def late_sum_kernel(o0, o1, o2, o3, *refs, n_e, inner):
     lasts, (small, own, q1, q2, q3) = refs[:n_e], refs[n_e:]
     width = own.shape[0]
@@ -445,8 +440,8 @@
     )
     for o, q in ((o0, own), (o1, q1), (o2, q2), (o3, q3)):
         grad = 0.0
-        for last, sender in zip(lasts, senders(n_e)):
-            grad += mm(chunk(o, sender, width)[...], last[inner:inner + width], (1, 1))
+        for j, last in enumerate(lasts):
+            grad += mm(o[j * width:(j + 1) * width], last[inner:inner + width], (1, 1))
         q[0:width] = grad.astype(q.dtype)
         if q is not own:
             q[width:] = wide.astype(bf16)
@@ -484,16 +479,13 @@
     out[...] = dr1[...] + inverse * weighted - x[...].astype(f32) * (inverse * inverse * row_dot)
 
 
-def qkv_grad_kernel(gathered, *refs, pieces, n_e, inner):
-    lasts, rest = refs[:len(pieces)], refs[len(pieces):]
+def qkv_grad_kernel(*refs, count, inner):
+    lasts, saved, rest = refs[:count], refs[count:2 * count], refs[2 * count:]
     out = rest[-1]
     model = out.shape[1]
-    stride = gathered.shape[0] // n_e
     total = 0.0 if len(rest) == 1 else rest[0][...]
-    for j, last in zip(pieces, lasts):
-        sender = senders(n_e)[j] if n_e > 1 else 0
-        h1 = chunk(gathered, sender, stride)[...][0:model]
-        total += mm(last[0:inner], h1, (1, 1))
+    for last, h in zip(lasts, saved):
+        total += mm(last[0:inner], h[0:model], (1, 1))
     out[...] = total
 
 
@@ -542,11 +534,8 @@
         v = lax.all_to_all(v, "expert", split_axis=0, concat_axis=0, tiled=True)
         return v.reshape(rows, w)
 
-    def over_pairs(v):
-        return [
-            lax.ppermute(v, "expert", [(i, (i + 2 * k) % n_e) for i in range(n_e)])
-            for k in range(1, n_e // 2)
-        ]
+    def step(v, k):
+        return lax.ppermute(v, "expert", [(i, (i + k) % n_e) for i in range(n_e)])
 
     def after(values, *others):
         return list(lax.optimization_barrier((tuple(values), others))[0])
@@ -584,8 +573,6 @@
         scratch=[pltpu.VMEM((model, tok), f32), pltpu.VMEM((model, tok), f32)],
     )
     got = [swap(p, k) for k, p in ((1, p1), (2, p2), (3, p3))]
-    if direct:
-        saved_all = lax.all_gather(saved, "expert", axis=0, tiled=True)
     dest, gain2, rw_own, qkv_wt = run(
         functools.partial(route_kernel, experts=experts, cap=cap, n_t=n_t),
         [
@@ -609,8 +596,15 @@
         fetch=(4, 5, 8),
         scratch=[pltpu.VMEM((2 * width + 16, tok), bf16)],
     )
-    in_rows = around_large(exchange(send_rows))
-    token_packs = around(after([token_pack], in_rows[1])[0])
+    in_rows = exchange(send_rows)
+    if direct:
+        (early,) = after([saved], in_rows)
+        in_rows = around_large(in_rows)
+        behind1, behind3 = step(early, 2), step(early, 6)
+        beside = swap(early, 1, "expert", n_e)
+        in_rows = after(in_rows, behind1, behind3, beside)
+    else:
+        in_rows = around_large(in_rows)
 
     own, across, mate, u, z, de, da = run(
         functools.partial(expert_kernel, n_t=n_t),
@@ -626,6 +620,9 @@
         ],
     )
     got = swap(mate, 1)
+    if direct:
+        early, behind1 = after([early, behind1], mate)
+        behind2, beside1 = step(early, 4), swap(behind1, 1, "expert", n_e)
     (across,) = run(pair_sum_kernel, [((rows, 2 * width), bf16)], across, got)
     far = swap(across, 2)
     up_grad, down_grad = run(
@@ -633,7 +630,11 @@
         [(up_weight.shape, f32), (down_weight.shape, f32)],
         *after([u, z, de, da], across),
     )
-    (far,) = after([far], up_grad, *token_packs[1:])
+    token_packs = around(after([token_pack], up_grad)[0])
+    if direct:
+        beside3 = swap(after([behind3], across)[0], 1, "expert", n_e)
+        (far,) = after([far], behind2, beside1, beside3)
+    (far,) = after([far], up_grad)
     (summed,) = run(expert_sum_kernel, [((rows, 2 * width), bf16)], own, got, far)
     back = exchange(summed)
     output, back_pack = run(
@@ -643,6 +644,9 @@
         fetch=(5,),
     )
     back_packs = around(back_pack)
+    if direct:
+        beside2 = swap(after([behind2], back_pack)[0], 1, "expert", n_e)
+        saved_all = [saved, behind1, behind2, behind3, beside, beside1, beside2, beside3]
 
     c0, c1, c2, c3, dr1, d_proj, d_att, d_logits, gain_terms, d_scores = run(
         functools.partial(backward_kernel, n_t=n_t),
@@ -673,29 +677,21 @@
         scratch=[pltpu.VMEM((model, tok), f32), padded],
     )
     if direct:
-        lasts = [last] + over_pairs(last)
-    got = [swap(c, k) for k, c in ((1, c1), (2, c2), (3, c3))]
-    (input_grad,) = run(
-        functools.partial(input_grad_kernel, n_t=n_t),
-        [((width, tok), f32)],
-        c0, *got, dr1, inv1, x, gain1,
-        fetch=(6,),
-    )
+        lasts = [last] + [step(last, k) for k in (2, 4, 6)]
     if direct:
         (att,) = run(
-            functools.partial(join_kernel, n_e=n_e),
-            [((n_e * width, tok), bf16)],
-            *after([saved_all], last),
+            join_kernel, [((n_e * width, tok), bf16)], *after(saved_all, last)
         )
-        atts = around_large(att)
         half = n_e // 2
         (part,) = run(
-            functools.partial(qkv_grad_kernel, pieces=range(half), n_e=n_e, inner=inner),
+            functools.partial(qkv_grad_kernel, count=half, inner=inner),
             [((inner, model), f32)],
-            saved_all, *lasts,
+            *lasts, *saved_all[:half],
         )
         lasts = lasts + [swap(v, 1, "expert", n_e) for v in lasts]
-        lasts[half:] = after(lasts[half:], part, input_grad)
+        atts = [att, swap(att, 1), swap(att, 2)]
+        atts.append(swap(after(atts[2:], lasts[half + 1])[0], 1))
+        lasts[half:] = after(lasts[half:], part)
         small, own, q1, q2, q3 = run(
             functools.partial(late_sum_kernel, n_e=n_e, inner=inner),
             [((height, model), f32), ((width, width), f32)]
@@ -703,11 +699,11 @@
             *atts, *lasts,
         )
         got = [swap(q, k) for k, q in ((1, q1), (2, q2), (3, q3))]
-        (part,) = after([part], own)
+        c1, c2, c3, part = after([c1, c2, c3, part], own)
         (qkv_grad,) = run(
-            functools.partial(qkv_grad_kernel, pieces=range(half, n_e), n_e=n_e, inner=inner),
+            functools.partial(qkv_grad_kernel, count=half, inner=inner),
             [((inner, model), f32)],
-            saved_all, *lasts[half:], part,
+            *lasts[half:], *saved_all[half:], part,
         )
         out_grad, first, second, router_grad, rel_grad = run(
             functools.partial(out_grad_kernel, n_t=n_t),
@@ -724,15 +720,22 @@
     else:
         small, out_grad = lax.psum((small, last.astype(f32)), "expert")
         (qkv_grad,) = run(
-            functools.partial(qkv_grad_kernel, pieces=range(1), n_e=1, inner=inner),
+            functools.partial(qkv_grad_kernel, count=1, inner=inner),
             [((inner, model), f32)],
-            saved, d_proj,
+            d_proj, saved,
         )
         qkv_grad = lax.psum(qkv_grad, "expert")
         first = lax.psum(small[experts + 1], "tensor")
         second = small[experts]
         router_grad = small[:experts]
         rel_grad = small[experts + 2:experts + 2 + n_heads, :n_buckets]
+    got = [swap(c, k) for k, c in ((1, c1), (2, c2), (3, c3))]
+    (input_grad,) = run(
+        functools.partial(input_grad_kernel, n_t=n_t),
+        [((width, tok), f32)],
+        c0, *got, dr1, inv1, x, gain1,
+        fetch=(6,),
+    )
     return (
         output.T,
         input_grad.T,

time: 159 us -> 161 us (1.013); the launches traced: 159 us -> 158 us
  blocking collectives: 34.9 us -> 16.8 us
  between operations: 14.3 us -> 1.16 us
  starting transfers between devices: 25.6 us -> 37.9 us
  local copies, waits for them, and re-layouts: 7.19 us -> 16.1 us
  waiting for transfers between devices: 52.9 us -> 61.7 us
    all_to_all x2 -> x1, blocking collectives: 34.9 us -> 16.8 us  [exchange(): v = lax.all_to_all(v, 'expert', split_axis=0, concat_axis=0, tiled=True)]
    ppermute x3 -> x6, waiting for transfers between devices: 12.7 us -> 26.4 us  [step(): return lax.ppermute(v, 'expert', [(i, (i + k) % n_e) for i in range(n_e)])]
    unnamed x36 -> x102, local copies, waits for them, and re-layouts: 6.5 us -> 15.4 us
    ppermute x3 -> x6, starting transfers between devices: 2.95 us -> 8.84 us  [step(): return lax.ppermute(v, 'expert', [(i, (i + k) % n_e) for i in range(n_e)])]
    ppermute x30 -> x34, waiting for transfers between devices: 40.2 us -> 34.6 us  [swap(): return lax.ppermute(v, axis, [(i, i ^ k) for i in range(n)])]
    all_to_all x0 -> x1, starting transfers between devices: none -> 4.04 us  [exchange(): v = lax.all_to_all(v, 'expert', split_axis=0, concat_axis=0, tiled=True)]
    ppermute x30 -> x34, starting transfers between devices: 22.6 us -> 25 us  [swap(): return lax.ppermute(v, axis, [(i, i ^ k) for i in range(n)])]
  transfers between devices with their start and end apart: 34 -> 41, of which waited for: 15 -> 18; matrix products, arithmetic and copies ran while one was open for 0% -> 0% of each run, Pallas kernels for 12% -> 9%
where the time goes in v6:
time: 161 us; the launch traced here: 158 us
  waiting for transfers between devices  61.7 us (38%)
  starting transfers between devices  37.9 us (24%)
  Pallas kernels  24.2 us (15%)
  blocking collectives  16.8 us (10%)
  local copies, waits for them, and re-layouts  16.1 us (10%)
    ppermute x34, waiting for transfers between devices, swap(): return lax.ppermute(v, axis, [(i, i ^ k) for i in range(n)])  34.6 us
    ppermute x6, waiting for transfers between devices, step(): return lax.ppermute(v, 'expert', [(i, (i + k) % n_e) for i in range(n_e)])  26.4 us
    ppermute x34, starting transfers between devices, swap(): return lax.ppermute(v, axis, [(i, i ^ k) for i in range(n)])  25 us
    pallas_call x17, Pallas kernels, run(): pl.pallas_call(whole, out_shape=[jax.ShapeDtypeStruct(s, d) for s, d in o...  24.2 us
    all_to_all x1, blocking collectives, exchange(): v = lax.all_to_all(v, 'expert', split_axis=0, concat_axis=0, tiled=True)  16.8 us
    unnamed x102, local copies, waits for them, and re-layouts  15.4 us
    ppermute x6, starting transfers between devices, step(): return lax.ppermute(v, 'expert', [(i, (i + k) % n_e) for i in range(n_e)])  8.84 us
    all_to_all x1, starting transfers between devices, exchange(): v = lax.all_to_all(v, 'expert', split_axis=0, concat_axis=0, tiled=True)  4.04 us
  transfers between devices with their start and end apart: 41, of which 18 were waited for; matrix products, arithmetic and copies ran while one was open for 0% of the time, Pallas kernels for 9%

profile of v6, /device:TPU:0, one launch (start us, length us, event | category | flops | bytes accessed | tf_op | source)
XLA Modules:
  0.0 157.9 jit_solution(11456256224106226562)
XLA Ops:
  1.2 2.6 %collective-permute-start.1 = (bf16[192,128]{1,0:T(8,128)(2,1)}, bf16[192,128]{1,0:T(8,128)(2,1)S(1)}, u32[]{:S(2)}, u32[]{:S(2)}) collective-permute-start(bf16[192,128]{1,0:T(8,128)(2,1)} %bitcast.27), channel_id=1, source_target_pairs={{0,2},{1,3},{2,0},{3,1},{4,6},{5,7},{6,4},{7,5},{8,10},{9,11},{10,... | collective-permute-start | bytes 147464 | tf_op jit(solution)/shard_map/ppermute | solution.py:522
  4.5 1.0 copy-done.2
  7.5 0.9 shard_map.204
  8.5 1.2 copy-done
  10.4 1.9 %shard_map.205 = (f32[192,128]{1,0:T(8,128)S(1)}, bf16[192,128]{1,0:T(8,128)(2,1)S(1)}, bf16[192,128]{1,0:T(8,128)(2,1)S(1)}, bf16[192,128]{1,0:T(8,128)(2,1)S(1...) custom-call(bf16[192,128]{1,0:T(8,128)(2,1)S(1)} %bitcast.29, ...), custom_call_target="tpu_custom_call" | custom-call | bytes 2412032 | tf_op jit(solution)/shard_map/pallas_call | solution.py:67
  12.6 2.0 %collective-permute-start.4 = (bf16[192,128]{1,0:T(8,128)(2,1)S(1)}, bf16[192,128]{1,0:T(8,128)(2,1)S(1)}, u32[]{:S(2)}, u32[]{:S(2)}) collective-permute-start(bf16[192,128]{1,0:T(8,128)(2,1)S(1)} %get-tuple-element.98), channel_id=1, source_target_pairs={{0,2},{1,3},{2,0},{3,1},{4,6},{5,7},{6,4},{7,5},{8,10},{9,11},{10,... | collective-permute-start | bytes 147464 | tf_op jit(solution)/shard_map/ppermute | solution.py:522
  15.4 1.4 collective-permute-done.4.refs_2_
  16.7 1.8 %collective-permute-done.5.refs_3_ = bf16[192,128]{1,0:T(8,128)(2,1)S(1)} collective-permute-done((bf16[192,128]{1,0:T(8,128)(2,1)S(1)}, bf16[192,128]{1,0:T(8,128)(2,1)S(1)}, u32[]{:S(2)}, u32[]{:S(2)}) %collective-permute-start.5) | collective-permute-done | bytes 49184 | tf_op jit(solution)/shard_map/ppermute | solution.py:522
  19.4 16.8 %all_to_all.10 = bf16[8,40,400]{2,1,0:T(8,128)(2,1)S(1)} all-to-all(bf16[8,40,400]{2,1,0:T(8,128)(2,1)S(1)} %bitcast.32), channel_id=1, replica_groups=mesh['expert'=8,'tensor'=4] {'expert'}, dimensions={0} | all-to-all | bytes 512000 | tf_op jit(solution)/shard_map/all_to_all | solution.py:534
  36.9 6.8 %collective-permute-done.7.refs_2_ = bf16[320,400]{1,0:T(8,128)(2,1)S(1)} collective-permute-done((bf16[320,400]{1,0:T(8,128)(2,1)S(1)}, bf16[320,400]{1,0:T(8,128)(2,1)S(1)}, u32[]{:S(2)}, u32[]{:S(2)}) %collective-permute-start.7) | collective-permute-done | bytes 256032 | tf_op jit(solution)/shard_map/ppermute | solution.py:522
  44.3 3.2 %collective-permute-start.10 = (bf16[960,128]{1,0:T(8,128)(2,1)S(1)}, bf16[960,128]{1,0:T(8,128)(2,1)S(1)}, u32[]{:S(2)}, u32[]{:S(2)}) collective-permute-start(bf16[960,128]{1,0:T(8,128)(2,1)S(1)} %get-tuple-element.147.refs_8_.refs_4_.refs_0_), channel_id=1, source_target_pairs={{0,24},{4,28},{8,0},{12,4},{16,8},{20,12},{24,16},{28,20},{1,25},{... | collective-permute-start | bytes 737288 | tf_op jit(solution)/shard_map/ppermute | solution.py:538
  47.5 1.8 %collective-permute-start.11 = (bf16[960,128]{1,0:T(8,128)(2,1)S(1)}, bf16[960,128]{1,0:T(8,128)(2,1)S(1)}, u32[]{:S(2)}, u32[]{:S(2)}) collective-permute-start(bf16[960,128]{1,0:T(8,128)(2,1)S(1)} %get-tuple-element.147.refs_8_.refs_4_.refs_0_), channel_id=1, source_target_pairs={{0,4},{4,0},{8,12},{12,8},{16,20},{20,16},{24,28},{28,24},{1,5},{5... | collective-permute-start | bytes 737288 | tf_op jit(solution)/shard_map/ppermute | solution.py:522
  49.3 5.0 %collective-permute-done.9.refs_5_.refs_1_ = bf16[960,128]{1,0:T(8,128)(2,1)S(1)} collective-permute-done((bf16[960,128]{1,0:T(8,128)(2,1)S(1)}, bf16[960,128]{1,0:T(8,128)(2,1)S(1)}, u32[]{:S(2)}, u32[]{:S(2)}) %collective-permute-start.9) | collective-permute-done | bytes 245792 | tf_op jit(solution)/shard_map/ppermute | solution.py:538
  54.3 3.8 %collective-permute-done.10.refs_7_.refs_3_ = bf16[960,128]{1,0:T(8,128)(2,1)S(1)} collective-permute-done((bf16[960,128]{1,0:T(8,128)(2,1)S(1)}, bf16[960,128]{1,0:T(8,128)(2,1)S(1)}, u32[]{:S(2)}, u32[]{:S(2)}) %collective-permute-start.10) | collective-permute-done | bytes 245792 | tf_op jit(solution)/shard_map/ppermute | solution.py:538
  58.1 3.0 %shard_map.208 = (bf16[320,384]{1,0:T(8,128)(2,1)S(1)}, bf16[320,384]{1,0:T(8,128)(2,1)S(1)}, bf16[640,384]{1,0:T(8,128)(2,1)S(1)}, bf16[320,768]{1,0:T(8,128)(2...) custom-call(bf16[320,400]{1,0:T(8,128)(2,1)S(1)} %bitcast.25, ...), custom_call_target="tpu_custom_call" | custom-call | bytes 6332416 | tf_op jit(solution)/shard_map/pallas_call | solution.py:67
  61.2 1.7 %collective-permute-start.17 = (bf16[960,128]{1,0:T(8,128)(2,1)S(1)}, bf16[960,128]{1,0:T(8,128)(2,1)S(1)}, u32[]{:S(2)}, u32[]{:S(2)}) collective-permute-start(bf16[960,128]{1,0:T(8,128)(2,1)S(1)} %get-tuple-element.147.refs_8_.refs_4_.refs_0_), channel_id=1, source_target_pairs={{0,16},{4,20},{8,24},{12,28},{16,0},{20,4},{24,8},{28,12},{1,17},{... | collective-permute-start | bytes 737288 | tf_op jit(solution)/shard_map/ppermute | solution.py:538
  62.9 1.8 %collective-permute-start.18 = (bf16[960,128]{1,0:T(8,128)(2,1)S(1)}, bf16[960,128]{1,0:T(8,128)(2,1)S(1)}, u32[]{:S(2)}, u32[]{:S(2)}) collective-permute-start(bf16[960,128]{1,0:T(8,128)(2,1)S(1)} %collective-permute-done.9.refs_5_.refs_1_), channel_id=1, source_target_pairs={{0,4},{4,0},{8,12},{12,8},{16,20},{20,16},{24,28},{28,24},{1,5},{5... | collective-permute-start | bytes 737288 | tf_op jit(solution)/shard_map/ppermute | solution.py:522
  64.8 1.0 collective-permute-start.16
  66.4 3.2 %shard_map.210 = (f32[1,768,768]{2,1,0:T(8,128)}, f32[1,768,768]{2,1,0:T(8,128)}) custom-call(bf16[320,768]{1,0:T(8,128)(2,1)S(1)} %get-tuple-element.118.refs_0_, bf16[320,768]{1,0:T(8,128)(2,1)S(1)} %get-tuple-element.119.refs_1_, bf16[320,768]{1,0:T(8,128)(2,1)S(1)} %get-tuple-element.120.refs_2_, bf16[320,768]{1,0:T(8,128)(2,1)S(1)} %get-tuple-element.121.refs_3_), custom_call_target="tpu_custom_call" | custom-call | bytes 6684672 | tf_op jit(solution)/shard_map/pallas_call | solution.py:67
  69.6 6.1 %collective-permute-done.17.refs_6_.refs_2_ = bf16[960,128]{1,0:T(8,128)(2,1)S(1)} collective-permute-done((bf16[960,128]{1,0:T(8,128)(2,1)S(1)}, bf16[960,128]{1,0:T(8,128)(2,1)S(1)}, u32[]{:S(2)}, u32[]{:S(2)}) %collective-permute-start.17) | collective-permute-done | bytes 245792 | tf_op jit(solution)/shard_map/ppermute | solution.py:538
  77.0 4.0 %all-to-all-start.1 = ((bf16[8,40,384]{2,1,0:T(8,128)(2,1)}), bf16[8,40,384]{2,1,0:T(8,128)(2,1)}, u32[]{:S(2)}, u32[]{:S(2)}) async-start(bf16[8,40,384]{2,1,0:T(8,128)(2,1)} %bitcast.11), calls=%async_computation.1 | async-start | bytes 491520 | tf_op jit(solution)/shard_map/all_to_all | solution.py:534
  81.2 1.4 collective-permute-start.14
  83.7 3.3 %collective-permute-done.14.refs_2_.refs_6_ = bf16[400,128]{1,0:T(8,128)(2,1)S(1)} collective-permute-done((bf16[400,128]{1,0:T(8,128)(2,1)S(1)}, bf16[400,128]{1,0:T(8,128)(2,1)S(1)}, u32[]{:S(2)}, u32[]{:S(2)}) %collective-permute-start.14) | collective-permute-done | bytes 102432 | tf_op jit(solution)/shard_map/ppermute | solution.py:522
  89.6 0.9 copy-done.17
  94.7 2.0 %shard_map.212 = (bf16[192,128]{1,0:T(8,128)(2,1)}, bf16[208,128]{1,0:T(8,128)(2,1)S(1)}) custom-call(bf16[400,128]{1,0:T(8,128)(2,1)S(1)} %get-tuple-element.123.refs_0_.refs_4_, bf16[400,128]{1,0:T(8,128)(2,1)S(1)} %copy-done.17, bf16[400,128]{1,0:T(8,128)(2,1)S(1)} %copy-done.20, bf16[400,128]{1,0:T(8,128)(2,1)S(1)} %copy-done.23, ...), custom_call_target="tpu_custom_call" | custom-call | bytes 909312 | tf_op jit(solution)/shard_map/pallas_call | solution.py:67
  96.7 1.4 collective-permute-start.26
  98.2 1.3 collective-permute-start.21
  99.9 2.5 %collective-permute-done.21.refs_2_ = bf16[208,128]{1,0:T(8,128)(2,1)S(1)} collective-permute-done((bf16[208,128]{1,0:T(8,128)(2,1)S(1)}, bf16[208,128]{1,0:T(8,128)(2,1)S(1)}, u32[]{:S(2)}, u32[]{:S(2)}) %collective-permute-start.21) | collective-permute-done | bytes 53280 | tf_op jit(solution)/shard_map/ppermute | solution.py:522
  102.3 1.1 collective-permute-done.22.refs_3_
  104.3 0.9 copy-done.30
  106.8 2.6 %shard_map.213 = (bf16[208,128]{1,0:T(8,128)(2,1)S(1)}, bf16[208,128]{1,0:T(8,128)(2,1)S(1)}, bf16[208,128]{1,0:T(8,128)(2,1)S(1)}, bf16[208,128]{1,0:T(8,128)(2...) custom-call(bf16[208,128]{1,0:T(8,128)(2,1)S(1)} %get-tuple-element., ...), custom_call_target="tpu_custom_call" | custom-call | bytes 3313664 | tf_op jit(solution)/shard_map/pallas_call | solution.py:67
  109.5 2.0 %shard_map.214 = (f32[16,768]{1,0:T(8,128)}, bf16[864,128]{1,0:T(8,128)(2,1)S(1)}) custom-call(bf16[400,128]{1,0:T(8,128)(2,1)S(1)} %get-tuple-element.123.refs_0_.refs_4_, bf16[400,128]{1,0:T(8,128)(2,1)S(1)} %copy-done.18, bf16[400,128]{1,0:T(8,128)(2,1)S(1)} %copy-done.21, bf16[400,128]{1,0:T(8,128)(2,1)S(1)} %copy-done.25, ...), custom_call_target="tpu_custom_call" | custom-call | bytes 2656704 | tf_op jit(solution)/shard_map/pallas_call | solution.py:67
  111.5 1.3 collective-permute-start.23
  112.9 1.2 collective-permute-start.28
  114.1 7.1 %collective-permute-done.23.refs_1_.refs_5_ = bf16[864,128]{1,0:T(8,128)(2,1)S(1)} collective-permute-done((bf16[864,128]{1,0:T(8,128)(2,1)S(1)}, bf16[864,128]{1,0:T(8,128)(2,1)S(1)}, u32[]{:S(2)}, u32[]{:S(2)}) %collective-permute-start.23) | collective-permute-done | bytes 221216 | tf_op jit(solution)/shard_map/ppermute | solution.py:538
  122.1 1.7 %collective-permute-start.25 = (bf16[864,128]{1,0:T(8,128)(2,1)S(1)}, bf16[864,128]{1,0:T(8,128)(2,1)S(1)}, u32[]{:S(2)}, u32[]{:S(2)}) collective-permute-start(bf16[864,128]{1,0:T(8,128)(2,1)S(1)} %get-tuple-element.145.refs_0_.refs_4_), channel_id=1, source_target_pairs={{0,24},{4,28},{8,0},{12,4},{16,8},{20,12},{24,16},{28,20},{1,25},{... | collective-permute-start | bytes 663560 | tf_op jit(solution)/shard_map/ppermute | solution.py:538
  123.8 4.3 %collective-permute-done.29.refs_9_.refs_1_ = bf16[864,128]{1,0:T(8,128)(2,1)S(1)} collective-permute-done((bf16[864,128]{1,0:T(8,128)(2,1)S(1)}, bf16[864,128]{1,0:T(8,128)(2,1)S(1)}, u32[]{:S(2)}, u32[]{:S(2)}) %collective-permute-start.29) | collective-permute-done | bytes 221216 | tf_op jit(solution)/shard_map/ppermute | solution.py:522
  128.8 4.4 %collective-permute-done.24.refs_2_.refs_6_ = bf16[864,128]{1,0:T(8,128)(2,1)S(1)} collective-permute-done((bf16[864,128]{1,0:T(8,128)(2,1)S(1)}, bf16[864,128]{1,0:T(8,128)(2,1)S(1)}, u32[]{:S(2)}, u32[]{:S(2)}) %collective-permute-start.24) | collective-permute-done | bytes 221216 | tf_op jit(solution)/shard_map/ppermute | solution.py:538
  133.1 1.4 collective-permute-start.32
  135.1 1.1 shard_map.215.refs_8_
  136.2 5.2 %collective-permute-done.32.refs_10_.refs_2_ = bf16[864,128]{1,0:T(8,128)(2,1)S(1)} collective-permute-done((bf16[864,128]{1,0:T(8,128)(2,1)S(1)}, bf16[864,128]{1,0:T(8,128)(2,1)S(1)}, u32[]{:S(2)}, u32[]{:S(2)}) %collective-permute-start.32) | collective-permute-done | bytes 221216 | tf_op jit(solution)/shard_map/ppermute | solution.py:522
  141.4 4.0 %collective-permute-done.33.refs_11_.refs_3_ = bf16[864,128]{1,0:T(8,128)(2,1)S(1)} collective-permute-done((bf16[864,128]{1,0:T(8,128)(2,1)S(1)}, bf16[864,128]{1,0:T(8,128)(2,1)S(1)}, u32[]{:S(2)}, u32[]{:S(2)}) %collective-permute-start.33) | collective-permute-done | bytes 221216 | tf_op jit(solution)/shard_map/ppermute | solution.py:522
  145.4 1.0 shard_map.217
  147.0 1.4 collective-permute-start.38
  148.5 1.4 collective-permute-start.35
  150.5 2.3 %shard_map.220 = f32[576,768]{1,0:T(8,128)} custom-call(bf16[864,128]{1,0:T(8,128)(2,1)S(1)} %collective-permute-done.31.refs_8_.refs_0_, bf16[864,128]{1,0:T(8,128)(2,1)S(1)} %collective-permute-done.29.refs_9_.refs_1_, bf16[864,128]{1,0:T(8,128)(2,1)S(1)} %collective-permute-done.32.refs_10_.refs_2_, ...), custom_call_target="tpu_custom_call" | custom-call | bytes 5406720 | tf_op jit(solution)/shard_map/pallas_call | solution.py:67
  152.9 3.1 %collective-permute-done.35.refs_2_ = bf16[208,128]{1,0:T(8,128)(2,1)S(1)} collective-permute-done((bf16[208,128]{1,0:T(8,128)(2,1)S(1)}, bf16[208,128]{1,0:T(8,128)(2,1)S(1)}, u32[]{:S(2)}, u32[]{:S(2)}) %collective-permute-start.35) | collective-permute-done | bytes 53280 | tf_op jit(solution)/shard_map/ppermute | solution.py:522
  156.8 1.1 shard_map.219
  (156 shorter events, 24.6 us)
Async XLA Ops:
  0.7 7.8 %collective-permute-start = (bf16[192,128]{1,0:T(8,128)(2,1)}, bf16[192,128]{1,0:T(8,128)(2,1)S(1)}, u32[]{:S(2)}, u32[]{:S(2)}) collective-permute-start(bf16[192,128]{1,0:T(8,128)(2,1)} %bitcast.26), channel_id=1, source_target_pairs={{0,1},{1,0},{2,3},{3,2},{4,5},{5,4},{6,7},{7,6},{8,9},{9,8},{10,11... | collective-permute-start | bytes 147464 | tf_op jit(solution)/shard_map/ppermute | solution.py:522
  1.2 7.3 %collective-permute-start.1 = (bf16[192,128]{1,0:T(8,128)(2,1)}, bf16[192,128]{1,0:T(8,128)(2,1)S(1)}, u32[]{:S(2)}, u32[]{:S(2)}) collective-permute-start(bf16[192,128]{1,0:T(8,128)(2,1)} %bitcast.27), channel_id=1, source_target_pairs={{0,2},{1,3},{2,0},{3,1},{4,6},{5,7},{6,4},{7,5},{8,10},{9,11},{10,... | collective-permute-start | bytes 147464 | tf_op jit(solution)/shard_map/ppermute | solution.py:522
  3.8 4.7 %collective-permute-start.2 = (bf16[192,128]{1,0:T(8,128)(2,1)}, bf16[192,128]{1,0:T(8,128)(2,1)S(1)}, u32[]{:S(2)}, u32[]{:S(2)}) collective-permute-start(bf16[192,128]{1,0:T(8,128)(2,1)} %bitcast.28), channel_id=1, source_target_pairs={{0,3},{1,2},{2,1},{3,0},{4,7},{5,6},{6,5},{7,4},{8,11},{9,10},{10,... | collective-permute-start | bytes 147464 | tf_op jit(solution)/shard_map/ppermute | solution.py:522
  10.4 47.7 %copy-start.4 = (bf16[1,768,768]{2,1,0:T(8,128)(2,1)S(1)}, bf16[1,768,768]{2,1,0:T(8,128)(2,1)}, u32[]{:S(2)}) copy-start(bf16[1,768,768]{2,1,0:T(8,128)(2,1)} %refs_4_.1) | copy-start | bytes 3538948
  10.4 47.7 %copy-start.5 = (bf16[1,768,768]{2,1,0:T(8,128)(2,1)S(1)}, bf16[1,768,768]{2,1,0:T(8,128)(2,1)}, u32[]{:S(2)}) copy-start(bf16[1,768,768]{2,1,0:T(8,128)(2,1)} %refs_5_.1) | copy-start | bytes 3538948
  12.4 24.5 %copy-start.33 = (bf16[576,128]{1,0:T(8,128)(2,1)}, bf16[576,128]{1,0:T(8,128)(2,1)S(1)}, u32[]{:S(2)}) copy-start(bf16[576,128]{1,0:T(8,128)(2,1)S(1)} %get-tuple-element.134.refs_13_) | copy-start | bytes 442372
  12.4 2.9 %collective-permute-start.3 = (bf16[192,128]{1,0:T(8,128)(2,1)S(1)}, bf16[192,128]{1,0:T(8,128)(2,1)S(1)}, u32[]{:S(2)}, u32[]{:S(2)}) collective-permute-start(bf16[192,128]{1,0:T(8,128)(2,1)S(1)} %get-tuple-element.97), channel_id=1, source_target_pairs={{0,1},{1,0},{2,3},{3,2},{4,5},{5,4},{6,7},{7,6},{8,9},{9,8},{10,11... | collective-permute-start | bytes 147464 | tf_op jit(solution)/shard_map/ppermute | solution.py:522
  12.6 4.1 %collective-permute-start.4 = (bf16[192,128]{1,0:T(8,128)(2,1)S(1)}, bf16[192,128]{1,0:T(8,128)(2,1)S(1)}, u32[]{:S(2)}, u32[]{:S(2)}) collective-permute-start(bf16[192,128]{1,0:T(8,128)(2,1)S(1)} %get-tuple-element.98), channel_id=1, source_target_pairs={{0,2},{1,3},{2,0},{3,1},{4,6},{5,7},{6,4},{7,5},{8,10},{9,11},{10,... | collective-permute-start | bytes 147464 | tf_op jit(solution)/shard_map/ppermute | solution.py:522
  14.6 4.0 %collective-permute-start.5 = (bf16[192,128]{1,0:T(8,128)(2,1)S(1)}, bf16[192,128]{1,0:T(8,128)(2,1)S(1)}, u32[]{:S(2)}, u32[]{:S(2)}) collective-permute-start(bf16[192,128]{1,0:T(8,128)(2,1)S(1)} %get-tuple-element.99), channel_id=1, source_target_pairs={{0,3},{1,2},{2,1},{3,0},{4,7},{5,6},{6,5},{7,4},{8,11},{9,10},{10,... | collective-permute-start | bytes 147464 | tf_op jit(solution)/shard_map/ppermute | solution.py:522
  15.4 20.8 %copy-start.40 = (f32[8,128]{1,0:T(8,128)}, f32[8,128]{1,0:T(8,128)S(1)}, u32[]{:S(2)}) copy-start(f32[8,128]{1,0:T(8,128)S(1)} %get-tuple-element.103.refs_9_.refs_4_) | copy-start | bytes 12292
  36.2 7.5 %collective-permute-start.7 = (bf16[320,400]{1,0:T(8,128)(2,1)S(1)}, bf16[320,400]{1,0:T(8,128)(2,1)S(1)}, u32[]{:S(2)}, u32[]{:S(2)}) collective-permute-start(bf16[320,400]{1,0:T(8,128)(2,1)S(1)} %bitcast.23), channel_id=1, source_target_pairs={{0,2},{1,3},{2,0},{3,1},{4,6},{5,7},{6,4},{7,5},{8,10},{9,11},{10,... | collective-permute-start | bytes 768008 | tf_op jit(solution)/shard_map/ppermute | solution.py:522
  36.9 21.2 %collective-permute-start.6 = (bf16[320,400]{1,0:T(8,128)(2,1)S(1)}, bf16[320,400]{1,0:T(8,128)(2,1)S(1)}, u32[]{:S(2)}, u32[]{:S(2)}) collective-permute-start(bf16[320,400]{1,0:T(8,128)(2,1)S(1)} %bitcast.24), channel_id=1, source_target_pairs={{0,1},{1,0},{2,3},{3,2},{4,5},{5,4},{6,7},{7,6},{8,9},{9,8},{10,11... | collective-permute-start | bytes 768008 | tf_op jit(solution)/shard_map/ppermute | solution.py:522
  43.7 14.4 %collective-permute-start.8 = (bf16[320,400]{1,0:T(8,128)(2,1)S(1)}, bf16[320,400]{1,0:T(8,128)(2,1)S(1)}, u32[]{:S(2)}, u32[]{:S(2)}) collective-permute-start(bf16[320,400]{1,0:T(8,128)(2,1)S(1)} %collective-permute-done.7.refs_2_), channel_id=1, source_target_pairs={{0,1},{1,0},{2,3},{3,2},{4,5},{5,4},{6,7},{7,6},{8,9},{9,8},{10,11... | collective-permute-start | bytes 768008 | tf_op jit(solution)/shard_map/ppermute | solution.py:522
  43.7 10.6 %collective-permute-start.9 = (bf16[960,128]{1,0:T(8,128)(2,1)S(1)}, bf16[960,128]{1,0:T(8,128)(2,1)S(1)}, u32[]{:S(2)}, u32[]{:S(2)}) collective-permute-start(bf16[960,128]{1,0:T(8,128)(2,1)S(1)} %get-tuple-element.147.refs_8_.refs_4_.refs_0_), channel_id=1, source_target_pairs={{0,8},{4,12},{8,16},{12,20},{16,24},{20,28},{24,0},{28,4},{1,9},{5... | collective-permute-start | bytes 737288 | tf_op jit(solution)/shard_map/ppermute | solution.py:538
  44.3 13.8 %collective-permute-start.10 = (bf16[960,128]{1,0:T(8,128)(2,1)S(1)}, bf16[960,128]{1,0:T(8,128)(2,1)S(1)}, u32[]{:S(2)}, u32[]{:S(2)}) collective-permute-start(bf16[960,128]{1,0:T(8,128)(2,1)S(1)} %get-tuple-element.147.refs_8_.refs_4_.refs_0_), channel_id=1, source_target_pairs={{0,24},{4,28},{8,0},{12,4},{16,8},{20,12},{24,16},{28,20},{1,25},{... | collective-permute-start | bytes 737288 | tf_op jit(solution)/shard_map/ppermute | solution.py:538
  47.5 10.5 %collective-permute-start.11 = (bf16[960,128]{1,0:T(8,128)(2,1)S(1)}, bf16[960,128]{1,0:T(8,128)(2,1)S(1)}, u32[]{:S(2)}, u32[]{:S(2)}) collective-permute-start(bf16[960,128]{1,0:T(8,128)(2,1)S(1)} %get-tuple-element.147.refs_8_.refs_4_.refs_0_), channel_id=1, source_target_pairs={{0,4},{4,0},{8,12},{12,8},{16,20},{20,16},{24,28},{28,24},{1,5},{5... | collective-permute-start | bytes 737288 | tf_op jit(solution)/shard_map/ppermute | solution.py:522
  61.1 3.6 %collective-permute-start.12 = (bf16[640,384]{1,0:T(8,128)(2,1)S(1)}, bf16[640,384]{1,0:T(8,128)(2,1)S(1)}, u32[]{:S(2)}, u32[]{:S(2)}) collective-permute-start(bf16[640,384]{1,0:T(8,128)(2,1)S(1)} %get-tuple-element.117), channel_id=1, source_target_pairs={{0,1},{1,0},{2,3},{3,2},{4,5},{5,4},{6,7},{7,6},{8,9},{9,8},{10,11... | collective-permute-start | bytes 1474568 | tf_op jit(solution)/shard_map/ppermute | solution.py:522
  61.2 14.5 %collective-permute-start.17 = (bf16[960,128]{1,0:T(8,128)(2,1)S(1)}, bf16[960,128]{1,0:T(8,128)(2,1)S(1)}, u32[]{:S(2)}, u32[]{:S(2)}) collective-permute-start(bf16[960,128]{1,0:T(8,128)(2,1)S(1)} %get-tuple-element.147.refs_8_.refs_4_.refs_0_), channel_id=1, source_target_pairs={{0,16},{4,20},{8,24},{12,28},{16,0},{20,4},{24,8},{28,12},{1,17},{... | collective-permute-start | bytes 737288 | tf_op jit(solution)/shard_map/ppermute | solution.py:538
  62.9 12.8 %collective-permute-start.18 = (bf16[960,128]{1,0:T(8,128)(2,1)S(1)}, bf16[960,128]{1,0:T(8,128)(2,1)S(1)}, u32[]{:S(2)}, u32[]{:S(2)}) collective-permute-start(bf16[960,128]{1,0:T(8,128)(2,1)S(1)} %collective-permute-done.9.refs_5_.refs_1_), channel_id=1, source_target_pairs={{0,4},{4,0},{8,12},{12,8},{16,20},{20,16},{24,28},{28,24},{1,5},{5... | collective-permute-start | bytes 737288 | tf_op jit(solution)/shard_map/ppermute | solution.py:522
  64.8 11.0 %collective-permute-start.16 = (bf16[320,384]{1,0:T(8,128)(2,1)S(1)}, bf16[320,384]{1,0:T(8,128)(2,1)S(1)}, u32[]{:S(2)}, u32[]{:S(2)}) collective-permute-start(bf16[320,384]{1,0:T(8,128)(2,1)S(1)} %shard_map.209), channel_id=1, source_target_pairs={{0,2},{1,3},{2,0},{3,1},{4,6},{5,7},{6,4},{7,5},{8,10},{9,11},{10,... | collective-permute-start | bytes 737288 | tf_op jit(solution)/shard_map/ppermute | solution.py:522
  65.8 10.4 %collective-permute-start.19 = (bf16[960,128]{1,0:T(8,128)(2,1)S(1)}, bf16[960,128]{1,0:T(8,128)(2,1)S(1)}, u32[]{:S(2)}, u32[]{:S(2)}) collective-permute-start(bf16[960,128]{1,0:T(8,128)(2,1)S(1)} %collective-permute-done.10.refs_7_.refs_3_), channel_id=1, source_target_pairs={{0,4},{4,0},{8,12},{12,8},{16,20},{20,16},{24,28},{28,24},{1,5},{5... | collective-permute-start | bytes 737288 | tf_op jit(solution)/shard_map/ppermute | solution.py:522
  66.4 37.0 %copy-start.3 = (bf16[192,768]{1,0:T(8,128)(2,1)S(1)}, bf16[192,768]{1,0:T(8,128)(2,1)}, u32[]{:S(2)}) copy-start(bf16[192,768]{1,0:T(8,128)(2,1)} %refs_11_.1) | copy-start | bytes 884740
  77.0 12.5 %all-to-all-start.1 = ((bf16[8,40,384]{2,1,0:T(8,128)(2,1)}), bf16[8,40,384]{2,1,0:T(8,128)(2,1)}, u32[]{:S(2)}, u32[]{:S(2)}) async-start(bf16[8,40,384]{2,1,0:T(8,128)(2,1)} %bitcast.11), calls=%async_computation.1 | async-start | bytes 491520 | tf_op jit(solution)/shard_map/all_to_all | solution.py:534
  81.1 1.9 %collective-permute-start.13 = (bf16[400,128]{1,0:T(8,128)(2,1)S(1)}, bf16[400,128]{1,0:T(8,128)(2,1)S(1)}, u32[]{:S(2)}, u32[]{:S(2)}) collective-permute-start(bf16[400,128]{1,0:T(8,128)(2,1)S(1)} %get-tuple-element.123.refs_0_.refs_4_), channel_id=1, source_target_pairs={{0,1},{1,0},{2,3},{3,2},{4,5},{5,4},{6,7},{7,6},{8,9},{9,8},{10,11... | collective-permute-start | bytes 307208 | tf_op jit(solution)/shard_map/ppermute | solution.py:522
  81.2 5.7 %collective-permute-start.14 = (bf16[400,128]{1,0:T(8,128)(2,1)S(1)}, bf16[400,128]{1,0:T(8,128)(2,1)S(1)}, u32[]{:S(2)}, u32[]{:S(2)}) collective-permute-start(bf16[400,128]{1,0:T(8,128)(2,1)S(1)} %get-tuple-element.123.refs_0_.refs_4_), channel_id=1, source_target_pairs={{0,2},{1,3},{2,0},{3,1},{4,6},{5,7},{6,4},{7,5},{8,10},{9,11},{10,... | collective-permute-start | bytes 307208 | tf_op jit(solution)/shard_map/ppermute | solution.py:522
  82.5 5.7 %collective-permute-start.15 = (bf16[400,128]{1,0:T(8,128)(2,1)S(1)}, bf16[400,128]{1,0:T(8,128)(2,1)S(1)}, u32[]{:S(2)}, u32[]{:S(2)}) collective-permute-start(bf16[400,128]{1,0:T(8,128)(2,1)S(1)} %get-tuple-element.123.refs_0_.refs_4_), channel_id=1, source_target_pairs={{0,3},{1,2},{2,1},{3,0},{4,7},{5,6},{6,5},{7,4},{8,11},{9,10},{10,... | collective-permute-start | bytes 307208 | tf_op jit(solution)/shard_map/ppermute | solution.py:522
  89.6 19.9 %copy-start.39 = (f32[1,768]{1,0:T(1,128)S(1)}, f32[1,768]{1,0:T(1,128)}, u32[]{:S(2)}) copy-start(f32[1,768]{1,0:T(1,128)} %copy-done.38) | copy-start | bytes 9220
  89.6 19.9 %copy-start.46 = (s32[112]{0:T(128)S(1)}, s32[112]{0:T(128)}, u32[]{:S(2)}) copy-start(s32[112]{0:T(128)} %param.24) | copy-start | bytes 1348
  96.7 16.1 %collective-permute-start.26 = (bf16[960,128]{1,0:T(8,128)(2,1)}, bf16[960,128]{1,0:T(8,128)(2,1)S(1)}, u32[]{:S(2)}, u32[]{:S(2)}) collective-permute-start(bf16[960,128]{1,0:T(8,128)(2,1)} %copy-done.8), channel_id=1, source_target_pairs={{0,4},{4,0},{8,12},{12,8},{16,20},{20,16},{24,28},{28,24},{1,5},{5... | collective-permute-start | bytes 737288 | tf_op jit(solution)/shard_map/ppermute | solution.py:522
  98.0 1.9 %collective-permute-start.20 = (bf16[208,128]{1,0:T(8,128)(2,1)S(1)}, bf16[208,128]{1,0:T(8,128)(2,1)S(1)}, u32[]{:S(2)}, u32[]{:S(2)}) collective-permute-start(bf16[208,128]{1,0:T(8,128)(2,1)S(1)} %get-tuple-element.132.refs_0_), channel_id=1, source_target_pairs={{0,1},{1,0},{2,3},{3,2},{4,5},{5,4},{6,7},{7,6},{8,9},{9,8},{10,11... | collective-permute-start | bytes 159752 | tf_op jit(solution)/shard_map/ppermute | solution.py:522
  98.2 4.1 %collective-permute-start.21 = (bf16[208,128]{1,0:T(8,128)(2,1)S(1)}, bf16[208,128]{1,0:T(8,128)(2,1)S(1)}, u32[]{:S(2)}, u32[]{:S(2)}) collective-permute-start(bf16[208,128]{1,0:T(8,128)(2,1)S(1)} %get-tuple-element.132.refs_0_), channel_id=1, source_target_pairs={{0,2},{1,3},{2,0},{3,1},{4,6},{5,7},{6,4},{7,5},{8,10},{9,11},{10,... | collective-permute-start | bytes 159752 | tf_op jit(solution)/shard_map/ppermute | solution.py:522
  99.5 3.9 %collective-permute-start.22 = (bf16[208,128]{1,0:T(8,128)(2,1)S(1)}, bf16[208,128]{1,0:T(8,128)(2,1)S(1)}, u32[]{:S(2)}, u32[]{:S(2)}) collective-permute-start(bf16[208,128]{1,0:T(8,128)(2,1)S(1)} %get-tuple-element.132.refs_0_), channel_id=1, source_target_pairs={{0,3},{1,2},{2,1},{3,0},{4,7},{5,6},{6,5},{7,4},{8,11},{9,10},{10,... | collective-permute-start | bytes 159752 | tf_op jit(solution)/shard_map/ppermute | solution.py:522
  111.5 9.7 %collective-permute-start.23 = (bf16[864,128]{1,0:T(8,128)(2,1)S(1)}, bf16[864,128]{1,0:T(8,128)(2,1)S(1)}, u32[]{:S(2)}, u32[]{:S(2)}) collective-permute-start(bf16[864,128]{1,0:T(8,128)(2,1)S(1)} %get-tuple-element.145.refs_0_.refs_4_), channel_id=1, source_target_pairs={{0,8},{4,12},{8,16},{12,20},{16,24},{20,28},{24,0},{28,4},{1,9},{5... | collective-permute-start | bytes 663560 | tf_op jit(solution)/shard_map/ppermute | solution.py:538
  112.9 15.2 %collective-permute-start.28 = (bf16[1536,128]{1,0:T(8,128)(2,1)S(1)}, bf16[1536,128]{1,0:T(8,128)(2,1)S(1)}, u32[]{:S(2)}, u32[]{:S(2)}) collective-permute-start(bf16[1536,128]{1,0:T(8,128)(2,1)S(1)} %shard_map.216.refs_0_), channel_id=1, source_target_pairs={{0,2},{1,3},{2,0},{3,1},{4,6},{5,7},{6,4},{7,5},{8,10},{9,11},{10,... | collective-permute-start | bytes 1179656 | tf_op jit(solution)/shard_map/ppermute | solution.py:522
  121.2 6.9 %collective-permute-start.29 = (bf16[864,128]{1,0:T(8,128)(2,1)S(1)}, bf16[864,128]{1,0:T(8,128)(2,1)S(1)}, u32[]{:S(2)}, u32[]{:S(2)}) collective-permute-start(bf16[864,128]{1,0:T(8,128)(2,1)S(1)} %collective-permute-done.23.refs_1_.refs_5_), channel_id=1, source_target_pairs={{0,4},{4,0},{8,12},{12,8},{16,20},{20,16},{24,28},{28,24},{1,5},{5... | collective-permute-start | bytes 663560 | tf_op jit(solution)/shard_map/ppermute | solution.py:522
  121.8 11.4 %collective-permute-start.24 = (bf16[864,128]{1,0:T(8,128)(2,1)S(1)}, bf16[864,128]{1,0:T(8,128)(2,1)S(1)}, u32[]{:S(2)}, u32[]{:S(2)}) collective-permute-start(bf16[864,128]{1,0:T(8,128)(2,1)S(1)} %get-tuple-element.145.refs_0_.refs_4_), channel_id=1, source_target_pairs={{0,16},{4,20},{8,24},{12,28},{16,0},{20,4},{24,8},{28,12},{1,17},{... | collective-permute-start | bytes 663560 | tf_op jit(solution)/shard_map/ppermute | solution.py:538
  122.1 12.5 %collective-permute-start.25 = (bf16[864,128]{1,0:T(8,128)(2,1)S(1)}, bf16[864,128]{1,0:T(8,128)(2,1)S(1)}, u32[]{:S(2)}, u32[]{:S(2)}) collective-permute-start(bf16[864,128]{1,0:T(8,128)(2,1)S(1)} %get-tuple-element.145.refs_0_.refs_4_), channel_id=1, source_target_pairs={{0,24},{4,28},{8,0},{12,4},{16,8},{20,12},{24,16},{28,20},{1,25},{... | collective-permute-start | bytes 663560 | tf_op jit(solution)/shard_map/ppermute | solution.py:538
  123.8 21.7 %collective-permute-start.27 = (bf16[1536,128]{1,0:T(8,128)(2,1)S(1)}, bf16[1536,128]{1,0:T(8,128)(2,1)S(1)}, u32[]{:S(2)}, u32[]{:S(2)}) collective-permute-start(bf16[1536,128]{1,0:T(8,128)(2,1)S(1)} %shard_map.216.refs_0_), channel_id=1, source_target_pairs={{0,1},{1,0},{2,3},{3,2},{4,5},{5,4},{6,7},{7,6},{8,9},{9,8},{10,11... | collective-permute-start | bytes 1179656 | tf_op jit(solution)/shard_map/ppermute | solution.py:522
  128.1 17.3 %collective-permute-start.30 = (bf16[1536,128]{1,0:T(8,128)(2,1)S(1)}, bf16[1536,128]{1,0:T(8,128)(2,1)S(1)}, u32[]{:S(2)}, u32[]{:S(2)}) collective-permute-start(bf16[1536,128]{1,0:T(8,128)(2,1)S(1)} %collective-permute-done.28.refs_2_), channel_id=1, source_target_pairs={{0,1},{1,0},{2,3},{3,2},{4,5},{5,4},{6,7},{7,6},{8,9},{9,8},{10,11... | collective-permute-start | bytes 1179656 | tf_op jit(solution)/shard_map/ppermute | solution.py:522
  128.1 8.1 %collective-permute-start.31 = (bf16[864,128]{1,0:T(8,128)(2,1)S(1)}, bf16[864,128]{1,0:T(8,128)(2,1)S(1)}, u32[]{:S(2)}, u32[]{:S(2)}) collective-permute-start(bf16[864,128]{1,0:T(8,128)(2,1)S(1)} %get-tuple-element.145.refs_0_.refs_4_), channel_id=1, source_target_pairs={{0,4},{4,0},{8,12},{12,8},{16,20},{20,16},{24,28},{28,24},{1,5},{5... | collective-permute-start | bytes 663560 | tf_op jit(solution)/shard_map/ppermute | solution.py:522
  133.1 8.3 %collective-permute-start.32 = (bf16[864,128]{1,0:T(8,128)(2,1)S(1)}, bf16[864,128]{1,0:T(8,128)(2,1)S(1)}, u32[]{:S(2)}, u32[]{:S(2)}) collective-permute-start(bf16[864,128]{1,0:T(8,128)(2,1)S(1)} %collective-permute-done.24.refs_2_.refs_6_), channel_id=1, source_target_pairs={{0,4},{4,0},{8,12},{12,8},{16,20},{20,16},{24,28},{28,24},{1,5},{5... | collective-permute-start | bytes 663560 | tf_op jit(solution)/shard_map/ppermute | solution.py:522
  134.5 10.9 %collective-permute-start.33 = (bf16[864,128]{1,0:T(8,128)(2,1)S(1)}, bf16[864,128]{1,0:T(8,128)(2,1)S(1)}, u32[]{:S(2)}, u32[]{:S(2)}) collective-permute-start(bf16[864,128]{1,0:T(8,128)(2,1)S(1)} %collective-permute-done.25.refs_3_.refs_7_), channel_id=1, source_target_pairs={{0,4},{4,0},{8,12},{12,8},{16,20},{20,16},{24,28},{28,24},{1,5},{5... | collective-permute-start | bytes 663560 | tf_op jit(solution)/shard_map/ppermute | solution.py:522
  146.4 3.4 %collective-permute-start.34 = (bf16[208,128]{1,0:T(8,128)(2,1)S(1)}, bf16[208,128]{1,0:T(8,128)(2,1)S(1)}, u32[]{:S(2)}, u32[]{:S(2)}) collective-permute-start(bf16[208,128]{1,0:T(8,128)(2,1)S(1)} %get-tuple-element.161), channel_id=1, source_target_pairs={{0,1},{1,0},{2,3},{3,2},{4,5},{5,4},{6,7},{7,6},{8,9},{9,8},{10,11... | collective-permute-start | bytes 159752 | tf_op jit(solution)/shard_map/ppermute | solution.py:522
  146.5 10.3 %collective-permute-start.37 = (bf16[208,192]{1,0:T(8,128)(2,1)S(1)}, bf16[208,192]{1,0:T(8,128)(2,1)S(1)}, u32[]{:S(2)}, u32[]{:S(2)}) collective-permute-start(bf16[208,192]{1,0:T(8,128)(2,1)S(1)} %get-tuple-element.165), channel_id=1, source_target_pairs={{0,1},{1,0},{2,3},{3,2},{4,5},{5,4},{6,7},{7,6},{8,9},{9,8},{10,11... | collective-permute-start | bytes 239624 | tf_op jit(solution)/shard_map/ppermute | solution.py:522
  147.0 9.8 %collective-permute-start.38 = (bf16[208,192]{1,0:T(8,128)(2,1)S(1)}, bf16[208,192]{1,0:T(8,128)(2,1)S(1)}, u32[]{:S(2)}, u32[]{:S(2)}) collective-permute-start(bf16[208,192]{1,0:T(8,128)(2,1)S(1)} %get-tuple-element.166), channel_id=1, source_target_pairs={{0,2},{1,3},{2,0},{3,1},{4,6},{5,7},{6,4},{7,5},{8,10},{9,11},{10,... | collective-permute-start | bytes 239624 | tf_op jit(solution)/shard_map/ppermute | solution.py:522
  148.4 8.4 %collective-permute-start.39 = (bf16[208,192]{1,0:T(8,128)(2,1)S(1)}, bf16[208,192]{1,0:T(8,128)(2,1)S(1)}, u32[]{:S(2)}, u32[]{:S(2)}) collective-permute-start(bf16[208,192]{1,0:T(8,128)(2,1)S(1)} %get-tuple-element.167), channel_id=1, source_target_pairs={{0,3},{1,2},{2,1},{3,0},{4,7},{5,6},{6,5},{7,4},{8,11},{9,10},{10,... | collective-permute-start | bytes 239624 | tf_op jit(solution)/shard_map/ppermute | solution.py:522
  148.5 7.5 %collective-permute-start.35 = (bf16[208,128]{1,0:T(8,128)(2,1)S(1)}, bf16[208,128]{1,0:T(8,128)(2,1)S(1)}, u32[]{:S(2)}, u32[]{:S(2)}) collective-permute-start(bf16[208,128]{1,0:T(8,128)(2,1)S(1)} %get-tuple-element.162), channel_id=1, source_target_pairs={{0,2},{1,3},{2,0},{3,1},{4,6},{5,7},{6,4},{7,5},{8,10},{9,11},{10,... | collective-permute-start | bytes 159752 | tf_op jit(solution)/shard_map/ppermute | solution.py:522
  149.9 6.1 %collective-permute-start.36 = (bf16[208,128]{1,0:T(8,128)(2,1)S(1)}, bf16[208,128]{1,0:T(8,128)(2,1)S(1)}, u32[]{:S(2)}, u32[]{:S(2)}) collective-permute-start(bf16[208,128]{1,0:T(8,128)(2,1)S(1)} %get-tuple-element.163), channel_id=1, source_target_pairs={{0,3},{1,2},{2,1},{3,0},{4,7},{5,6},{6,5},{7,4},{8,11},{9,10},{10,... | collective-permute-start | bytes 159752 | tf_op jit(solution)/shard_map/ppermute | solution.py:522
  (44 other events, 193.7 us)

commit v7 on v6

--- a/solution.py
+++ b/solution.py
@@ -599,10 +599,9 @@
     in_rows = exchange(send_rows)
     if direct:
         (early,) = after([saved], in_rows)
-        in_rows = around_large(in_rows)
-        behind1, behind3 = step(early, 2), step(early, 6)
-        beside = swap(early, 1, "expert", n_e)
-        in_rows = after(in_rows, behind1, behind3, beside)
+        behind1, beside = step(early, 2), swap(early, 1, "expert", n_e)
+        (far,) = after([swap(in_rows, 2)], behind1, beside)
+        in_rows = [in_rows, swap(in_rows, 1), far, swap(far, 1)]
     else:
         in_rows = around_large(in_rows)
 
@@ -622,7 +621,8 @@
     got = swap(mate, 1)
     if direct:
         early, behind1 = after([early, behind1], mate)
-        behind2, beside1 = step(early, 4), swap(behind1, 1, "expert", n_e)
+        behind2, behind3 = step(behind1, 2), step(early, 6)
+        beside1 = swap(behind1, 1, "expert", n_e)
     (across,) = run(pair_sum_kernel, [((rows, 2 * width), bf16)], across, got)
     far = swap(across, 2)
     up_grad, down_grad = run(
@@ -630,11 +630,10 @@
         [(up_weight.shape, f32), (down_weight.shape, f32)],
         *after([u, z, de, da], across),
     )
-    token_packs = around(after([token_pack], up_grad)[0])
+    token_packs = around(after([token_pack], across)[0])
     if direct:
-        beside3 = swap(after([behind3], across)[0], 1, "expert", n_e)
-        (far,) = after([far], behind2, beside1, beside3)
-    (far,) = after([far], up_grad)
+        (far,) = after([far], behind2, behind3, beside1)
+    (far,) = after([far], up_grad, *token_packs[1:])
     (summed,) = run(expert_sum_kernel, [((rows, 2 * width), bf16)], own, got, far)
     back = exchange(summed)
     output, back_pack = run(
@@ -645,7 +644,9 @@
     )
     back_packs = around(back_pack)
     if direct:
-        beside2 = swap(after([behind2], back_pack)[0], 1, "expert", n_e)
+        beside2, beside3 = (
+            swap(v, 1, "expert", n_e) for v in after([behind2, behind3], back_pack)
+        )
         saved_all = [saved, behind1, behind2, behind3, beside, beside1, beside2, beside3]
 
     c0, c1, c2, c3, dr1, d_proj, d_att, d_logits, gain_terms, d_scores = run(
@@ -677,10 +678,20 @@
         scratch=[pltpu.VMEM((model, tok), f32), padded],
     )
     if direct:
-        lasts = [last] + [step(last, k) for k in (2, 4, 6)]
+        lasts = [last, step(last, 2)]
+        lasts += [step(lasts[1], 2), step(last, 6)]
+        across1 = swap(lasts[1], 1, "expert", n_e)
+        c1, c2, c3 = after([c1, c2, c3], across1)
+    got = [swap(c, k) for k, c in ((1, c1), (2, c2), (3, c3))]
+    (input_grad,) = run(
+        functools.partial(input_grad_kernel, n_t=n_t),
+        [((width, tok), f32)],
+        c0, *got, dr1, inv1, x, gain1,
+        fetch=(6,),
+    )
     if direct:
         (att,) = run(
-            join_kernel, [((n_e * width, tok), bf16)], *after(saved_all, last)
+            join_kernel, [((n_e * width, tok), bf16)], *after(saved_all, lasts[1])
         )
         half = n_e // 2
         (part,) = run(
@@ -688,7 +699,10 @@
             [((inner, model), f32)],
             *lasts, *saved_all[:half],
         )
-        lasts = lasts + [swap(v, 1, "expert", n_e) for v in lasts]
+        lasts[2:] = after(lasts[2:], input_grad)
+        lasts += [
+            across1 if j == 1 else swap(v, 1, "expert", n_e) for j, v in enumerate(lasts)
+        ]
         atts = [att, swap(att, 1), swap(att, 2)]
         atts.append(swap(after(atts[2:], lasts[half + 1])[0], 1))
         lasts[half:] = after(lasts[half:], part)
@@ -699,7 +713,7 @@
             *atts, *lasts,
         )
         got = [swap(q, k) for k, q in ((1, q1), (2, q2), (3, q3))]
-        c1, c2, c3, part = after([c1, c2, c3, part], own)
+        (part,) = after([part], own)
         (qkv_grad,) = run(
             functools.partial(qkv_grad_kernel, count=half, inner=inner),
             [((inner, model), f32)],
@@ -729,13 +743,6 @@
         second = small[experts]
         router_grad = small[:experts]
         rel_grad = small[experts + 2:experts + 2 + n_heads, :n_buckets]
-    got = [swap(c, k) for k, c in ((1, c1), (2, c2), (3, c3))]
-    (input_grad,) = run(
-        functools.partial(input_grad_kernel, n_t=n_t),
-        [((width, tok), f32)],
-        c0, *got, dr1, inv1, x, gain1,
-        fetch=(6,),
-    )
     return (
         output.T,
         input_grad.T,

time: 161 us -> 148 us (0.919); the launches traced: 158 us -> 148 us
  blocking collectives: 16.8 us -> 29.7 us
  local copies, waits for them, and re-layouts: 16.1 us -> 5.64 us
  starting transfers between devices: 37.9 us -> 32.2 us
  waiting for transfers between devices: 61.7 us -> 56.7 us
  Pallas kernels: 24.2 us -> 22.5 us
    all_to_all x1 -> x2, blocking collectives: 16.8 us -> 29.7 us  [exchange(): v = lax.all_to_all(v, 'expert', split_axis=0, concat_axis=0, tiled=True)]
    unnamed x102 -> x32, local copies, waits for them, and re-layouts: 15.4 us -> 4.95 us
    ppermute x6, waiting for transfers between devices: 26.4 us -> 16.3 us  [step(): return lax.ppermute(v, 'expert', [(i, (i + k) % n_e) for i in range(n_e)])]
    ppermute x34, waiting for transfers between devices: 34.6 us -> 40.4 us  [swap(): return lax.ppermute(v, axis, [(i, i ^ k) for i in range(n)])]
    all_to_all x1 -> x0, starting transfers between devices: 4.04 us -> none  [exchange(): v = lax.all_to_all(v, 'expert', split_axis=0, concat_axis=0, tiled=True)]
    pallas_call x17, Pallas kernels: 24.2 us -> 22.5 us  [run(): pl.pallas_call(whole, out_shape=[jax.ShapeDtypeStruct(s, d) for s, d in o...]
  transfers between devices with their start and end apart: 41 -> 40, of which waited for: 18 -> 21; matrix products, arithmetic and copies ran while one was open for 0% -> 0% of each run, Pallas kernels for 9% -> 9%
where the time goes in v7:
time: 148 us
  waiting for transfers between devices  56.7 us (38%)
  starting transfers between devices  32.2 us (22%)
  blocking collectives  29.7 us (20%)
  Pallas kernels  22.5 us (15%)
  local copies, waits for them, and re-layouts  5.64 us (4%)
    ppermute x34, waiting for transfers between devices, swap(): return lax.ppermute(v, axis, [(i, i ^ k) for i in range(n)])  40.4 us
    all_to_all x2, blocking collectives, exchange(): v = lax.all_to_all(v, 'expert', split_axis=0, concat_axis=0, tiled=True)  29.7 us
    ppermute x34, starting transfers between devices, swap(): return lax.ppermute(v, axis, [(i, i ^ k) for i in range(n)])  24.5 us
    pallas_call x17, Pallas kernels, run(): pl.pallas_call(whole, out_shape=[jax.ShapeDtypeStruct(s, d) for s, d in o...  22.5 us
    ppermute x6, waiting for transfers between devices, step(): return lax.ppermute(v, 'expert', [(i, (i + k) % n_e) for i in range(n_e)])  16.3 us
    ppermute x6, starting transfers between devices, step(): return lax.ppermute(v, 'expert', [(i, (i + k) % n_e) for i in range(n_e)])  7.64 us
    unnamed x32, local copies, waits for them, and re-layouts  4.95 us
  transfers between devices with their start and end apart: 40, of which 21 were waited for; matrix products, arithmetic and copies ran while one was open for 0% of the time, Pallas kernels for 9%

profile of v7, /device:TPU:0, one launch (start us, length us, event | category | flops | bytes accessed | tf_op | source)
XLA Modules:
  0.0 147.6 jit_solution(6183883384187311340)
XLA Ops:
  1.2 2.6 %collective-permute-start.1 = (bf16[192,128]{1,0:T(8,128)(2,1)}, bf16[192,128]{1,0:T(8,128)(2,1)S(1)}, u32[]{:S(2)}, u32[]{:S(2)}) collective-permute-start(bf16[192,128]{1,0:T(8,128)(2,1)} %bitcast.29), channel_id=1, source_target_pairs={{0,2},{1,3},{2,0},{3,1},{4,6},{5,7},{6,4},{7,5},{8,10},{9,11},{10,... | collective-permute-start | bytes 147464 | tf_op jit(solution)/shard_map/ppermute | solution.py:522
  8.5 1.2 copy-done
  10.4 1.9 %shard_map.205 = (f32[192,128]{1,0:T(8,128)S(1)}, bf16[192,128]{1,0:T(8,128)(2,1)S(1)}, bf16[192,128]{1,0:T(8,128)(2,1)S(1)}, bf16[192,128]{1,0:T(8,128)(2,1)S(1...) custom-call(bf16[192,128]{1,0:T(8,128)(2,1)S(1)} %bitcast.31, ...), custom_call_target="tpu_custom_call" | custom-call | bytes 2412032 | tf_op jit(solution)/shard_map/pallas_call | solution.py:67
  12.6 2.0 %collective-permute-start.4 = (bf16[192,128]{1,0:T(8,128)(2,1)S(1)}, bf16[192,128]{1,0:T(8,128)(2,1)S(1)}, u32[]{:S(2)}, u32[]{:S(2)}) collective-permute-start(bf16[192,128]{1,0:T(8,128)(2,1)S(1)} %get-tuple-element.97), channel_id=1, source_target_pairs={{0,2},{1,3},{2,0},{3,1},{4,6},{5,7},{6,4},{7,5},{8,10},{9,11},{10,... | collective-permute-start | bytes 147464 | tf_op jit(solution)/shard_map/ppermute | solution.py:522
  15.3 1.4 collective-permute-done.4.refs_2_
  16.7 1.8 %collective-permute-done.5.refs_3_ = bf16[192,128]{1,0:T(8,128)(2,1)S(1)} collective-permute-done((bf16[192,128]{1,0:T(8,128)(2,1)S(1)}, bf16[192,128]{1,0:T(8,128)(2,1)S(1)}, u32[]{:S(2)}, u32[]{:S(2)}) %collective-permute-start.5) | collective-permute-done | bytes 49184 | tf_op jit(solution)/shard_map/ppermute | solution.py:522
  19.3 16.8 %all_to_all.10 = bf16[8,40,400]{2,1,0:T(8,128)(2,1)S(1)} all-to-all(bf16[8,40,400]{2,1,0:T(8,128)(2,1)S(1)} %bitcast.34), channel_id=1, replica_groups=mesh['expert'=8,'tensor'=4] {'expert'}, dimensions={0} | all-to-all | bytes 512000 | tf_op jit(solution)/shard_map/all_to_all | solution.py:534
  38.0 6.8 %collective-permute-done.8.refs_1_.refs_5_ = bf16[960,128]{1,0:T(8,128)(2,1)S(1)} collective-permute-done((bf16[960,128]{1,0:T(8,128)(2,1)S(1)}, bf16[960,128]{1,0:T(8,128)(2,1)S(1)}, u32[]{:S(2)}, u32[]{:S(2)}) %collective-permute-start.8) | collective-permute-done | bytes 245792 | tf_op jit(solution)/shard_map/ppermute | solution.py:538
  44.8 1.6 %collective-permute-done.10.refs_3_ = bf16[320,400]{1,0:T(8,128)(2,1)S(1)} collective-permute-done((bf16[320,400]{1,0:T(8,128)(2,1)S(1)}, bf16[320,400]{1,0:T(8,128)(2,1)S(1)}, u32[]{:S(2)}, u32[]{:S(2)}) %collective-permute-start.10) | collective-permute-done | bytes 256032 | tf_op jit(solution)/shard_map/ppermute | solution.py:522
  46.5 3.0 %shard_map.208 = (bf16[320,384]{1,0:T(8,128)(2,1)S(1)}, bf16[320,384]{1,0:T(8,128)(2,1)S(1)}, bf16[640,384]{1,0:T(8,128)(2,1)S(1)}, bf16[320,768]{1,0:T(8,128)(2...) custom-call(bf16[320,400]{1,0:T(8,128)(2,1)S(1)} %bitcast.25, ...), custom_call_target="tpu_custom_call" | custom-call | bytes 6332416 | tf_op jit(solution)/shard_map/pallas_call | solution.py:67
  49.8 3.7 %collective-permute-start.17 = (bf16[960,128]{1,0:T(8,128)(2,1)S(1)}, bf16[960,128]{1,0:T(8,128)(2,1)S(1)}, u32[]{:S(2)}, u32[]{:S(2)}) collective-permute-start(bf16[960,128]{1,0:T(8,128)(2,1)S(1)} %get-tuple-element.147.refs_8_.refs_0_.refs_4_), channel_id=1, source_target_pairs={{0,24},{4,28},{8,0},{12,4},{16,8},{20,12},{24,16},{28,20},{1,25},{... | collective-permute-start | bytes 737288 | tf_op jit(solution)/shard_map/ppermute | solution.py:538
  53.5 1.2 collective-permute-start.18
  54.8 1.2 collective-permute-start.15
  56.0 4.3 %collective-permute-done.16.refs_2_.refs_6_ = bf16[960,128]{1,0:T(8,128)(2,1)S(1)} collective-permute-done((bf16[960,128]{1,0:T(8,128)(2,1)S(1)}, bf16[960,128]{1,0:T(8,128)(2,1)S(1)}, u32[]{:S(2)}, u32[]{:S(2)}) %collective-permute-start.16) | collective-permute-done | bytes 245792 | tf_op jit(solution)/shard_map/ppermute | solution.py:538
  60.3 1.3 collective-permute-start.13
  61.6 1.6 %collective-permute-done.17.refs_3_.refs_7_ = bf16[960,128]{1,0:T(8,128)(2,1)S(1)} collective-permute-done((bf16[960,128]{1,0:T(8,128)(2,1)S(1)}, bf16[960,128]{1,0:T(8,128)(2,1)S(1)}, u32[]{:S(2)}, u32[]{:S(2)}) %collective-permute-start.17) | collective-permute-done | bytes 245792 | tf_op jit(solution)/shard_map/ppermute | solution.py:538
  63.7 3.2 %shard_map.210 = (f32[1,768,768]{2,1,0:T(8,128)}, f32[1,768,768]{2,1,0:T(8,128)}) custom-call(bf16[320,768]{1,0:T(8,128)(2,1)S(1)} %get-tuple-element.120.refs_0_, bf16[320,768]{1,0:T(8,128)(2,1)S(1)} %get-tuple-element.121.refs_1_, bf16[320,768]{1,0:T(8,128)(2,1)S(1)} %get-tuple-element.122.refs_2_, bf16[320,768]{1,0:T(8,128)(2,1)S(1)} %get-tuple-element.123.refs_3_), custom_call_target="tpu_custom_call" | custom-call | bytes 6684672 | tf_op jit(solution)/shard_map/pallas_call | solution.py:67
  66.9 1.4 collective-permute-done.14.refs_3_.refs_7_
  68.3 12.8 %all_to_all.11 = bf16[8,40,384]{2,1,0:T(8,128)(2,1)S(1)} all-to-all(bf16[8,40,384]{2,1,0:T(8,128)(2,1)S(1)} %bitcast.26), channel_id=1, replica_groups=mesh['expert'=8,'tensor'=4] {'expert'}, dimensions={0} | all-to-all | bytes 491520 | tf_op jit(solution)/shard_map/all_to_all | solution.py:534
  81.2 1.0 shard_map.212
  82.3 1.2 collective-permute-start.20
  84.1 1.3 collective-permute-start.27
  87.3 2.5 %shard_map.213 = (bf16[208,128]{1,0:T(8,128)(2,1)S(1)}, bf16[208,128]{1,0:T(8,128)(2,1)S(1)}, bf16[208,128]{1,0:T(8,128)(2,1)S(1)}, bf16[208,128]{1,0:T(8,128)(2...) custom-call(bf16[208,128]{1,0:T(8,128)(2,1)S(1)} %get-tuple-element., ...), custom_call_target="tpu_custom_call" | custom-call | bytes 3313664 | tf_op jit(solution)/shard_map/pallas_call | solution.py:67
  89.9 2.0 %shard_map.214 = (f32[16,768]{1,0:T(8,128)}, bf16[864,128]{1,0:T(8,128)(2,1)S(1)}) custom-call(bf16[400,128]{1,0:T(8,128)(2,1)S(1)} %get-tuple-element.110.refs_0_.refs_4_, bf16[400,128]{1,0:T(8,128)(2,1)S(1)} %collective-permute-done.12.refs_1_.refs_5_, bf16[400,128]{1,0:T(8,128)(2,1)S(1)} %collective-permute-done.13.refs_2_.refs_6_, ...), custom_call_target="tpu_custom_call" | custom-call | bytes 2656704 | tf_op jit(solution)/shard_map/pallas_call | solution.py:67
  91.9 1.0 collective-permute-start.22
  93.0 4.6 %collective-permute-done.28.refs_7_ = bf16[960,128]{1,0:T(8,128)(2,1)S(1)} collective-permute-done((bf16[960,128]{1,0:T(8,128)(2,1)S(1)}, bf16[960,128]{1,0:T(8,128)(2,1)S(1)}, u32[]{:S(2)}, u32[]{:S(2)}) %collective-permute-start.28) | collective-permute-done | bytes 245792 | tf_op jit(solution)/shard_map/ppermute | solution.py:522
  97.6 3.7 %collective-permute-done.22.refs_1_.refs_5_ = bf16[864,128]{1,0:T(8,128)(2,1)S(1)} collective-permute-done((bf16[864,128]{1,0:T(8,128)(2,1)S(1)}, bf16[864,128]{1,0:T(8,128)(2,1)S(1)}, u32[]{:S(2)}, u32[]{:S(2)}) %collective-permute-start.22) | collective-permute-done | bytes 221216 | tf_op jit(solution)/shard_map/ppermute | solution.py:538
  101.3 1.3 collective-permute-start.30
  102.5 1.3 collective-permute-start.23
  103.8 2.0 %collective-permute-start.32 = (bf16[864,128]{1,0:T(8,128)(2,1)S(1)}, bf16[864,128]{1,0:T(8,128)(2,1)S(1)}, u32[]{:S(2)}, u32[]{:S(2)}) collective-permute-start(bf16[864,128]{1,0:T(8,128)(2,1)S(1)} %collective-permute-done.22.refs_1_.refs_5_), channel_id=1, source_target_pairs={{0,8},{4,12},{8,16},{12,20},{16,24},{20,28},{24,0},{28,4},{1,9},{5... | collective-permute-start | bytes 663560 | tf_op jit(solution)/shard_map/ppermute | solution.py:538
  105.9 3.1 %collective-permute-done.23.refs_9_.refs_1_ = bf16[864,128]{1,0:T(8,128)(2,1)S(1)} collective-permute-done((bf16[864,128]{1,0:T(8,128)(2,1)S(1)}, bf16[864,128]{1,0:T(8,128)(2,1)S(1)}, u32[]{:S(2)}, u32[]{:S(2)}) %collective-permute-start.23) | collective-permute-done | bytes 221216 | tf_op jit(solution)/shard_map/ppermute | solution.py:522
  108.9 2.7 %collective-permute-done.30.refs_2_ = bf16[1536,128]{1,0:T(8,128)(2,1)S(1)} collective-permute-done((bf16[1536,128]{1,0:T(8,128)(2,1)S(1)}, bf16[1536,128]{1,0:T(8,128)(2,1)S(1)}, u32[]{:S(2)}, u32[]{:S(2)}) %collective-permute-start.30) | collective-permute-done | bytes 393248 | tf_op jit(solution)/shard_map/ppermute | solution.py:522
  112.2 1.3 collective-permute-done.24.refs_1_
  113.5 1.2 collective-permute-start.25
  114.7 2.9 %collective-permute-done.25.refs_2_ = bf16[208,128]{1,0:T(8,128)(2,1)S(1)} collective-permute-done((bf16[208,128]{1,0:T(8,128)(2,1)S(1)}, bf16[208,128]{1,0:T(8,128)(2,1)S(1)}, u32[]{:S(2)}, u32[]{:S(2)}) %collective-permute-start.25) | collective-permute-done | bytes 53280 | tf_op jit(solution)/shard_map/ppermute | solution.py:522
  117.6 3.9 %collective-permute-done.26.refs_3_ = bf16[208,128]{1,0:T(8,128)(2,1)S(1)} collective-permute-done((bf16[208,128]{1,0:T(8,128)(2,1)S(1)}, bf16[208,128]{1,0:T(8,128)(2,1)S(1)}, u32[]{:S(2)}, u32[]{:S(2)}) %collective-permute-start.26) | collective-permute-done | bytes 53280 | tf_op jit(solution)/shard_map/ppermute | solution.py:522
  121.5 1.3 collective-permute-start.34
  124.4 1.3 collective-permute-start.36
  125.7 1.1 shard_map.217.refs_8_
  126.8 3.0 %collective-permute-done.34.refs_8_.refs_0_ = bf16[864,128]{1,0:T(8,128)(2,1)S(1)} collective-permute-done((bf16[864,128]{1,0:T(8,128)(2,1)S(1)}, bf16[864,128]{1,0:T(8,128)(2,1)S(1)}, u32[]{:S(2)}, u32[]{:S(2)}) %collective-permute-start.34) | collective-permute-done | bytes 221216 | tf_op jit(solution)/shard_map/ppermute | solution.py:522
  129.8 4.7 %collective-permute-done.35.refs_10_.refs_2_ = bf16[864,128]{1,0:T(8,128)(2,1)S(1)} collective-permute-done((bf16[864,128]{1,0:T(8,128)(2,1)S(1)}, bf16[864,128]{1,0:T(8,128)(2,1)S(1)}, u32[]{:S(2)}, u32[]{:S(2)}) %collective-permute-start.35) | collective-permute-done | bytes 221216 | tf_op jit(solution)/shard_map/ppermute | solution.py:522
  134.6 3.6 %collective-permute-done.36.refs_11_.refs_3_ = bf16[864,128]{1,0:T(8,128)(2,1)S(1)} collective-permute-done((bf16[864,128]{1,0:T(8,128)(2,1)S(1)}, bf16[864,128]{1,0:T(8,128)(2,1)S(1)}, u32[]{:S(2)}, u32[]{:S(2)}) %collective-permute-start.36) | collective-permute-done | bytes 221216 | tf_op jit(solution)/shard_map/ppermute | solution.py:522
  138.2 1.0 shard_map.218
  139.5 1.6 %collective-permute-start.39 = (bf16[208,192]{1,0:T(8,128)(2,1)S(1)}, bf16[208,192]{1,0:T(8,128)(2,1)S(1)}, u32[]{:S(2)}, u32[]{:S(2)}) collective-permute-start(bf16[208,192]{1,0:T(8,128)(2,1)S(1)} %get-tuple-element.165), channel_id=1, source_target_pairs={{0,3},{1,2},{2,1},{3,0},{4,7},{5,6},{6,5},{7,4},{8,11},{9,10},{10,... | collective-permute-start | bytes 239624 | tf_op jit(solution)/shard_map/ppermute | solution.py:522
  141.2 2.3 %shard_map.220 = f32[576,768]{1,0:T(8,128)} custom-call(bf16[864,128]{1,0:T(8,128)(2,1)S(1)} %collective-permute-done.34.refs_8_.refs_0_, bf16[864,128]{1,0:T(8,128)(2,1)S(1)} %collective-permute-done.23.refs_9_.refs_1_, bf16[864,128]{1,0:T(8,128)(2,1)S(1)} %collective-permute-done.35.refs_10_.refs_2_, ...), custom_call_target="tpu_custom_call" | custom-call | bytes 5406720 | tf_op jit(solution)/shard_map/pallas_call | solution.py:67
  143.5 1.6 %collective-permute-done.38.refs_2_ = bf16[208,192]{1,0:T(8,128)(2,1)S(1)} collective-permute-done((bf16[208,192]{1,0:T(8,128)(2,1)S(1)}, bf16[208,192]{1,0:T(8,128)(2,1)S(1)}, u32[]{:S(2)}, u32[]{:S(2)}) %collective-permute-start.38) | collective-permute-done | bytes 79904 | tf_op jit(solution)/shard_map/ppermute | solution.py:522
  145.1 1.4 collective-permute-done.39.refs_3_
  146.5 1.1 shard_map.219
  (85 shorter events, 15.6 us)
Async XLA Ops:
  0.6 13.9 %copy-start.9 = (bf16[768,8]{0,1:T(8,128)(2,1)S(1)}, bf16[768,8]{0,1:T(8,128)(2,1)}, u32[]{:S(2)}) copy-start(bf16[768,8]{0,1:T(8,128)(2,1)} %param.19) | copy-start | bytes 36868
  0.7 7.8 %collective-permute-start = (bf16[192,128]{1,0:T(8,128)(2,1)}, bf16[192,128]{1,0:T(8,128)(2,1)S(1)}, u32[]{:S(2)}, u32[]{:S(2)}) collective-permute-start(bf16[192,128]{1,0:T(8,128)(2,1)} %bitcast.28), channel_id=1, source_target_pairs={{0,1},{1,0},{2,3},{3,2},{4,5},{5,4},{6,7},{7,6},{8,9},{9,8},{10,11... | collective-permute-start | bytes 147464 | tf_op jit(solution)/shard_map/ppermute | solution.py:522
  1.2 7.3 %collective-permute-start.1 = (bf16[192,128]{1,0:T(8,128)(2,1)}, bf16[192,128]{1,0:T(8,128)(2,1)S(1)}, u32[]{:S(2)}, u32[]{:S(2)}) collective-permute-start(bf16[192,128]{1,0:T(8,128)(2,1)} %bitcast.29), channel_id=1, source_target_pairs={{0,2},{1,3},{2,0},{3,1},{4,6},{5,7},{6,4},{7,5},{8,10},{9,11},{10,... | collective-permute-start | bytes 147464 | tf_op jit(solution)/shard_map/ppermute | solution.py:522
  3.8 4.7 %collective-permute-start.2 = (bf16[192,128]{1,0:T(8,128)(2,1)}, bf16[192,128]{1,0:T(8,128)(2,1)S(1)}, u32[]{:S(2)}, u32[]{:S(2)}) collective-permute-start(bf16[192,128]{1,0:T(8,128)(2,1)} %bitcast.30), channel_id=1, source_target_pairs={{0,3},{1,2},{2,1},{3,0},{4,7},{5,6},{6,5},{7,4},{8,11},{9,10},{10,... | collective-permute-start | bytes 147464 | tf_op jit(solution)/shard_map/ppermute | solution.py:522
  7.5 7.1 %copy-start.10 = (s32[128,2]{0,1:T(2,128)S(1)}, s32[128,2]{0,1:T(2,128)}, u32[]{:S(2)}) copy-start(s32[128,2]{0,1:T(2,128)} %param.22) | copy-start | bytes 3076
  7.5 11.1 %copy-start.7 = (bf16[128,192]{0,1:T(8,128)(2,1)S(1)}, bf16[128,192]{0,1:T(8,128)(2,1)}, u32[]{:S(2)}) copy-start(bf16[128,192]{0,1:T(8,128)(2,1)} %param.13) | copy-start | bytes 147460
  7.5 11.1 %copy-start.8 = (bf16[128,192]{0,1:T(8,128)(2,1)S(1)}, bf16[128,192]{0,1:T(8,128)(2,1)}, u32[]{:S(2)}) copy-start(bf16[128,192]{0,1:T(8,128)(2,1)} %param.25) | copy-start | bytes 147460
  10.4 36.0 %copy-start.4 = (bf16[1,768,768]{2,1,0:T(8,128)(2,1)S(1)}, bf16[1,768,768]{2,1,0:T(8,128)(2,1)}, u32[]{:S(2)}) copy-start(bf16[1,768,768]{2,1,0:T(8,128)(2,1)} %refs_4_.1) | copy-start | bytes 3538948
  10.4 36.0 %copy-start.5 = (bf16[1,768,768]{2,1,0:T(8,128)(2,1)S(1)}, bf16[1,768,768]{2,1,0:T(8,128)(2,1)}, u32[]{:S(2)}) copy-start(bf16[1,768,768]{2,1,0:T(8,128)(2,1)} %refs_5_.1) | copy-start | bytes 3538948
  12.4 2.9 %collective-permute-start.3 = (bf16[192,128]{1,0:T(8,128)(2,1)S(1)}, bf16[192,128]{1,0:T(8,128)(2,1)S(1)}, u32[]{:S(2)}, u32[]{:S(2)}) collective-permute-start(bf16[192,128]{1,0:T(8,128)(2,1)S(1)} %get-tuple-element.96), channel_id=1, source_target_pairs={{0,1},{1,0},{2,3},{3,2},{4,5},{5,4},{6,7},{7,6},{8,9},{9,8},{10,11... | collective-permute-start | bytes 147464 | tf_op jit(solution)/shard_map/ppermute | solution.py:522
  12.6 4.1 %collective-permute-start.4 = (bf16[192,128]{1,0:T(8,128)(2,1)S(1)}, bf16[192,128]{1,0:T(8,128)(2,1)S(1)}, u32[]{:S(2)}, u32[]{:S(2)}) collective-permute-start(bf16[192,128]{1,0:T(8,128)(2,1)S(1)} %get-tuple-element.97), channel_id=1, source_target_pairs={{0,2},{1,3},{2,0},{3,1},{4,6},{5,7},{6,4},{7,5},{8,10},{9,11},{10,... | collective-permute-start | bytes 147464 | tf_op jit(solution)/shard_map/ppermute | solution.py:522
  14.5 4.0 %collective-permute-start.5 = (bf16[192,128]{1,0:T(8,128)(2,1)S(1)}, bf16[192,128]{1,0:T(8,128)(2,1)S(1)}, u32[]{:S(2)}, u32[]{:S(2)}) collective-permute-start(bf16[192,128]{1,0:T(8,128)(2,1)S(1)} %get-tuple-element.98), channel_id=1, source_target_pairs={{0,3},{1,2},{2,1},{3,0},{4,7},{5,6},{6,5},{7,4},{8,11},{9,10},{10,... | collective-permute-start | bytes 147464 | tf_op jit(solution)/shard_map/ppermute | solution.py:522
  36.1 8.7 %collective-permute-start.7 = (bf16[320,400]{1,0:T(8,128)(2,1)S(1)}, bf16[320,400]{1,0:T(8,128)(2,1)S(1)}, u32[]{:S(2)}, u32[]{:S(2)}) collective-permute-start(bf16[320,400]{1,0:T(8,128)(2,1)S(1)} %bitcast.23), channel_id=1, source_target_pairs={{0,2},{1,3},{2,0},{3,1},{4,6},{5,7},{6,4},{7,5},{8,10},{9,11},{10,... | collective-permute-start | bytes 768008 | tf_op jit(solution)/shard_map/ppermute | solution.py:522
  36.8 8.0 %collective-permute-start.8 = (bf16[960,128]{1,0:T(8,128)(2,1)S(1)}, bf16[960,128]{1,0:T(8,128)(2,1)S(1)}, u32[]{:S(2)}, u32[]{:S(2)}) collective-permute-start(bf16[960,128]{1,0:T(8,128)(2,1)S(1)} %get-tuple-element.147.refs_8_.refs_0_.refs_4_), channel_id=1, source_target_pairs={{0,8},{4,12},{8,16},{12,20},{16,24},{20,28},{24,0},{28,4},{1,9},{5... | collective-permute-start | bytes 737288 | tf_op jit(solution)/shard_map/ppermute | solution.py:538
  37.6 7.3 %collective-permute-start.9 = (bf16[960,128]{1,0:T(8,128)(2,1)S(1)}, bf16[960,128]{1,0:T(8,128)(2,1)S(1)}, u32[]{:S(2)}, u32[]{:S(2)}) collective-permute-start(bf16[960,128]{1,0:T(8,128)(2,1)S(1)} %get-tuple-element.147.refs_8_.refs_0_.refs_4_), channel_id=1, source_target_pairs={{0,4},{4,0},{8,12},{12,8},{16,20},{20,16},{24,28},{28,24},{1,5},{5... | collective-permute-start | bytes 737288 | tf_op jit(solution)/shard_map/ppermute | solution.py:522
  38.0 6.8 %collective-permute-start.6 = (bf16[320,400]{1,0:T(8,128)(2,1)S(1)}, bf16[320,400]{1,0:T(8,128)(2,1)S(1)}, u32[]{:S(2)}, u32[]{:S(2)}) collective-permute-start(bf16[320,400]{1,0:T(8,128)(2,1)S(1)} %bitcast.24), channel_id=1, source_target_pairs={{0,1},{1,0},{2,3},{3,2},{4,5},{5,4},{6,7},{7,6},{8,9},{9,8},{10,11... | collective-permute-start | bytes 768008 | tf_op jit(solution)/shard_map/ppermute | solution.py:522
  44.8 1.6 %collective-permute-start.10 = (bf16[320,400]{1,0:T(8,128)(2,1)S(1)}, bf16[320,400]{1,0:T(8,128)(2,1)S(1)}, u32[]{:S(2)}, u32[]{:S(2)}) collective-permute-start(bf16[320,400]{1,0:T(8,128)(2,1)S(1)} %collective-permute-done.7.refs_2_), channel_id=1, source_target_pairs={{0,1},{1,0},{2,3},{3,2},{4,5},{5,4},{6,7},{7,6},{8,9},{9,8},{10,11... | collective-permute-start | bytes 768008 | tf_op jit(solution)/shard_map/ppermute | solution.py:522
  49.4 5.3 %collective-permute-start.11 = (bf16[640,384]{1,0:T(8,128)(2,1)S(1)}, bf16[640,384]{1,0:T(8,128)(2,1)S(1)}, u32[]{:S(2)}, u32[]{:S(2)}) collective-permute-start(bf16[640,384]{1,0:T(8,128)(2,1)S(1)} %get-tuple-element.109), channel_id=1, source_target_pairs={{0,1},{1,0},{2,3},{3,2},{4,5},{5,4},{6,7},{7,6},{8,9},{9,8},{10,11... | collective-permute-start | bytes 1474568 | tf_op jit(solution)/shard_map/ppermute | solution.py:522
  49.6 10.6 %collective-permute-start.16 = (bf16[960,128]{1,0:T(8,128)(2,1)S(1)}, bf16[960,128]{1,0:T(8,128)(2,1)S(1)}, u32[]{:S(2)}, u32[]{:S(2)}) collective-permute-start(bf16[960,128]{1,0:T(8,128)(2,1)S(1)} %collective-permute-done.8.refs_1_.refs_5_), channel_id=1, source_target_pairs={{0,8},{4,12},{8,16},{12,20},{16,24},{20,28},{24,0},{28,4},{1,9},{5... | collective-permute-start | bytes 737288 | tf_op jit(solution)/shard_map/ppermute | solution.py:538
  49.8 13.4 %collective-permute-start.17 = (bf16[960,128]{1,0:T(8,128)(2,1)S(1)}, bf16[960,128]{1,0:T(8,128)(2,1)S(1)}, u32[]{:S(2)}, u32[]{:S(2)}) collective-permute-start(bf16[960,128]{1,0:T(8,128)(2,1)S(1)} %get-tuple-element.147.refs_8_.refs_0_.refs_4_), channel_id=1, source_target_pairs={{0,24},{4,28},{8,0},{12,4},{16,8},{20,12},{24,16},{28,20},{1,25},{... | collective-permute-start | bytes 737288 | tf_op jit(solution)/shard_map/ppermute | solution.py:538
  53.5 13.4 %collective-permute-start.18 = (bf16[960,128]{1,0:T(8,128)(2,1)S(1)}, bf16[960,128]{1,0:T(8,128)(2,1)S(1)}, u32[]{:S(2)}, u32[]{:S(2)}) collective-permute-start(bf16[960,128]{1,0:T(8,128)(2,1)S(1)} %collective-permute-done.8.refs_1_.refs_5_), channel_id=1, source_target_pairs={{0,4},{4,0},{8,12},{12,8},{16,20},{20,16},{24,28},{28,24},{1,5},{5... | collective-permute-start | bytes 737288 | tf_op jit(solution)/shard_map/ppermute | solution.py:522
  54.8 12.1 %collective-permute-start.15 = (bf16[320,384]{1,0:T(8,128)(2,1)S(1)}, bf16[320,384]{1,0:T(8,128)(2,1)S(1)}, u32[]{:S(2)}, u32[]{:S(2)}) collective-permute-start(bf16[320,384]{1,0:T(8,128)(2,1)S(1)} %shard_map.209), channel_id=1, source_target_pairs={{0,2},{1,3},{2,0},{3,1},{4,6},{5,7},{6,4},{7,5},{8,10},{9,11},{10,... | collective-permute-start | bytes 737288 | tf_op jit(solution)/shard_map/ppermute | solution.py:522
  55.9 10.9 %collective-permute-start.12 = (bf16[400,128]{1,0:T(8,128)(2,1)S(1)}, bf16[400,128]{1,0:T(8,128)(2,1)S(1)}, u32[]{:S(2)}, u32[]{:S(2)}) collective-permute-start(bf16[400,128]{1,0:T(8,128)(2,1)S(1)} %get-tuple-element.110.refs_0_.refs_4_), channel_id=1, source_target_pairs={{0,1},{1,0},{2,3},{3,2},{4,5},{5,4},{6,7},{7,6},{8,9},{9,8},{10,11... | collective-permute-start | bytes 307208 | tf_op jit(solution)/shard_map/ppermute | solution.py:522
  60.3 6.6 %collective-permute-start.13 = (bf16[400,128]{1,0:T(8,128)(2,1)S(1)}, bf16[400,128]{1,0:T(8,128)(2,1)S(1)}, u32[]{:S(2)}, u32[]{:S(2)}) collective-permute-start(bf16[400,128]{1,0:T(8,128)(2,1)S(1)} %get-tuple-element.110.refs_0_.refs_4_), channel_id=1, source_target_pairs={{0,2},{1,3},{2,0},{3,1},{4,6},{5,7},{6,4},{7,5},{8,10},{9,11},{10,... | collective-permute-start | bytes 307208 | tf_op jit(solution)/shard_map/ppermute | solution.py:522
  63.1 5.1 %collective-permute-start.14 = (bf16[400,128]{1,0:T(8,128)(2,1)S(1)}, bf16[400,128]{1,0:T(8,128)(2,1)S(1)}, u32[]{:S(2)}, u32[]{:S(2)}) collective-permute-start(bf16[400,128]{1,0:T(8,128)(2,1)S(1)} %get-tuple-element.110.refs_0_.refs_4_), channel_id=1, source_target_pairs={{0,3},{1,2},{2,1},{3,0},{4,7},{5,6},{6,5},{7,4},{8,11},{9,10},{10,... | collective-permute-start | bytes 307208 | tf_op jit(solution)/shard_map/ppermute | solution.py:522
  63.7 23.7 %copy-start.3 = (bf16[192,768]{1,0:T(8,128)(2,1)S(1)}, bf16[192,768]{1,0:T(8,128)(2,1)}, u32[]{:S(2)}) copy-start(bf16[192,768]{1,0:T(8,128)(2,1)} %refs_11_.1) | copy-start | bytes 884740
  81.2 8.7 %copy-start.13 = (s32[112]{0:T(128)S(1)}, s32[112]{0:T(128)}, u32[]{:S(2)}) copy-start(s32[112]{0:T(128)} %param.24) | copy-start | bytes 1348
  82.2 4.0 %collective-permute-start.19 = (bf16[208,128]{1,0:T(8,128)(2,1)S(1)}, bf16[208,128]{1,0:T(8,128)(2,1)S(1)}, u32[]{:S(2)}, u32[]{:S(2)}) collective-permute-start(bf16[208,128]{1,0:T(8,128)(2,1)S(1)} %get-tuple-element.127.refs_0_), channel_id=1, source_target_pairs={{0,1},{1,0},{2,3},{3,2},{4,5},{5,4},{6,7},{7,6},{8,9},{9,8},{10,11... | collective-permute-start | bytes 159752 | tf_op jit(solution)/shard_map/ppermute | solution.py:522
  82.3 4.3 %collective-permute-start.20 = (bf16[208,128]{1,0:T(8,128)(2,1)S(1)}, bf16[208,128]{1,0:T(8,128)(2,1)S(1)}, u32[]{:S(2)}, u32[]{:S(2)}) collective-permute-start(bf16[208,128]{1,0:T(8,128)(2,1)S(1)} %get-tuple-element.127.refs_0_), channel_id=1, source_target_pairs={{0,2},{1,3},{2,0},{3,1},{4,6},{5,7},{6,4},{7,5},{8,10},{9,11},{10,... | collective-permute-start | bytes 159752 | tf_op jit(solution)/shard_map/ppermute | solution.py:522
  83.5 3.8 %collective-permute-start.21 = (bf16[208,128]{1,0:T(8,128)(2,1)S(1)}, bf16[208,128]{1,0:T(8,128)(2,1)S(1)}, u32[]{:S(2)}, u32[]{:S(2)}) collective-permute-start(bf16[208,128]{1,0:T(8,128)(2,1)S(1)} %get-tuple-element.127.refs_0_), channel_id=1, source_target_pairs={{0,3},{1,2},{2,1},{3,0},{4,7},{5,6},{6,5},{7,4},{8,11},{9,10},{10,... | collective-permute-start | bytes 159752 | tf_op jit(solution)/shard_map/ppermute | solution.py:522
  84.1 8.8 %collective-permute-start.27 = (bf16[960,128]{1,0:T(8,128)(2,1)S(1)}, bf16[960,128]{1,0:T(8,128)(2,1)S(1)}, u32[]{:S(2)}, u32[]{:S(2)}) collective-permute-start(bf16[960,128]{1,0:T(8,128)(2,1)S(1)} %collective-permute-done.16.refs_2_.refs_6_), channel_id=1, source_target_pairs={{0,4},{4,0},{8,12},{12,8},{16,20},{20,16},{24,28},{28,24},{1,5},{5... | collective-permute-start | bytes 737288 | tf_op jit(solution)/shard_map/ppermute | solution.py:522
  85.4 12.2 %collective-permute-start.28 = (bf16[960,128]{1,0:T(8,128)(2,1)S(1)}, bf16[960,128]{1,0:T(8,128)(2,1)S(1)}, u32[]{:S(2)}, u32[]{:S(2)}) collective-permute-start(bf16[960,128]{1,0:T(8,128)(2,1)S(1)} %collective-permute-done.17.refs_3_.refs_7_), channel_id=1, source_target_pairs={{0,4},{4,0},{8,12},{12,8},{16,20},{20,16},{24,28},{28,24},{1,5},{5... | collective-permute-start | bytes 737288 | tf_op jit(solution)/shard_map/ppermute | solution.py:522
  91.9 9.3 %collective-permute-start.22 = (bf16[864,128]{1,0:T(8,128)(2,1)S(1)}, bf16[864,128]{1,0:T(8,128)(2,1)S(1)}, u32[]{:S(2)}, u32[]{:S(2)}) collective-permute-start(bf16[864,128]{1,0:T(8,128)(2,1)S(1)} %get-tuple-element.140.refs_0_.refs_4_), channel_id=1, source_target_pairs={{0,8},{4,12},{8,16},{12,20},{16,24},{20,28},{24,0},{28,4},{1,9},{5... | collective-permute-start | bytes 663560 | tf_op jit(solution)/shard_map/ppermute | solution.py:538
  101.3 10.4 %collective-permute-start.30 = (bf16[1536,128]{1,0:T(8,128)(2,1)S(1)}, bf16[1536,128]{1,0:T(8,128)(2,1)S(1)}, u32[]{:S(2)}, u32[]{:S(2)}) collective-permute-start(bf16[1536,128]{1,0:T(8,128)(2,1)S(1)} %shard_map.216.refs_0_), channel_id=1, source_target_pairs={{0,2},{1,3},{2,0},{3,1},{4,6},{5,7},{6,4},{7,5},{8,10},{9,11},{10,... | collective-permute-start | bytes 1179656 | tf_op jit(solution)/shard_map/ppermute | solution.py:522
  102.5 6.4 %collective-permute-start.23 = (bf16[864,128]{1,0:T(8,128)(2,1)S(1)}, bf16[864,128]{1,0:T(8,128)(2,1)S(1)}, u32[]{:S(2)}, u32[]{:S(2)}) collective-permute-start(bf16[864,128]{1,0:T(8,128)(2,1)S(1)} %collective-permute-done.22.refs_1_.refs_5_), channel_id=1, source_target_pairs={{0,4},{4,0},{8,12},{12,8},{16,20},{20,16},{24,28},{28,24},{1,5},{5... | collective-permute-start | bytes 663560 | tf_op jit(solution)/shard_map/ppermute | solution.py:522
  103.8 19.8 %collective-permute-start.33 = (bf16[864,128]{1,0:T(8,128)(2,1)S(1)}, bf16[864,128]{1,0:T(8,128)(2,1)S(1)}, u32[]{:S(2)}, u32[]{:S(2)}) collective-permute-start(bf16[864,128]{1,0:T(8,128)(2,1)S(1)} %get-tuple-element.140.refs_0_.refs_4_), channel_id=1, source_target_pairs={{0,24},{4,28},{8,0},{12,4},{16,8},{20,12},{24,16},{28,20},{1,25},{... | collective-permute-start | bytes 663560 | tf_op jit(solution)/shard_map/ppermute | solution.py:538
  103.8 19.8 %collective-permute-start.32 = (bf16[864,128]{1,0:T(8,128)(2,1)S(1)}, bf16[864,128]{1,0:T(8,128)(2,1)S(1)}, u32[]{:S(2)}, u32[]{:S(2)}) collective-permute-start(bf16[864,128]{1,0:T(8,128)(2,1)S(1)} %collective-permute-done.22.refs_1_.refs_5_), channel_id=1, source_target_pairs={{0,8},{4,12},{8,16},{12,20},{16,24},{20,28},{24,0},{28,4},{1,9},{5... | collective-permute-start | bytes 663560 | tf_op jit(solution)/shard_map/ppermute | solution.py:538
  105.9 32.4 %collective-permute-start.29 = (bf16[1536,128]{1,0:T(8,128)(2,1)S(1)}, bf16[1536,128]{1,0:T(8,128)(2,1)S(1)}, u32[]{:S(2)}, u32[]{:S(2)}) collective-permute-start(bf16[1536,128]{1,0:T(8,128)(2,1)S(1)} %shard_map.216.refs_0_), channel_id=1, source_target_pairs={{0,1},{1,0},{2,3},{3,2},{4,5},{5,4},{6,7},{7,6},{8,9},{9,8},{10,11... | collective-permute-start | bytes 1179656 | tf_op jit(solution)/shard_map/ppermute | solution.py:522
  111.7 26.5 %collective-permute-start.31 = (bf16[1536,128]{1,0:T(8,128)(2,1)S(1)}, bf16[1536,128]{1,0:T(8,128)(2,1)S(1)}, u32[]{:S(2)}, u32[]{:S(2)}) collective-permute-start(bf16[1536,128]{1,0:T(8,128)(2,1)S(1)} %collective-permute-done.30.refs_2_), channel_id=1, source_target_pairs={{0,1},{1,0},{2,3},{3,2},{4,5},{5,4},{6,7},{7,6},{8,9},{9,8},{10,11... | collective-permute-start | bytes 1179656 | tf_op jit(solution)/shard_map/ppermute | solution.py:522
  111.7 1.8 %collective-permute-start.24 = (bf16[208,128]{1,0:T(8,128)(2,1)S(1)}, bf16[208,128]{1,0:T(8,128)(2,1)S(1)}, u32[]{:S(2)}, u32[]{:S(2)}) collective-permute-start(bf16[208,128]{1,0:T(8,128)(2,1)S(1)} %get-tuple-element.141), channel_id=1, source_target_pairs={{0,1},{1,0},{2,3},{3,2},{4,5},{5,4},{6,7},{7,6},{8,9},{9,8},{10,11... | collective-permute-start | bytes 159752 | tf_op jit(solution)/shard_map/ppermute | solution.py:522
  113.5 4.1 %collective-permute-start.25 = (bf16[208,128]{1,0:T(8,128)(2,1)S(1)}, bf16[208,128]{1,0:T(8,128)(2,1)S(1)}, u32[]{:S(2)}, u32[]{:S(2)}) collective-permute-start(bf16[208,128]{1,0:T(8,128)(2,1)S(1)} %get-tuple-element.142), channel_id=1, source_target_pairs={{0,2},{1,3},{2,0},{3,1},{4,6},{5,7},{6,4},{7,5},{8,10},{9,11},{10,... | collective-permute-start | bytes 159752 | tf_op jit(solution)/shard_map/ppermute | solution.py:522
  117.6 3.9 %collective-permute-start.26 = (bf16[208,128]{1,0:T(8,128)(2,1)S(1)}, bf16[208,128]{1,0:T(8,128)(2,1)S(1)}, u32[]{:S(2)}, u32[]{:S(2)}) collective-permute-start(bf16[208,128]{1,0:T(8,128)(2,1)S(1)} %get-tuple-element.143), channel_id=1, source_target_pairs={{0,3},{1,2},{2,1},{3,0},{4,7},{5,6},{6,5},{7,4},{8,11},{9,10},{10,... | collective-permute-start | bytes 159752 | tf_op jit(solution)/shard_map/ppermute | solution.py:522
  121.5 8.3 %collective-permute-start.34 = (bf16[864,128]{1,0:T(8,128)(2,1)S(1)}, bf16[864,128]{1,0:T(8,128)(2,1)S(1)}, u32[]{:S(2)}, u32[]{:S(2)}) collective-permute-start(bf16[864,128]{1,0:T(8,128)(2,1)S(1)} %get-tuple-element.140.refs_0_.refs_4_), channel_id=1, source_target_pairs={{0,4},{4,0},{8,12},{12,8},{16,20},{20,16},{24,28},{28,24},{1,5},{5... | collective-permute-start | bytes 663560 | tf_op jit(solution)/shard_map/ppermute | solution.py:522
  123.6 10.9 %collective-permute-start.35 = (bf16[864,128]{1,0:T(8,128)(2,1)S(1)}, bf16[864,128]{1,0:T(8,128)(2,1)S(1)}, u32[]{:S(2)}, u32[]{:S(2)}) collective-permute-start(bf16[864,128]{1,0:T(8,128)(2,1)S(1)} %collective-permute-done.32.refs_2_.refs_6_), channel_id=1, source_target_pairs={{0,4},{4,0},{8,12},{12,8},{16,20},{20,16},{24,28},{28,24},{1,5},{5... | collective-permute-start | bytes 663560 | tf_op jit(solution)/shard_map/ppermute | solution.py:522
  124.4 13.8 %collective-permute-start.36 = (bf16[864,128]{1,0:T(8,128)(2,1)S(1)}, bf16[864,128]{1,0:T(8,128)(2,1)S(1)}, u32[]{:S(2)}, u32[]{:S(2)}) collective-permute-start(bf16[864,128]{1,0:T(8,128)(2,1)S(1)} %collective-permute-done.33.refs_3_.refs_7_), channel_id=1, source_target_pairs={{0,4},{4,0},{8,12},{12,8},{16,20},{20,16},{24,28},{28,24},{1,5},{5... | collective-permute-start | bytes 663560 | tf_op jit(solution)/shard_map/ppermute | solution.py:522
  139.2 4.3 %collective-permute-start.37 = (bf16[208,192]{1,0:T(8,128)(2,1)S(1)}, bf16[208,192]{1,0:T(8,128)(2,1)S(1)}, u32[]{:S(2)}, u32[]{:S(2)}) collective-permute-start(bf16[208,192]{1,0:T(8,128)(2,1)S(1)} %get-tuple-element.163), channel_id=1, source_target_pairs={{0,1},{1,0},{2,3},{3,2},{4,5},{5,4},{6,7},{7,6},{8,9},{9,8},{10,11... | collective-permute-start | bytes 239624 | tf_op jit(solution)/shard_map/ppermute | solution.py:522
  139.3 5.8 %collective-permute-start.38 = (bf16[208,192]{1,0:T(8,128)(2,1)S(1)}, bf16[208,192]{1,0:T(8,128)(2,1)S(1)}, u32[]{:S(2)}, u32[]{:S(2)}) collective-permute-start(bf16[208,192]{1,0:T(8,128)(2,1)S(1)} %get-tuple-element.164), channel_id=1, source_target_pairs={{0,2},{1,3},{2,0},{3,1},{4,6},{5,7},{6,4},{7,5},{8,10},{9,11},{10,... | collective-permute-start | bytes 239624 | tf_op jit(solution)/shard_map/ppermute | solution.py:522
  139.5 7.0 %collective-permute-start.39 = (bf16[208,192]{1,0:T(8,128)(2,1)S(1)}, bf16[208,192]{1,0:T(8,128)(2,1)S(1)}, u32[]{:S(2)}, u32[]{:S(2)}) collective-permute-start(bf16[208,192]{1,0:T(8,128)(2,1)S(1)} %get-tuple-element.165), channel_id=1, source_target_pairs={{0,3},{1,2},{2,1},{3,0},{4,7},{5,6},{6,5},{7,4},{8,11},{9,10},{10,... | collective-permute-start | bytes 239624 | tf_op jit(solution)/shard_map/ppermute | solution.py:522
  (8 other events, 16.1 us)

commit v8 on v7

--- a/solution.py
+++ b/solution.py
@@ -678,11 +678,13 @@
         scratch=[pltpu.VMEM((model, tok), f32), padded],
     )
     if direct:
-        lasts = [last, step(last, 2)]
-        lasts += [step(lasts[1], 2), step(last, 6)]
-        across1 = swap(lasts[1], 1, "expert", n_e)
-        c1, c2, c3 = after([c1, c2, c3], across1)
-    got = [swap(c, k) for k, c in ((1, c1), (2, c2), (3, c3))]
+        got = [swap(c, k) for k, c in ((1, c1), (2, c2), (3, c3))]
+        (last,) = after([last], *got)
+        next_to = swap(last, 1, "expert", n_e)
+        last1, last3 = after([step(last, 2), step(last, 6)], next_to)
+        lasts = [last, last1, step(last1, 2), last3]
+    else:
+        got = [swap(c, k) for k, c in ((1, c1), (2, c2), (3, c3))]
     (input_grad,) = run(
         functools.partial(input_grad_kernel, n_t=n_t),
         [((width, tok), f32)],
@@ -699,10 +701,7 @@
             [((inner, model), f32)],
             *lasts, *saved_all[:half],
         )
-        lasts[2:] = after(lasts[2:], input_grad)
-        lasts += [
-            across1 if j == 1 else swap(v, 1, "expert", n_e) for j, v in enumerate(lasts)
-        ]
+        lasts += [next_to] + [swap(v, 1, "expert", n_e) for v in lasts[1:]]
         atts = [att, swap(att, 1), swap(att, 2)]
         atts.append(swap(after(atts[2:], lasts[half + 1])[0], 1))
         lasts[half:] = after(lasts[half:], part)

time: 148 us -> 142 us (0.959)
  starting transfers between devices: 32.2 us -> 28.6 us
    ppermute x6, waiting for transfers between devices: 16.3 us -> 12.1 us  [step(): return lax.ppermute(v, 'expert', [(i, (i + k) % n_e) for i in range(n_e)])]
    ppermute x6, starting transfers between devices: 7.64 us -> 4.52 us  [step(): return lax.ppermute(v, 'expert', [(i, (i + k) % n_e) for i in range(n_e)])]
    ppermute x34, waiting for transfers between devices: 40.4 us -> 43.4 us  [swap(): return lax.ppermute(v, axis, [(i, i ^ k) for i in range(n)])]
  transfers between devices with their start and end apart: 40 -> 40, of which waited for: 21 -> 16; matrix products, arithmetic and copies ran while one was open for 0% -> 0% of each run, Pallas kernels for 9% -> 8%
where the time goes in v8:
time: 142 us; the launch traced here: 141 us
  waiting for transfers between devices  55.5 us (39%)
  starting transfers between devices  28.6 us (20%)
  blocking collectives  28.3 us (20%)
  Pallas kernels  22.5 us (16%)
  local copies, waits for them, and re-layouts  5.64 us (4%)
    ppermute x34, waiting for transfers between devices, swap(): return lax.ppermute(v, axis, [(i, i ^ k) for i in range(n)])  43.4 us
    all_to_all x2, blocking collectives, exchange(): v = lax.all_to_all(v, 'expert', split_axis=0, concat_axis=0, tiled=True)  28.3 us
    ppermute x34, starting transfers between devices, swap(): return lax.ppermute(v, axis, [(i, i ^ k) for i in range(n)])  24.1 us
    pallas_call x17, Pallas kernels, run(): pl.pallas_call(whole, out_shape=[jax.ShapeDtypeStruct(s, d) for s, d in o...  22.5 us
    ppermute x6, waiting for transfers between devices, step(): return lax.ppermute(v, 'expert', [(i, (i + k) % n_e) for i in range(n_e)])  12.1 us
    unnamed x32, local copies, waits for them, and re-layouts  4.95 us
    ppermute x6, starting transfers between devices, step(): return lax.ppermute(v, 'expert', [(i, (i + k) % n_e) for i in range(n_e)])  4.52 us
  transfers between devices with their start and end apart: 40, of which 16 were waited for; matrix products, arithmetic and copies ran while one was open for 0% of the time, Pallas kernels for 8%

profile of v8, /device:TPU:0, one launch (start us, length us, event | category | flops | bytes accessed | tf_op | source)
XLA Modules:
  0.0 141.4 jit_solution(7325845442344658581)
XLA Ops:
  0.7 2.5 %collective-permute-start.2 = (bf16[192,128]{1,0:T(8,128)(2,1)}, bf16[192,128]{1,0:T(8,128)(2,1)S(1)}, u32[]{:S(2)}, u32[]{:S(2)}) collective-permute-start(bf16[192,128]{1,0:T(8,128)(2,1)} %bitcast.28), channel_id=1, source_target_pairs={{0,3},{1,2},{2,1},{3,0},{4,7},{5,6},{6,5},{7,4},{8,11},{9,10},{10,... | collective-permute-start | bytes 147464 | tf_op jit(solution)/shard_map/ppermute | solution.py:522
  4.5 1.0 copy-done.2
  7.5 0.9 shard_map.204
  8.4 1.2 copy-done
  9.6 0.8 copy-done.6
  10.4 1.9 %shard_map.205 = (f32[192,128]{1,0:T(8,128)S(1)}, bf16[192,128]{1,0:T(8,128)(2,1)S(1)}, bf16[192,128]{1,0:T(8,128)(2,1)S(1)}, bf16[192,128]{1,0:T(8,128)(2,1)S(1...) custom-call(bf16[192,128]{1,0:T(8,128)(2,1)S(1)} %bitcast.31, ...), custom_call_target="tpu_custom_call" | custom-call | bytes 2412032 | tf_op jit(solution)/shard_map/pallas_call | solution.py:67
  12.9 1.4 %collective-permute-start.4 = (bf16[192,128]{1,0:T(8,128)(2,1)S(1)}, bf16[192,128]{1,0:T(8,128)(2,1)S(1)}, u32[]{:S(2)}, u32[]{:S(2)}) collective-permute-start(bf16[192,128]{1,0:T(8,128)(2,1)S(1)} %get-tuple-element.95), channel_id=1, source_target_pairs={{0,2},{1,3},{2,0},{3,1},{4,6},{5,7},{6,4},{7,5},{8,10},{9,11},{10,... | collective-permute-start | bytes 147464 | tf_op jit(solution)/shard_map/ppermute | solution.py:522
  15.1 1.9 %collective-permute-done.4.refs_2_ = bf16[192,128]{1,0:T(8,128)(2,1)S(1)} collective-permute-done((bf16[192,128]{1,0:T(8,128)(2,1)S(1)}, bf16[192,128]{1,0:T(8,128)(2,1)S(1)}, u32[]{:S(2)}, u32[]{:S(2)}) %collective-permute-start.4) | collective-permute-done | bytes 49184 | tf_op jit(solution)/shard_map/ppermute | solution.py:522
  17.0 1.1 collective-permute-done.5.refs_3_
  18.8 16.8 %all_to_all.10 = bf16[8,40,400]{2,1,0:T(8,128)(2,1)S(1)} all-to-all(bf16[8,40,400]{2,1,0:T(8,128)(2,1)S(1)} %bitcast.34), channel_id=1, replica_groups=mesh['expert'=8,'tensor'=4] {'expert'}, dimensions={0} | all-to-all | bytes 512000 | tf_op jit(solution)/shard_map/all_to_all | solution.py:534
  35.6 1.1 collective-permute-start.7
  36.7 0.8 collective-permute-start.9
  37.9 5.0 %collective-permute-done.9.refs_4_ = bf16[960,128]{1,0:T(8,128)(2,1)S(1)} collective-permute-done((bf16[960,128]{1,0:T(8,128)(2,1)S(1)}, bf16[960,128]{1,0:T(8,128)(2,1)S(1)}, u32[]{:S(2)}, u32[]{:S(2)}) %collective-permute-start.9) | collective-permute-done | bytes 245792 | tf_op jit(solution)/shard_map/ppermute | solution.py:522
  42.9 2.8 %collective-permute-done.8.refs_1_.refs_5_ = bf16[960,128]{1,0:T(8,128)(2,1)S(1)} collective-permute-done((bf16[960,128]{1,0:T(8,128)(2,1)S(1)}, bf16[960,128]{1,0:T(8,128)(2,1)S(1)}, u32[]{:S(2)}, u32[]{:S(2)}) %collective-permute-start.8) | collective-permute-done | bytes 245792 | tf_op jit(solution)/shard_map/ppermute | solution.py:538
  45.7 1.6 %collective-permute-done.10.refs_3_ = bf16[320,400]{1,0:T(8,128)(2,1)S(1)} collective-permute-done((bf16[320,400]{1,0:T(8,128)(2,1)S(1)}, bf16[320,400]{1,0:T(8,128)(2,1)S(1)}, u32[]{:S(2)}, u32[]{:S(2)}) %collective-permute-start.10) | collective-permute-done | bytes 256032 | tf_op jit(solution)/shard_map/ppermute | solution.py:522
  47.3 3.0 %shard_map.208 = (bf16[320,384]{1,0:T(8,128)(2,1)S(1)}, bf16[320,384]{1,0:T(8,128)(2,1)S(1)}, bf16[640,384]{1,0:T(8,128)(2,1)S(1)}, bf16[320,768]{1,0:T(8,128)(2...) custom-call(bf16[320,400]{1,0:T(8,128)(2,1)S(1)} %bitcast.25, ...), custom_call_target="tpu_custom_call" | custom-call | bytes 6332416 | tf_op jit(solution)/shard_map/pallas_call | solution.py:67
  50.9 1.2 collective-permute-start.18
  52.1 1.5 %collective-permute-start.16 = (bf16[960,128]{1,0:T(8,128)(2,1)S(1)}, bf16[960,128]{1,0:T(8,128)(2,1)S(1)}, u32[]{:S(2)}, u32[]{:S(2)}) collective-permute-start(bf16[960,128]{1,0:T(8,128)(2,1)S(1)} %collective-permute-done.8.refs_1_.refs_5_), channel_id=1, source_target_pairs={{0,8},{4,12},{8,16},{12,20},{16,24},{20,28},{24,0},{28,4},{1,9},{5... | collective-permute-start | bytes 737288 | tf_op jit(solution)/shard_map/ppermute | solution.py:538
  53.6 1.0 collective-permute-start.15
  54.7 9.3 %collective-permute-done.17.refs_3_.refs_7_ = bf16[960,128]{1,0:T(8,128)(2,1)S(1)} collective-permute-done((bf16[960,128]{1,0:T(8,128)(2,1)S(1)}, bf16[960,128]{1,0:T(8,128)(2,1)S(1)}, u32[]{:S(2)}, u32[]{:S(2)}) %collective-permute-start.17) | collective-permute-done | bytes 245792 | tf_op jit(solution)/shard_map/ppermute | solution.py:538
  64.0 0.9 collective-permute-start.13
  64.9 3.2 %shard_map.210 = (f32[1,768,768]{2,1,0:T(8,128)}, f32[1,768,768]{2,1,0:T(8,128)}) custom-call(bf16[320,768]{1,0:T(8,128)(2,1)S(1)} %get-tuple-element.118.refs_0_, bf16[320,768]{1,0:T(8,128)(2,1)S(1)} %get-tuple-element.119.refs_1_, bf16[320,768]{1,0:T(8,128)(2,1)S(1)} %get-tuple-element.120.refs_2_, bf16[320,768]{1,0:T(8,128)(2,1)S(1)} %get-tuple-element.121.refs_3_), custom_call_target="tpu_custom_call" | custom-call | bytes 6684672 | tf_op jit(solution)/shard_map/pallas_call | solution.py:67
  68.7 11.5 %all_to_all.11 = bf16[8,40,384]{2,1,0:T(8,128)(2,1)S(1)} all-to-all(bf16[8,40,384]{2,1,0:T(8,128)(2,1)S(1)} %bitcast.26), channel_id=1, replica_groups=mesh['expert'=8,'tensor'=4] {'expert'}, dimensions={0} | all-to-all | bytes 491520 | tf_op jit(solution)/shard_map/all_to_all | solution.py:534
  80.2 1.0 shard_map.212
  81.3 1.2 collective-permute-start.20
  83.2 2.2 %collective-permute-done.21.refs_3_ = bf16[208,128]{1,0:T(8,128)(2,1)S(1)} collective-permute-done((bf16[208,128]{1,0:T(8,128)(2,1)S(1)}, bf16[208,128]{1,0:T(8,128)(2,1)S(1)}, u32[]{:S(2)}, u32[]{:S(2)}) %collective-permute-start.21) | collective-permute-done | bytes 53280 | tf_op jit(solution)/shard_map/ppermute | solution.py:522
  86.0 2.6 %shard_map.213 = (bf16[208,128]{1,0:T(8,128)(2,1)S(1)}, bf16[208,128]{1,0:T(8,128)(2,1)S(1)}, bf16[208,128]{1,0:T(8,128)(2,1)S(1)}, bf16[208,128]{1,0:T(8,128)(2...) custom-call(bf16[208,128]{1,0:T(8,128)(2,1)S(1)} %get-tuple-element., ...), custom_call_target="tpu_custom_call" | custom-call | bytes 3313664 | tf_op jit(solution)/shard_map/pallas_call | solution.py:67
  88.8 1.1 collective-permute-start.23
  90.6 1.3 collective-permute-start.25
  92.6 2.0 %shard_map.215 = (f32[16,768]{1,0:T(8,128)}, bf16[864,128]{1,0:T(8,128)(2,1)S(1)}) custom-call(bf16[400,128]{1,0:T(8,128)(2,1)S(1)} %get-tuple-element.108.refs_0_.refs_4_, bf16[400,128]{1,0:T(8,128)(2,1)S(1)} %collective-permute-done.12.refs_1_.refs_5_, bf16[400,128]{1,0:T(8,128)(2,1)S(1)} %collective-permute-done.13.refs_2_.refs_6_, ...), custom_call_target="tpu_custom_call" | custom-call | bytes 2656704 | tf_op jit(solution)/shard_map/pallas_call | solution.py:67
  94.7 1.4 collective-permute-start.29
  96.0 1.7 %collective-permute-start.28 = (bf16[864,128]{1,0:T(8,128)(2,1)S(1)}, bf16[864,128]{1,0:T(8,128)(2,1)S(1)}, u32[]{:S(2)}, u32[]{:S(2)}) collective-permute-start(bf16[864,128]{1,0:T(8,128)(2,1)S(1)} %get-tuple-element.142.refs_0_.refs_4_), channel_id=1, source_target_pairs={{0,24},{4,28},{8,0},{12,4},{16,8},{20,12},{24,16},{28,20},{1,25},{... | collective-permute-start | bytes 663560 | tf_op jit(solution)/shard_map/ppermute | solution.py:538
  98.1 10.7 %collective-permute-done.29.refs_8_.refs_0_ = bf16[864,128]{1,0:T(8,128)(2,1)S(1)} collective-permute-done((bf16[864,128]{1,0:T(8,128)(2,1)S(1)}, bf16[864,128]{1,0:T(8,128)(2,1)S(1)}, u32[]{:S(2)}, u32[]{:S(2)}) %collective-permute-start.29) | collective-permute-done | bytes 221216 | tf_op jit(solution)/shard_map/ppermute | solution.py:522
  108.9 1.2 collective-permute-start.31
  110.0 1.3 collective-permute-start.32
  111.6 5.0 %collective-permute-done.32.refs_9_.refs_1_ = bf16[864,128]{1,0:T(8,128)(2,1)S(1)} collective-permute-done((bf16[864,128]{1,0:T(8,128)(2,1)S(1)}, bf16[864,128]{1,0:T(8,128)(2,1)S(1)}, u32[]{:S(2)}, u32[]{:S(2)}) %collective-permute-start.32) | collective-permute-done | bytes 221216 | tf_op jit(solution)/shard_map/ppermute | solution.py:522
  116.6 2.9 %collective-permute-done.31.refs_2_ = bf16[1536,128]{1,0:T(8,128)(2,1)S(1)} collective-permute-done((bf16[1536,128]{1,0:T(8,128)(2,1)S(1)}, bf16[1536,128]{1,0:T(8,128)(2,1)S(1)}, u32[]{:S(2)}, u32[]{:S(2)}) %collective-permute-start.31) | collective-permute-done | bytes 393248 | tf_op jit(solution)/shard_map/ppermute | solution.py:522
  119.5 1.3 collective-permute-start.36
  121.5 1.1 shard_map.217.refs_8_
  122.6 5.1 %collective-permute-done.36.refs_11_.refs_3_ = bf16[864,128]{1,0:T(8,128)(2,1)S(1)} collective-permute-done((bf16[864,128]{1,0:T(8,128)(2,1)S(1)}, bf16[864,128]{1,0:T(8,128)(2,1)S(1)}, u32[]{:S(2)}, u32[]{:S(2)}) %collective-permute-start.36) | collective-permute-done | bytes 221216 | tf_op jit(solution)/shard_map/ppermute | solution.py:522
  127.7 4.4 %collective-permute-done.35.refs_10_.refs_2_ = bf16[864,128]{1,0:T(8,128)(2,1)S(1)} collective-permute-done((bf16[864,128]{1,0:T(8,128)(2,1)S(1)}, bf16[864,128]{1,0:T(8,128)(2,1)S(1)}, u32[]{:S(2)}, u32[]{:S(2)}) %collective-permute-start.35) | collective-permute-done | bytes 221216 | tf_op jit(solution)/shard_map/ppermute | solution.py:522
  132.1 1.0 shard_map.218
  133.2 1.2 collective-permute-start.38
  135.0 0.8 shard_map.214
  135.8 2.3 %shard_map.220 = f32[576,768]{1,0:T(8,128)} custom-call(bf16[864,128]{1,0:T(8,128)(2,1)S(1)} %collective-permute-done.29.refs_8_.refs_0_, bf16[864,128]{1,0:T(8,128)(2,1)S(1)} %collective-permute-done.32.refs_9_.refs_1_, bf16[864,128]{1,0:T(8,128)(2,1)S(1)} %collective-permute-done.35.refs_10_.refs_2_, ...), custom_call_target="tpu_custom_call" | custom-call | bytes 5406720 | tf_op jit(solution)/shard_map/pallas_call | solution.py:67
  138.1 0.9 collective-permute-done.38.refs_2_
  139.0 1.4 collective-permute-done.39.refs_3_
  140.4 1.1 shard_map.219
  (85 shorter events, 12.2 us)
Async XLA Ops:
  0.6 13.7 %copy-start.9 = (bf16[768,8]{0,1:T(8,128)(2,1)S(1)}, bf16[768,8]{0,1:T(8,128)(2,1)}, u32[]{:S(2)}) copy-start(bf16[768,8]{0,1:T(8,128)(2,1)} %param.19) | copy-start | bytes 36868
  0.7 7.7 %collective-permute-start.2 = (bf16[192,128]{1,0:T(8,128)(2,1)}, bf16[192,128]{1,0:T(8,128)(2,1)S(1)}, u32[]{:S(2)}, u32[]{:S(2)}) collective-permute-start(bf16[192,128]{1,0:T(8,128)(2,1)} %bitcast.28), channel_id=1, source_target_pairs={{0,3},{1,2},{2,1},{3,0},{4,7},{5,6},{6,5},{7,4},{8,11},{9,10},{10,... | collective-permute-start | bytes 147464 | tf_op jit(solution)/shard_map/ppermute | solution.py:522
  3.1 5.3 %collective-permute-start.1 = (bf16[192,128]{1,0:T(8,128)(2,1)}, bf16[192,128]{1,0:T(8,128)(2,1)S(1)}, u32[]{:S(2)}, u32[]{:S(2)}) collective-permute-start(bf16[192,128]{1,0:T(8,128)(2,1)} %bitcast.29), channel_id=1, source_target_pairs={{0,2},{1,3},{2,0},{3,1},{4,6},{5,7},{6,4},{7,5},{8,10},{9,11},{10,... | collective-permute-start | bytes 147464 | tf_op jit(solution)/shard_map/ppermute | solution.py:522
  3.8 4.6 %collective-permute-start = (bf16[192,128]{1,0:T(8,128)(2,1)}, bf16[192,128]{1,0:T(8,128)(2,1)S(1)}, u32[]{:S(2)}, u32[]{:S(2)}) collective-permute-start(bf16[192,128]{1,0:T(8,128)(2,1)} %bitcast.30), channel_id=1, source_target_pairs={{0,1},{1,0},{2,3},{3,2},{4,5},{5,4},{6,7},{7,6},{8,9},{9,8},{10,11... | collective-permute-start | bytes 147464 | tf_op jit(solution)/shard_map/ppermute | solution.py:522
  7.5 6.9 %copy-start.10 = (s32[128,2]{0,1:T(2,128)S(1)}, s32[128,2]{0,1:T(2,128)}, u32[]{:S(2)}) copy-start(s32[128,2]{0,1:T(2,128)} %param.22) | copy-start | bytes 3076
  7.5 10.6 %copy-start.7 = (bf16[128,192]{0,1:T(8,128)(2,1)S(1)}, bf16[128,192]{0,1:T(8,128)(2,1)}, u32[]{:S(2)}) copy-start(bf16[128,192]{0,1:T(8,128)(2,1)} %param.13) | copy-start | bytes 147460
  7.5 10.6 %copy-start.8 = (bf16[128,192]{0,1:T(8,128)(2,1)S(1)}, bf16[128,192]{0,1:T(8,128)(2,1)}, u32[]{:S(2)}) copy-start(bf16[128,192]{0,1:T(8,128)(2,1)} %param.25) | copy-start | bytes 147460
  10.4 36.9 %copy-start.4 = (bf16[1,768,768]{2,1,0:T(8,128)(2,1)S(1)}, bf16[1,768,768]{2,1,0:T(8,128)(2,1)}, u32[]{:S(2)}) copy-start(bf16[1,768,768]{2,1,0:T(8,128)(2,1)} %refs_4_.1) | copy-start | bytes 3538948
  10.4 36.9 %copy-start.5 = (bf16[1,768,768]{2,1,0:T(8,128)(2,1)S(1)}, bf16[1,768,768]{2,1,0:T(8,128)(2,1)}, u32[]{:S(2)}) copy-start(bf16[1,768,768]{2,1,0:T(8,128)(2,1)} %refs_5_.1) | copy-start | bytes 3538948
  12.3 2.7 %collective-permute-start.3 = (bf16[192,128]{1,0:T(8,128)(2,1)S(1)}, bf16[192,128]{1,0:T(8,128)(2,1)S(1)}, u32[]{:S(2)}, u32[]{:S(2)}) collective-permute-start(bf16[192,128]{1,0:T(8,128)(2,1)S(1)} %get-tuple-element.94), channel_id=1, source_target_pairs={{0,1},{1,0},{2,3},{3,2},{4,5},{5,4},{6,7},{7,6},{8,9},{9,8},{10,11... | collective-permute-start | bytes 147464 | tf_op jit(solution)/shard_map/ppermute | solution.py:522
  12.9 4.1 %collective-permute-start.4 = (bf16[192,128]{1,0:T(8,128)(2,1)S(1)}, bf16[192,128]{1,0:T(8,128)(2,1)S(1)}, u32[]{:S(2)}, u32[]{:S(2)}) collective-permute-start(bf16[192,128]{1,0:T(8,128)(2,1)S(1)} %get-tuple-element.95), channel_id=1, source_target_pairs={{0,2},{1,3},{2,0},{3,1},{4,6},{5,7},{6,4},{7,5},{8,10},{9,11},{10,... | collective-permute-start | bytes 147464 | tf_op jit(solution)/shard_map/ppermute | solution.py:522
  14.3 3.8 %collective-permute-start.5 = (bf16[192,128]{1,0:T(8,128)(2,1)S(1)}, bf16[192,128]{1,0:T(8,128)(2,1)S(1)}, u32[]{:S(2)}, u32[]{:S(2)}) collective-permute-start(bf16[192,128]{1,0:T(8,128)(2,1)S(1)} %get-tuple-element.96), channel_id=1, source_target_pairs={{0,3},{1,2},{2,1},{3,0},{4,7},{5,6},{6,5},{7,4},{8,11},{9,10},{10,... | collective-permute-start | bytes 147464 | tf_op jit(solution)/shard_map/ppermute | solution.py:522
  35.6 10.0 %collective-permute-start.7 = (bf16[320,400]{1,0:T(8,128)(2,1)S(1)}, bf16[320,400]{1,0:T(8,128)(2,1)S(1)}, u32[]{:S(2)}, u32[]{:S(2)}) collective-permute-start(bf16[320,400]{1,0:T(8,128)(2,1)S(1)} %bitcast.23), channel_id=1, source_target_pairs={{0,2},{1,3},{2,0},{3,1},{4,6},{5,7},{6,4},{7,5},{8,10},{9,11},{10,... | collective-permute-start | bytes 768008 | tf_op jit(solution)/shard_map/ppermute | solution.py:522
  36.7 6.2 %collective-permute-start.9 = (bf16[960,128]{1,0:T(8,128)(2,1)S(1)}, bf16[960,128]{1,0:T(8,128)(2,1)S(1)}, u32[]{:S(2)}, u32[]{:S(2)}) collective-permute-start(bf16[960,128]{1,0:T(8,128)(2,1)S(1)} %get-tuple-element.144.refs_8_.refs_0_.refs_4_), channel_id=1, source_target_pairs={{0,4},{4,0},{8,12},{12,8},{16,20},{20,16},{24,28},{28,24},{1,5},{5... | collective-permute-start | bytes 737288 | tf_op jit(solution)/shard_map/ppermute | solution.py:522
  37.5 8.1 %collective-permute-start.8 = (bf16[960,128]{1,0:T(8,128)(2,1)S(1)}, bf16[960,128]{1,0:T(8,128)(2,1)S(1)}, u32[]{:S(2)}, u32[]{:S(2)}) collective-permute-start(bf16[960,128]{1,0:T(8,128)(2,1)S(1)} %get-tuple-element.144.refs_8_.refs_0_.refs_4_), channel_id=1, source_target_pairs={{0,8},{4,12},{8,16},{12,20},{16,24},{20,28},{24,0},{28,4},{1,9},{5... | collective-permute-start | bytes 737288 | tf_op jit(solution)/shard_map/ppermute | solution.py:538
  37.9 7.8 %collective-permute-start.6 = (bf16[320,400]{1,0:T(8,128)(2,1)S(1)}, bf16[320,400]{1,0:T(8,128)(2,1)S(1)}, u32[]{:S(2)}, u32[]{:S(2)}) collective-permute-start(bf16[320,400]{1,0:T(8,128)(2,1)S(1)} %bitcast.24), channel_id=1, source_target_pairs={{0,1},{1,0},{2,3},{3,2},{4,5},{5,4},{6,7},{7,6},{8,9},{9,8},{10,11... | collective-permute-start | bytes 768008 | tf_op jit(solution)/shard_map/ppermute | solution.py:522
  45.7 1.6 %collective-permute-start.10 = (bf16[320,400]{1,0:T(8,128)(2,1)S(1)}, bf16[320,400]{1,0:T(8,128)(2,1)S(1)}, u32[]{:S(2)}, u32[]{:S(2)}) collective-permute-start(bf16[320,400]{1,0:T(8,128)(2,1)S(1)} %collective-permute-done.7.refs_2_), channel_id=1, source_target_pairs={{0,1},{1,0},{2,3},{3,2},{4,5},{5,4},{6,7},{7,6},{8,9},{9,8},{10,11... | collective-permute-start | bytes 768008 | tf_op jit(solution)/shard_map/ppermute | solution.py:522
  50.3 3.3 %collective-permute-start.11 = (bf16[640,384]{1,0:T(8,128)(2,1)S(1)}, bf16[640,384]{1,0:T(8,128)(2,1)S(1)}, u32[]{:S(2)}, u32[]{:S(2)}) collective-permute-start(bf16[640,384]{1,0:T(8,128)(2,1)S(1)} %get-tuple-element.107), channel_id=1, source_target_pairs={{0,1},{1,0},{2,3},{3,2},{4,5},{5,4},{6,7},{7,6},{8,9},{9,8},{10,11... | collective-permute-start | bytes 1474568 | tf_op jit(solution)/shard_map/ppermute | solution.py:522
  50.5 13.5 %collective-permute-start.17 = (bf16[960,128]{1,0:T(8,128)(2,1)S(1)}, bf16[960,128]{1,0:T(8,128)(2,1)S(1)}, u32[]{:S(2)}, u32[]{:S(2)}) collective-permute-start(bf16[960,128]{1,0:T(8,128)(2,1)S(1)} %get-tuple-element.144.refs_8_.refs_0_.refs_4_), channel_id=1, source_target_pairs={{0,24},{4,28},{8,0},{12,4},{16,8},{20,12},{24,16},{28,20},{1,25},{... | collective-permute-start | bytes 737288 | tf_op jit(solution)/shard_map/ppermute | solution.py:538
  50.9 14.0 %collective-permute-start.18 = (bf16[960,128]{1,0:T(8,128)(2,1)S(1)}, bf16[960,128]{1,0:T(8,128)(2,1)S(1)}, u32[]{:S(2)}, u32[]{:S(2)}) collective-permute-start(bf16[960,128]{1,0:T(8,128)(2,1)S(1)} %collective-permute-done.8.refs_1_.refs_5_), channel_id=1, source_target_pairs={{0,4},{4,0},{8,12},{12,8},{16,20},{20,16},{24,28},{28,24},{1,5},{5... | collective-permute-start | bytes 737288 | tf_op jit(solution)/shard_map/ppermute | solution.py:522
  52.1 16.0 %collective-permute-start.16 = (bf16[960,128]{1,0:T(8,128)(2,1)S(1)}, bf16[960,128]{1,0:T(8,128)(2,1)S(1)}, u32[]{:S(2)}, u32[]{:S(2)}) collective-permute-start(bf16[960,128]{1,0:T(8,128)(2,1)S(1)} %collective-permute-done.8.refs_1_.refs_5_), channel_id=1, source_target_pairs={{0,8},{4,12},{8,16},{12,20},{16,24},{20,28},{24,0},{28,4},{1,9},{5... | collective-permute-start | bytes 737288 | tf_op jit(solution)/shard_map/ppermute | solution.py:538
  53.6 14.4 %collective-permute-start.15 = (bf16[320,384]{1,0:T(8,128)(2,1)S(1)}, bf16[320,384]{1,0:T(8,128)(2,1)S(1)}, u32[]{:S(2)}, u32[]{:S(2)}) collective-permute-start(bf16[320,384]{1,0:T(8,128)(2,1)S(1)} %shard_map.209), channel_id=1, source_target_pairs={{0,2},{1,3},{2,0},{3,1},{4,6},{5,7},{6,4},{7,5},{8,10},{9,11},{10,... | collective-permute-start | bytes 737288 | tf_op jit(solution)/shard_map/ppermute | solution.py:522
  54.7 13.4 %collective-permute-start.14 = (bf16[400,128]{1,0:T(8,128)(2,1)S(1)}, bf16[400,128]{1,0:T(8,128)(2,1)S(1)}, u32[]{:S(2)}, u32[]{:S(2)}) collective-permute-start(bf16[400,128]{1,0:T(8,128)(2,1)S(1)} %get-tuple-element.108.refs_0_.refs_4_), channel_id=1, source_target_pairs={{0,3},{1,2},{2,1},{3,0},{4,7},{5,6},{6,5},{7,4},{8,11},{9,10},{10,... | collective-permute-start | bytes 307208 | tf_op jit(solution)/shard_map/ppermute | solution.py:522
  64.0 4.7 %collective-permute-start.13 = (bf16[400,128]{1,0:T(8,128)(2,1)S(1)}, bf16[400,128]{1,0:T(8,128)(2,1)S(1)}, u32[]{:S(2)}, u32[]{:S(2)}) collective-permute-start(bf16[400,128]{1,0:T(8,128)(2,1)S(1)} %get-tuple-element.108.refs_0_.refs_4_), channel_id=1, source_target_pairs={{0,2},{1,3},{2,0},{3,1},{4,6},{5,7},{6,4},{7,5},{8,10},{9,11},{10,... | collective-permute-start | bytes 307208 | tf_op jit(solution)/shard_map/ppermute | solution.py:522
  64.9 3.8 %collective-permute-start.12 = (bf16[400,128]{1,0:T(8,128)(2,1)S(1)}, bf16[400,128]{1,0:T(8,128)(2,1)S(1)}, u32[]{:S(2)}, u32[]{:S(2)}) collective-permute-start(bf16[400,128]{1,0:T(8,128)(2,1)S(1)} %get-tuple-element.108.refs_0_.refs_4_), channel_id=1, source_target_pairs={{0,1},{1,0},{2,3},{3,2},{4,5},{5,4},{6,7},{7,6},{8,9},{9,8},{10,11... | collective-permute-start | bytes 307208 | tf_op jit(solution)/shard_map/ppermute | solution.py:522
  64.9 21.2 %copy-start.3 = (bf16[192,768]{1,0:T(8,128)(2,1)S(1)}, bf16[192,768]{1,0:T(8,128)(2,1)}, u32[]{:S(2)}) copy-start(bf16[192,768]{1,0:T(8,128)(2,1)} %refs_11_.1) | copy-start | bytes 884740
  80.2 12.4 %copy-start.13 = (s32[112]{0:T(128)S(1)}, s32[112]{0:T(128)}, u32[]{:S(2)}) copy-start(s32[112]{0:T(128)} %param.24) | copy-start | bytes 1348
  81.2 4.1 %collective-permute-start.21 = (bf16[208,128]{1,0:T(8,128)(2,1)S(1)}, bf16[208,128]{1,0:T(8,128)(2,1)S(1)}, u32[]{:S(2)}, u32[]{:S(2)}) collective-permute-start(bf16[208,128]{1,0:T(8,128)(2,1)S(1)} %get-tuple-element.125.refs_0_), channel_id=1, source_target_pairs={{0,3},{1,2},{2,1},{3,0},{4,7},{5,6},{6,5},{7,4},{8,11},{9,10},{10,... | collective-permute-start | bytes 159752 | tf_op jit(solution)/shard_map/ppermute | solution.py:522
  81.3 4.7 %collective-permute-start.20 = (bf16[208,128]{1,0:T(8,128)(2,1)S(1)}, bf16[208,128]{1,0:T(8,128)(2,1)S(1)}, u32[]{:S(2)}, u32[]{:S(2)}) collective-permute-start(bf16[208,128]{1,0:T(8,128)(2,1)S(1)} %get-tuple-element.125.refs_0_), channel_id=1, source_target_pairs={{0,2},{1,3},{2,0},{3,1},{4,6},{5,7},{6,4},{7,5},{8,10},{9,11},{10,... | collective-permute-start | bytes 159752 | tf_op jit(solution)/shard_map/ppermute | solution.py:522
  82.5 3.5 %collective-permute-start.19 = (bf16[208,128]{1,0:T(8,128)(2,1)S(1)}, bf16[208,128]{1,0:T(8,128)(2,1)S(1)}, u32[]{:S(2)}, u32[]{:S(2)}) collective-permute-start(bf16[208,128]{1,0:T(8,128)(2,1)S(1)} %get-tuple-element.125.refs_0_), channel_id=1, source_target_pairs={{0,1},{1,0},{2,3},{3,2},{4,5},{5,4},{6,7},{7,6},{8,9},{9,8},{10,11... | collective-permute-start | bytes 159752 | tf_op jit(solution)/shard_map/ppermute | solution.py:522
  88.6 6.0 %collective-permute-start.22 = (bf16[208,128]{1,0:T(8,128)(2,1)S(1)}, bf16[208,128]{1,0:T(8,128)(2,1)S(1)}, u32[]{:S(2)}, u32[]{:S(2)}) collective-permute-start(bf16[208,128]{1,0:T(8,128)(2,1)S(1)} %get-tuple-element.130), channel_id=1, source_target_pairs={{0,1},{1,0},{2,3},{3,2},{4,5},{5,4},{6,7},{7,6},{8,9},{9,8},{10,11... | collective-permute-start | bytes 159752 | tf_op jit(solution)/shard_map/ppermute | solution.py:522
  88.8 5.9 %collective-permute-start.23 = (bf16[208,128]{1,0:T(8,128)(2,1)S(1)}, bf16[208,128]{1,0:T(8,128)(2,1)S(1)}, u32[]{:S(2)}, u32[]{:S(2)}) collective-permute-start(bf16[208,128]{1,0:T(8,128)(2,1)S(1)} %get-tuple-element.131), channel_id=1, source_target_pairs={{0,2},{1,3},{2,0},{3,1},{4,6},{5,7},{6,4},{7,5},{8,10},{9,11},{10,... | collective-permute-start | bytes 159752 | tf_op jit(solution)/shard_map/ppermute | solution.py:522
  89.9 4.8 %collective-permute-start.24 = (bf16[208,128]{1,0:T(8,128)(2,1)S(1)}, bf16[208,128]{1,0:T(8,128)(2,1)S(1)}, u32[]{:S(2)}, u32[]{:S(2)}) collective-permute-start(bf16[208,128]{1,0:T(8,128)(2,1)S(1)} %get-tuple-element.132), channel_id=1, source_target_pairs={{0,3},{1,2},{2,1},{3,0},{4,7},{5,6},{6,5},{7,4},{8,11},{9,10},{10,... | collective-permute-start | bytes 159752 | tf_op jit(solution)/shard_map/ppermute | solution.py:522
  90.6 18.2 %collective-permute-start.25 = (bf16[960,128]{1,0:T(8,128)(2,1)S(1)}, bf16[960,128]{1,0:T(8,128)(2,1)S(1)}, u32[]{:S(2)}, u32[]{:S(2)}) collective-permute-start(bf16[960,128]{1,0:T(8,128)(2,1)S(1)} %collective-permute-done.16.refs_2_.refs_6_), channel_id=1, source_target_pairs={{0,4},{4,0},{8,12},{12,8},{16,20},{20,16},{24,28},{28,24},{1,5},{5... | collective-permute-start | bytes 737288 | tf_op jit(solution)/shard_map/ppermute | solution.py:522
  91.9 16.9 %collective-permute-start.26 = (bf16[960,128]{1,0:T(8,128)(2,1)S(1)}, bf16[960,128]{1,0:T(8,128)(2,1)S(1)}, u32[]{:S(2)}, u32[]{:S(2)}) collective-permute-start(bf16[960,128]{1,0:T(8,128)(2,1)S(1)} %collective-permute-done.17.refs_3_.refs_7_), channel_id=1, source_target_pairs={{0,4},{4,0},{8,12},{12,8},{16,20},{20,16},{24,28},{28,24},{1,5},{5... | collective-permute-start | bytes 737288 | tf_op jit(solution)/shard_map/ppermute | solution.py:522
  94.7 14.1 %collective-permute-start.29 = (bf16[864,128]{1,0:T(8,128)(2,1)S(1)}, bf16[864,128]{1,0:T(8,128)(2,1)S(1)}, u32[]{:S(2)}, u32[]{:S(2)}) collective-permute-start(bf16[864,128]{1,0:T(8,128)(2,1)S(1)} %get-tuple-element.142.refs_0_.refs_4_), channel_id=1, source_target_pairs={{0,4},{4,0},{8,12},{12,8},{16,20},{20,16},{24,28},{28,24},{1,5},{5... | collective-permute-start | bytes 663560 | tf_op jit(solution)/shard_map/ppermute | solution.py:522
  96.0 12.8 %collective-permute-start.28 = (bf16[864,128]{1,0:T(8,128)(2,1)S(1)}, bf16[864,128]{1,0:T(8,128)(2,1)S(1)}, u32[]{:S(2)}, u32[]{:S(2)}) collective-permute-start(bf16[864,128]{1,0:T(8,128)(2,1)S(1)} %get-tuple-element.142.refs_0_.refs_4_), channel_id=1, source_target_pairs={{0,24},{4,28},{8,0},{12,4},{16,8},{20,12},{24,16},{28,20},{1,25},{... | collective-permute-start | bytes 663560 | tf_op jit(solution)/shard_map/ppermute | solution.py:538
  97.7 11.1 %collective-permute-start.27 = (bf16[864,128]{1,0:T(8,128)(2,1)S(1)}, bf16[864,128]{1,0:T(8,128)(2,1)S(1)}, u32[]{:S(2)}, u32[]{:S(2)}) collective-permute-start(bf16[864,128]{1,0:T(8,128)(2,1)S(1)} %get-tuple-element.142.refs_0_.refs_4_), channel_id=1, source_target_pairs={{0,8},{4,12},{8,16},{12,20},{16,24},{20,28},{24,0},{28,4},{1,9},{5... | collective-permute-start | bytes 663560 | tf_op jit(solution)/shard_map/ppermute | solution.py:538
  108.9 10.6 %collective-permute-start.31 = (bf16[1536,128]{1,0:T(8,128)(2,1)S(1)}, bf16[1536,128]{1,0:T(8,128)(2,1)S(1)}, u32[]{:S(2)}, u32[]{:S(2)}) collective-permute-start(bf16[1536,128]{1,0:T(8,128)(2,1)S(1)} %shard_map.216.refs_0_), channel_id=1, source_target_pairs={{0,2},{1,3},{2,0},{3,1},{4,6},{5,7},{6,4},{7,5},{8,10},{9,11},{10,... | collective-permute-start | bytes 1179656 | tf_op jit(solution)/shard_map/ppermute | solution.py:522
  110.0 6.6 %collective-permute-start.32 = (bf16[864,128]{1,0:T(8,128)(2,1)S(1)}, bf16[864,128]{1,0:T(8,128)(2,1)S(1)}, u32[]{:S(2)}, u32[]{:S(2)}) collective-permute-start(bf16[864,128]{1,0:T(8,128)(2,1)S(1)} %collective-permute-done.27.refs_1_.refs_5_), channel_id=1, source_target_pairs={{0,4},{4,0},{8,12},{12,8},{16,20},{20,16},{24,28},{28,24},{1,5},{5... | collective-permute-start | bytes 663560 | tf_op jit(solution)/shard_map/ppermute | solution.py:522
  111.3 9.5 %collective-permute-start.34 = (bf16[864,128]{1,0:T(8,128)(2,1)S(1)}, bf16[864,128]{1,0:T(8,128)(2,1)S(1)}, u32[]{:S(2)}, u32[]{:S(2)}) collective-permute-start(bf16[864,128]{1,0:T(8,128)(2,1)S(1)} %collective-permute-done.27.refs_1_.refs_5_), channel_id=1, source_target_pairs={{0,8},{4,12},{8,16},{12,20},{16,24},{20,28},{24,0},{28,4},{1,9},{5... | collective-permute-start | bytes 663560 | tf_op jit(solution)/shard_map/ppermute | solution.py:538
  111.6 20.5 %collective-permute-start.30 = (bf16[1536,128]{1,0:T(8,128)(2,1)S(1)}, bf16[1536,128]{1,0:T(8,128)(2,1)S(1)}, u32[]{:S(2)}, u32[]{:S(2)}) collective-permute-start(bf16[1536,128]{1,0:T(8,128)(2,1)S(1)} %shard_map.216.refs_0_), channel_id=1, source_target_pairs={{0,1},{1,0},{2,3},{3,2},{4,5},{5,4},{6,7},{7,6},{8,9},{9,8},{10,11... | collective-permute-start | bytes 1179656 | tf_op jit(solution)/shard_map/ppermute | solution.py:522
  119.5 12.6 %collective-permute-start.33 = (bf16[1536,128]{1,0:T(8,128)(2,1)S(1)}, bf16[1536,128]{1,0:T(8,128)(2,1)S(1)}, u32[]{:S(2)}, u32[]{:S(2)}) collective-permute-start(bf16[1536,128]{1,0:T(8,128)(2,1)S(1)} %collective-permute-done.31.refs_2_), channel_id=1, source_target_pairs={{0,1},{1,0},{2,3},{3,2},{4,5},{5,4},{6,7},{7,6},{8,9},{9,8},{10,11... | collective-permute-start | bytes 1179656 | tf_op jit(solution)/shard_map/ppermute | solution.py:522
  119.5 8.2 %collective-permute-start.36 = (bf16[864,128]{1,0:T(8,128)(2,1)S(1)}, bf16[864,128]{1,0:T(8,128)(2,1)S(1)}, u32[]{:S(2)}, u32[]{:S(2)}) collective-permute-start(bf16[864,128]{1,0:T(8,128)(2,1)S(1)} %collective-permute-done.28.refs_3_.refs_7_), channel_id=1, source_target_pairs={{0,4},{4,0},{8,12},{12,8},{16,20},{20,16},{24,28},{28,24},{1,5},{5... | collective-permute-start | bytes 663560 | tf_op jit(solution)/shard_map/ppermute | solution.py:522
  120.8 11.3 %collective-permute-start.35 = (bf16[864,128]{1,0:T(8,128)(2,1)S(1)}, bf16[864,128]{1,0:T(8,128)(2,1)S(1)}, u32[]{:S(2)}, u32[]{:S(2)}) collective-permute-start(bf16[864,128]{1,0:T(8,128)(2,1)S(1)} %collective-permute-done.34.refs_2_.refs_6_), channel_id=1, source_target_pairs={{0,4},{4,0},{8,12},{12,8},{16,20},{20,16},{24,28},{28,24},{1,5},{5... | collective-permute-start | bytes 663560 | tf_op jit(solution)/shard_map/ppermute | solution.py:522
  133.1 5.1 %collective-permute-start.37 = (bf16[208,192]{1,0:T(8,128)(2,1)S(1)}, bf16[208,192]{1,0:T(8,128)(2,1)S(1)}, u32[]{:S(2)}, u32[]{:S(2)}) collective-permute-start(bf16[208,192]{1,0:T(8,128)(2,1)S(1)} %get-tuple-element.159), channel_id=1, source_target_pairs={{0,1},{1,0},{2,3},{3,2},{4,5},{5,4},{6,7},{7,6},{8,9},{9,8},{10,11... | collective-permute-start | bytes 239624 | tf_op jit(solution)/shard_map/ppermute | solution.py:522
  133.2 5.8 %collective-permute-start.38 = (bf16[208,192]{1,0:T(8,128)(2,1)S(1)}, bf16[208,192]{1,0:T(8,128)(2,1)S(1)}, u32[]{:S(2)}, u32[]{:S(2)}) collective-permute-start(bf16[208,192]{1,0:T(8,128)(2,1)S(1)} %get-tuple-element.160), channel_id=1, source_target_pairs={{0,2},{1,3},{2,0},{3,1},{4,6},{5,7},{6,4},{7,5},{8,10},{9,11},{10,... | collective-permute-start | bytes 239624 | tf_op jit(solution)/shard_map/ppermute | solution.py:522
  134.3 6.0 %collective-permute-start.39 = (bf16[208,192]{1,0:T(8,128)(2,1)S(1)}, bf16[208,192]{1,0:T(8,128)(2,1)S(1)}, u32[]{:S(2)}, u32[]{:S(2)}) collective-permute-start(bf16[208,192]{1,0:T(8,128)(2,1)S(1)} %get-tuple-element.161), channel_id=1, source_target_pairs={{0,3},{1,2},{2,1},{3,0},{4,7},{5,6},{6,5},{7,4},{8,11},{9,10},{10,... | collective-permute-start | bytes 239624 | tf_op jit(solution)/shard_map/ppermute | solution.py:522
  (8 other events, 15.8 us)

commit v9 on v8

--- a/solution.py
+++ b/solution.py
@@ -630,7 +630,7 @@
         [(up_weight.shape, f32), (down_weight.shape, f32)],
         *after([u, z, de, da], across),
     )
-    token_packs = around(after([token_pack], across)[0])
+    token_packs = around(after([token_pack], up_grad)[0])
     if direct:
         (far,) = after([far], behind2, behind3, beside1)
     (far,) = after([far], up_grad, *token_packs[1:])
@@ -664,6 +664,8 @@
         fetch=(8, 9, 11),
         scratch=[pltpu.VMEM((model, tok), f32)] * 4,
     )
+    if direct:
+        (d_scores,) = after([d_scores], beside2, beside3)
     height = experts + 8
     if direct:
         last_shape = (inner + width + height * (model // tok), tok)

time: 142 us -> 140 us (0.986)
    ppermute x34, waiting for transfers between devices: 43.4 us -> 41.4 us  [swap(): return lax.ppermute(v, axis, [(i, i ^ k) for i in range(n)])]
    ppermute x6, waiting for transfers between devices: 12.1 us -> 14.1 us  [step(): return lax.ppermute(v, 'expert', [(i, (i + k) % n_e) for i in range(n_e)])]
  transfers between devices with their start and end apart: 40 -> 40, of which waited for: 16 -> 19; matrix products, arithmetic and copies ran while one was open for 0% -> 0% of each run, Pallas kernels for 8% -> 10%
where the time goes in v9:
time: 140 us
  waiting for transfers between devices  55.5 us (40%)
  starting transfers between devices  28 us (20%)
  blocking collectives  27.3 us (20%)
  Pallas kernels  22.5 us (16%)
  local copies, waits for them, and re-layouts  5.64 us (4%)
    ppermute x34, waiting for transfers between devices, swap(): return lax.ppermute(v, axis, [(i, i ^ k) for i in range(n)])  41.4 us
    all_to_all x2, blocking collectives, exchange(): v = lax.all_to_all(v, 'expert', split_axis=0, concat_axis=0, tiled=True)  27.3 us
    ppermute x34, starting transfers between devices, swap(): return lax.ppermute(v, axis, [(i, i ^ k) for i in range(n)])  23 us
    pallas_call x17, Pallas kernels, run(): pl.pallas_call(whole, out_shape=[jax.ShapeDtypeStruct(s, d) for s, d in o...  22.5 us
    ppermute x6, waiting for transfers between devices, step(): return lax.ppermute(v, 'expert', [(i, (i + k) % n_e) for i in range(n_e)])  14.1 us
    ppermute x6, starting transfers between devices, step(): return lax.ppermute(v, 'expert', [(i, (i + k) % n_e) for i in range(n_e)])  4.96 us
    unnamed x32, local copies, waits for them, and re-layouts  4.95 us
  transfers between devices with their start and end apart: 40, of which 19 were waited for; matrix products, arithmetic and copies ran while one was open for 0% of the time, Pallas kernels for 10%

profile of v9, /device:TPU:0, one launch (start us, length us, event | category | flops | bytes accessed | tf_op | source)
XLA Modules:
  0.0 139.8 jit_solution(9824681469732599080)
XLA Ops:
  0.7 2.5 %collective-permute-start.2 = (bf16[192,128]{1,0:T(8,128)(2,1)}, bf16[192,128]{1,0:T(8,128)(2,1)S(1)}, u32[]{:S(2)}, u32[]{:S(2)}) collective-permute-start(bf16[192,128]{1,0:T(8,128)(2,1)} %bitcast.28), channel_id=1, source_target_pairs={{0,3},{1,2},{2,1},{3,0},{4,7},{5,6},{6,5},{7,4},{8,11},{9,10},{10,... | collective-permute-start | bytes 147464 | tf_op jit(solution)/shard_map/ppermute | solution.py:522
  4.5 1.0 copy-done.2
  7.5 0.9 shard_map.204
  8.4 1.2 copy-done
  10.4 1.9 %shard_map.205 = (f32[192,128]{1,0:T(8,128)S(1)}, bf16[192,128]{1,0:T(8,128)(2,1)S(1)}, bf16[192,128]{1,0:T(8,128)(2,1)S(1)}, bf16[192,128]{1,0:T(8,128)(2,1)S(1...) custom-call(bf16[192,128]{1,0:T(8,128)(2,1)S(1)} %bitcast.31, ...), custom_call_target="tpu_custom_call" | custom-call | bytes 2412032 | tf_op jit(solution)/shard_map/pallas_call | solution.py:67
  12.9 1.4 %collective-permute-start.4 = (bf16[192,128]{1,0:T(8,128)(2,1)S(1)}, bf16[192,128]{1,0:T(8,128)(2,1)S(1)}, u32[]{:S(2)}, u32[]{:S(2)}) collective-permute-start(bf16[192,128]{1,0:T(8,128)(2,1)S(1)} %get-tuple-element.96), channel_id=1, source_target_pairs={{0,2},{1,3},{2,0},{3,1},{4,6},{5,7},{6,4},{7,5},{8,10},{9,11},{10,... | collective-permute-start | bytes 147464 | tf_op jit(solution)/shard_map/ppermute | solution.py:522
  15.1 1.9 %collective-permute-done.4.refs_2_ = bf16[192,128]{1,0:T(8,128)(2,1)S(1)} collective-permute-done((bf16[192,128]{1,0:T(8,128)(2,1)S(1)}, bf16[192,128]{1,0:T(8,128)(2,1)S(1)}, u32[]{:S(2)}, u32[]{:S(2)}) %collective-permute-start.4) | collective-permute-done | bytes 49184 | tf_op jit(solution)/shard_map/ppermute | solution.py:522
  17.0 1.1 collective-permute-done.5.refs_3_
  18.8 16.8 %all_to_all.10 = bf16[8,40,400]{2,1,0:T(8,128)(2,1)S(1)} all-to-all(bf16[8,40,400]{2,1,0:T(8,128)(2,1)S(1)} %bitcast.34), channel_id=1, replica_groups=mesh['expert'=8,'tensor'=4] {'expert'}, dimensions={0} | all-to-all | bytes 512000 | tf_op jit(solution)/shard_map/all_to_all | solution.py:534
  35.6 1.1 collective-permute-start.7
  37.9 5.0 %collective-permute-done.9.refs_4_ = bf16[960,128]{1,0:T(8,128)(2,1)S(1)} collective-permute-done((bf16[960,128]{1,0:T(8,128)(2,1)S(1)}, bf16[960,128]{1,0:T(8,128)(2,1)S(1)}, u32[]{:S(2)}, u32[]{:S(2)}) %collective-permute-start.9) | collective-permute-done | bytes 245792 | tf_op jit(solution)/shard_map/ppermute | solution.py:522
  42.9 2.8 %collective-permute-done.8.refs_1_.refs_5_ = bf16[960,128]{1,0:T(8,128)(2,1)S(1)} collective-permute-done((bf16[960,128]{1,0:T(8,128)(2,1)S(1)}, bf16[960,128]{1,0:T(8,128)(2,1)S(1)}, u32[]{:S(2)}, u32[]{:S(2)}) %collective-permute-start.8) | collective-permute-done | bytes 245792 | tf_op jit(solution)/shard_map/ppermute | solution.py:538
  45.7 1.6 %collective-permute-done.10.refs_3_ = bf16[320,400]{1,0:T(8,128)(2,1)S(1)} collective-permute-done((bf16[320,400]{1,0:T(8,128)(2,1)S(1)}, bf16[320,400]{1,0:T(8,128)(2,1)S(1)}, u32[]{:S(2)}, u32[]{:S(2)}) %collective-permute-start.10) | collective-permute-done | bytes 256032 | tf_op jit(solution)/shard_map/ppermute | solution.py:522
  47.3 3.0 %shard_map.208 = (bf16[320,384]{1,0:T(8,128)(2,1)S(1)}, bf16[320,384]{1,0:T(8,128)(2,1)S(1)}, bf16[640,384]{1,0:T(8,128)(2,1)S(1)}, bf16[320,768]{1,0:T(8,128)(2...) custom-call(bf16[320,400]{1,0:T(8,128)(2,1)S(1)} %bitcast.25, ...), custom_call_target="tpu_custom_call" | custom-call | bytes 6332416 | tf_op jit(solution)/shard_map/pallas_call | solution.py:67
  50.9 1.2 collective-permute-start.18
  52.1 1.5 %collective-permute-start.16 = (bf16[960,128]{1,0:T(8,128)(2,1)S(1)}, bf16[960,128]{1,0:T(8,128)(2,1)S(1)}, u32[]{:S(2)}, u32[]{:S(2)}) collective-permute-start(bf16[960,128]{1,0:T(8,128)(2,1)S(1)} %collective-permute-done.8.refs_1_.refs_5_), channel_id=1, source_target_pairs={{0,8},{4,12},{8,16},{12,20},{16,24},{20,28},{24,0},{28,4},{1,9},{5... | collective-permute-start | bytes 737288 | tf_op jit(solution)/shard_map/ppermute | solution.py:538
  53.6 1.0 collective-permute-start.15
  54.7 3.2 %shard_map.210 = (f32[1,768,768]{2,1,0:T(8,128)}, f32[1,768,768]{2,1,0:T(8,128)}) custom-call(bf16[320,768]{1,0:T(8,128)(2,1)S(1)} %get-tuple-element.113.refs_0_, bf16[320,768]{1,0:T(8,128)(2,1)S(1)} %get-tuple-element.114.refs_1_, bf16[320,768]{1,0:T(8,128)(2,1)S(1)} %get-tuple-element.115.refs_2_, bf16[320,768]{1,0:T(8,128)(2,1)S(1)} %get-tuple-element.116.refs_3_), custom_call_target="tpu_custom_call" | custom-call | bytes 6684672 | tf_op jit(solution)/shard_map/pallas_call | solution.py:67
  57.9 6.1 %collective-permute-done.17.refs_3_.refs_7_ = bf16[960,128]{1,0:T(8,128)(2,1)S(1)} collective-permute-done((bf16[960,128]{1,0:T(8,128)(2,1)S(1)}, bf16[960,128]{1,0:T(8,128)(2,1)S(1)}, u32[]{:S(2)}, u32[]{:S(2)}) %collective-permute-start.17) | collective-permute-done | bytes 245792 | tf_op jit(solution)/shard_map/ppermute | solution.py:538
  64.9 3.8 %collective-permute-done.13.refs_2_.refs_6_ = bf16[400,128]{1,0:T(8,128)(2,1)S(1)} collective-permute-done((bf16[400,128]{1,0:T(8,128)(2,1)S(1)}, bf16[400,128]{1,0:T(8,128)(2,1)S(1)}, u32[]{:S(2)}, u32[]{:S(2)}) %collective-permute-start.13) | collective-permute-done | bytes 102432 | tf_op jit(solution)/shard_map/ppermute | solution.py:522
  68.7 10.5 %all_to_all.11 = bf16[8,40,384]{2,1,0:T(8,128)(2,1)S(1)} all-to-all(bf16[8,40,384]{2,1,0:T(8,128)(2,1)S(1)} %bitcast.26), channel_id=1, replica_groups=mesh['expert'=8,'tensor'=4] {'expert'}, dimensions={0} | all-to-all | bytes 491520 | tf_op jit(solution)/shard_map/all_to_all | solution.py:534
  79.3 1.0 shard_map.212
  80.3 1.0 collective-permute-start.25
  81.3 1.1 collective-permute-start.26
  82.4 0.9 collective-permute-start.20
  83.3 1.0 collective-permute-start.19
  84.2 1.7 %collective-permute-done.21.refs_3_ = bf16[208,128]{1,0:T(8,128)(2,1)S(1)} collective-permute-done((bf16[208,128]{1,0:T(8,128)(2,1)S(1)}, bf16[208,128]{1,0:T(8,128)(2,1)S(1)}, u32[]{:S(2)}, u32[]{:S(2)}) %collective-permute-start.21) | collective-permute-done | bytes 53280 | tf_op jit(solution)/shard_map/ppermute | solution.py:522
  85.9 1.2 collective-permute-done.20.refs_2_
  87.1 2.6 %shard_map.213 = (bf16[208,128]{1,0:T(8,128)(2,1)S(1)}, bf16[208,128]{1,0:T(8,128)(2,1)S(1)}, bf16[208,128]{1,0:T(8,128)(2,1)S(1)}, bf16[208,128]{1,0:T(8,128)(2...) custom-call(bf16[208,128]{1,0:T(8,128)(2,1)S(1)} %get-tuple-element., ...), custom_call_target="tpu_custom_call" | custom-call | bytes 3313664 | tf_op jit(solution)/shard_map/pallas_call | solution.py:67
  89.8 1.2 collective-permute-start.23
  91.6 2.0 %shard_map.215 = (f32[16,768]{1,0:T(8,128)}, bf16[864,128]{1,0:T(8,128)(2,1)S(1)}) custom-call(bf16[400,128]{1,0:T(8,128)(2,1)S(1)} %get-tuple-element.118.refs_0_.refs_4_, bf16[400,128]{1,0:T(8,128)(2,1)S(1)} %collective-permute-done.12.refs_1_.refs_5_, bf16[400,128]{1,0:T(8,128)(2,1)S(1)} %collective-permute-done.13.refs_2_.refs_6_, ...), custom_call_target="tpu_custom_call" | custom-call | bytes 2656704 | tf_op jit(solution)/shard_map/pallas_call | solution.py:67
  94.1 1.0 collective-permute-done.24.refs_3_
  95.5 1.7 %collective-permute-start.28 = (bf16[864,128]{1,0:T(8,128)(2,1)S(1)}, bf16[864,128]{1,0:T(8,128)(2,1)S(1)}, u32[]{:S(2)}, u32[]{:S(2)}) collective-permute-start(bf16[864,128]{1,0:T(8,128)(2,1)S(1)} %get-tuple-element.144.refs_0_.refs_4_), channel_id=1, source_target_pairs={{0,24},{4,28},{8,0},{12,4},{16,8},{20,12},{24,16},{28,20},{1,25},{... | collective-permute-start | bytes 663560 | tf_op jit(solution)/shard_map/ppermute | solution.py:538
  97.6 4.9 %collective-permute-done.29.refs_8_.refs_0_ = bf16[864,128]{1,0:T(8,128)(2,1)S(1)} collective-permute-done((bf16[864,128]{1,0:T(8,128)(2,1)S(1)}, bf16[864,128]{1,0:T(8,128)(2,1)S(1)}, u32[]{:S(2)}, u32[]{:S(2)}) %collective-permute-start.29) | collective-permute-done | bytes 221216 | tf_op jit(solution)/shard_map/ppermute | solution.py:522
  102.5 5.2 %collective-permute-done.28.refs_3_.refs_7_ = bf16[864,128]{1,0:T(8,128)(2,1)S(1)} collective-permute-done((bf16[864,128]{1,0:T(8,128)(2,1)S(1)}, bf16[864,128]{1,0:T(8,128)(2,1)S(1)}, u32[]{:S(2)}, u32[]{:S(2)}) %collective-permute-start.28) | collective-permute-done | bytes 221216 | tf_op jit(solution)/shard_map/ppermute | solution.py:538
  107.7 1.0 collective-permute-start.31
  108.7 1.3 collective-permute-start.32
  110.7 4.1 %collective-permute-done.32.refs_9_.refs_1_ = bf16[864,128]{1,0:T(8,128)(2,1)S(1)} collective-permute-done((bf16[864,128]{1,0:T(8,128)(2,1)S(1)}, bf16[864,128]{1,0:T(8,128)(2,1)S(1)}, u32[]{:S(2)}, u32[]{:S(2)}) %collective-permute-start.32) | collective-permute-done | bytes 221216 | tf_op jit(solution)/shard_map/ppermute | solution.py:522
  114.8 3.0 %collective-permute-done.31.refs_2_ = bf16[1536,128]{1,0:T(8,128)(2,1)S(1)} collective-permute-done((bf16[1536,128]{1,0:T(8,128)(2,1)S(1)}, bf16[1536,128]{1,0:T(8,128)(2,1)S(1)}, u32[]{:S(2)}, u32[]{:S(2)}) %collective-permute-start.31) | collective-permute-done | bytes 393248 | tf_op jit(solution)/shard_map/ppermute | solution.py:522
  117.8 1.2 collective-permute-start.36
  119.9 1.1 shard_map.217.refs_8_
  121.0 5.1 %collective-permute-done.36.refs_11_.refs_3_ = bf16[864,128]{1,0:T(8,128)(2,1)S(1)} collective-permute-done((bf16[864,128]{1,0:T(8,128)(2,1)S(1)}, bf16[864,128]{1,0:T(8,128)(2,1)S(1)}, u32[]{:S(2)}, u32[]{:S(2)}) %collective-permute-start.36) | collective-permute-done | bytes 221216 | tf_op jit(solution)/shard_map/ppermute | solution.py:522
  126.1 4.4 %collective-permute-done.35.refs_10_.refs_2_ = bf16[864,128]{1,0:T(8,128)(2,1)S(1)} collective-permute-done((bf16[864,128]{1,0:T(8,128)(2,1)S(1)}, bf16[864,128]{1,0:T(8,128)(2,1)S(1)}, u32[]{:S(2)}, u32[]{:S(2)}) %collective-permute-start.35) | collective-permute-done | bytes 221216 | tf_op jit(solution)/shard_map/ppermute | solution.py:522
  130.4 1.0 shard_map.218
  131.5 1.0 collective-permute-start.38
  134.2 2.3 %shard_map.220 = f32[576,768]{1,0:T(8,128)} custom-call(bf16[864,128]{1,0:T(8,128)(2,1)S(1)} %collective-permute-done.29.refs_8_.refs_0_, bf16[864,128]{1,0:T(8,128)(2,1)S(1)} %collective-permute-done.32.refs_9_.refs_1_, bf16[864,128]{1,0:T(8,128)(2,1)S(1)} %collective-permute-done.35.refs_10_.refs_2_, ...), custom_call_target="tpu_custom_call" | custom-call | bytes 5406720 | tf_op jit(solution)/shard_map/pallas_call | solution.py:67
  137.3 1.4 collective-permute-done.39.refs_3_
  138.7 1.1 shard_map.219
  (85 shorter events, 15.2 us)
Async XLA Ops:
  0.6 13.7 %copy-start.9 = (bf16[768,8]{0,1:T(8,128)(2,1)S(1)}, bf16[768,8]{0,1:T(8,128)(2,1)}, u32[]{:S(2)}) copy-start(bf16[768,8]{0,1:T(8,128)(2,1)} %param.19) | copy-start | bytes 36868
  0.7 7.7 %collective-permute-start.2 = (bf16[192,128]{1,0:T(8,128)(2,1)}, bf16[192,128]{1,0:T(8,128)(2,1)S(1)}, u32[]{:S(2)}, u32[]{:S(2)}) collective-permute-start(bf16[192,128]{1,0:T(8,128)(2,1)} %bitcast.28), channel_id=1, source_target_pairs={{0,3},{1,2},{2,1},{3,0},{4,7},{5,6},{6,5},{7,4},{8,11},{9,10},{10,... | collective-permute-start | bytes 147464 | tf_op jit(solution)/shard_map/ppermute | solution.py:522
  3.1 5.3 %collective-permute-start.1 = (bf16[192,128]{1,0:T(8,128)(2,1)}, bf16[192,128]{1,0:T(8,128)(2,1)S(1)}, u32[]{:S(2)}, u32[]{:S(2)}) collective-permute-start(bf16[192,128]{1,0:T(8,128)(2,1)} %bitcast.29), channel_id=1, source_target_pairs={{0,2},{1,3},{2,0},{3,1},{4,6},{5,7},{6,4},{7,5},{8,10},{9,11},{10,... | collective-permute-start | bytes 147464 | tf_op jit(solution)/shard_map/ppermute | solution.py:522
  3.8 4.6 %collective-permute-start = (bf16[192,128]{1,0:T(8,128)(2,1)}, bf16[192,128]{1,0:T(8,128)(2,1)S(1)}, u32[]{:S(2)}, u32[]{:S(2)}) collective-permute-start(bf16[192,128]{1,0:T(8,128)(2,1)} %bitcast.30), channel_id=1, source_target_pairs={{0,1},{1,0},{2,3},{3,2},{4,5},{5,4},{6,7},{7,6},{8,9},{9,8},{10,11... | collective-permute-start | bytes 147464 | tf_op jit(solution)/shard_map/ppermute | solution.py:522
  7.5 6.9 %copy-start.10 = (s32[128,2]{0,1:T(2,128)S(1)}, s32[128,2]{0,1:T(2,128)}, u32[]{:S(2)}) copy-start(s32[128,2]{0,1:T(2,128)} %param.22) | copy-start | bytes 3076
  7.5 10.6 %copy-start.7 = (bf16[128,192]{0,1:T(8,128)(2,1)S(1)}, bf16[128,192]{0,1:T(8,128)(2,1)}, u32[]{:S(2)}) copy-start(bf16[128,192]{0,1:T(8,128)(2,1)} %param.13) | copy-start | bytes 147460
  7.5 10.6 %copy-start.8 = (bf16[128,192]{0,1:T(8,128)(2,1)S(1)}, bf16[128,192]{0,1:T(8,128)(2,1)}, u32[]{:S(2)}) copy-start(bf16[128,192]{0,1:T(8,128)(2,1)} %param.25) | copy-start | bytes 147460
  10.4 36.9 %copy-start.4 = (bf16[1,768,768]{2,1,0:T(8,128)(2,1)S(1)}, bf16[1,768,768]{2,1,0:T(8,128)(2,1)}, u32[]{:S(2)}) copy-start(bf16[1,768,768]{2,1,0:T(8,128)(2,1)} %refs_4_.1) | copy-start | bytes 3538948
  10.4 36.9 %copy-start.5 = (bf16[1,768,768]{2,1,0:T(8,128)(2,1)S(1)}, bf16[1,768,768]{2,1,0:T(8,128)(2,1)}, u32[]{:S(2)}) copy-start(bf16[1,768,768]{2,1,0:T(8,128)(2,1)} %refs_5_.1) | copy-start | bytes 3538948
  12.3 2.7 %collective-permute-start.3 = (bf16[192,128]{1,0:T(8,128)(2,1)S(1)}, bf16[192,128]{1,0:T(8,128)(2,1)S(1)}, u32[]{:S(2)}, u32[]{:S(2)}) collective-permute-start(bf16[192,128]{1,0:T(8,128)(2,1)S(1)} %get-tuple-element.95), channel_id=1, source_target_pairs={{0,1},{1,0},{2,3},{3,2},{4,5},{5,4},{6,7},{7,6},{8,9},{9,8},{10,11... | collective-permute-start | bytes 147464 | tf_op jit(solution)/shard_map/ppermute | solution.py:522
  12.9 4.1 %collective-permute-start.4 = (bf16[192,128]{1,0:T(8,128)(2,1)S(1)}, bf16[192,128]{1,0:T(8,128)(2,1)S(1)}, u32[]{:S(2)}, u32[]{:S(2)}) collective-permute-start(bf16[192,128]{1,0:T(8,128)(2,1)S(1)} %get-tuple-element.96), channel_id=1, source_target_pairs={{0,2},{1,3},{2,0},{3,1},{4,6},{5,7},{6,4},{7,5},{8,10},{9,11},{10,... | collective-permute-start | bytes 147464 | tf_op jit(solution)/shard_map/ppermute | solution.py:522
  14.3 3.8 %collective-permute-start.5 = (bf16[192,128]{1,0:T(8,128)(2,1)S(1)}, bf16[192,128]{1,0:T(8,128)(2,1)S(1)}, u32[]{:S(2)}, u32[]{:S(2)}) collective-permute-start(bf16[192,128]{1,0:T(8,128)(2,1)S(1)} %get-tuple-element.97), channel_id=1, source_target_pairs={{0,3},{1,2},{2,1},{3,0},{4,7},{5,6},{6,5},{7,4},{8,11},{9,10},{10,... | collective-permute-start | bytes 147464 | tf_op jit(solution)/shard_map/ppermute | solution.py:522
  35.6 10.0 %collective-permute-start.7 = (bf16[320,400]{1,0:T(8,128)(2,1)S(1)}, bf16[320,400]{1,0:T(8,128)(2,1)S(1)}, u32[]{:S(2)}, u32[]{:S(2)}) collective-permute-start(bf16[320,400]{1,0:T(8,128)(2,1)S(1)} %bitcast.23), channel_id=1, source_target_pairs={{0,2},{1,3},{2,0},{3,1},{4,6},{5,7},{6,4},{7,5},{8,10},{9,11},{10,... | collective-permute-start | bytes 768008 | tf_op jit(solution)/shard_map/ppermute | solution.py:522
  36.7 6.2 %collective-permute-start.9 = (bf16[960,128]{1,0:T(8,128)(2,1)S(1)}, bf16[960,128]{1,0:T(8,128)(2,1)S(1)}, u32[]{:S(2)}, u32[]{:S(2)}) collective-permute-start(bf16[960,128]{1,0:T(8,128)(2,1)S(1)} %get-tuple-element.146.refs_8_.refs_0_.refs_4_), channel_id=1, source_target_pairs={{0,4},{4,0},{8,12},{12,8},{16,20},{20,16},{24,28},{28,24},{1,5},{5... | collective-permute-start | bytes 737288 | tf_op jit(solution)/shard_map/ppermute | solution.py:522
  37.5 8.1 %collective-permute-start.8 = (bf16[960,128]{1,0:T(8,128)(2,1)S(1)}, bf16[960,128]{1,0:T(8,128)(2,1)S(1)}, u32[]{:S(2)}, u32[]{:S(2)}) collective-permute-start(bf16[960,128]{1,0:T(8,128)(2,1)S(1)} %get-tuple-element.146.refs_8_.refs_0_.refs_4_), channel_id=1, source_target_pairs={{0,8},{4,12},{8,16},{12,20},{16,24},{20,28},{24,0},{28,4},{1,9},{5... | collective-permute-start | bytes 737288 | tf_op jit(solution)/shard_map/ppermute | solution.py:538
  37.9 7.8 %collective-permute-start.6 = (bf16[320,400]{1,0:T(8,128)(2,1)S(1)}, bf16[320,400]{1,0:T(8,128)(2,1)S(1)}, u32[]{:S(2)}, u32[]{:S(2)}) collective-permute-start(bf16[320,400]{1,0:T(8,128)(2,1)S(1)} %bitcast.24), channel_id=1, source_target_pairs={{0,1},{1,0},{2,3},{3,2},{4,5},{5,4},{6,7},{7,6},{8,9},{9,8},{10,11... | collective-permute-start | bytes 768008 | tf_op jit(solution)/shard_map/ppermute | solution.py:522
  45.7 1.6 %collective-permute-start.10 = (bf16[320,400]{1,0:T(8,128)(2,1)S(1)}, bf16[320,400]{1,0:T(8,128)(2,1)S(1)}, u32[]{:S(2)}, u32[]{:S(2)}) collective-permute-start(bf16[320,400]{1,0:T(8,128)(2,1)S(1)} %collective-permute-done.7.refs_2_), channel_id=1, source_target_pairs={{0,1},{1,0},{2,3},{3,2},{4,5},{5,4},{6,7},{7,6},{8,9},{9,8},{10,11... | collective-permute-start | bytes 768008 | tf_op jit(solution)/shard_map/ppermute | solution.py:522
  50.3 3.3 %collective-permute-start.11 = (bf16[640,384]{1,0:T(8,128)(2,1)S(1)}, bf16[640,384]{1,0:T(8,128)(2,1)S(1)}, u32[]{:S(2)}, u32[]{:S(2)}) collective-permute-start(bf16[640,384]{1,0:T(8,128)(2,1)S(1)} %get-tuple-element.112), channel_id=1, source_target_pairs={{0,1},{1,0},{2,3},{3,2},{4,5},{5,4},{6,7},{7,6},{8,9},{9,8},{10,11... | collective-permute-start | bytes 1474568 | tf_op jit(solution)/shard_map/ppermute | solution.py:522
  50.5 13.5 %collective-permute-start.17 = (bf16[960,128]{1,0:T(8,128)(2,1)S(1)}, bf16[960,128]{1,0:T(8,128)(2,1)S(1)}, u32[]{:S(2)}, u32[]{:S(2)}) collective-permute-start(bf16[960,128]{1,0:T(8,128)(2,1)S(1)} %get-tuple-element.146.refs_8_.refs_0_.refs_4_), channel_id=1, source_target_pairs={{0,24},{4,28},{8,0},{12,4},{16,8},{20,12},{24,16},{28,20},{1,25},{... | collective-permute-start | bytes 737288 | tf_op jit(solution)/shard_map/ppermute | solution.py:538
  50.9 14.0 %collective-permute-start.18 = (bf16[960,128]{1,0:T(8,128)(2,1)S(1)}, bf16[960,128]{1,0:T(8,128)(2,1)S(1)}, u32[]{:S(2)}, u32[]{:S(2)}) collective-permute-start(bf16[960,128]{1,0:T(8,128)(2,1)S(1)} %collective-permute-done.8.refs_1_.refs_5_), channel_id=1, source_target_pairs={{0,4},{4,0},{8,12},{12,8},{16,20},{20,16},{24,28},{28,24},{1,5},{5... | collective-permute-start | bytes 737288 | tf_op jit(solution)/shard_map/ppermute | solution.py:522
  52.1 12.8 %collective-permute-start.16 = (bf16[960,128]{1,0:T(8,128)(2,1)S(1)}, bf16[960,128]{1,0:T(8,128)(2,1)S(1)}, u32[]{:S(2)}, u32[]{:S(2)}) collective-permute-start(bf16[960,128]{1,0:T(8,128)(2,1)S(1)} %collective-permute-done.8.refs_1_.refs_5_), channel_id=1, source_target_pairs={{0,8},{4,12},{8,16},{12,20},{16,24},{20,28},{24,0},{28,4},{1,9},{5... | collective-permute-start | bytes 737288 | tf_op jit(solution)/shard_map/ppermute | solution.py:538
  53.6 11.2 %collective-permute-start.15 = (bf16[320,384]{1,0:T(8,128)(2,1)S(1)}, bf16[320,384]{1,0:T(8,128)(2,1)S(1)}, u32[]{:S(2)}, u32[]{:S(2)}) collective-permute-start(bf16[320,384]{1,0:T(8,128)(2,1)S(1)} %shard_map.209), channel_id=1, source_target_pairs={{0,2},{1,3},{2,0},{3,1},{4,6},{5,7},{6,4},{7,5},{8,10},{9,11},{10,... | collective-permute-start | bytes 737288 | tf_op jit(solution)/shard_map/ppermute | solution.py:522
  54.7 32.4 %copy-start.3 = (bf16[192,768]{1,0:T(8,128)(2,1)S(1)}, bf16[192,768]{1,0:T(8,128)(2,1)}, u32[]{:S(2)}) copy-start(bf16[192,768]{1,0:T(8,128)(2,1)} %refs_11_.1) | copy-start | bytes 884740
  57.8 7.0 %collective-permute-start.14 = (bf16[400,128]{1,0:T(8,128)(2,1)S(1)}, bf16[400,128]{1,0:T(8,128)(2,1)S(1)}, u32[]{:S(2)}, u32[]{:S(2)}) collective-permute-start(bf16[400,128]{1,0:T(8,128)(2,1)S(1)} %get-tuple-element.118.refs_0_.refs_4_), channel_id=1, source_target_pairs={{0,3},{1,2},{2,1},{3,0},{4,7},{5,6},{6,5},{7,4},{8,11},{9,10},{10,... | collective-permute-start | bytes 307208 | tf_op jit(solution)/shard_map/ppermute | solution.py:522
  64.0 4.7 %collective-permute-start.13 = (bf16[400,128]{1,0:T(8,128)(2,1)S(1)}, bf16[400,128]{1,0:T(8,128)(2,1)S(1)}, u32[]{:S(2)}, u32[]{:S(2)}) collective-permute-start(bf16[400,128]{1,0:T(8,128)(2,1)S(1)} %get-tuple-element.118.refs_0_.refs_4_), channel_id=1, source_target_pairs={{0,2},{1,3},{2,0},{3,1},{4,6},{5,7},{6,4},{7,5},{8,10},{9,11},{10,... | collective-permute-start | bytes 307208 | tf_op jit(solution)/shard_map/ppermute | solution.py:522
  64.9 3.8 %collective-permute-start.12 = (bf16[400,128]{1,0:T(8,128)(2,1)S(1)}, bf16[400,128]{1,0:T(8,128)(2,1)S(1)}, u32[]{:S(2)}, u32[]{:S(2)}) collective-permute-start(bf16[400,128]{1,0:T(8,128)(2,1)S(1)} %get-tuple-element.118.refs_0_.refs_4_), channel_id=1, source_target_pairs={{0,1},{1,0},{2,3},{3,2},{4,5},{5,4},{6,7},{7,6},{8,9},{9,8},{10,11... | collective-permute-start | bytes 307208 | tf_op jit(solution)/shard_map/ppermute | solution.py:522
  79.3 12.4 %copy-start.13 = (s32[112]{0:T(128)S(1)}, s32[112]{0:T(128)}, u32[]{:S(2)}) copy-start(s32[112]{0:T(128)} %param.24) | copy-start | bytes 1348
  80.3 11.3 %collective-permute-start.25 = (bf16[960,128]{1,0:T(8,128)(2,1)S(1)}, bf16[960,128]{1,0:T(8,128)(2,1)S(1)}, u32[]{:S(2)}, u32[]{:S(2)}) collective-permute-start(bf16[960,128]{1,0:T(8,128)(2,1)S(1)} %collective-permute-done.16.refs_2_.refs_6_), channel_id=1, source_target_pairs={{0,4},{4,0},{8,12},{12,8},{16,20},{20,16},{24,28},{28,24},{1,5},{5... | collective-permute-start | bytes 737288 | tf_op jit(solution)/shard_map/ppermute | solution.py:522
  81.3 10.3 %collective-permute-start.26 = (bf16[960,128]{1,0:T(8,128)(2,1)S(1)}, bf16[960,128]{1,0:T(8,128)(2,1)S(1)}, u32[]{:S(2)}, u32[]{:S(2)}) collective-permute-start(bf16[960,128]{1,0:T(8,128)(2,1)S(1)} %collective-permute-done.17.refs_3_.refs_7_), channel_id=1, source_target_pairs={{0,4},{4,0},{8,12},{12,8},{16,20},{20,16},{24,28},{28,24},{1,5},{5... | collective-permute-start | bytes 737288 | tf_op jit(solution)/shard_map/ppermute | solution.py:522
  82.4 3.6 %collective-permute-start.21 = (bf16[208,128]{1,0:T(8,128)(2,1)S(1)}, bf16[208,128]{1,0:T(8,128)(2,1)S(1)}, u32[]{:S(2)}, u32[]{:S(2)}) collective-permute-start(bf16[208,128]{1,0:T(8,128)(2,1)S(1)} %get-tuple-element.126.refs_0_), channel_id=1, source_target_pairs={{0,3},{1,2},{2,1},{3,0},{4,7},{5,6},{6,5},{7,4},{8,11},{9,10},{10,... | collective-permute-start | bytes 159752 | tf_op jit(solution)/shard_map/ppermute | solution.py:522
  82.4 4.7 %collective-permute-start.20 = (bf16[208,128]{1,0:T(8,128)(2,1)S(1)}, bf16[208,128]{1,0:T(8,128)(2,1)S(1)}, u32[]{:S(2)}, u32[]{:S(2)}) collective-permute-start(bf16[208,128]{1,0:T(8,128)(2,1)S(1)} %get-tuple-element.126.refs_0_), channel_id=1, source_target_pairs={{0,2},{1,3},{2,0},{3,1},{4,6},{5,7},{6,4},{7,5},{8,10},{9,11},{10,... | collective-permute-start | bytes 159752 | tf_op jit(solution)/shard_map/ppermute | solution.py:522
  83.3 3.8 %collective-permute-start.19 = (bf16[208,128]{1,0:T(8,128)(2,1)S(1)}, bf16[208,128]{1,0:T(8,128)(2,1)S(1)}, u32[]{:S(2)}, u32[]{:S(2)}) collective-permute-start(bf16[208,128]{1,0:T(8,128)(2,1)S(1)} %get-tuple-element.126.refs_0_), channel_id=1, source_target_pairs={{0,1},{1,0},{2,3},{3,2},{4,5},{5,4},{6,7},{7,6},{8,9},{9,8},{10,11... | collective-permute-start | bytes 159752 | tf_op jit(solution)/shard_map/ppermute | solution.py:522
  89.7 4.0 %collective-permute-start.22 = (bf16[208,128]{1,0:T(8,128)(2,1)S(1)}, bf16[208,128]{1,0:T(8,128)(2,1)S(1)}, u32[]{:S(2)}, u32[]{:S(2)}) collective-permute-start(bf16[208,128]{1,0:T(8,128)(2,1)S(1)} %get-tuple-element.131), channel_id=1, source_target_pairs={{0,1},{1,0},{2,3},{3,2},{4,5},{5,4},{6,7},{7,6},{8,9},{9,8},{10,11... | collective-permute-start | bytes 159752 | tf_op jit(solution)/shard_map/ppermute | solution.py:522
  89.8 4.2 %collective-permute-start.23 = (bf16[208,128]{1,0:T(8,128)(2,1)S(1)}, bf16[208,128]{1,0:T(8,128)(2,1)S(1)}, u32[]{:S(2)}, u32[]{:S(2)}) collective-permute-start(bf16[208,128]{1,0:T(8,128)(2,1)S(1)} %get-tuple-element.132), channel_id=1, source_target_pairs={{0,2},{1,3},{2,0},{3,1},{4,6},{5,7},{6,4},{7,5},{8,10},{9,11},{10,... | collective-permute-start | bytes 159752 | tf_op jit(solution)/shard_map/ppermute | solution.py:522
  91.0 4.1 %collective-permute-start.24 = (bf16[208,128]{1,0:T(8,128)(2,1)S(1)}, bf16[208,128]{1,0:T(8,128)(2,1)S(1)}, u32[]{:S(2)}, u32[]{:S(2)}) collective-permute-start(bf16[208,128]{1,0:T(8,128)(2,1)S(1)} %get-tuple-element.133), channel_id=1, source_target_pairs={{0,3},{1,2},{2,1},{3,0},{4,7},{5,6},{6,5},{7,4},{8,11},{9,10},{10,... | collective-permute-start | bytes 159752 | tf_op jit(solution)/shard_map/ppermute | solution.py:522
  95.0 7.4 %collective-permute-start.29 = (bf16[864,128]{1,0:T(8,128)(2,1)S(1)}, bf16[864,128]{1,0:T(8,128)(2,1)S(1)}, u32[]{:S(2)}, u32[]{:S(2)}) collective-permute-start(bf16[864,128]{1,0:T(8,128)(2,1)S(1)} %get-tuple-element.144.refs_0_.refs_4_), channel_id=1, source_target_pairs={{0,4},{4,0},{8,12},{12,8},{16,20},{20,16},{24,28},{28,24},{1,5},{5... | collective-permute-start | bytes 663560 | tf_op jit(solution)/shard_map/ppermute | solution.py:522
  95.5 12.1 %collective-permute-start.28 = (bf16[864,128]{1,0:T(8,128)(2,1)S(1)}, bf16[864,128]{1,0:T(8,128)(2,1)S(1)}, u32[]{:S(2)}, u32[]{:S(2)}) collective-permute-start(bf16[864,128]{1,0:T(8,128)(2,1)S(1)} %get-tuple-element.144.refs_0_.refs_4_), channel_id=1, source_target_pairs={{0,24},{4,28},{8,0},{12,4},{16,8},{20,12},{24,16},{28,20},{1,25},{... | collective-permute-start | bytes 663560 | tf_op jit(solution)/shard_map/ppermute | solution.py:538
  97.2 10.5 %collective-permute-start.27 = (bf16[864,128]{1,0:T(8,128)(2,1)S(1)}, bf16[864,128]{1,0:T(8,128)(2,1)S(1)}, u32[]{:S(2)}, u32[]{:S(2)}) collective-permute-start(bf16[864,128]{1,0:T(8,128)(2,1)S(1)} %get-tuple-element.144.refs_0_.refs_4_), channel_id=1, source_target_pairs={{0,8},{4,12},{8,16},{12,20},{16,24},{20,28},{24,0},{28,4},{1,9},{5... | collective-permute-start | bytes 663560 | tf_op jit(solution)/shard_map/ppermute | solution.py:538
  107.7 10.1 %collective-permute-start.31 = (bf16[1536,128]{1,0:T(8,128)(2,1)S(1)}, bf16[1536,128]{1,0:T(8,128)(2,1)S(1)}, u32[]{:S(2)}, u32[]{:S(2)}) collective-permute-start(bf16[1536,128]{1,0:T(8,128)(2,1)S(1)} %shard_map.216.refs_0_), channel_id=1, source_target_pairs={{0,2},{1,3},{2,0},{3,1},{4,6},{5,7},{6,4},{7,5},{8,10},{9,11},{10,... | collective-permute-start | bytes 1179656 | tf_op jit(solution)/shard_map/ppermute | solution.py:522
  108.7 6.1 %collective-permute-start.32 = (bf16[864,128]{1,0:T(8,128)(2,1)S(1)}, bf16[864,128]{1,0:T(8,128)(2,1)S(1)}, u32[]{:S(2)}, u32[]{:S(2)}) collective-permute-start(bf16[864,128]{1,0:T(8,128)(2,1)S(1)} %collective-permute-done.27.refs_1_.refs_5_), channel_id=1, source_target_pairs={{0,4},{4,0},{8,12},{12,8},{16,20},{20,16},{24,28},{28,24},{1,5},{5... | collective-permute-start | bytes 663560 | tf_op jit(solution)/shard_map/ppermute | solution.py:522
  110.0 9.1 %collective-permute-start.34 = (bf16[864,128]{1,0:T(8,128)(2,1)S(1)}, bf16[864,128]{1,0:T(8,128)(2,1)S(1)}, u32[]{:S(2)}, u32[]{:S(2)}) collective-permute-start(bf16[864,128]{1,0:T(8,128)(2,1)S(1)} %collective-permute-done.27.refs_1_.refs_5_), channel_id=1, source_target_pairs={{0,8},{4,12},{8,16},{12,20},{16,24},{20,28},{24,0},{28,4},{1,9},{5... | collective-permute-start | bytes 663560 | tf_op jit(solution)/shard_map/ppermute | solution.py:538
  110.7 19.7 %collective-permute-start.30 = (bf16[1536,128]{1,0:T(8,128)(2,1)S(1)}, bf16[1536,128]{1,0:T(8,128)(2,1)S(1)}, u32[]{:S(2)}, u32[]{:S(2)}) collective-permute-start(bf16[1536,128]{1,0:T(8,128)(2,1)S(1)} %shard_map.216.refs_0_), channel_id=1, source_target_pairs={{0,1},{1,0},{2,3},{3,2},{4,5},{5,4},{6,7},{7,6},{8,9},{9,8},{10,11... | collective-permute-start | bytes 1179656 | tf_op jit(solution)/shard_map/ppermute | solution.py:522
  117.8 12.6 %collective-permute-start.33 = (bf16[1536,128]{1,0:T(8,128)(2,1)S(1)}, bf16[1536,128]{1,0:T(8,128)(2,1)S(1)}, u32[]{:S(2)}, u32[]{:S(2)}) collective-permute-start(bf16[1536,128]{1,0:T(8,128)(2,1)S(1)} %collective-permute-done.31.refs_2_), channel_id=1, source_target_pairs={{0,1},{1,0},{2,3},{3,2},{4,5},{5,4},{6,7},{7,6},{8,9},{9,8},{10,11... | collective-permute-start | bytes 1179656 | tf_op jit(solution)/shard_map/ppermute | solution.py:522
  117.8 8.2 %collective-permute-start.36 = (bf16[864,128]{1,0:T(8,128)(2,1)S(1)}, bf16[864,128]{1,0:T(8,128)(2,1)S(1)}, u32[]{:S(2)}, u32[]{:S(2)}) collective-permute-start(bf16[864,128]{1,0:T(8,128)(2,1)S(1)} %collective-permute-done.28.refs_3_.refs_7_), channel_id=1, source_target_pairs={{0,4},{4,0},{8,12},{12,8},{16,20},{20,16},{24,28},{28,24},{1,5},{5... | collective-permute-start | bytes 663560 | tf_op jit(solution)/shard_map/ppermute | solution.py:522
  119.1 11.3 %collective-permute-start.35 = (bf16[864,128]{1,0:T(8,128)(2,1)S(1)}, bf16[864,128]{1,0:T(8,128)(2,1)S(1)}, u32[]{:S(2)}, u32[]{:S(2)}) collective-permute-start(bf16[864,128]{1,0:T(8,128)(2,1)S(1)} %collective-permute-done.34.refs_2_.refs_6_), channel_id=1, source_target_pairs={{0,4},{4,0},{8,12},{12,8},{16,20},{20,16},{24,28},{28,24},{1,5},{5... | collective-permute-start | bytes 663560 | tf_op jit(solution)/shard_map/ppermute | solution.py:522
  131.4 5.1 %collective-permute-start.37 = (bf16[208,192]{1,0:T(8,128)(2,1)S(1)}, bf16[208,192]{1,0:T(8,128)(2,1)S(1)}, u32[]{:S(2)}, u32[]{:S(2)}) collective-permute-start(bf16[208,192]{1,0:T(8,128)(2,1)S(1)} %get-tuple-element.161), channel_id=1, source_target_pairs={{0,1},{1,0},{2,3},{3,2},{4,5},{5,4},{6,7},{7,6},{8,9},{9,8},{10,11... | collective-permute-start | bytes 239624 | tf_op jit(solution)/shard_map/ppermute | solution.py:522
  131.5 5.8 %collective-permute-start.38 = (bf16[208,192]{1,0:T(8,128)(2,1)S(1)}, bf16[208,192]{1,0:T(8,128)(2,1)S(1)}, u32[]{:S(2)}, u32[]{:S(2)}) collective-permute-start(bf16[208,192]{1,0:T(8,128)(2,1)S(1)} %get-tuple-element.162), channel_id=1, source_target_pairs={{0,2},{1,3},{2,0},{3,1},{4,6},{5,7},{6,4},{7,5},{8,10},{9,11},{10,... | collective-permute-start | bytes 239624 | tf_op jit(solution)/shard_map/ppermute | solution.py:522
  132.5 6.2 %collective-permute-start.39 = (bf16[208,192]{1,0:T(8,128)(2,1)S(1)}, bf16[208,192]{1,0:T(8,128)(2,1)S(1)}, u32[]{:S(2)}, u32[]{:S(2)}) collective-permute-start(bf16[208,192]{1,0:T(8,128)(2,1)S(1)} %get-tuple-element.163), channel_id=1, source_target_pairs={{0,3},{1,2},{2,1},{3,0},{4,7},{5,6},{6,5},{7,4},{8,11},{9,10},{10,... | collective-permute-start | bytes 239624 | tf_op jit(solution)/shard_map/ppermute | solution.py:522
  (8 other events, 15.8 us)

commit v10 on v9

--- a/solution.py
+++ b/solution.py
@@ -705,7 +705,7 @@
         )
         lasts += [next_to] + [swap(v, 1, "expert", n_e) for v in lasts[1:]]
         atts = [att, swap(att, 1), swap(att, 2)]
-        atts.append(swap(after(atts[2:], lasts[half + 1])[0], 1))
+        atts.append(swap(after(atts[2:], lasts[half + 3])[0], 1))
         lasts[half:] = after(lasts[half:], part)
         small, own, q1, q2, q3 = run(
             functools.partial(late_sum_kernel, n_e=n_e, inner=inner),

time: 140 us -> 140 us (level)
  no operation moved by 1% of the time
where the time goes in v10:
time: 140 us
  waiting for transfers between devices  55.5 us (40%)
  starting transfers between devices  28 us (20%)
  blocking collectives  27.3 us (20%)
  Pallas kernels  22.5 us (16%)
  local copies, waits for them, and re-layouts  5.64 us (4%)
    ppermute x34, waiting for transfers between devices, swap(): return lax.ppermute(v, axis, [(i, i ^ k) for i in range(n)])  41.4 us
    all_to_all x2, blocking collectives, exchange(): v = lax.all_to_all(v, 'expert', split_axis=0, concat_axis=0, tiled=True)  27.3 us
    ppermute x34, starting transfers between devices, swap(): return lax.ppermute(v, axis, [(i, i ^ k) for i in range(n)])  23 us
    pallas_call x17, Pallas kernels, run(): pl.pallas_call(whole, out_shape=[jax.ShapeDtypeStruct(s, d) for s, d in o...  22.5 us
    ppermute x6, waiting for transfers between devices, step(): return lax.ppermute(v, 'expert', [(i, (i + k) % n_e) for i in range(n_e)])  14.1 us
    ppermute x6, starting transfers between devices, step(): return lax.ppermute(v, 'expert', [(i, (i + k) % n_e) for i in range(n_e)])  4.96 us
    unnamed x32, local copies, waits for them, and re-layouts  4.95 us
  transfers between devices with their start and end apart: 40, of which 19 were waited for; matrix products, arithmetic and copies ran while one was open for 0% of the time, Pallas kernels for 10%

profile of v10, /device:TPU:0, one launch (start us, length us, event | category | flops | bytes accessed | tf_op | source)
XLA Modules:
  0.0 139.8 jit_solution(16409082750466851923)
XLA Ops:
  0.7 2.5 %collective-permute-start.2 = (bf16[192,128]{1,0:T(8,128)(2,1)}, bf16[192,128]{1,0:T(8,128)(2,1)S(1)}, u32[]{:S(2)}, u32[]{:S(2)}) collective-permute-start(bf16[192,128]{1,0:T(8,128)(2,1)} %bitcast.28), channel_id=1, source_target_pairs={{0,3},{1,2},{2,1},{3,0},{4,7},{5,6},{6,5},{7,4},{8,11},{9,10},{10,... | collective-permute-start | bytes 147464 | tf_op jit(solution)/shard_map/ppermute | solution.py:522
  4.5 1.0 copy-done.2
  7.5 0.9 shard_map.204
  8.4 1.2 copy-done
  10.4 1.9 %shard_map.205 = (f32[192,128]{1,0:T(8,128)S(1)}, bf16[192,128]{1,0:T(8,128)(2,1)S(1)}, bf16[192,128]{1,0:T(8,128)(2,1)S(1)}, bf16[192,128]{1,0:T(8,128)(2,1)S(1...) custom-call(bf16[192,128]{1,0:T(8,128)(2,1)S(1)} %bitcast.31, ...), custom_call_target="tpu_custom_call" | custom-call | bytes 2412032 | tf_op jit(solution)/shard_map/pallas_call | solution.py:67
  12.9 1.4 %collective-permute-start.4 = (bf16[192,128]{1,0:T(8,128)(2,1)S(1)}, bf16[192,128]{1,0:T(8,128)(2,1)S(1)}, u32[]{:S(2)}, u32[]{:S(2)}) collective-permute-start(bf16[192,128]{1,0:T(8,128)(2,1)S(1)} %get-tuple-element.96), channel_id=1, source_target_pairs={{0,2},{1,3},{2,0},{3,1},{4,6},{5,7},{6,4},{7,5},{8,10},{9,11},{10,... | collective-permute-start | bytes 147464 | tf_op jit(solution)/shard_map/ppermute | solution.py:522
  15.1 1.9 %collective-permute-done.4.refs_2_ = bf16[192,128]{1,0:T(8,128)(2,1)S(1)} collective-permute-done((bf16[192,128]{1,0:T(8,128)(2,1)S(1)}, bf16[192,128]{1,0:T(8,128)(2,1)S(1)}, u32[]{:S(2)}, u32[]{:S(2)}) %collective-permute-start.4) | collective-permute-done | bytes 49184 | tf_op jit(solution)/shard_map/ppermute | solution.py:522
  17.0 1.1 collective-permute-done.5.refs_3_
  18.8 16.8 %all_to_all.10 = bf16[8,40,400]{2,1,0:T(8,128)(2,1)S(1)} all-to-all(bf16[8,40,400]{2,1,0:T(8,128)(2,1)S(1)} %bitcast.34), channel_id=1, replica_groups=mesh['expert'=8,'tensor'=4] {'expert'}, dimensions={0} | all-to-all | bytes 512000 | tf_op jit(solution)/shard_map/all_to_all | solution.py:534
  35.6 1.1 collective-permute-start.7
  37.9 5.0 %collective-permute-done.9.refs_4_ = bf16[960,128]{1,0:T(8,128)(2,1)S(1)} collective-permute-done((bf16[960,128]{1,0:T(8,128)(2,1)S(1)}, bf16[960,128]{1,0:T(8,128)(2,1)S(1)}, u32[]{:S(2)}, u32[]{:S(2)}) %collective-permute-start.9) | collective-permute-done | bytes 245792 | tf_op jit(solution)/shard_map/ppermute | solution.py:522
  42.9 2.8 %collective-permute-done.8.refs_1_.refs_5_ = bf16[960,128]{1,0:T(8,128)(2,1)S(1)} collective-permute-done((bf16[960,128]{1,0:T(8,128)(2,1)S(1)}, bf16[960,128]{1,0:T(8,128)(2,1)S(1)}, u32[]{:S(2)}, u32[]{:S(2)}) %collective-permute-start.8) | collective-permute-done | bytes 245792 | tf_op jit(solution)/shard_map/ppermute | solution.py:538
  45.7 1.6 %collective-permute-done.10.refs_3_ = bf16[320,400]{1,0:T(8,128)(2,1)S(1)} collective-permute-done((bf16[320,400]{1,0:T(8,128)(2,1)S(1)}, bf16[320,400]{1,0:T(8,128)(2,1)S(1)}, u32[]{:S(2)}, u32[]{:S(2)}) %collective-permute-start.10) | collective-permute-done | bytes 256032 | tf_op jit(solution)/shard_map/ppermute | solution.py:522
  47.3 3.0 %shard_map.208 = (bf16[320,384]{1,0:T(8,128)(2,1)S(1)}, bf16[320,384]{1,0:T(8,128)(2,1)S(1)}, bf16[640,384]{1,0:T(8,128)(2,1)S(1)}, bf16[320,768]{1,0:T(8,128)(2...) custom-call(bf16[320,400]{1,0:T(8,128)(2,1)S(1)} %bitcast.25, ...), custom_call_target="tpu_custom_call" | custom-call | bytes 6332416 | tf_op jit(solution)/shard_map/pallas_call | solution.py:67
  50.9 1.2 collective-permute-start.18
  52.1 1.5 %collective-permute-start.16 = (bf16[960,128]{1,0:T(8,128)(2,1)S(1)}, bf16[960,128]{1,0:T(8,128)(2,1)S(1)}, u32[]{:S(2)}, u32[]{:S(2)}) collective-permute-start(bf16[960,128]{1,0:T(8,128)(2,1)S(1)} %collective-permute-done.8.refs_1_.refs_5_), channel_id=1, source_target_pairs={{0,8},{4,12},{8,16},{12,20},{16,24},{20,28},{24,0},{28,4},{1,9},{5... | collective-permute-start | bytes 737288 | tf_op jit(solution)/shard_map/ppermute | solution.py:538
  53.6 1.0 collective-permute-start.15
  54.7 3.2 %shard_map.210 = (f32[1,768,768]{2,1,0:T(8,128)}, f32[1,768,768]{2,1,0:T(8,128)}) custom-call(bf16[320,768]{1,0:T(8,128)(2,1)S(1)} %get-tuple-element.113.refs_0_, bf16[320,768]{1,0:T(8,128)(2,1)S(1)} %get-tuple-element.114.refs_1_, bf16[320,768]{1,0:T(8,128)(2,1)S(1)} %get-tuple-element.115.refs_2_, bf16[320,768]{1,0:T(8,128)(2,1)S(1)} %get-tuple-element.116.refs_3_), custom_call_target="tpu_custom_call" | custom-call | bytes 6684672 | tf_op jit(solution)/shard_map/pallas_call | solution.py:67
  57.9 6.1 %collective-permute-done.17.refs_3_.refs_7_ = bf16[960,128]{1,0:T(8,128)(2,1)S(1)} collective-permute-done((bf16[960,128]{1,0:T(8,128)(2,1)S(1)}, bf16[960,128]{1,0:T(8,128)(2,1)S(1)}, u32[]{:S(2)}, u32[]{:S(2)}) %collective-permute-start.17) | collective-permute-done | bytes 245792 | tf_op jit(solution)/shard_map/ppermute | solution.py:538
  64.9 3.8 %collective-permute-done.13.refs_2_.refs_6_ = bf16[400,128]{1,0:T(8,128)(2,1)S(1)} collective-permute-done((bf16[400,128]{1,0:T(8,128)(2,1)S(1)}, bf16[400,128]{1,0:T(8,128)(2,1)S(1)}, u32[]{:S(2)}, u32[]{:S(2)}) %collective-permute-start.13) | collective-permute-done | bytes 102432 | tf_op jit(solution)/shard_map/ppermute | solution.py:522
  68.7 10.5 %all_to_all.11 = bf16[8,40,384]{2,1,0:T(8,128)(2,1)S(1)} all-to-all(bf16[8,40,384]{2,1,0:T(8,128)(2,1)S(1)} %bitcast.26), channel_id=1, replica_groups=mesh['expert'=8,'tensor'=4] {'expert'}, dimensions={0} | all-to-all | bytes 491520 | tf_op jit(solution)/shard_map/all_to_all | solution.py:534
  79.3 1.0 shard_map.212
  80.3 1.0 collective-permute-start.25
  81.3 1.1 collective-permute-start.26
  82.4 0.9 collective-permute-start.20
  83.3 1.0 collective-permute-start.19
  84.2 1.7 %collective-permute-done.21.refs_3_ = bf16[208,128]{1,0:T(8,128)(2,1)S(1)} collective-permute-done((bf16[208,128]{1,0:T(8,128)(2,1)S(1)}, bf16[208,128]{1,0:T(8,128)(2,1)S(1)}, u32[]{:S(2)}, u32[]{:S(2)}) %collective-permute-start.21) | collective-permute-done | bytes 53280 | tf_op jit(solution)/shard_map/ppermute | solution.py:522
  85.9 1.2 collective-permute-done.20.refs_2_
  87.1 2.6 %shard_map.213 = (bf16[208,128]{1,0:T(8,128)(2,1)S(1)}, bf16[208,128]{1,0:T(8,128)(2,1)S(1)}, bf16[208,128]{1,0:T(8,128)(2,1)S(1)}, bf16[208,128]{1,0:T(8,128)(2...) custom-call(bf16[208,128]{1,0:T(8,128)(2,1)S(1)} %get-tuple-element., ...), custom_call_target="tpu_custom_call" | custom-call | bytes 3313664 | tf_op jit(solution)/shard_map/pallas_call | solution.py:67
  89.8 1.2 collective-permute-start.23
  91.6 2.0 %shard_map.215 = (f32[16,768]{1,0:T(8,128)}, bf16[864,128]{1,0:T(8,128)(2,1)S(1)}) custom-call(bf16[400,128]{1,0:T(8,128)(2,1)S(1)} %get-tuple-element.118.refs_0_.refs_4_, bf16[400,128]{1,0:T(8,128)(2,1)S(1)} %collective-permute-done.12.refs_1_.refs_5_, bf16[400,128]{1,0:T(8,128)(2,1)S(1)} %collective-permute-done.13.refs_2_.refs_6_, ...), custom_call_target="tpu_custom_call" | custom-call | bytes 2656704 | tf_op jit(solution)/shard_map/pallas_call | solution.py:67
  94.1 1.0 collective-permute-done.24.refs_3_
  95.5 1.7 %collective-permute-start.28 = (bf16[864,128]{1,0:T(8,128)(2,1)S(1)}, bf16[864,128]{1,0:T(8,128)(2,1)S(1)}, u32[]{:S(2)}, u32[]{:S(2)}) collective-permute-start(bf16[864,128]{1,0:T(8,128)(2,1)S(1)} %get-tuple-element.144.refs_0_.refs_4_), channel_id=1, source_target_pairs={{0,24},{4,28},{8,0},{12,4},{16,8},{20,12},{24,16},{28,20},{1,25},{... | collective-permute-start | bytes 663560 | tf_op jit(solution)/shard_map/ppermute | solution.py:538
  97.6 4.9 %collective-permute-done.29.refs_8_.refs_0_ = bf16[864,128]{1,0:T(8,128)(2,1)S(1)} collective-permute-done((bf16[864,128]{1,0:T(8,128)(2,1)S(1)}, bf16[864,128]{1,0:T(8,128)(2,1)S(1)}, u32[]{:S(2)}, u32[]{:S(2)}) %collective-permute-start.29) | collective-permute-done | bytes 221216 | tf_op jit(solution)/shard_map/ppermute | solution.py:522
  102.5 5.2 %collective-permute-done.28.refs_3_.refs_7_ = bf16[864,128]{1,0:T(8,128)(2,1)S(1)} collective-permute-done((bf16[864,128]{1,0:T(8,128)(2,1)S(1)}, bf16[864,128]{1,0:T(8,128)(2,1)S(1)}, u32[]{:S(2)}, u32[]{:S(2)}) %collective-permute-start.28) | collective-permute-done | bytes 221216 | tf_op jit(solution)/shard_map/ppermute | solution.py:538
  107.7 1.0 collective-permute-start.31
  108.7 1.3 collective-permute-start.32
  110.7 4.1 %collective-permute-done.32.refs_11_.refs_3_ = bf16[864,128]{1,0:T(8,128)(2,1)S(1)} collective-permute-done((bf16[864,128]{1,0:T(8,128)(2,1)S(1)}, bf16[864,128]{1,0:T(8,128)(2,1)S(1)}, u32[]{:S(2)}, u32[]{:S(2)}) %collective-permute-start.32) | collective-permute-done | bytes 221216 | tf_op jit(solution)/shard_map/ppermute | solution.py:522
  114.8 3.0 %collective-permute-done.31.refs_2_ = bf16[1536,128]{1,0:T(8,128)(2,1)S(1)} collective-permute-done((bf16[1536,128]{1,0:T(8,128)(2,1)S(1)}, bf16[1536,128]{1,0:T(8,128)(2,1)S(1)}, u32[]{:S(2)}, u32[]{:S(2)}) %collective-permute-start.31) | collective-permute-done | bytes 393248 | tf_op jit(solution)/shard_map/ppermute | solution.py:522
  117.8 1.2 collective-permute-start.35
  119.9 1.1 shard_map.217.refs_8_
  121.0 5.1 %collective-permute-done.35.refs_9_.refs_1_ = bf16[864,128]{1,0:T(8,128)(2,1)S(1)} collective-permute-done((bf16[864,128]{1,0:T(8,128)(2,1)S(1)}, bf16[864,128]{1,0:T(8,128)(2,1)S(1)}, u32[]{:S(2)}, u32[]{:S(2)}) %collective-permute-start.35) | collective-permute-done | bytes 221216 | tf_op jit(solution)/shard_map/ppermute | solution.py:522
  126.1 4.4 %collective-permute-done.36.refs_10_.refs_2_ = bf16[864,128]{1,0:T(8,128)(2,1)S(1)} collective-permute-done((bf16[864,128]{1,0:T(8,128)(2,1)S(1)}, bf16[864,128]{1,0:T(8,128)(2,1)S(1)}, u32[]{:S(2)}, u32[]{:S(2)}) %collective-permute-start.36) | collective-permute-done | bytes 221216 | tf_op jit(solution)/shard_map/ppermute | solution.py:522
  130.4 1.0 shard_map.218
  131.5 1.0 collective-permute-start.38
  134.2 2.3 %shard_map.220 = f32[576,768]{1,0:T(8,128)} custom-call(bf16[864,128]{1,0:T(8,128)(2,1)S(1)} %collective-permute-done.29.refs_8_.refs_0_, bf16[864,128]{1,0:T(8,128)(2,1)S(1)} %collective-permute-done.35.refs_9_.refs_1_, bf16[864,128]{1,0:T(8,128)(2,1)S(1)} %collective-permute-done.36.refs_10_.refs_2_, ...), custom_call_target="tpu_custom_call" | custom-call | bytes 5406720 | tf_op jit(solution)/shard_map/pallas_call | solution.py:67
  137.3 1.4 collective-permute-done.39.refs_3_
  138.7 1.1 shard_map.219
  (85 shorter events, 15.2 us)
Async XLA Ops:
  0.6 13.7 %copy-start.9 = (bf16[768,8]{0,1:T(8,128)(2,1)S(1)}, bf16[768,8]{0,1:T(8,128)(2,1)}, u32[]{:S(2)}) copy-start(bf16[768,8]{0,1:T(8,128)(2,1)} %param.19) | copy-start | bytes 36868
  0.7 7.7 %collective-permute-start.2 = (bf16[192,128]{1,0:T(8,128)(2,1)}, bf16[192,128]{1,0:T(8,128)(2,1)S(1)}, u32[]{:S(2)}, u32[]{:S(2)}) collective-permute-start(bf16[192,128]{1,0:T(8,128)(2,1)} %bitcast.28), channel_id=1, source_target_pairs={{0,3},{1,2},{2,1},{3,0},{4,7},{5,6},{6,5},{7,4},{8,11},{9,10},{10,... | collective-permute-start | bytes 147464 | tf_op jit(solution)/shard_map/ppermute | solution.py:522
  3.1 5.3 %collective-permute-start.1 = (bf16[192,128]{1,0:T(8,128)(2,1)}, bf16[192,128]{1,0:T(8,128)(2,1)S(1)}, u32[]{:S(2)}, u32[]{:S(2)}) collective-permute-start(bf16[192,128]{1,0:T(8,128)(2,1)} %bitcast.29), channel_id=1, source_target_pairs={{0,2},{1,3},{2,0},{3,1},{4,6},{5,7},{6,4},{7,5},{8,10},{9,11},{10,... | collective-permute-start | bytes 147464 | tf_op jit(solution)/shard_map/ppermute | solution.py:522
  3.8 4.6 %collective-permute-start = (bf16[192,128]{1,0:T(8,128)(2,1)}, bf16[192,128]{1,0:T(8,128)(2,1)S(1)}, u32[]{:S(2)}, u32[]{:S(2)}) collective-permute-start(bf16[192,128]{1,0:T(8,128)(2,1)} %bitcast.30), channel_id=1, source_target_pairs={{0,1},{1,0},{2,3},{3,2},{4,5},{5,4},{6,7},{7,6},{8,9},{9,8},{10,11... | collective-permute-start | bytes 147464 | tf_op jit(solution)/shard_map/ppermute | solution.py:522
  7.5 6.9 %copy-start.10 = (s32[128,2]{0,1:T(2,128)S(1)}, s32[128,2]{0,1:T(2,128)}, u32[]{:S(2)}) copy-start(s32[128,2]{0,1:T(2,128)} %param.22) | copy-start | bytes 3076
  7.5 10.6 %copy-start.7 = (bf16[128,192]{0,1:T(8,128)(2,1)S(1)}, bf16[128,192]{0,1:T(8,128)(2,1)}, u32[]{:S(2)}) copy-start(bf16[128,192]{0,1:T(8,128)(2,1)} %param.13) | copy-start | bytes 147460
  7.5 10.6 %copy-start.8 = (bf16[128,192]{0,1:T(8,128)(2,1)S(1)}, bf16[128,192]{0,1:T(8,128)(2,1)}, u32[]{:S(2)}) copy-start(bf16[128,192]{0,1:T(8,128)(2,1)} %param.25) | copy-start | bytes 147460
  10.4 36.9 %copy-start.4 = (bf16[1,768,768]{2,1,0:T(8,128)(2,1)S(1)}, bf16[1,768,768]{2,1,0:T(8,128)(2,1)}, u32[]{:S(2)}) copy-start(bf16[1,768,768]{2,1,0:T(8,128)(2,1)} %refs_4_.1) | copy-start | bytes 3538948
  10.4 36.9 %copy-start.5 = (bf16[1,768,768]{2,1,0:T(8,128)(2,1)S(1)}, bf16[1,768,768]{2,1,0:T(8,128)(2,1)}, u32[]{:S(2)}) copy-start(bf16[1,768,768]{2,1,0:T(8,128)(2,1)} %refs_5_.1) | copy-start | bytes 3538948
  12.3 2.7 %collective-permute-start.3 = (bf16[192,128]{1,0:T(8,128)(2,1)S(1)}, bf16[192,128]{1,0:T(8,128)(2,1)S(1)}, u32[]{:S(2)}, u32[]{:S(2)}) collective-permute-start(bf16[192,128]{1,0:T(8,128)(2,1)S(1)} %get-tuple-element.95), channel_id=1, source_target_pairs={{0,1},{1,0},{2,3},{3,2},{4,5},{5,4},{6,7},{7,6},{8,9},{9,8},{10,11... | collective-permute-start | bytes 147464 | tf_op jit(solution)/shard_map/ppermute | solution.py:522
  12.9 4.1 %collective-permute-start.4 = (bf16[192,128]{1,0:T(8,128)(2,1)S(1)}, bf16[192,128]{1,0:T(8,128)(2,1)S(1)}, u32[]{:S(2)}, u32[]{:S(2)}) collective-permute-start(bf16[192,128]{1,0:T(8,128)(2,1)S(1)} %get-tuple-element.96), channel_id=1, source_target_pairs={{0,2},{1,3},{2,0},{3,1},{4,6},{5,7},{6,4},{7,5},{8,10},{9,11},{10,... | collective-permute-start | bytes 147464 | tf_op jit(solution)/shard_map/ppermute | solution.py:522
  14.3 3.8 %collective-permute-start.5 = (bf16[192,128]{1,0:T(8,128)(2,1)S(1)}, bf16[192,128]{1,0:T(8,128)(2,1)S(1)}, u32[]{:S(2)}, u32[]{:S(2)}) collective-permute-start(bf16[192,128]{1,0:T(8,128)(2,1)S(1)} %get-tuple-element.97), channel_id=1, source_target_pairs={{0,3},{1,2},{2,1},{3,0},{4,7},{5,6},{6,5},{7,4},{8,11},{9,10},{10,... | collective-permute-start | bytes 147464 | tf_op jit(solution)/shard_map/ppermute | solution.py:522
  35.6 10.0 %collective-permute-start.7 = (bf16[320,400]{1,0:T(8,128)(2,1)S(1)}, bf16[320,400]{1,0:T(8,128)(2,1)S(1)}, u32[]{:S(2)}, u32[]{:S(2)}) collective-permute-start(bf16[320,400]{1,0:T(8,128)(2,1)S(1)} %bitcast.23), channel_id=1, source_target_pairs={{0,2},{1,3},{2,0},{3,1},{4,6},{5,7},{6,4},{7,5},{8,10},{9,11},{10,... | collective-permute-start | bytes 768008 | tf_op jit(solution)/shard_map/ppermute | solution.py:522
  36.7 6.2 %collective-permute-start.9 = (bf16[960,128]{1,0:T(8,128)(2,1)S(1)}, bf16[960,128]{1,0:T(8,128)(2,1)S(1)}, u32[]{:S(2)}, u32[]{:S(2)}) collective-permute-start(bf16[960,128]{1,0:T(8,128)(2,1)S(1)} %get-tuple-element.146.refs_8_.refs_0_.refs_4_), channel_id=1, source_target_pairs={{0,4},{4,0},{8,12},{12,8},{16,20},{20,16},{24,28},{28,24},{1,5},{5... | collective-permute-start | bytes 737288 | tf_op jit(solution)/shard_map/ppermute | solution.py:522
  37.5 8.1 %collective-permute-start.8 = (bf16[960,128]{1,0:T(8,128)(2,1)S(1)}, bf16[960,128]{1,0:T(8,128)(2,1)S(1)}, u32[]{:S(2)}, u32[]{:S(2)}) collective-permute-start(bf16[960,128]{1,0:T(8,128)(2,1)S(1)} %get-tuple-element.146.refs_8_.refs_0_.refs_4_), channel_id=1, source_target_pairs={{0,8},{4,12},{8,16},{12,20},{16,24},{20,28},{24,0},{28,4},{1,9},{5... | collective-permute-start | bytes 737288 | tf_op jit(solution)/shard_map/ppermute | solution.py:538
  37.9 7.8 %collective-permute-start.6 = (bf16[320,400]{1,0:T(8,128)(2,1)S(1)}, bf16[320,400]{1,0:T(8,128)(2,1)S(1)}, u32[]{:S(2)}, u32[]{:S(2)}) collective-permute-start(bf16[320,400]{1,0:T(8,128)(2,1)S(1)} %bitcast.24), channel_id=1, source_target_pairs={{0,1},{1,0},{2,3},{3,2},{4,5},{5,4},{6,7},{7,6},{8,9},{9,8},{10,11... | collective-permute-start | bytes 768008 | tf_op jit(solution)/shard_map/ppermute | solution.py:522
  45.7 1.6 %collective-permute-start.10 = (bf16[320,400]{1,0:T(8,128)(2,1)S(1)}, bf16[320,400]{1,0:T(8,128)(2,1)S(1)}, u32[]{:S(2)}, u32[]{:S(2)}) collective-permute-start(bf16[320,400]{1,0:T(8,128)(2,1)S(1)} %collective-permute-done.7.refs_2_), channel_id=1, source_target_pairs={{0,1},{1,0},{2,3},{3,2},{4,5},{5,4},{6,7},{7,6},{8,9},{9,8},{10,11... | collective-permute-start | bytes 768008 | tf_op jit(solution)/shard_map/ppermute | solution.py:522
  50.3 3.3 %collective-permute-start.11 = (bf16[640,384]{1,0:T(8,128)(2,1)S(1)}, bf16[640,384]{1,0:T(8,128)(2,1)S(1)}, u32[]{:S(2)}, u32[]{:S(2)}) collective-permute-start(bf16[640,384]{1,0:T(8,128)(2,1)S(1)} %get-tuple-element.112), channel_id=1, source_target_pairs={{0,1},{1,0},{2,3},{3,2},{4,5},{5,4},{6,7},{7,6},{8,9},{9,8},{10,11... | collective-permute-start | bytes 1474568 | tf_op jit(solution)/shard_map/ppermute | solution.py:522
  50.5 13.5 %collective-permute-start.17 = (bf16[960,128]{1,0:T(8,128)(2,1)S(1)}, bf16[960,128]{1,0:T(8,128)(2,1)S(1)}, u32[]{:S(2)}, u32[]{:S(2)}) collective-permute-start(bf16[960,128]{1,0:T(8,128)(2,1)S(1)} %get-tuple-element.146.refs_8_.refs_0_.refs_4_), channel_id=1, source_target_pairs={{0,24},{4,28},{8,0},{12,4},{16,8},{20,12},{24,16},{28,20},{1,25},{... | collective-permute-start | bytes 737288 | tf_op jit(solution)/shard_map/ppermute | solution.py:538
  50.9 14.0 %collective-permute-start.18 = (bf16[960,128]{1,0:T(8,128)(2,1)S(1)}, bf16[960,128]{1,0:T(8,128)(2,1)S(1)}, u32[]{:S(2)}, u32[]{:S(2)}) collective-permute-start(bf16[960,128]{1,0:T(8,128)(2,1)S(1)} %collective-permute-done.8.refs_1_.refs_5_), channel_id=1, source_target_pairs={{0,4},{4,0},{8,12},{12,8},{16,20},{20,16},{24,28},{28,24},{1,5},{5... | collective-permute-start | bytes 737288 | tf_op jit(solution)/shard_map/ppermute | solution.py:522
  52.1 12.8 %collective-permute-start.16 = (bf16[960,128]{1,0:T(8,128)(2,1)S(1)}, bf16[960,128]{1,0:T(8,128)(2,1)S(1)}, u32[]{:S(2)}, u32[]{:S(2)}) collective-permute-start(bf16[960,128]{1,0:T(8,128)(2,1)S(1)} %collective-permute-done.8.refs_1_.refs_5_), channel_id=1, source_target_pairs={{0,8},{4,12},{8,16},{12,20},{16,24},{20,28},{24,0},{28,4},{1,9},{5... | collective-permute-start | bytes 737288 | tf_op jit(solution)/shard_map/ppermute | solution.py:538
  53.6 11.2 %collective-permute-start.15 = (bf16[320,384]{1,0:T(8,128)(2,1)S(1)}, bf16[320,384]{1,0:T(8,128)(2,1)S(1)}, u32[]{:S(2)}, u32[]{:S(2)}) collective-permute-start(bf16[320,384]{1,0:T(8,128)(2,1)S(1)} %shard_map.209), channel_id=1, source_target_pairs={{0,2},{1,3},{2,0},{3,1},{4,6},{5,7},{6,4},{7,5},{8,10},{9,11},{10,... | collective-permute-start | bytes 737288 | tf_op jit(solution)/shard_map/ppermute | solution.py:522
  54.7 32.4 %copy-start.3 = (bf16[192,768]{1,0:T(8,128)(2,1)S(1)}, bf16[192,768]{1,0:T(8,128)(2,1)}, u32[]{:S(2)}) copy-start(bf16[192,768]{1,0:T(8,128)(2,1)} %refs_11_.1) | copy-start | bytes 884740
  57.8 7.0 %collective-permute-start.14 = (bf16[400,128]{1,0:T(8,128)(2,1)S(1)}, bf16[400,128]{1,0:T(8,128)(2,1)S(1)}, u32[]{:S(2)}, u32[]{:S(2)}) collective-permute-start(bf16[400,128]{1,0:T(8,128)(2,1)S(1)} %get-tuple-element.118.refs_0_.refs_4_), channel_id=1, source_target_pairs={{0,3},{1,2},{2,1},{3,0},{4,7},{5,6},{6,5},{7,4},{8,11},{9,10},{10,... | collective-permute-start | bytes 307208 | tf_op jit(solution)/shard_map/ppermute | solution.py:522
  64.0 4.7 %collective-permute-start.13 = (bf16[400,128]{1,0:T(8,128)(2,1)S(1)}, bf16[400,128]{1,0:T(8,128)(2,1)S(1)}, u32[]{:S(2)}, u32[]{:S(2)}) collective-permute-start(bf16[400,128]{1,0:T(8,128)(2,1)S(1)} %get-tuple-element.118.refs_0_.refs_4_), channel_id=1, source_target_pairs={{0,2},{1,3},{2,0},{3,1},{4,6},{5,7},{6,4},{7,5},{8,10},{9,11},{10,... | collective-permute-start | bytes 307208 | tf_op jit(solution)/shard_map/ppermute | solution.py:522
  64.9 3.8 %collective-permute-start.12 = (bf16[400,128]{1,0:T(8,128)(2,1)S(1)}, bf16[400,128]{1,0:T(8,128)(2,1)S(1)}, u32[]{:S(2)}, u32[]{:S(2)}) collective-permute-start(bf16[400,128]{1,0:T(8,128)(2,1)S(1)} %get-tuple-element.118.refs_0_.refs_4_), channel_id=1, source_target_pairs={{0,1},{1,0},{2,3},{3,2},{4,5},{5,4},{6,7},{7,6},{8,9},{9,8},{10,11... | collective-permute-start | bytes 307208 | tf_op jit(solution)/shard_map/ppermute | solution.py:522
  79.3 12.4 %copy-start.13 = (s32[112]{0:T(128)S(1)}, s32[112]{0:T(128)}, u32[]{:S(2)}) copy-start(s32[112]{0:T(128)} %param.24) | copy-start | bytes 1348
  80.3 11.3 %collective-permute-start.25 = (bf16[960,128]{1,0:T(8,128)(2,1)S(1)}, bf16[960,128]{1,0:T(8,128)(2,1)S(1)}, u32[]{:S(2)}, u32[]{:S(2)}) collective-permute-start(bf16[960,128]{1,0:T(8,128)(2,1)S(1)} %collective-permute-done.16.refs_2_.refs_6_), channel_id=1, source_target_pairs={{0,4},{4,0},{8,12},{12,8},{16,20},{20,16},{24,28},{28,24},{1,5},{5... | collective-permute-start | bytes 737288 | tf_op jit(solution)/shard_map/ppermute | solution.py:522
  81.3 10.3 %collective-permute-start.26 = (bf16[960,128]{1,0:T(8,128)(2,1)S(1)}, bf16[960,128]{1,0:T(8,128)(2,1)S(1)}, u32[]{:S(2)}, u32[]{:S(2)}) collective-permute-start(bf16[960,128]{1,0:T(8,128)(2,1)S(1)} %collective-permute-done.17.refs_3_.refs_7_), channel_id=1, source_target_pairs={{0,4},{4,0},{8,12},{12,8},{16,20},{20,16},{24,28},{28,24},{1,5},{5... | collective-permute-start | bytes 737288 | tf_op jit(solution)/shard_map/ppermute | solution.py:522
  82.4 3.6 %collective-permute-start.21 = (bf16[208,128]{1,0:T(8,128)(2,1)S(1)}, bf16[208,128]{1,0:T(8,128)(2,1)S(1)}, u32[]{:S(2)}, u32[]{:S(2)}) collective-permute-start(bf16[208,128]{1,0:T(8,128)(2,1)S(1)} %get-tuple-element.126.refs_0_), channel_id=1, source_target_pairs={{0,3},{1,2},{2,1},{3,0},{4,7},{5,6},{6,5},{7,4},{8,11},{9,10},{10,... | collective-permute-start | bytes 159752 | tf_op jit(solution)/shard_map/ppermute | solution.py:522
  82.4 4.7 %collective-permute-start.20 = (bf16[208,128]{1,0:T(8,128)(2,1)S(1)}, bf16[208,128]{1,0:T(8,128)(2,1)S(1)}, u32[]{:S(2)}, u32[]{:S(2)}) collective-permute-start(bf16[208,128]{1,0:T(8,128)(2,1)S(1)} %get-tuple-element.126.refs_0_), channel_id=1, source_target_pairs={{0,2},{1,3},{2,0},{3,1},{4,6},{5,7},{6,4},{7,5},{8,10},{9,11},{10,... | collective-permute-start | bytes 159752 | tf_op jit(solution)/shard_map/ppermute | solution.py:522
  83.3 3.8 %collective-permute-start.19 = (bf16[208,128]{1,0:T(8,128)(2,1)S(1)}, bf16[208,128]{1,0:T(8,128)(2,1)S(1)}, u32[]{:S(2)}, u32[]{:S(2)}) collective-permute-start(bf16[208,128]{1,0:T(8,128)(2,1)S(1)} %get-tuple-element.126.refs_0_), channel_id=1, source_target_pairs={{0,1},{1,0},{2,3},{3,2},{4,5},{5,4},{6,7},{7,6},{8,9},{9,8},{10,11... | collective-permute-start | bytes 159752 | tf_op jit(solution)/shard_map/ppermute | solution.py:522
  89.7 4.0 %collective-permute-start.22 = (bf16[208,128]{1,0:T(8,128)(2,1)S(1)}, bf16[208,128]{1,0:T(8,128)(2,1)S(1)}, u32[]{:S(2)}, u32[]{:S(2)}) collective-permute-start(bf16[208,128]{1,0:T(8,128)(2,1)S(1)} %get-tuple-element.131), channel_id=1, source_target_pairs={{0,1},{1,0},{2,3},{3,2},{4,5},{5,4},{6,7},{7,6},{8,9},{9,8},{10,11... | collective-permute-start | bytes 159752 | tf_op jit(solution)/shard_map/ppermute | solution.py:522
  89.8 4.2 %collective-permute-start.23 = (bf16[208,128]{1,0:T(8,128)(2,1)S(1)}, bf16[208,128]{1,0:T(8,128)(2,1)S(1)}, u32[]{:S(2)}, u32[]{:S(2)}) collective-permute-start(bf16[208,128]{1,0:T(8,128)(2,1)S(1)} %get-tuple-element.132), channel_id=1, source_target_pairs={{0,2},{1,3},{2,0},{3,1},{4,6},{5,7},{6,4},{7,5},{8,10},{9,11},{10,... | collective-permute-start | bytes 159752 | tf_op jit(solution)/shard_map/ppermute | solution.py:522
  91.0 4.1 %collective-permute-start.24 = (bf16[208,128]{1,0:T(8,128)(2,1)S(1)}, bf16[208,128]{1,0:T(8,128)(2,1)S(1)}, u32[]{:S(2)}, u32[]{:S(2)}) collective-permute-start(bf16[208,128]{1,0:T(8,128)(2,1)S(1)} %get-tuple-element.133), channel_id=1, source_target_pairs={{0,3},{1,2},{2,1},{3,0},{4,7},{5,6},{6,5},{7,4},{8,11},{9,10},{10,... | collective-permute-start | bytes 159752 | tf_op jit(solution)/shard_map/ppermute | solution.py:522
  95.0 7.4 %collective-permute-start.29 = (bf16[864,128]{1,0:T(8,128)(2,1)S(1)}, bf16[864,128]{1,0:T(8,128)(2,1)S(1)}, u32[]{:S(2)}, u32[]{:S(2)}) collective-permute-start(bf16[864,128]{1,0:T(8,128)(2,1)S(1)} %get-tuple-element.144.refs_0_.refs_4_), channel_id=1, source_target_pairs={{0,4},{4,0},{8,12},{12,8},{16,20},{20,16},{24,28},{28,24},{1,5},{5... | collective-permute-start | bytes 663560 | tf_op jit(solution)/shard_map/ppermute | solution.py:522
  95.5 12.1 %collective-permute-start.28 = (bf16[864,128]{1,0:T(8,128)(2,1)S(1)}, bf16[864,128]{1,0:T(8,128)(2,1)S(1)}, u32[]{:S(2)}, u32[]{:S(2)}) collective-permute-start(bf16[864,128]{1,0:T(8,128)(2,1)S(1)} %get-tuple-element.144.refs_0_.refs_4_), channel_id=1, source_target_pairs={{0,24},{4,28},{8,0},{12,4},{16,8},{20,12},{24,16},{28,20},{1,25},{... | collective-permute-start | bytes 663560 | tf_op jit(solution)/shard_map/ppermute | solution.py:538
  97.2 10.5 %collective-permute-start.27 = (bf16[864,128]{1,0:T(8,128)(2,1)S(1)}, bf16[864,128]{1,0:T(8,128)(2,1)S(1)}, u32[]{:S(2)}, u32[]{:S(2)}) collective-permute-start(bf16[864,128]{1,0:T(8,128)(2,1)S(1)} %get-tuple-element.144.refs_0_.refs_4_), channel_id=1, source_target_pairs={{0,8},{4,12},{8,16},{12,20},{16,24},{20,28},{24,0},{28,4},{1,9},{5... | collective-permute-start | bytes 663560 | tf_op jit(solution)/shard_map/ppermute | solution.py:538
  107.7 10.1 %collective-permute-start.31 = (bf16[1536,128]{1,0:T(8,128)(2,1)S(1)}, bf16[1536,128]{1,0:T(8,128)(2,1)S(1)}, u32[]{:S(2)}, u32[]{:S(2)}) collective-permute-start(bf16[1536,128]{1,0:T(8,128)(2,1)S(1)} %shard_map.216.refs_0_), channel_id=1, source_target_pairs={{0,2},{1,3},{2,0},{3,1},{4,6},{5,7},{6,4},{7,5},{8,10},{9,11},{10,... | collective-permute-start | bytes 1179656 | tf_op jit(solution)/shard_map/ppermute | solution.py:522
  108.7 6.1 %collective-permute-start.32 = (bf16[864,128]{1,0:T(8,128)(2,1)S(1)}, bf16[864,128]{1,0:T(8,128)(2,1)S(1)}, u32[]{:S(2)}, u32[]{:S(2)}) collective-permute-start(bf16[864,128]{1,0:T(8,128)(2,1)S(1)} %collective-permute-done.28.refs_3_.refs_7_), channel_id=1, source_target_pairs={{0,4},{4,0},{8,12},{12,8},{16,20},{20,16},{24,28},{28,24},{1,5},{5... | collective-permute-start | bytes 663560 | tf_op jit(solution)/shard_map/ppermute | solution.py:522
  110.0 9.1 %collective-permute-start.34 = (bf16[864,128]{1,0:T(8,128)(2,1)S(1)}, bf16[864,128]{1,0:T(8,128)(2,1)S(1)}, u32[]{:S(2)}, u32[]{:S(2)}) collective-permute-start(bf16[864,128]{1,0:T(8,128)(2,1)S(1)} %collective-permute-done.27.refs_1_.refs_5_), channel_id=1, source_target_pairs={{0,8},{4,12},{8,16},{12,20},{16,24},{20,28},{24,0},{28,4},{1,9},{5... | collective-permute-start | bytes 663560 | tf_op jit(solution)/shard_map/ppermute | solution.py:538
  110.7 19.7 %collective-permute-start.30 = (bf16[1536,128]{1,0:T(8,128)(2,1)S(1)}, bf16[1536,128]{1,0:T(8,128)(2,1)S(1)}, u32[]{:S(2)}, u32[]{:S(2)}) collective-permute-start(bf16[1536,128]{1,0:T(8,128)(2,1)S(1)} %shard_map.216.refs_0_), channel_id=1, source_target_pairs={{0,1},{1,0},{2,3},{3,2},{4,5},{5,4},{6,7},{7,6},{8,9},{9,8},{10,11... | collective-permute-start | bytes 1179656 | tf_op jit(solution)/shard_map/ppermute | solution.py:522
  117.8 12.6 %collective-permute-start.33 = (bf16[1536,128]{1,0:T(8,128)(2,1)S(1)}, bf16[1536,128]{1,0:T(8,128)(2,1)S(1)}, u32[]{:S(2)}, u32[]{:S(2)}) collective-permute-start(bf16[1536,128]{1,0:T(8,128)(2,1)S(1)} %collective-permute-done.31.refs_2_), channel_id=1, source_target_pairs={{0,1},{1,0},{2,3},{3,2},{4,5},{5,4},{6,7},{7,6},{8,9},{9,8},{10,11... | collective-permute-start | bytes 1179656 | tf_op jit(solution)/shard_map/ppermute | solution.py:522
  117.8 8.2 %collective-permute-start.35 = (bf16[864,128]{1,0:T(8,128)(2,1)S(1)}, bf16[864,128]{1,0:T(8,128)(2,1)S(1)}, u32[]{:S(2)}, u32[]{:S(2)}) collective-permute-start(bf16[864,128]{1,0:T(8,128)(2,1)S(1)} %collective-permute-done.27.refs_1_.refs_5_), channel_id=1, source_target_pairs={{0,4},{4,0},{8,12},{12,8},{16,20},{20,16},{24,28},{28,24},{1,5},{5... | collective-permute-start | bytes 663560 | tf_op jit(solution)/shard_map/ppermute | solution.py:522
  119.1 11.3 %collective-permute-start.36 = (bf16[864,128]{1,0:T(8,128)(2,1)S(1)}, bf16[864,128]{1,0:T(8,128)(2,1)S(1)}, u32[]{:S(2)}, u32[]{:S(2)}) collective-permute-start(bf16[864,128]{1,0:T(8,128)(2,1)S(1)} %collective-permute-done.34.refs_2_.refs_6_), channel_id=1, source_target_pairs={{0,4},{4,0},{8,12},{12,8},{16,20},{20,16},{24,28},{28,24},{1,5},{5... | collective-permute-start | bytes 663560 | tf_op jit(solution)/shard_map/ppermute | solution.py:522
  131.4 5.1 %collective-permute-start.37 = (bf16[208,192]{1,0:T(8,128)(2,1)S(1)}, bf16[208,192]{1,0:T(8,128)(2,1)S(1)}, u32[]{:S(2)}, u32[]{:S(2)}) collective-permute-start(bf16[208,192]{1,0:T(8,128)(2,1)S(1)} %get-tuple-element.161), channel_id=1, source_target_pairs={{0,1},{1,0},{2,3},{3,2},{4,5},{5,4},{6,7},{7,6},{8,9},{9,8},{10,11... | collective-permute-start | bytes 239624 | tf_op jit(solution)/shard_map/ppermute | solution.py:522
  131.5 5.8 %collective-permute-start.38 = (bf16[208,192]{1,0:T(8,128)(2,1)S(1)}, bf16[208,192]{1,0:T(8,128)(2,1)S(1)}, u32[]{:S(2)}, u32[]{:S(2)}) collective-permute-start(bf16[208,192]{1,0:T(8,128)(2,1)S(1)} %get-tuple-element.162), channel_id=1, source_target_pairs={{0,2},{1,3},{2,0},{3,1},{4,6},{5,7},{6,4},{7,5},{8,10},{9,11},{10,... | collective-permute-start | bytes 239624 | tf_op jit(solution)/shard_map/ppermute | solution.py:522
  132.5 6.2 %collective-permute-start.39 = (bf16[208,192]{1,0:T(8,128)(2,1)S(1)}, bf16[208,192]{1,0:T(8,128)(2,1)S(1)}, u32[]{:S(2)}, u32[]{:S(2)}) collective-permute-start(bf16[208,192]{1,0:T(8,128)(2,1)S(1)} %get-tuple-element.163), channel_id=1, source_target_pairs={{0,3},{1,2},{2,1},{3,0},{4,7},{5,6},{6,5},{7,4},{8,11},{9,10},{10,... | collective-permute-start | bytes 239624 | tf_op jit(solution)/shard_map/ppermute | solution.py:522
  (8 other events, 15.8 us)
